TPU v7x, 32 devices: a whole 2x2x4 slice. The times are simulated.
32 devices in a mesh: pipe: 4 (over z), dp: 8 (over y, x, core).
Axes of the slice: x: 2, y: 2, z: 4, core: 2. Of those that a mesh axis runs over, the one named last changes fastest.
Arguments:
- hidden: bfloat16 [256, 2048], P('dp', 'pipe'), may hold values from -6 to 6
- lengths: int32 [32, 4], P('dp'), may hold values from 1 to 3, as said below
- route: int32 [32, 2], P('dp'), may hold values from 0 to 7, as said below
- gain: float32 [8, 2048], P('pipe'), may hold values from 0.5 to 1.5
- key_weight: bfloat16 [8, 2048, 128], P('pipe'), may hold values from -0.125 to 0.125
- value_weight: bfloat16 [8, 2048, 128], P('pipe'), may hold values from -0.125 to 0.125
- cotangent: bfloat16 [256, 2048], P('dp'), may hold values from -6 to 6
Outputs:
- input_grad: bfloat16 [256, 2048], P('dp', 'pipe')
- key_grad: float32 [8, 2048, 128], P('pipe', 'dp')
- value_grad: float32 [8, 2048, 128], P('pipe', 'dp')
Inputs may be any that keep to these rules, and one draw needn't show every extreme that they name: `lengths`: in every micro-batch the first 2 documents fill exactly the first 4 rows, and the others the rest. `route`: for each micro-batch index and each column, the destinations of the 8 groups are all different; and the 8 halves of one group go to 8 different groups.
All inputs are finite; a program needn't handle non-finite values.
Results may differ from a plain program's by a relative error of at most 0.035.
Values may be sent and summed in bfloat16 or wider, within the bound.
No kernel may reach another device: no remote copies, remote signals or barrier semaphores. Data moves between devices by JAX's collectives and lax.ppermute only.
A program may use at most 64 MiB of HBM per device.

v0:
```python
import jax
import jax.numpy as jnp
from jax import lax
from jax.sharding import PartitionSpec as P

ROPE_BASE = 500000.0
EPSILON = 1e-05
NEGATIVE = -1e30


def shifted(value, axis, steps):
    count = lax.axis_size(axis)
    pairs = [(source, (source + steps) % count) for source in range(count)]
    return lax.ppermute(value, axis, pairs)


def spread(value, axis, root):
    mine = lax.axis_index(axis) == root
    return lax.psum(jnp.where(mine, value, jnp.zeros_like(value)), axis)


def document_positions(lengths, row_count):
    doc_ends = jnp.cumsum(lengths, axis=-1)
    doc_starts = doc_ends - lengths
    row_numbers = jnp.arange(row_count, dtype=jnp.int32)
    document = jnp.sum(
        (row_numbers[None, :, None] >= doc_ends[:, None, :-1]).astype(jnp.int32),
        axis=-1,
        dtype=jnp.int32,
    )
    picked = document[:, :, None] == jnp.arange(lengths.shape[1], dtype=jnp.int32)[None, None, :]
    opening = jnp.sum(jnp.where(picked, doc_starts[:, None, :], 0), axis=-1, dtype=jnp.int32)
    return (document, row_numbers[None, :] - opening)


def rotary_tables(position, head_size):
    frequency = ROPE_BASE ** (-(jnp.arange(head_size // 2, dtype=jnp.float32) * 2.0 / head_size))
    angles = position.astype(jnp.float32)[..., None] * frequency
    return (jnp.cos(angles), jnp.sin(angles))


def rotate(vectors, cosine_table, sine_table):
    midpoint = vectors.shape[-1] // 2
    front_half = vectors[..., :midpoint]
    rear_half = vectors[..., midpoint:]
    return jnp.concatenate(
        [
            front_half * cosine_table - rear_half * sine_table,
            rear_half * cosine_table + front_half * sine_table,
        ],
        axis=-1,
    )


def normalize(hidden_in, gain_row):
    return (
        hidden_in
        * lax.rsqrt(jnp.mean(hidden_in * hidden_in, axis=-1, keepdims=True) + EPSILON)
        * gain_row
    )


def attend_layer(
    hidden_in,
    gain_row,
    key_proj,
    value_proj,
    key_zero,
    value_zero,
    document,
    position,
    cosine_table,
    sine_table,
):
    batch_count, row_count, feature_count = hidden_in.shape
    head_size = key_proj.shape[1]
    head_count = feature_count // head_size
    normed = normalize(hidden_in, gain_row)
    packed = normed.astype(jnp.bfloat16)
    flattened = packed.reshape(batch_count * row_count, feature_count)
    key_pre = (
        jnp.dot(flattened, key_proj, preferred_element_type=jnp.float32).reshape(
            batch_count, row_count, head_size
        )
        + key_zero
    )
    value_pre = (
        jnp.dot(flattened, value_proj, preferred_element_type=jnp.float32).reshape(
            batch_count, row_count, head_size
        )
        + value_zero
    )
    queries = rotate(
        normed.reshape(batch_count, row_count, head_count, head_size),
        cosine_table[:, :, None, :],
        sine_table[:, :, None, :],
    ).astype(jnp.bfloat16)
    key_vecs = rotate(key_pre, cosine_table, sine_table).astype(jnp.bfloat16)
    values = value_pre.astype(jnp.bfloat16)
    scores = jnp.einsum(
        "bshd,btd->bhst", queries, key_vecs, preferred_element_type=jnp.float32
    ) * head_size ** (-0.5)
    allowed = (document[:, :, None] == document[:, None, :]) & (
        position[:, None, :] <= position[:, :, None]
    )
    scores = jnp.where(allowed[:, None, :, :], scores, NEGATIVE)
    ceiling = lax.stop_gradient(jnp.max(scores, axis=-1, keepdims=True))
    raised = jnp.exp(scores - ceiling)
    weights = (raised / jnp.sum(raised, axis=-1, keepdims=True)).astype(jnp.bfloat16)
    mixture = jnp.einsum(
        "bhst,btd->bshd", weights, values, preferred_element_type=jnp.float32
    ).reshape(batch_count, row_count, feature_count)
    return hidden_in + mixture


def select_row(array, index_value):
    return lax.dynamic_index_in_dim(array, index_value, 0, keepdims=False)


def section_hop(payload, offset):
    return shifted(payload, "pipe", offset)


def body(hidden, lengths, route, gain, key_weight, value_weight, cotangent):
    group_count = lax.axis_size("dp")
    section_count = lax.axis_size("pipe")
    section_index = lax.axis_index("pipe")
    micro_count, doc_count = lengths.shape
    source_rows, column_count = hidden.shape
    row_count = source_rows // micro_count
    half_rows = row_count // 2
    half_count = 2 * micro_count
    feature_count = gain.shape[1]
    head_size = key_weight.shape[2]
    document, position = document_positions(lengths, row_count)
    row_tags = (document * row_count + position).reshape(half_count, half_rows)
    own_halves = hidden.reshape(half_count, half_rows, column_count)
    route_flat = route.reshape(half_count)
    send_order = jnp.argsort(route_flat)
    outgoing = own_halves[send_order]
    outgoing_tags = row_tags[send_order]
    arrived, arrived_tags, arrived_slots = (
        lax.all_to_all(outgoing, "dp", split_axis=0, concat_axis=0, tiled=True),
        lax.all_to_all(outgoing_tags, "dp", split_axis=0, concat_axis=0, tiled=True),
        lax.all_to_all(send_order, "dp", split_axis=0, concat_axis=0, tiled=True),
    )
    placing = jnp.argsort(arrived_slots)
    received = arrived[placing].reshape(micro_count, row_count, column_count)
    recv_tags = arrived_tags[placing].reshape(micro_count, row_count)
    recv_document = recv_tags // row_count
    recv_position = recv_tags % row_count
    cosine_table, sine_table = rotary_tables(recv_position, head_size)
    full_rows = lax.all_gather(
        received.reshape(micro_count * row_count, column_count), "pipe", axis=1, tiled=True
    )
    full_rows = full_rows.reshape(micro_count, row_count, feature_count).astype(jnp.float32)
    upstream_all = cotangent.reshape(micro_count, row_count, feature_count).astype(jnp.float32)
    tick_count = 2 * section_count + micro_count - 1
    zero_index = jnp.zeros((), jnp.int32)
    zero_terms = jnp.zeros((1, row_count, head_size), jnp.float32)

    def layer_inputs(virtual, micro_index):
        return (
            select_row(gain, virtual),
            select_row(key_weight, virtual),
            select_row(value_weight, virtual),
            lax.dynamic_index_in_dim(recv_document, micro_index, 0, True),
            lax.dynamic_index_in_dim(recv_position, micro_index, 0, True),
            lax.dynamic_index_in_dim(cosine_table, micro_index, 0, True),
            lax.dynamic_index_in_dim(sine_table, micro_index, 0, True),
        )

    def forward_tick(tick, carry):
        incoming, saved = carry
        first_pass = tick - section_index
        second_pass = first_pass - section_count
        use_first = (first_pass >= 0) & (first_pass < micro_count)
        use_second = (second_pass >= 0) & (second_pass < micro_count)
        active = use_first | use_second
        virtual = use_second.astype(jnp.int32)
        micro_index = jnp.clip(jnp.where(use_second, second_pass, first_pass), 0, micro_count - 1)
        current = jnp.where(
            (section_index == 0) & use_first, select_row(full_rows, micro_index), incoming
        )
        gain_row, key_proj, value_proj, doc_rows, pos_rows, cos_rows, sin_rows = layer_inputs(
            virtual, micro_index
        )
        produced = attend_layer(
            current[None],
            gain_row,
            key_proj,
            value_proj,
            zero_terms,
            zero_terms,
            doc_rows,
            pos_rows,
            cos_rows,
            sin_rows,
        )[0]
        previous = saved[virtual, micro_index]
        saved = lax.dynamic_update_slice(
            saved,
            jnp.where(active, current, previous)[None, None],
            (virtual, micro_index, zero_index, zero_index),
        )
        return (section_hop(produced, 1), saved)

    forward_start = (
        jnp.zeros((row_count, feature_count), jnp.float32),
        jnp.zeros((2, micro_count, row_count, feature_count), jnp.float32),
    )
    leftover, saved = lax.fori_loop(0, tick_count, forward_tick, forward_start)

    def backward_tick(tick, carry):
        incoming, terms, input_grads = carry
        second_pass = tick - (section_count - 1 - section_index)
        first_pass = second_pass - section_count
        use_first = (first_pass >= 0) & (first_pass < micro_count)
        use_second = (second_pass >= 0) & (second_pass < micro_count)
        active = use_first | use_second
        virtual = use_second.astype(jnp.int32)
        micro_index = jnp.clip(jnp.where(use_second, second_pass, first_pass), 0, micro_count - 1)
        upstream = jnp.where(
            (section_index == section_count - 1) & use_second,
            select_row(upstream_all, micro_index),
            incoming,
        )
        stored = saved[virtual, micro_index]
        gain_row, key_proj, value_proj, doc_rows, pos_rows, cos_rows, sin_rows = layer_inputs(
            virtual, micro_index
        )

        def pull_layer():

            def local_layer(layer_in, key_zero, value_zero):
                return attend_layer(
                    layer_in,
                    gain_row,
                    key_proj,
                    value_proj,
                    key_zero,
                    value_zero,
                    doc_rows,
                    pos_rows,
                    cos_rows,
                    sin_rows,
                )

            layer_out, pullback = jax.vjp(local_layer, stored[None], zero_terms, zero_terms)
            grad_rows, key_part, value_part = pullback(upstream[None])
            return (
                grad_rows[0],
                jnp.concatenate([key_part[0], value_part[0]], axis=-1).astype(jnp.bfloat16),
            )

        grad_rows, pair_terms = pull_layer()
        previous_terms = terms[virtual, micro_index]
        terms = lax.dynamic_update_slice(
            terms,
            jnp.where(active, pair_terms, previous_terms)[None, None],
            (virtual, micro_index, zero_index, zero_index),
        )
        keep_grad = (section_index == 0) & use_first
        previous_grad = input_grads[micro_index]
        input_grads = lax.dynamic_update_slice(
            input_grads,
            jnp.where(keep_grad, grad_rows, previous_grad)[None],
            (micro_index, zero_index, zero_index),
        )
        return (section_hop(grad_rows, -1), terms, input_grads)

    backward_start = (
        jnp.zeros((row_count, feature_count), jnp.float32),
        jnp.zeros((2, micro_count, row_count, 2 * head_size), jnp.bfloat16),
        jnp.zeros((micro_count, row_count, feature_count), jnp.float32),
    )
    leftover, terms, input_grads = lax.fori_loop(0, tick_count, backward_tick, backward_start)
    packed_all = normalize(saved, gain[:, None, None, :]).astype(jnp.bfloat16)
    summed = lax.psum_scatter(
        jnp.einsum("vmsw,vmsc->wvc", packed_all, terms, preferred_element_type=jnp.float32).reshape(
            feature_count, 4 * head_size
        ),
        "dp",
        scatter_dimension=0,
        tiled=True,
    )
    summed = summed.reshape(feature_count // group_count, 2, 2, head_size)
    key_out = jnp.transpose(summed[:, :, 0, :], (1, 0, 2))
    value_out = jnp.transpose(summed[:, :, 1, :], (1, 0, 2))
    everywhere = spread(input_grads.astype(jnp.bfloat16), "pipe", 0)
    own_grads = lax.dynamic_slice_in_dim(everywhere, section_index * column_count, column_count, 2)
    grad_halves = own_grads.reshape(half_count, half_rows, column_count)
    returning = grad_halves[arrived_slots]
    returned = lax.all_to_all(returning, "dp", split_axis=0, concat_axis=0, tiled=True)
    source_grad = returned[route_flat]
    return (source_grad.reshape(source_rows, column_count), key_out, value_out)


def solution(mesh):
    placed = (
        P("dp", "pipe"),
        P("dp", None),
        P("dp", None),
        P("pipe", None),
        P("pipe", None, None),
        P("pipe", None, None),
        P("dp", None),
    )
    return jax.shard_map(
        body,
        mesh=mesh,
        in_specs=placed,
        out_specs=(P("dp", "pipe"), P("pipe", "dp", None), P("pipe", "dp", None)),
        check_vma=False,
    )
```

profile of v0, /device:TPU:0, one launch (start us, length us, event | category | flops | bytes accessed | tf_op | source)
XLA Modules:
  0.0 380.8 jit_solution(4590609770468937308)
XLA Ops:
  10.5 5.2 %all-to-all-start.1 = ((s32[8,1,1]{2,1,0:T(1,128)}), s32[8,1,1]{2,1,0:T(1,128)S(1)}, u32[]{:S(2)}, u32[]{:S(2)}) async-start(s32[8,1,1]{2,1,0:T(1,128)} %copy.64), calls=%async_computation.1 | async-start | bytes 8192 | tf_op jit(solution)/shard_map/all_to_all | solution.py:145
  21.7 4.2 %all-to-all-start = ((s32[8,1,4]{2,1,0:T(1,128)}), s32[8,1,4]{2,1,0:T(1,128)S(1)}, u32[]{:S(2)}, u32[]{:S(2)}) async-start(s32[8,1,4]{2,1,0:T(1,128)} %bitcast.90), calls=%async_computation | async-start | bytes 8192 | tf_op jit(solution)/shard_map/all_to_all | solution.py:144
  27.2 3.4 all-to-all-done
  30.5 3.3 all-to-all-start.2
  34.7 3.9 %all-to-all-done.2 = bf16[8,4,512]{2,1,0:T(4,128)(2,1)S(1)} async-done(((bf16[8,4,512]{2,1,0:T(4,128)(2,1)}), bf16[8,4,512]{2,1,0:T(4,128)(2,1)S(1)}, u32[]{:S(2)}, u32[]{:S(2)}) %all-to-all-start.2) | async-done | bytes 32800 | tf_op jit(solution)/shard_map/all_to_all | solution.py:143
  39.3 13.7 %all_gather.3 = bf16[32,2048]{1,0:T(8,128)(2,1)S(1)} all-gather(bf16[32,512]{1,0:T(8,128)(2,1)S(1)} %reshape_reshape.3), channel_id=1, replica_groups=mesh['pipe'=4,'dp'=8] {'pipe'}, dimensions={1}, use_global_device_ids=true | all-gather | bytes 163840 | tf_op jit(solution)/shard_map/all_gather | solution.py:153
  53.0 115.4 %while.36 = (s32[]{:T(128)}, f32[8,2048]{1,0:T(8,128)S(1)}, f32[2,4,8,2048]{3,2,1,0:T(8,128)S(1)}, s32[]{:T(128)}, pred[]{:T(512)}, /*index=5*/f32[4,8,2048]{2,1...) while((s32[]{:T(128)}, f32[8,2048]{1,0:T(8,128)S(1)}, ...), condition=%wide.region_9.10_spmd, body=%wide.region_5.9_spmd.sunk | while | flops 9274331 | bytes 2702735 | solution.py:212
  55.9 1.4 convolution_bitcast_fusion.9
  57.4 1.8 collective-permute-start
  59.2 4.3 %collective-permute-done = f32[8,2048]{1,0:T(8,128)S(1)} collective-permute-done((f32[8,2048]{1,0:T(8,128)S(1)}, f32[8,2048]{1,0:T(8,128)S(1)}, u32[]{:S(2)}, u32[]{:S(2)}) %collective-permute-start) | collective-permute-done | bytes 65568 | tf_op jit(solution)/shard_map/while/body/eval_jaxpr/ppermute | solution.py:14
  66.4 1.4 convolution_bitcast_fusion.9
  67.9 6.0 %collective-permute-done = f32[8,2048]{1,0:T(8,128)S(1)} collective-permute-done((f32[8,2048]{1,0:T(8,128)S(1)}, f32[8,2048]{1,0:T(8,128)S(1)}, u32[]{:S(2)}, u32[]{:S(2)}) %collective-permute-start) | collective-permute-done | bytes 65568 | tf_op jit(solution)/shard_map/while/body/eval_jaxpr/ppermute | solution.py:14
  76.8 1.4 convolution_bitcast_fusion.9
  78.3 6.0 %collective-permute-done = f32[8,2048]{1,0:T(8,128)S(1)} collective-permute-done((f32[8,2048]{1,0:T(8,128)S(1)}, f32[8,2048]{1,0:T(8,128)S(1)}, u32[]{:S(2)}, u32[]{:S(2)}) %collective-permute-start) | collective-permute-done | bytes 65568 | tf_op jit(solution)/shard_map/while/body/eval_jaxpr/ppermute | solution.py:14
  87.2 1.4 convolution_bitcast_fusion.9
  88.8 6.0 %collective-permute-done = f32[8,2048]{1,0:T(8,128)S(1)} collective-permute-done((f32[8,2048]{1,0:T(8,128)S(1)}, f32[8,2048]{1,0:T(8,128)S(1)}, u32[]{:S(2)}, u32[]{:S(2)}) %collective-permute-start) | collective-permute-done | bytes 65568 | tf_op jit(solution)/shard_map/while/body/eval_jaxpr/ppermute | solution.py:14
  97.7 1.4 convolution_bitcast_fusion.9
  99.2 6.0 %collective-permute-done = f32[8,2048]{1,0:T(8,128)S(1)} collective-permute-done((f32[8,2048]{1,0:T(8,128)S(1)}, f32[8,2048]{1,0:T(8,128)S(1)}, u32[]{:S(2)}, u32[]{:S(2)}) %collective-permute-start) | collective-permute-done | bytes 65568 | tf_op jit(solution)/shard_map/while/body/eval_jaxpr/ppermute | solution.py:14
  109.6 6.6 %collective-permute-done = f32[8,2048]{1,0:T(8,128)S(1)} collective-permute-done((f32[8,2048]{1,0:T(8,128)S(1)}, f32[8,2048]{1,0:T(8,128)S(1)}, u32[]{:S(2)}, u32[]{:S(2)}) %collective-permute-start) | collective-permute-done | bytes 65568 | tf_op jit(solution)/shard_map/while/body/eval_jaxpr/ppermute | solution.py:14
  120.6 6.0 %collective-permute-done = f32[8,2048]{1,0:T(8,128)S(1)} collective-permute-done((f32[8,2048]{1,0:T(8,128)S(1)}, f32[8,2048]{1,0:T(8,128)S(1)}, u32[]{:S(2)}, u32[]{:S(2)}) %collective-permute-start) | collective-permute-done | bytes 65568 | tf_op jit(solution)/shard_map/while/body/eval_jaxpr/ppermute | solution.py:14
  131.1 6.0 %collective-permute-done = f32[8,2048]{1,0:T(8,128)S(1)} collective-permute-done((f32[8,2048]{1,0:T(8,128)S(1)}, f32[8,2048]{1,0:T(8,128)S(1)}, u32[]{:S(2)}, u32[]{:S(2)}) %collective-permute-start) | collective-permute-done | bytes 65568 | tf_op jit(solution)/shard_map/while/body/eval_jaxpr/ppermute | solution.py:14
  140.0 1.4 convolution_bitcast_fusion.9
  141.5 6.0 %collective-permute-done = f32[8,2048]{1,0:T(8,128)S(1)} collective-permute-done((f32[8,2048]{1,0:T(8,128)S(1)}, f32[8,2048]{1,0:T(8,128)S(1)}, u32[]{:S(2)}, u32[]{:S(2)}) %collective-permute-start) | collective-permute-done | bytes 65568 | tf_op jit(solution)/shard_map/while/body/eval_jaxpr/ppermute | solution.py:14
  150.4 1.4 convolution_bitcast_fusion.9
  151.9 6.0 %collective-permute-done = f32[8,2048]{1,0:T(8,128)S(1)} collective-permute-done((f32[8,2048]{1,0:T(8,128)S(1)}, f32[8,2048]{1,0:T(8,128)S(1)}, u32[]{:S(2)}, u32[]{:S(2)}) %collective-permute-start) | collective-permute-done | bytes 65568 | tf_op jit(solution)/shard_map/while/body/eval_jaxpr/ppermute | solution.py:14
  162.4 6.0 %collective-permute-done = f32[8,2048]{1,0:T(8,128)S(1)} collective-permute-done((f32[8,2048]{1,0:T(8,128)S(1)}, f32[8,2048]{1,0:T(8,128)S(1)}, u32[]{:S(2)}, u32[]{:S(2)}) %collective-permute-start) | collective-permute-done | bytes 65568 | tf_op jit(solution)/shard_map/while/body/eval_jaxpr/ppermute | solution.py:14
  168.6 146.0 %while.37 = (s32[]{:T(128)}, f32[8,2048]{1,0:T(8,128)S(1)}, bf16[2,4,8,256]{3,2,1,0:T(8,128)(2,1)S(1)}, bf16[4,8,2048]{2,1,0:T(8,128)(2,1)S(1)}, s32[]{:T(128)},...) while((s32[]{:T(128)}, f32[8,2048]{1,0:T(8,128)S(1)}, ...), condition=%wide.region_16.17_spmd, body=%wide.region_10.16_spmd.sunk | while | flops 18770692 | bytes 8675411 | solution.py:277
  171.9 1.5 fusion.188
  176.3 4.2 %collective-permute-done.1 = f32[8,2048]{1,0:T(8,128)S(1)} collective-permute-done((f32[8,2048]{1,0:T(8,128)S(1)}, f32[8,2048]{1,0:T(8,128)S(1)}, u32[]{:S(2)}, u32[]{:S(2)}) %collective-permute-start.1) | collective-permute-done | bytes 65568 | tf_op jit(solution)/shard_map/while/body/eval_jaxpr/ppermute | solution.py:14
  183.7 1.5 fusion.188
  187.9 1.9 collective-permute-start.1
  189.8 2.4 collective-permute-done.1
  195.5 1.5 fusion.188
  199.7 3.7 collective-permute-start.1
  203.4 1.8 collective-permute-done.1
  208.5 1.5 fusion.188
  212.7 4.2 %collective-permute-start.1 = (f32[8,2048]{1,0:T(8,128)S(1)}, f32[8,2048]{1,0:T(8,128)S(1)}, u32[]{:S(2)}, u32[]{:S(2)}) collective-permute-start(f32[8,2048]{1,0:T(8,128)S(1)} %get-tuple-element.998), channel_id=1, source_target_pairs={{0,24},{8,0},{16,8},{24,16},{1,25},{9,1},{17,9},{25,17},{2,26},{10... | collective-permute-start | bytes 196616 | tf_op jit(solution)/shard_map/while/body/eval_jaxpr/ppermute | solution.py:14
  217.0 1.8 collective-permute-done.1
  222.1 1.5 fusion.188
  226.3 4.2 %collective-permute-start.1 = (f32[8,2048]{1,0:T(8,128)S(1)}, f32[8,2048]{1,0:T(8,128)S(1)}, u32[]{:S(2)}, u32[]{:S(2)}) collective-permute-start(f32[8,2048]{1,0:T(8,128)S(1)} %get-tuple-element.998), channel_id=1, source_target_pairs={{0,24},{8,0},{16,8},{24,16},{1,25},{9,1},{17,9},{25,17},{2,26},{10... | collective-permute-start | bytes 196616 | tf_op jit(solution)/shard_map/while/body/eval_jaxpr/ppermute | solution.py:14
  230.6 1.8 collective-permute-done.1
  235.7 1.5 fusion.188
  239.9 4.2 %collective-permute-start.1 = (f32[8,2048]{1,0:T(8,128)S(1)}, f32[8,2048]{1,0:T(8,128)S(1)}, u32[]{:S(2)}, u32[]{:S(2)}) collective-permute-start(f32[8,2048]{1,0:T(8,128)S(1)} %get-tuple-element.998), channel_id=1, source_target_pairs={{0,24},{8,0},{16,8},{24,16},{1,25},{9,1},{17,9},{25,17},{2,26},{10... | collective-permute-start | bytes 196616 | tf_op jit(solution)/shard_map/while/body/eval_jaxpr/ppermute | solution.py:14
  244.2 1.8 collective-permute-done.1
  249.3 1.5 fusion.188
  253.5 4.2 %collective-permute-start.1 = (f32[8,2048]{1,0:T(8,128)S(1)}, f32[8,2048]{1,0:T(8,128)S(1)}, u32[]{:S(2)}, u32[]{:S(2)}) collective-permute-start(f32[8,2048]{1,0:T(8,128)S(1)} %get-tuple-element.998), channel_id=1, source_target_pairs={{0,24},{8,0},{16,8},{24,16},{1,25},{9,1},{17,9},{25,17},{2,26},{10... | collective-permute-start | bytes 196616 | tf_op jit(solution)/shard_map/while/body/eval_jaxpr/ppermute | solution.py:14
  257.8 1.8 collective-permute-done.1
  262.9 1.5 fusion.188
  267.1 4.2 %collective-permute-start.1 = (f32[8,2048]{1,0:T(8,128)S(1)}, f32[8,2048]{1,0:T(8,128)S(1)}, u32[]{:S(2)}, u32[]{:S(2)}) collective-permute-start(f32[8,2048]{1,0:T(8,128)S(1)} %get-tuple-element.998), channel_id=1, source_target_pairs={{0,24},{8,0},{16,8},{24,16},{1,25},{9,1},{17,9},{25,17},{2,26},{10... | collective-permute-start | bytes 196616 | tf_op jit(solution)/shard_map/while/body/eval_jaxpr/ppermute | solution.py:14
  271.4 1.8 collective-permute-done.1
  276.5 1.5 fusion.188
  280.7 4.2 %collective-permute-start.1 = (f32[8,2048]{1,0:T(8,128)S(1)}, f32[8,2048]{1,0:T(8,128)S(1)}, u32[]{:S(2)}, u32[]{:S(2)}) collective-permute-start(f32[8,2048]{1,0:T(8,128)S(1)} %get-tuple-element.998), channel_id=1, source_target_pairs={{0,24},{8,0},{16,8},{24,16},{1,25},{9,1},{17,9},{25,17},{2,26},{10... | collective-permute-start | bytes 196616 | tf_op jit(solution)/shard_map/while/body/eval_jaxpr/ppermute | solution.py:14
  285.0 2.4 collective-permute-done.1
  290.6 1.5 fusion.188
  294.8 4.3 %collective-permute-start.1 = (f32[8,2048]{1,0:T(8,128)S(1)}, f32[8,2048]{1,0:T(8,128)S(1)}, u32[]{:S(2)}, u32[]{:S(2)}) collective-permute-start(f32[8,2048]{1,0:T(8,128)S(1)} %get-tuple-element.998), channel_id=1, source_target_pairs={{0,24},{8,0},{16,8},{24,16},{1,25},{9,1},{17,9},{25,17},{2,26},{10... | collective-permute-start | bytes 196616 | tf_op jit(solution)/shard_map/while/body/eval_jaxpr/ppermute | solution.py:14
  299.2 1.8 collective-permute-done.1
  304.3 1.5 fusion.188
  308.5 4.2 %collective-permute-start.1 = (f32[8,2048]{1,0:T(8,128)S(1)}, f32[8,2048]{1,0:T(8,128)S(1)}, u32[]{:S(2)}, u32[]{:S(2)}) collective-permute-start(f32[8,2048]{1,0:T(8,128)S(1)} %get-tuple-element.998), channel_id=1, source_target_pairs={{0,24},{8,0},{16,8},{24,16},{1,25},{9,1},{17,9},{25,17},{2,26},{10... | collective-permute-start | bytes 196616 | tf_op jit(solution)/shard_map/while/body/eval_jaxpr/ppermute | solution.py:14
  312.8 1.8 collective-permute-done.1
  315.4 3.4 fusion.94
  318.9 30.9 %all-reduce.6.cloned.1.call-done = bf16[4,8,2048]{2,1,0:T(8,128)(2,1)} async-done(((bf16[4,8,2048]{2,1,0:T(8,128)(2,1)}), bf16[4,8,2048]{2,1,0:T(8,128)(2,1)}) %all-reduce.6.cloned.1.call-update) | async-done | bytes 131088 | tf_op jit(solution)/shard_map/psum | solution.py:19
  351.8 3.7 all-to-all-start.3
  355.4 4.8 %all-to-all-done.3 = bf16[8,4,512]{2,1,0:T(4,128)(2,1)S(1)} async-done(((bf16[8,4,512]{2,1,0:T(4,128)(2,1)}), bf16[8,4,512]{2,1,0:T(4,128)(2,1)S(1)}, u32[]{:S(2)}, u32[]{:S(2)}) %all-to-all-start.3) | async-done | bytes 32800 | tf_op jit(solution)/shard_map/all_to_all | solution.py:294
  361.5 9.2 %reduce-scatter.2.cloned.1.call-done = f32[256,512]{0,1:T(8,128)} async-done(((f32[2048,512]{0,1:T(8,128)}), f32[256,512]{0,1:T(8,128)}) %reduce-scatter.2.cloned.1.call-update) | async-done | bytes 524304 | tf_op jit(solution)/shard_map/reduce_scatter | solution.py:279
  (582 shorter events, 121.1 us)
Async XLA Ops:
  10.5 11.2 %all-to-all-start.1 = ((s32[8,1,1]{2,1,0:T(1,128)}), s32[8,1,1]{2,1,0:T(1,128)S(1)}, u32[]{:S(2)}, u32[]{:S(2)}) async-start(s32[8,1,1]{2,1,0:T(1,128)} %copy.64), calls=%async_computation.1 | async-start | bytes 8192 | tf_op jit(solution)/shard_map/all_to_all | solution.py:145
  21.7 8.8 %all-to-all-start = ((s32[8,1,4]{2,1,0:T(1,128)}), s32[8,1,4]{2,1,0:T(1,128)S(1)}, u32[]{:S(2)}, u32[]{:S(2)}) async-start(s32[8,1,4]{2,1,0:T(1,128)} %bitcast.90), calls=%async_computation | async-start | bytes 8192 | tf_op jit(solution)/shard_map/all_to_all | solution.py:144
  30.5 8.1 %all-to-all-start.2 = ((bf16[8,4,512]{2,1,0:T(4,128)(2,1)}), bf16[8,4,512]{2,1,0:T(4,128)(2,1)S(1)}, u32[]{:S(2)}, u32[]{:S(2)}) async-start(bf16[8,4,512]{2,1,0:T(4,128)(2,1)} %gather_fusion.2), calls=%async_computation.2 | async-start | bytes 65536 | tf_op jit(solution)/shard_map/all_to_all | solution.py:143
  33.9 315.9 %all-reduce.6.cloned.1.call-start = ((), (), s32[]{:S(2)}) async-start(), calls=%async_computation.5 | async-start | bytes 262144 | tf_op jit(solution)/shard_map/psum | solution.py:19
  57.4 6.1 %collective-permute-start = (f32[8,2048]{1,0:T(8,128)S(1)}, f32[8,2048]{1,0:T(8,128)S(1)}, u32[]{:S(2)}, u32[]{:S(2)}) collective-permute-start(f32[8,2048]{1,0:T(8,128)S(1)} %bitcast_add_fusion.2), channel_id=1, source_target_pairs={{0,8},{8,16},{16,24},{24,0},{1,9},{9,17},{17,25},{25,1},{2,10},{10... | collective-permute-start | bytes 196616 | tf_op jit(solution)/shard_map/while/body/eval_jaxpr/ppermute | solution.py:14
  67.8 6.1 %collective-permute-start = (f32[8,2048]{1,0:T(8,128)S(1)}, f32[8,2048]{1,0:T(8,128)S(1)}, u32[]{:S(2)}, u32[]{:S(2)}) collective-permute-start(f32[8,2048]{1,0:T(8,128)S(1)} %bitcast_add_fusion.2), channel_id=1, source_target_pairs={{0,8},{8,16},{16,24},{24,0},{1,9},{9,17},{17,25},{25,1},{2,10},{10... | collective-permute-start | bytes 196616 | tf_op jit(solution)/shard_map/while/body/eval_jaxpr/ppermute | solution.py:14
  78.2 6.1 %collective-permute-start = (f32[8,2048]{1,0:T(8,128)S(1)}, f32[8,2048]{1,0:T(8,128)S(1)}, u32[]{:S(2)}, u32[]{:S(2)}) collective-permute-start(f32[8,2048]{1,0:T(8,128)S(1)} %bitcast_add_fusion.2), channel_id=1, source_target_pairs={{0,8},{8,16},{16,24},{24,0},{1,9},{9,17},{17,25},{25,1},{2,10},{10... | collective-permute-start | bytes 196616 | tf_op jit(solution)/shard_map/while/body/eval_jaxpr/ppermute | solution.py:14
  88.7 6.1 %collective-permute-start = (f32[8,2048]{1,0:T(8,128)S(1)}, f32[8,2048]{1,0:T(8,128)S(1)}, u32[]{:S(2)}, u32[]{:S(2)}) collective-permute-start(f32[8,2048]{1,0:T(8,128)S(1)} %bitcast_add_fusion.2), channel_id=1, source_target_pairs={{0,8},{8,16},{16,24},{24,0},{1,9},{9,17},{17,25},{25,1},{2,10},{10... | collective-permute-start | bytes 196616 | tf_op jit(solution)/shard_map/while/body/eval_jaxpr/ppermute | solution.py:14
  99.1 6.1 %collective-permute-start = (f32[8,2048]{1,0:T(8,128)S(1)}, f32[8,2048]{1,0:T(8,128)S(1)}, u32[]{:S(2)}, u32[]{:S(2)}) collective-permute-start(f32[8,2048]{1,0:T(8,128)S(1)} %bitcast_add_fusion.2), channel_id=1, source_target_pairs={{0,8},{8,16},{16,24},{24,0},{1,9},{9,17},{17,25},{25,1},{2,10},{10... | collective-permute-start | bytes 196616 | tf_op jit(solution)/shard_map/while/body/eval_jaxpr/ppermute | solution.py:14
  109.6 6.7 %collective-permute-start = (f32[8,2048]{1,0:T(8,128)S(1)}, f32[8,2048]{1,0:T(8,128)S(1)}, u32[]{:S(2)}, u32[]{:S(2)}) collective-permute-start(f32[8,2048]{1,0:T(8,128)S(1)} %bitcast_add_fusion.2), channel_id=1, source_target_pairs={{0,8},{8,16},{16,24},{24,0},{1,9},{9,17},{17,25},{25,1},{2,10},{10... | collective-permute-start | bytes 196616 | tf_op jit(solution)/shard_map/while/body/eval_jaxpr/ppermute | solution.py:14
  120.5 6.1 %collective-permute-start = (f32[8,2048]{1,0:T(8,128)S(1)}, f32[8,2048]{1,0:T(8,128)S(1)}, u32[]{:S(2)}, u32[]{:S(2)}) collective-permute-start(f32[8,2048]{1,0:T(8,128)S(1)} %bitcast_add_fusion.2), channel_id=1, source_target_pairs={{0,8},{8,16},{16,24},{24,0},{1,9},{9,17},{17,25},{25,1},{2,10},{10... | collective-permute-start | bytes 196616 | tf_op jit(solution)/shard_map/while/body/eval_jaxpr/ppermute | solution.py:14
  131.0 6.1 %collective-permute-start = (f32[8,2048]{1,0:T(8,128)S(1)}, f32[8,2048]{1,0:T(8,128)S(1)}, u32[]{:S(2)}, u32[]{:S(2)}) collective-permute-start(f32[8,2048]{1,0:T(8,128)S(1)} %bitcast_add_fusion.2), channel_id=1, source_target_pairs={{0,8},{8,16},{16,24},{24,0},{1,9},{9,17},{17,25},{25,1},{2,10},{10... | collective-permute-start | bytes 196616 | tf_op jit(solution)/shard_map/while/body/eval_jaxpr/ppermute | solution.py:14
  141.4 6.1 %collective-permute-start = (f32[8,2048]{1,0:T(8,128)S(1)}, f32[8,2048]{1,0:T(8,128)S(1)}, u32[]{:S(2)}, u32[]{:S(2)}) collective-permute-start(f32[8,2048]{1,0:T(8,128)S(1)} %bitcast_add_fusion.2), channel_id=1, source_target_pairs={{0,8},{8,16},{16,24},{24,0},{1,9},{9,17},{17,25},{25,1},{2,10},{10... | collective-permute-start | bytes 196616 | tf_op jit(solution)/shard_map/while/body/eval_jaxpr/ppermute | solution.py:14
  151.9 6.1 %collective-permute-start = (f32[8,2048]{1,0:T(8,128)S(1)}, f32[8,2048]{1,0:T(8,128)S(1)}, u32[]{:S(2)}, u32[]{:S(2)}) collective-permute-start(f32[8,2048]{1,0:T(8,128)S(1)} %bitcast_add_fusion.2), channel_id=1, source_target_pairs={{0,8},{8,16},{16,24},{24,0},{1,9},{9,17},{17,25},{25,1},{2,10},{10... | collective-permute-start | bytes 196616 | tf_op jit(solution)/shard_map/while/body/eval_jaxpr/ppermute | solution.py:14
  162.3 6.1 %collective-permute-start = (f32[8,2048]{1,0:T(8,128)S(1)}, f32[8,2048]{1,0:T(8,128)S(1)}, u32[]{:S(2)}, u32[]{:S(2)}) collective-permute-start(f32[8,2048]{1,0:T(8,128)S(1)} %bitcast_add_fusion.2), channel_id=1, source_target_pairs={{0,8},{8,16},{16,24},{24,0},{1,9},{9,17},{17,25},{25,1},{2,10},{10... | collective-permute-start | bytes 196616 | tf_op jit(solution)/shard_map/while/body/eval_jaxpr/ppermute | solution.py:14
  168.6 7.0 %copy-start = (bf16[2,2048,128]{2,1,0:T(8,128)(2,1)S(1)}, bf16[2,2048,128]{2,1,0:T(8,128)(2,1)}, u32[]{:S(2)}) copy-start(bf16[2,2048,128]{2,1,0:T(8,128)(2,1)} %get-tuple-element.1112) | copy-start | bytes 3145732 | tf_op jit(solution)/shard_map/while
  176.1 4.3 %collective-permute-start.1 = (f32[8,2048]{1,0:T(8,128)S(1)}, f32[8,2048]{1,0:T(8,128)S(1)}, u32[]{:S(2)}, u32[]{:S(2)}) collective-permute-start(f32[8,2048]{1,0:T(8,128)S(1)} %get-tuple-element.998), channel_id=1, source_target_pairs={{0,24},{8,0},{16,8},{24,16},{1,25},{9,1},{17,9},{25,17},{2,26},{10... | collective-permute-start | bytes 196616 | tf_op jit(solution)/shard_map/while/body/eval_jaxpr/ppermute | solution.py:14
  180.4 7.0 %copy-start = (bf16[2,2048,128]{2,1,0:T(8,128)(2,1)S(1)}, bf16[2,2048,128]{2,1,0:T(8,128)(2,1)}, u32[]{:S(2)}) copy-start(bf16[2,2048,128]{2,1,0:T(8,128)(2,1)} %get-tuple-element.1112) | copy-start | bytes 3145732 | tf_op jit(solution)/shard_map/while
  187.9 4.3 %collective-permute-start.1 = (f32[8,2048]{1,0:T(8,128)S(1)}, f32[8,2048]{1,0:T(8,128)S(1)}, u32[]{:S(2)}, u32[]{:S(2)}) collective-permute-start(f32[8,2048]{1,0:T(8,128)S(1)} %get-tuple-element.998), channel_id=1, source_target_pairs={{0,24},{8,0},{16,8},{24,16},{1,25},{9,1},{17,9},{25,17},{2,26},{10... | collective-permute-start | bytes 196616 | tf_op jit(solution)/shard_map/while/body/eval_jaxpr/ppermute | solution.py:14
  192.2 7.0 %copy-start = (bf16[2,2048,128]{2,1,0:T(8,128)(2,1)S(1)}, bf16[2,2048,128]{2,1,0:T(8,128)(2,1)}, u32[]{:S(2)}) copy-start(bf16[2,2048,128]{2,1,0:T(8,128)(2,1)} %get-tuple-element.1112) | copy-start | bytes 3145732 | tf_op jit(solution)/shard_map/while
  199.7 5.6 %collective-permute-start.1 = (f32[8,2048]{1,0:T(8,128)S(1)}, f32[8,2048]{1,0:T(8,128)S(1)}, u32[]{:S(2)}, u32[]{:S(2)}) collective-permute-start(f32[8,2048]{1,0:T(8,128)S(1)} %get-tuple-element.998), channel_id=1, source_target_pairs={{0,24},{8,0},{16,8},{24,16},{1,25},{9,1},{17,9},{25,17},{2,26},{10... | collective-permute-start | bytes 196616 | tf_op jit(solution)/shard_map/while/body/eval_jaxpr/ppermute | solution.py:14
  205.2 7.0 %copy-start = (bf16[2,2048,128]{2,1,0:T(8,128)(2,1)S(1)}, bf16[2,2048,128]{2,1,0:T(8,128)(2,1)}, u32[]{:S(2)}) copy-start(bf16[2,2048,128]{2,1,0:T(8,128)(2,1)} %get-tuple-element.1112) | copy-start | bytes 3145732 | tf_op jit(solution)/shard_map/while
  212.7 6.1 %collective-permute-start.1 = (f32[8,2048]{1,0:T(8,128)S(1)}, f32[8,2048]{1,0:T(8,128)S(1)}, u32[]{:S(2)}, u32[]{:S(2)}) collective-permute-start(f32[8,2048]{1,0:T(8,128)S(1)} %get-tuple-element.998), channel_id=1, source_target_pairs={{0,24},{8,0},{16,8},{24,16},{1,25},{9,1},{17,9},{25,17},{2,26},{10... | collective-permute-start | bytes 196616 | tf_op jit(solution)/shard_map/while/body/eval_jaxpr/ppermute | solution.py:14
  218.8 7.0 %copy-start = (bf16[2,2048,128]{2,1,0:T(8,128)(2,1)S(1)}, bf16[2,2048,128]{2,1,0:T(8,128)(2,1)}, u32[]{:S(2)}) copy-start(bf16[2,2048,128]{2,1,0:T(8,128)(2,1)} %get-tuple-element.1112) | copy-start | bytes 3145732 | tf_op jit(solution)/shard_map/while
  226.3 6.1 %collective-permute-start.1 = (f32[8,2048]{1,0:T(8,128)S(1)}, f32[8,2048]{1,0:T(8,128)S(1)}, u32[]{:S(2)}, u32[]{:S(2)}) collective-permute-start(f32[8,2048]{1,0:T(8,128)S(1)} %get-tuple-element.998), channel_id=1, source_target_pairs={{0,24},{8,0},{16,8},{24,16},{1,25},{9,1},{17,9},{25,17},{2,26},{10... | collective-permute-start | bytes 196616 | tf_op jit(solution)/shard_map/while/body/eval_jaxpr/ppermute | solution.py:14
  232.4 7.0 %copy-start = (bf16[2,2048,128]{2,1,0:T(8,128)(2,1)S(1)}, bf16[2,2048,128]{2,1,0:T(8,128)(2,1)}, u32[]{:S(2)}) copy-start(bf16[2,2048,128]{2,1,0:T(8,128)(2,1)} %get-tuple-element.1112) | copy-start | bytes 3145732 | tf_op jit(solution)/shard_map/while
  239.9 6.1 %collective-permute-start.1 = (f32[8,2048]{1,0:T(8,128)S(1)}, f32[8,2048]{1,0:T(8,128)S(1)}, u32[]{:S(2)}, u32[]{:S(2)}) collective-permute-start(f32[8,2048]{1,0:T(8,128)S(1)} %get-tuple-element.998), channel_id=1, source_target_pairs={{0,24},{8,0},{16,8},{24,16},{1,25},{9,1},{17,9},{25,17},{2,26},{10... | collective-permute-start | bytes 196616 | tf_op jit(solution)/shard_map/while/body/eval_jaxpr/ppermute | solution.py:14
  246.0 7.0 %copy-start = (bf16[2,2048,128]{2,1,0:T(8,128)(2,1)S(1)}, bf16[2,2048,128]{2,1,0:T(8,128)(2,1)}, u32[]{:S(2)}) copy-start(bf16[2,2048,128]{2,1,0:T(8,128)(2,1)} %get-tuple-element.1112) | copy-start | bytes 3145732 | tf_op jit(solution)/shard_map/while
  253.5 6.1 %collective-permute-start.1 = (f32[8,2048]{1,0:T(8,128)S(1)}, f32[8,2048]{1,0:T(8,128)S(1)}, u32[]{:S(2)}, u32[]{:S(2)}) collective-permute-start(f32[8,2048]{1,0:T(8,128)S(1)} %get-tuple-element.998), channel_id=1, source_target_pairs={{0,24},{8,0},{16,8},{24,16},{1,25},{9,1},{17,9},{25,17},{2,26},{10... | collective-permute-start | bytes 196616 | tf_op jit(solution)/shard_map/while/body/eval_jaxpr/ppermute | solution.py:14
  259.6 7.0 %copy-start = (bf16[2,2048,128]{2,1,0:T(8,128)(2,1)S(1)}, bf16[2,2048,128]{2,1,0:T(8,128)(2,1)}, u32[]{:S(2)}) copy-start(bf16[2,2048,128]{2,1,0:T(8,128)(2,1)} %get-tuple-element.1112) | copy-start | bytes 3145732 | tf_op jit(solution)/shard_map/while
  267.1 6.1 %collective-permute-start.1 = (f32[8,2048]{1,0:T(8,128)S(1)}, f32[8,2048]{1,0:T(8,128)S(1)}, u32[]{:S(2)}, u32[]{:S(2)}) collective-permute-start(f32[8,2048]{1,0:T(8,128)S(1)} %get-tuple-element.998), channel_id=1, source_target_pairs={{0,24},{8,0},{16,8},{24,16},{1,25},{9,1},{17,9},{25,17},{2,26},{10... | collective-permute-start | bytes 196616 | tf_op jit(solution)/shard_map/while/body/eval_jaxpr/ppermute | solution.py:14
  273.2 7.0 %copy-start = (bf16[2,2048,128]{2,1,0:T(8,128)(2,1)S(1)}, bf16[2,2048,128]{2,1,0:T(8,128)(2,1)}, u32[]{:S(2)}) copy-start(bf16[2,2048,128]{2,1,0:T(8,128)(2,1)} %get-tuple-element.1112) | copy-start | bytes 3145732 | tf_op jit(solution)/shard_map/while
  280.7 6.7 %collective-permute-start.1 = (f32[8,2048]{1,0:T(8,128)S(1)}, f32[8,2048]{1,0:T(8,128)S(1)}, u32[]{:S(2)}, u32[]{:S(2)}) collective-permute-start(f32[8,2048]{1,0:T(8,128)S(1)} %get-tuple-element.998), channel_id=1, source_target_pairs={{0,24},{8,0},{16,8},{24,16},{1,25},{9,1},{17,9},{25,17},{2,26},{10... | collective-permute-start | bytes 196616 | tf_op jit(solution)/shard_map/while/body/eval_jaxpr/ppermute | solution.py:14
  287.3 7.0 %copy-start = (bf16[2,2048,128]{2,1,0:T(8,128)(2,1)S(1)}, bf16[2,2048,128]{2,1,0:T(8,128)(2,1)}, u32[]{:S(2)}) copy-start(bf16[2,2048,128]{2,1,0:T(8,128)(2,1)} %get-tuple-element.1112) | copy-start | bytes 3145732 | tf_op jit(solution)/shard_map/while
  294.8 6.2 %collective-permute-start.1 = (f32[8,2048]{1,0:T(8,128)S(1)}, f32[8,2048]{1,0:T(8,128)S(1)}, u32[]{:S(2)}, u32[]{:S(2)}) collective-permute-start(f32[8,2048]{1,0:T(8,128)S(1)} %get-tuple-element.998), channel_id=1, source_target_pairs={{0,24},{8,0},{16,8},{24,16},{1,25},{9,1},{17,9},{25,17},{2,26},{10... | collective-permute-start | bytes 196616 | tf_op jit(solution)/shard_map/while/body/eval_jaxpr/ppermute | solution.py:14
  301.0 7.0 %copy-start = (bf16[2,2048,128]{2,1,0:T(8,128)(2,1)S(1)}, bf16[2,2048,128]{2,1,0:T(8,128)(2,1)}, u32[]{:S(2)}) copy-start(bf16[2,2048,128]{2,1,0:T(8,128)(2,1)} %get-tuple-element.1112) | copy-start | bytes 3145732 | tf_op jit(solution)/shard_map/while
  308.5 6.1 %collective-permute-start.1 = (f32[8,2048]{1,0:T(8,128)S(1)}, f32[8,2048]{1,0:T(8,128)S(1)}, u32[]{:S(2)}, u32[]{:S(2)}) collective-permute-start(f32[8,2048]{1,0:T(8,128)S(1)} %get-tuple-element.998), channel_id=1, source_target_pairs={{0,24},{8,0},{16,8},{24,16},{1,25},{9,1},{17,9},{25,17},{2,26},{10... | collective-permute-start | bytes 196616 | tf_op jit(solution)/shard_map/while/body/eval_jaxpr/ppermute | solution.py:14
  315.3 55.3 %reduce-scatter.2.cloned.1.call-start = ((), (), s32[]{:S(2)}) async-start(), calls=%async_computation.6 | async-start | bytes 4718592 | tf_op jit(solution)/shard_map/reduce_scatter | solution.py:279
  351.8 8.5 %all-to-all-start.3 = ((bf16[8,4,512]{2,1,0:T(4,128)(2,1)}), bf16[8,4,512]{2,1,0:T(4,128)(2,1)S(1)}, u32[]{:S(2)}, u32[]{:S(2)}) async-start(bf16[8,4,512]{2,1,0:T(4,128)(2,1)} %gather_fusion.4), calls=%async_computation.3 | async-start | bytes 65536 | tf_op jit(solution)/shard_map/all_to_all | solution.py:294
Sparse Core Ops, SparseCore 0:
  315.4 34.2 all-reduce.5
Sparse Core Ops, SparseCore 1:
  319.5 51.1 reduce-scatter.1
where the time goes:
time: 385 us; the launch traced here: 381 us
  waiting for transfers between devices  141 us (37%)
  matrix products  94.7 us (25%)
  starting transfers between devices  58.2 us (15%)
  local copies, waits for them, and re-layouts  31.2 us (8%)
  other arithmetic  24.2 us (6%)
  between operations  15.6 us (4%)
  blocking collectives  13.7 us (4%)
    ppermute x22, waiting for transfers between devices, shifted(): return lax.ppermute(value, axis, pairs)  88.8 us
    dot_general x33, matrix products, attend_layer(): jnp.dot(flattened, key_proj, preferred_element_type=jnp.float32)  42.5 us
    ppermute x22, starting transfers between devices, shifted(): return lax.ppermute(value, axis, pairs)  41.8 us
    dot_general x33, matrix products, attend_layer(): jnp.einsum('bhst,btd->bshd', weights, values, preferred_element_type=jnp....  34.2 us
    psum x1, waiting for transfers between devices, spread(): return lax.psum(jnp.where(mine, value, jnp.zeros_like(value)), axis)  30.9 us
    dynamic_slice x22, local copies, waits for them, and re-layouts, select_row(): return lax.dynamic_index_in_dim(array, index_value, 0, keepdims=False)  16.9 us
    all_gather x1, blocking collectives, body(): lax.all_gather(received.reshape(micro_count * row_count, column_count), '...  13.7 us
    dot_general x44, matrix products, attend_layer(): jnp.einsum('bshd,btd->bhst', queries, key_vecs, preferred_element_type=jn...  10.5 us
  transfers between devices with their start and end apart: 28, of which 27 were waited for; matrix products, arithmetic and copies ran while one was open for 4% of the time, Pallas kernels for 0%

commit v1 on v0

v1 whole, which is shorter than its diff:
```python
import functools

import jax
import jax.numpy as jnp
from jax import lax
from jax.experimental import pallas as pl
from jax.experimental.pallas import tpu as pltpu
from jax.sharding import PartitionSpec as P

ROPE_BASE = 500000.0
EPSILON = 1e-05
NEGATIVE = -1e30
LANES = 128
SAVED = 5
VMEM_BYTES = 56 * 1024 * 1024


def iota(shape, dim):
    return lax.broadcasted_iota(jnp.int32, shape, dim)


def as_float(flags):
    return jnp.where(flags, 1.0, 0.0).astype(jnp.float32)


def contract(left, right, left_dim, right_dim):
    return lax.dot_general(
        left, right, (((left_dim,), (right_dim,)), ((), ())), preferred_element_type=jnp.float32
    )


def pieces_of(column_count):
    return 2 if column_count % (2 * LANES) == 0 else 1


def pack_kernel(lengths_ref, route_ref, hidden_ref, out_ref, *, groups):
    micro_count, doc_count = lengths_ref.shape
    source_rows, column_count = hidden_ref.shape
    row_count = source_rows // micro_count
    half = row_count // 2
    pieces = pieces_of(column_count)
    width = column_count // pieces
    total = out_ref.shape[0]

    shape = (source_rows, LANES)
    batch, offset = iota(shape, 0) // row_count, iota(shape, 0) % row_count
    document = jnp.zeros(shape, jnp.int32)
    opening = jnp.zeros(shape, jnp.int32)
    for micro in range(micro_count):
        end = jnp.int32(0)
        for doc in range(doc_count - 1):
            end = end + lengths_ref[micro, doc]
            passed = (batch == micro) & (offset >= end)
            document = document + jnp.where(passed, 1, 0)
            opening = jnp.where(passed, end, opening)
    lane = iota(shape, 1)
    first = offset < half
    tags = jnp.where(
        lane == 0,
        jnp.where(first, 1, 0),
        jnp.where(
            lane == 1,
            jnp.where(first, 0, 1),
            jnp.where(lane == 2, document, jnp.where(lane == 3, offset - opening, 0)),
        ),
    )
    tags = tags.astype(jnp.float32).astype(jnp.bfloat16)

    shape = (total, source_rows)
    row, source = iota(shape, 0), iota(shape, 1)
    slot = source // half
    target = jnp.full(shape, -1, jnp.int32)
    for micro in range(micro_count):
        for side in range(2):
            target = jnp.where(
                slot == 2 * micro + side, micro * groups + route_ref[micro, side], target
            )
    going = target == row // row_count
    inner, wanted = row % row_count, source % half
    packed = jnp.zeros((total, width), jnp.float32)
    for piece in range(pieces):
        chosen = as_float(going & (inner == piece * half + wanted)).astype(jnp.bfloat16)
        packed += contract(chosen, hidden_ref[:, piece * width : (piece + 1) * width], 1, 0)
    chosen = as_float(going & (inner % half == wanted)).astype(jnp.bfloat16)
    out_ref[:, :width] = packed.astype(jnp.bfloat16)
    out_ref[:, width:] = contract(chosen, tags, 1, 0).astype(jnp.bfloat16)


def choosers(tags, row_count, pieces):
    half = row_count // 2
    shape = (tags.shape[0], row_count)
    inner, wanted = iota(shape, 0) % row_count, iota(shape, 1)
    came = jnp.where(wanted < half, tags[:, 0:1], tags[:, 1:2])
    return [
        jnp.where(inner == piece * half + wanted % half, came, 0.0).astype(jnp.bfloat16)
        for piece in range(pieces)
    ]


def turned(vector, cosine, sine):
    return vector * cosine + pltpu.roll(vector, vector.shape[1] // 2, 1) * sine


def heads_down(rows, head_size):
    count = rows.shape[1] // head_size
    return jnp.concatenate(
        [rows[:, head * head_size : (head + 1) * head_size] for head in range(count)], axis=0
    )


def heads_across(stacked, row_count):
    count = stacked.shape[0] // row_count
    return jnp.concatenate(
        [stacked[head * row_count : (head + 1) * row_count] for head in range(count)], axis=1
    )


def forward_layer(rows, gain_row, weight, cosine, sine, allowed):
    row_count, feature_count = rows.shape
    head_size = cosine.shape[1]
    scale = lax.rsqrt(jnp.sum(rows * rows, axis=1, keepdims=True) / feature_count + EPSILON)
    normed = rows * scale * gain_row
    pair = jnp.dot(normed.astype(jnp.bfloat16), weight, preferred_element_type=jnp.float32)
    stacked = heads_down(normed, head_size)
    repeats = stacked.shape[0] // row_count
    queries = turned(
        stacked, jnp.tile(cosine, (repeats, 1)), jnp.tile(sine, (repeats, 1))
    ).astype(jnp.bfloat16)
    keys = turned(pair[:, :head_size], cosine, sine).astype(jnp.bfloat16)
    values = pair[:, head_size:].astype(jnp.bfloat16)
    scores = contract(keys, queries, 1, 1) * head_size ** (-0.5)
    scores = jnp.where(allowed, scores, NEGATIVE)
    raised = jnp.exp(scores - jnp.max(scores, axis=0, keepdims=True))
    weights = raised / jnp.sum(raised, axis=0, keepdims=True)
    mixed = contract(weights.astype(jnp.bfloat16), values, 0, 0)
    kept = (scale, queries, keys, values, weights)
    return rows + heads_across(mixed, row_count), kept


def backward_layer(upstream, rows, gain_row, weight, cosine, sine, kept):
    scale, queries, keys, values, weights = kept
    row_count, feature_count = rows.shape
    head_size = cosine.shape[1]
    stacked = heads_down(upstream, head_size).astype(jnp.bfloat16)
    d_weights = contract(values, stacked, 1, 1).astype(jnp.bfloat16).astype(jnp.float32)
    d_values = contract(weights.astype(jnp.bfloat16), stacked, 1, 0)
    d_scores = weights * (d_weights - jnp.sum(d_weights * weights, axis=0, keepdims=True))
    d_scores = (d_scores * head_size ** (-0.5)).astype(jnp.bfloat16)
    d_keys = contract(d_scores, queries, 1, 0)
    terms = jnp.concatenate([turned(d_keys, cosine, -sine), d_values], axis=1)
    terms = terms.astype(jnp.bfloat16)
    d_queries = contract(d_scores, keys, 0, 0)
    repeats = stacked.shape[0] // row_count
    d_queries = turned(d_queries, jnp.tile(cosine, (repeats, 1)), jnp.tile(-sine, (repeats, 1)))
    d_normed = contract(terms, weight, 1, 1) + heads_across(d_queries, row_count)
    scaled = d_normed * gain_row
    inner = jnp.sum(scaled * rows, axis=1, keepdims=True) / feature_count
    return upstream + scale * scaled - rows * (scale * scale * scale * inner), terms


def save_layer(index, rows, kept, rows_ref, scale_ref, queries_ref, pair_ref, weights_ref):
    scale, queries, keys, values, weights = kept
    rows_ref[index] = rows
    scale_ref[index] = jnp.broadcast_to(scale, scale_ref.shape[1:])
    queries_ref[index] = queries
    pair_ref[index] = jnp.concatenate([keys, values], axis=1).astype(jnp.float32)
    weights_ref[index] = weights


def load_layer(index, rows_ref, scale_ref, queries_ref, pair_ref, weights_ref):
    pair = pair_ref[index].astype(jnp.bfloat16)
    head_size = pair.shape[1] // 2
    kept = (
        scale_ref[index][:, 0:1],
        queries_ref[index],
        pair[:, :head_size],
        pair[:, head_size:],
        weights_ref[index],
    )
    return rows_ref[index], kept


def saved_shapes(count, row_count, feature_count, head_size):
    heads = feature_count // head_size
    return [
        jax.ShapeDtypeStruct((count, row_count, feature_count), jnp.float32),
        jax.ShapeDtypeStruct((count, row_count, LANES), jnp.float32),
        jax.ShapeDtypeStruct((count, heads * row_count, head_size), jnp.bfloat16),
        jax.ShapeDtypeStruct((count, row_count, 2 * head_size), jnp.float32),
        jax.ShapeDtypeStruct((count, row_count, heads * row_count), jnp.float32),
    ]


def repeat_steps(count, step, carry):
    if count <= 8:
        for index in range(count):
            carry = step(index, carry)
        return carry
    return lax.fori_loop(0, count, step, carry)


def forward_steps(rows, own, gain_ref, weight_ref, tables, saved):
    cosine, sine, allowed = tables

    def step(index, rows):
        place = lax.bitwise_xor(own, index)
        gain_row = gain_ref[pl.ds(place, 1), :]
        after, kept = forward_layer(rows, gain_row, weight_ref[place], cosine, sine, allowed)
        save_layer(index, rows, kept, *saved)
        return after

    return repeat_steps(weight_ref.shape[0], step, rows)


def backward_steps(upstream, own, gain_ref, weight_ref, tables, saved, out_ref, groups):
    cosine, sine, _ = tables
    count = weight_ref.shape[0]
    share = weight_ref.shape[1] // groups
    term_width = weight_ref.shape[2]
    grad_width = out_ref.shape[3] - share - term_width

    def step(back, upstream):
        index = count - 1 - back
        place = lax.bitwise_xor(own, index)
        gain_row = gain_ref[pl.ds(place, 1), :]
        rows, kept = load_layer(index, *saved)
        before, terms = backward_layer(
            upstream, rows, gain_row, weight_ref[place], cosine, sine, kept
        )
        packed = (rows * kept[0] * gain_row).astype(jnp.bfloat16)
        for group in range(groups):
            out_ref[index, group, :, :term_width] = terms
            out_ref[index, group, :, term_width + grad_width :] = packed[
                :, group * share : (group + 1) * share
            ]
        return before

    return repeat_steps(count, step, upstream)


def fill(turn, pieces, gain_ref, weight_ref, sems):
    gains, key_ref, value_ref, shares = pieces
    groups = len(shares)
    share = weight_ref.shape[1] // groups
    head_size = key_ref.shape[2]
    own = lax.axis_index("dp")
    copies = [
        pltpu.make_async_copy(key_ref.at[turn], weight_ref.at[0, :, :head_size], sems.at[groups]),
        pltpu.make_async_copy(
            value_ref.at[turn], weight_ref.at[0, :, head_size:], sems.at[groups + 1]
        ),
    ]
    for offset, ref in enumerate(shares):
        start = pl.multiple_of(lax.bitwise_xor(own, offset) * share, share)
        copies.append(
            pltpu.make_async_copy(
                ref, weight_ref.at[pl.ds(1, ref.shape[0]), pl.ds(start, share)], sems.at[offset]
            )
        )
    for copy in copies:
        copy.start()
    for place, ref in enumerate(gains):
        gain_ref[pl.ds(place, 1), :] = ref[pl.ds(turn, 1), :]
    return copies


def first_kernel(arrived_ref, *rest, sections, groups, turn):
    pieces, rest = split_pieces(rest, sections, groups)
    rows_ref, table_ref, tags_ref, *saved, gain_ref, weight_ref, sems = rest
    copies = fill(turn, pieces, gain_ref, weight_ref, sems)
    row_count, feature_count = rows_ref.shape
    head_size = weight_ref.shape[2] // 2
    column_count = feature_count // sections
    pieces = pieces_of(column_count)
    width = column_count // pieces
    block = arrived_ref.shape[0] // sections
    tags = arrived_ref[:block, width:].astype(jnp.float32)
    tags_ref[...] = tags
    chosen = choosers(tags, row_count, pieces)
    cuts = []
    for section in range(sections):
        part = arrived_ref[section * block : (section + 1) * block, :width]
        cuts += [contract(chooser, part, 0, 0) for chooser in chosen]
    rows = jnp.concatenate(cuts, axis=1)
    own = contract(chosen[0], tags.astype(jnp.bfloat16), 0, 0)
    document, position = own[:, 2:3], own[:, 3:4]
    lane = iota((1, head_size), 1)
    middle = head_size // 2
    exponent = (lane % middle).astype(jnp.float32) * (2.0 / head_size)
    angles = position * jnp.exp(exponent * -jnp.log(jnp.float32(ROPE_BASE)))
    cosine = jnp.cos(angles)
    sine = jnp.where(lane < middle, -jnp.sin(angles), jnp.sin(angles))
    shape = (row_count, row_count * feature_count // head_size)
    pick = as_float(iota(shape, 1) % row_count == iota(shape, 0))
    document_across = jnp.sum(document * pick, axis=0, keepdims=True)
    position_across = jnp.sum(position * pick, axis=0, keepdims=True)
    allowed = (document == document_across) & (position <= position_across)
    table_ref[0, :, :head_size] = cosine
    table_ref[1, :, :head_size] = sine
    table_ref[2] = as_float(allowed)
    for copy in copies:
        copy.wait()
    own = lax.axis_index("pipe")
    tables = (cosine, sine, allowed)
    rows_ref[...] = forward_steps(rows, own, gain_ref, weight_ref, tables, saved)


def tables_of(table_ref, head_size):
    return table_ref[0, :, :head_size], table_ref[1, :, :head_size], table_ref[2] > 0.5


def split_pieces(refs, sections, groups):
    gains, rest = refs[:sections], refs[sections:]
    return (gains, rest[0], rest[1], rest[2 : 2 + groups]), rest[2 + groups :]


def second_kernel(rows_ref, upstream_ref, table_ref, *rest, sections, groups, turn):
    pieces, rest = split_pieces(rest, sections, groups)
    upstream_out, out_ref, *saved, gain_ref, weight_ref, sems = rest
    copies = fill(turn, pieces, gain_ref, weight_ref, sems)
    own = lax.axis_index("pipe")
    tables = tables_of(table_ref, weight_ref.shape[2] // 2)
    for copy in copies:
        copy.wait()
    forward_steps(rows_ref[...], own, gain_ref, weight_ref, tables, saved)
    upstream_out[...] = backward_steps(
        upstream_ref[...], own, gain_ref, weight_ref, tables, saved, out_ref, groups
    )


def third_kernel(upstream_ref, table_ref, tags_ref, *rest, sections, groups, turn):
    saved, rest = rest[:SAVED], rest[SAVED:]
    pieces, rest = split_pieces(rest, sections, groups)
    out_ref, gain_ref, weight_ref, sems = rest
    copies = fill(turn, pieces, gain_ref, weight_ref, sems)
    own = lax.axis_index("pipe")
    sections, feature_count, term_width = weight_ref.shape
    tables = tables_of(table_ref, term_width // 2)
    for copy in copies:
        copy.wait()
    grads = backward_steps(
        upstream_ref[...], own, gain_ref, weight_ref, tables, saved, out_ref, groups
    ).astype(jnp.bfloat16)
    row_count = grads.shape[0]
    column_count = feature_count // sections
    pieces = pieces_of(column_count)
    width = column_count // pieces
    chosen = choosers(tags_ref[...], row_count, pieces)
    for section in range(sections):
        start = section * column_count
        going = contract(chosen[0], grads[:, start : start + width], 1, 0)
        for piece in range(1, pieces):
            left = start + piece * width
            going += contract(chosen[piece], grads[:, left : left + width], 1, 0)
        going = going.astype(jnp.bfloat16)
        for group in range(groups):
            out_ref[section, group, :, term_width : term_width + width] = going[
                group * row_count : (group + 1) * row_count
            ]


def last_kernel(
    route_ref, late_ref, early_ref, grad_ref, key_ref, value_ref, *, groups, width
):
    micro_count = route_ref.shape[0]
    source_rows, column_count = grad_ref.shape
    row_count = source_rows // micro_count
    half = row_count // 2
    pieces = column_count // width
    head_size = key_ref.shape[2]
    term_width = 2 * head_size
    for index, (ref, gap) in enumerate(((late_ref, width), (early_ref, 0))):
        total = contract(ref[:, term_width + gap :], ref[:, :term_width], 0, 0)
        key_ref[index] = total[:, :head_size]
        value_ref[index] = total[:, head_size:]
    shape = (source_rows, late_ref.shape[0])
    row, source = iota(shape, 1), iota(shape, 0)
    slot = source // half
    target = jnp.full(shape, -1, jnp.int32)
    for micro in range(micro_count):
        for side in range(2):
            target = jnp.where(
                slot == 2 * micro + side, micro * groups + route_ref[micro, side], target
            )
    going = target == row // row_count
    inner, wanted = row % row_count, source % half
    for piece in range(pieces):
        chosen = as_float(going & (inner == piece * half + wanted)).astype(jnp.bfloat16)
        grad_ref[:, piece * width : (piece + 1) * width] = contract(
            chosen, late_ref[:, term_width : term_width + width], 1, 0
        ).astype(jnp.bfloat16)


def call(kernel, outs, operands, scalars=0, whole=0, scratch=()):
    spaces = [pltpu.SMEM] * scalars + [pltpu.VMEM] * (len(operands) - scalars - whole)
    spaces += [pl.ANY] * whole
    return pl.pallas_call(
        kernel,
        out_shape=outs,
        in_specs=[pl.BlockSpec(memory_space=space) for space in spaces],
        out_specs=[pl.BlockSpec(memory_space=pltpu.VMEM)] * len(outs),
        scratch_shapes=scratch,
        compiler_params=pltpu.CompilerParams(vmem_limit_bytes=VMEM_BYTES),
    )(*operands)


def exchange(blocks):
    return lax.all_to_all(blocks, ("pipe", "dp"), split_axis=0, concat_axis=0, tiled=True)


def swapped(value, axis, mask):
    pairs = [(source, source ^ mask) for source in range(lax.axis_size(axis))]
    return lax.ppermute(value, axis, pairs)


def gather_shares(own_share):
    sections, groups = lax.axis_size("pipe"), lax.axis_size("dp")
    column = jnp.stack([swapped(own_share, "pipe", mask) for mask in range(1, sections)])
    plane = [column] + [swapped(column, "dp", 2 * mask) for mask in range(1, groups // 2)]
    shares = []
    for part in plane:
        shares += [part, swapped(part, "dp", 1)]
    return shares


def body(hidden, lengths, route, gain, key_weight, value_weight, cotangent):
    groups = lax.axis_size("dp")
    sections = lax.axis_size("pipe")
    group_index = lax.axis_index("dp")
    section_index = lax.axis_index("pipe")
    micro_count = lengths.shape[0]
    assert micro_count == sections
    source_rows, column_count = hidden.shape
    row_count = source_rows // micro_count
    feature_count = gain.shape[1]
    head_size = key_weight.shape[2]
    heads = feature_count // head_size
    share = feature_count // groups
    width = column_count // pieces_of(column_count)
    devices = sections * groups

    shares = []
    for turn in range(2):
        parts = [
            lax.dynamic_slice(array, (turn, group_index * share, 0), (1, share, head_size))[0]
            for array in (key_weight, value_weight)
        ]
        shares.append(gather_shares(jnp.concatenate(parts, axis=1)))
    gains = [gain] + [swapped(gain, "pipe", mask) for mask in range(1, sections)]

    def layers_call(kernel, turn, outs, operands):
        return call(
            functools.partial(kernel, sections=sections, groups=groups, turn=turn),
            outs,
            (*operands, *gains, key_weight, value_weight, *shares[turn]),
            whole=2 + groups,
            scratch=[
                pltpu.VMEM((sections, feature_count), jnp.float32),
                pltpu.VMEM((sections, feature_count, 2 * head_size), jnp.bfloat16),
                pltpu.SemaphoreType.DMA((groups + 2,)),
            ],
        )

    (outgoing,) = call(
        functools.partial(pack_kernel, groups=groups),
        [jax.ShapeDtypeStruct((devices * row_count, width + LANES), jnp.bfloat16)],
        (lengths, route, hidden),
        scalars=2,
    )
    arrived = exchange(outgoing.reshape(devices, row_count, width + LANES)).reshape(
        devices * row_count, width + LANES
    )
    upstream = lax.dynamic_slice_in_dim(
        cotangent, section_index * row_count, row_count, 0
    ).astype(jnp.float32)

    saved = saved_shapes(sections, row_count, feature_count, head_size)
    rows_shape = jax.ShapeDtypeStruct((row_count, feature_count), jnp.float32)
    middle, tables, tags, *kept = layers_call(
        first_kernel,
        0,
        [
            rows_shape,
            jax.ShapeDtypeStruct((3, row_count, heads * row_count), jnp.float32),
            jax.ShapeDtypeStruct((groups * row_count, LANES), jnp.float32),
            *saved,
        ],
        (arrived,),
    )
    early_shape = (sections, groups, row_count, 2 * head_size + share)
    late_shape = early_shape[:3] + (early_shape[3] + width,)
    upstream, early, *_ = layers_call(
        second_kernel,
        1,
        [rows_shape, jax.ShapeDtypeStruct(early_shape, jnp.bfloat16), *saved],
        (middle, upstream, tables),
    )
    early = exchange(early.reshape((devices,) + early_shape[2:]))
    (late,) = layers_call(
        third_kernel,
        0,
        [jax.ShapeDtypeStruct(late_shape, jnp.bfloat16)],
        (upstream, tables, tags, *kept),
    )
    late = exchange(late.reshape((devices,) + late_shape[2:]))
    grad_shape = jax.ShapeDtypeStruct((2, share, head_size), jnp.float32)
    return tuple(
        call(
            functools.partial(last_kernel, groups=groups, width=width),
            [jax.ShapeDtypeStruct((source_rows, column_count), jnp.bfloat16)] + [grad_shape] * 2,
            (
                route,
                late.reshape(devices * row_count, late_shape[3]),
                early.reshape(devices * row_count, early_shape[3]),
            ),
            scalars=1,
        )
    )


def solution(mesh):
    placed = (
        P("dp", "pipe"),
        P("dp", None),
        P("dp", None),
        P("pipe", None),
        P("pipe", None, None),
        P("pipe", None, None),
        P("dp", None),
    )
    return jax.shard_map(
        body,
        mesh=mesh,
        in_specs=placed,
        out_specs=(P("dp", "pipe"), P("pipe", "dp", None), P("pipe", "dp", None)),
        check_vma=False,
    )
```

time: 385 us -> 128 us (0.33)
  waiting for transfers between devices: 141 us -> 42.5 us
  matrix products: 94.7 us -> 0 us
  local copies, waits for them, and re-layouts: 31.2 us -> 2.43 us
  Pallas kernels: 0 us -> 28.6 us
  starting transfers between devices: 58.2 us -> 35 us
  other arithmetic: 24.2 us -> 1.51 us
  between operations: 15.6 us -> 0.85 us
    dot_general x122 -> x0, matrix products: 94.7 us -> none  [the longest x33 42.5 us: attend_layer(): jnp.dot(flattened, key_proj, preferred_element_type=jnp.float32)]
    ppermute x22 -> x23, waiting for transfers between devices: 88.8 us -> 32 us  [swapped(): return lax.ppermute(value, axis, pairs)]
    psum x1 -> x0, waiting for transfers between devices: 30.9 us -> none  [spread(): return lax.psum(jnp.where(mine, value, jnp.zeros_like(value)), axis)]
    pallas_call x0 -> x5, Pallas kernels: none -> 28.6 us  [call(): pl.pallas_call(kernel, out_shape=outs, in_specs=[pl.BlockSpec(memory_spac...]
    dynamic_slice x34 -> x0, local copies, waits for them, and re-layouts: 17.8 us -> none  [the longest x22 16.9 us: select_row(): return lax.dynamic_index_in_dim(array, index_value, 0, keepdims=False)]
    all_to_all x0 -> x1, blocking collectives: none -> 16.5 us  [exchange(): lax.all_to_all(blocks, ('pipe', 'dp'), split_axis=0, concat_axis=0, tiled...]
    all_gather x1 -> x0, blocking collectives: 13.7 us -> none  [body(): lax.all_gather(received.reshape(micro_count * row_count, column_count), '...]
    ppermute x22 -> x23, starting transfers between devices: 41.8 us -> 28.4 us  [swapped(): return lax.ppermute(value, axis, pairs)]
  transfers between devices with their start and end apart: 28 -> 25, of which waited for: 27 -> 10; matrix products, arithmetic and copies ran while one was open for 4% -> 2% of each run, Pallas kernels for 0% -> 13%
where the time goes in v1:
time: 128 us; the launch traced here: 127 us
  waiting for transfers between devices  42.5 us (33%)
  starting transfers between devices  35 us (27%)
  Pallas kernels  28.6 us (22%)
  blocking collectives  16.5 us (13%)
  local copies, waits for them, and re-layouts  2.43 us (2%)
  other arithmetic  1.51 us (1%)
    ppermute x23, waiting for transfers between devices, swapped(): return lax.ppermute(value, axis, pairs)  32 us
    pallas_call x5, Pallas kernels, call(): pl.pallas_call(kernel, out_shape=outs, in_specs=[pl.BlockSpec(memory_spac...  28.6 us
    ppermute x23, starting transfers between devices, swapped(): return lax.ppermute(value, axis, pairs)  28.4 us
    all_to_all x1, blocking collectives, exchange(): lax.all_to_all(blocks, ('pipe', 'dp'), split_axis=0, concat_axis=0, tiled...  16.5 us
    all_to_all x2, waiting for transfers between devices, exchange(): lax.all_to_all(blocks, ('pipe', 'dp'), split_axis=0, concat_axis=0, tiled...  10.6 us
    all_to_all x2, starting transfers between devices, exchange(): lax.all_to_all(blocks, ('pipe', 'dp'), split_axis=0, concat_axis=0, tiled...  6.52 us
  transfers between devices with their start and end apart: 25, of which 10 were waited for; matrix products, arithmetic and copies ran while one was open for 2% of the time, Pallas kernels for 13%

profile of v1, /device:TPU:0, one launch (start us, length us, event | category | flops | bytes accessed | tf_op | source)
XLA Modules:
  0.0 127.4 jit_solution(10432698862354048808)
XLA Ops:
  0.6 1.0 dynamic-slice_bitcast_fusion
  1.6 5.1 %collective-permute-start.15 = (bf16[256,256]{1,0:T(8,128)(2,1)S(1)}, bf16[256,256]{1,0:T(8,128)(2,1)S(1)}, u32[]{:S(2)}, u32[]{:S(2)}) collective-permute-start(bf16[256,256]{1,0:T(8,128)(2,1)S(1)} %pad_maximum_fusion.3), channel_id=1, source_target_pairs={{0,24},{8,16},{16,8},{24,0},{1,25},{9,17},{17,9},{25,1},{2,26},{10... | collective-permute-start | bytes 393224 | tf_op jit(solution)/shard_map/ppermute | solution.py:413
  6.7 0.0 collective-permute-start.14
  6.7 0.6 collective-permute-start.13
  7.4 3.8 %collective-permute-start.5 = (bf16[256,256]{1,0:T(8,128)(2,1)S(1)}, bf16[256,256]{1,0:T(8,128)(2,1)S(1)}, u32[]{:S(2)}, u32[]{:S(2)}) collective-permute-start(bf16[256,256]{1,0:T(8,128)(2,1)S(1)} %pad_maximum_fusion.2), channel_id=1, source_target_pairs={{0,24},{8,16},{16,8},{24,0},{1,25},{9,17},{17,9},{25,1},{2,26},{10... | collective-permute-start | bytes 393224 | tf_op jit(solution)/shard_map/ppermute | solution.py:413
  11.2 0.0 collective-permute-start.4
  11.2 0.0 collective-permute-done.15
  11.2 6.2 %collective-permute-start.3 = (bf16[256,256]{1,0:T(8,128)(2,1)S(1)}, bf16[256,256]{1,0:T(8,128)(2,1)S(1)}, u32[]{:S(2)}, u32[]{:S(2)}) collective-permute-start(bf16[256,256]{1,0:T(8,128)(2,1)S(1)} %pad_maximum_fusion.2), channel_id=1, source_target_pairs={{0,8},{8,0},{16,24},{24,16},{1,9},{9,1},{17,25},{25,17},{2,10},{10... | collective-permute-start | bytes 393224 | tf_op jit(solution)/shard_map/ppermute | solution.py:413
  17.4 7.0 %collective-permute-done.14 = bf16[256,256]{1,0:T(8,128)(2,1)S(1)} collective-permute-done((bf16[256,256]{1,0:T(8,128)(2,1)S(1)}, bf16[256,256]{1,0:T(8,128)(2,1)S(1)}, u32[]{:S(2)}, u32[]{:S(2)}) %collective-permute-start.14) | collective-permute-done | bytes 131104 | tf_op jit(solution)/shard_map/ppermute | solution.py:413
  24.4 0.0 collective-permute-done.13
  24.4 0.0 copy-start.1
  24.5 2.5 %collective-permute-start.21 = (bf16[3,256,256]{2,1,0:T(8,128)(2,1)S(1)}, bf16[3,256,256]{2,1,0:T(8,128)(2,1)}, u32[]{:S(2)}, u32[]{:S(2)}) collective-permute-start(bf16[3,256,256]{2,1,0:T(8,128)(2,1)S(1)} %pad_maximum_fusion.1.rest_6_), channel_id=1, source_target_pairs={{0,6},{1,7},{2,4},{3,5},{4,2},{5,3},{6,0},{7,1},{8,14},{9,15},{10,... | collective-permute-start | bytes 1179656 | tf_op jit(solution)/shard_map/ppermute | solution.py:413
  27.0 0.5 collective-permute-start.19
  27.5 0.0 collective-permute-done.5
  27.5 1.6 %collective-permute-done.4 = bf16[256,256]{1,0:T(8,128)(2,1)S(1)} collective-permute-done((bf16[256,256]{1,0:T(8,128)(2,1)S(1)}, bf16[256,256]{1,0:T(8,128)(2,1)S(1)}, u32[]{:S(2)}, u32[]{:S(2)}) %collective-permute-start.4) | collective-permute-done | bytes 131104 | tf_op jit(solution)/shard_map/ppermute | solution.py:413
  29.0 0.0 collective-permute-done.3
  29.1 0.0 copy-start
  29.1 2.5 %collective-permute-start.11 = (bf16[3,256,256]{2,1,0:T(8,128)(2,1)S(1)}, bf16[3,256,256]{2,1,0:T(8,128)(2,1)S(1)}, u32[]{:S(2)}, u32[]{:S(2)}) collective-permute-start(bf16[3,256,256]{2,1,0:T(8,128)(2,1)S(1)} %pad_maximum_fusion.rest_6_.rest_11_), channel_id=1, source_target_pairs={{0,6},{1,7},{2,4},{3,5},{4,2},{5,3},{6,0},{7,1},{8,14},{9,15},{10,... | collective-permute-start | bytes 1179656 | tf_op jit(solution)/shard_map/ppermute | solution.py:413
  31.6 0.5 collective-permute-start.9
  32.1 0.0 copy-done.10
  32.1 2.5 %collective-permute-start.2 = (f32[2,2048]{1,0:T(2,128)S(1)}, f32[2,2048]{1,0:T(2,128)S(1)}, u32[]{:S(2)}, u32[]{:S(2)}) collective-permute-start(f32[2,2048]{1,0:T(2,128)S(1)} %copy-done.10), channel_id=1, source_target_pairs={{0,24},{8,16},{16,8},{24,0},{1,25},{9,17},{17,9},{25,1},{2,26},{10... | collective-permute-start | bytes 49160 | tf_op jit(solution)/shard_map/ppermute | solution.py:413
  34.6 3.1 %collective-permute-done.2.rest_3_.rest_8_ = f32[2,2048]{1,0:T(2,128)S(1)} collective-permute-done((f32[2,2048]{1,0:T(2,128)S(1)}, f32[2,2048]{1,0:T(2,128)S(1)}, u32[]{:S(2)}, u32[]{:S(2)}) %collective-permute-start.2) | collective-permute-done | bytes 16416 | tf_op jit(solution)/shard_map/ppermute | solution.py:413
  37.7 0.0 collective-permute-start.1
  37.7 4.6 %collective-permute-done.1.rest_2_.rest_7_ = f32[2,2048]{1,0:T(2,128)S(1)} collective-permute-done((f32[2,2048]{1,0:T(2,128)S(1)}, f32[2,2048]{1,0:T(2,128)S(1)}, u32[]{:S(2)}, u32[]{:S(2)}) %collective-permute-start.1) | collective-permute-done | bytes 16416 | tf_op jit(solution)/shard_map/ppermute | solution.py:413
  42.3 0.1 collective-permute-start
  42.4 3.6 %collective-permute-done.rest_1_.rest_6_ = f32[2,2048]{1,0:T(2,128)S(1)} collective-permute-done((f32[2,2048]{1,0:T(2,128)S(1)}, f32[2,2048]{1,0:T(2,128)S(1)}, u32[]{:S(2)}, u32[]{:S(2)}) %collective-permute-start) | collective-permute-done | bytes 16416 | tf_op jit(solution)/shard_map/ppermute | solution.py:413
  46.1 0.5 collective-permute-start.17
  46.6 0.1 copy-done.13
  46.7 0.0 collective-permute-done.21.rest_12_
  46.7 1.5 %collective-permute-start.7 = (bf16[3,256,256]{2,1,0:T(8,128)(2,1)S(1)}, bf16[3,256,256]{2,1,0:T(8,128)(2,1)S(1)}, u32[]{:S(2)}, u32[]{:S(2)}) collective-permute-start(bf16[3,256,256]{2,1,0:T(8,128)(2,1)S(1)} %pad_maximum_fusion.rest_6_.rest_11_), channel_id=1, source_target_pairs={{0,2},{1,3},{2,0},{3,1},{4,6},{5,7},{6,4},{7,5},{8,10},{9,11},{10,... | collective-permute-start | bytes 1179656 | tf_op jit(solution)/shard_map/ppermute | solution.py:413
  48.2 3.5 %collective-permute-done.19.rest_10_ = bf16[3,256,256]{2,1,0:T(8,128)(2,1)} collective-permute-done((bf16[3,256,256]{2,1,0:T(8,128)(2,1)S(1)}, bf16[3,256,256]{2,1,0:T(8,128)(2,1)}, u32[]{:S(2)}, u32[]{:S(2)}) %collective-permute-start.19) | collective-permute-done | bytes 393248 | tf_op jit(solution)/shard_map/ppermute | solution.py:413
  51.7 0.0 collective-permute-start.6
  51.7 0.0 collective-permute-done.11.rest_12_.rest_17_
  51.7 0.5 collective-permute-start.12
  52.2 7.7 %collective-permute-done.9.rest_10_.rest_15_ = bf16[3,256,256]{2,1,0:T(8,128)(2,1)S(1)} collective-permute-done((bf16[3,256,256]{2,1,0:T(8,128)(2,1)S(1)}, bf16[3,256,256]{2,1,0:T(8,128)(2,1)S(1)}, u32[]{:S(2)}, u32[]{:S(2)}) %collective-permute-start.9) | collective-permute-done | bytes 393248 | tf_op jit(solution)/shard_map/ppermute | solution.py:413
  59.9 0.0 collective-permute-start.10
  59.9 0.0 collective-permute-done.17.rest_8_
  59.9 0.5 collective-permute-start.16
  60.4 0.8 collective-permute-done.7.rest_8_.rest_13_
  61.2 0.0 collective-permute-start.8
  61.2 0.0 collective-permute-done.6.rest_7_.rest_12_
  61.3 0.5 collective-permute-start.22
  61.8 0.0 collective-permute-done.12.rest_13_.rest_18_
  61.8 0.1 collective-permute-start.20
  61.8 0.0 collective-permute-done.10.rest_11_.rest_16_
  61.9 0.4 collective-permute-start.18
  62.3 0.7 copy.11.route_ref
  62.9 1.7 %shard_map.94 = bf16[256,384]{1,0:T(8,128)(2,1)} custom-call(s32[4,4]{1,0:T(4,128)} %lengths_ref.1, s32[4,2]{1,0:T(4,128)} %copy.11.route_ref, bf16[32,512]{1,0:T(8,128)(2,1)} %hidden_ref.1), custom_call_target="tpu_custom_call" | custom-call | tf_op jit(solution)/shard_map/pallas_call | solution.py:397
  64.6 3.8 %all-to-all-start = ((bf16[32,8,384]{2,1,0:T(8,128)(2,1)}), bf16[32,8,384]{2,1,0:T(8,128)(2,1)}, u32[]{:S(2)}, u32[]{:S(2)}) async-start(bf16[32,8,384]{2,1,0:T(8,128)(2,1)} %bitcast.23), calls=%async_computation | async-start | bytes 393216 | tf_op jit(solution)/shard_map/all_to_all | solution.py:408
  68.5 1.4 %dynamic-slice_convert_fusion.upstream_ref = f32[8,2048]{1,0:T(8,128)} fusion(bf16[32,2048]{1,0:T(8,128)(2,1)} %param.13, s32[]{:T(128)S(6)} %select_n.10), kind=kLoop, calls=%fused_computation.8 | loop fusion | flops 16384 | bytes 98308 | tf_op jit(solution)/shard_map/convert_element_type | solution.py:475
  69.8 7.5 %all-to-all-done = bf16[32,8,384]{2,1,0:T(8,128)(2,1)} async-done(((bf16[32,8,384]{2,1,0:T(8,128)(2,1)}), bf16[32,8,384]{2,1,0:T(8,128)(2,1)}, u32[]{:S(2)}, u32[]{:S(2)}) %all-to-all-start) | async-done | bytes 196640 | tf_op jit(solution)/shard_map/all_to_all | solution.py:408
  77.3 0.0 collective-permute-done.8.rest_9_.rest_14_
  77.4 0.7 copy-done.8
  78.1 7.2 %shard_map.95 = (f32[8,2048]{1,0:T(8,128)}, f32[3,8,128]{2,1,0:T(8,128)}, f32[64,128]{1,0:T(8,128)}, f32[4,8,2048]{2,1,0:T(8,128)}, f32[4,8,128]{2,1,0:T(8,128)}...) custom-call(bf16[256,384]{1,0:T(8,128)(2,1)} %bitcast.1.arrived_ref, ...), custom_call_target="tpu_custom_call" | custom-call | tf_op jit(solution)/shard_map/pallas_call | solution.py:397
  85.3 0.0 collective-permute-done.16.rest_7_
  85.3 0.0 collective-permute-done.22.rest_13_
  85.3 0.0 collective-permute-done.20.rest_11_
  85.4 0.0 collective-permute-done.18.rest_9_
  85.4 10.1 %shard_map.96 = (f32[8,2048]{1,0:T(8,128)}, bf16[4,8,8,512]{3,2,1,0:T(8,128)(2,1)}, f32[4,8,2048]{2,1,0:T(8,128)}, f32[4,8,128]{2,1,0:T(8,128)}, bf16[4,128,128]...) custom-call(f32[8,2048]{1,0:T(8,128)} %get-tuple-element.13.rows_ref, ...), custom_call_target="tpu_custom_call" | custom-call | tf_op jit(solution)/shard_map/pallas_call | solution.py:397
  95.5 2.7 %all-to-all-start.2 = ((bf16[32,8,512]{2,1,0:T(8,128)(2,1)}), bf16[32,8,512]{2,1,0:T(8,128)(2,1)S(1)}, u32[]{:S(2)}, u32[]{:S(2)}) async-start(bf16[32,8,512]{2,1,0:T(8,128)(2,1)} %bitcast.24), calls=%async_computation.2 | async-start | bytes 524288 | tf_op jit(solution)/shard_map/all_to_all | solution.py:408
  98.2 7.5 %shard_map.97 = bf16[4,8,8,768]{3,2,1,0:T(8,128)(2,1)} custom-call(f32[8,2048]{1,0:T(8,128)} %get-tuple-element.15.upstream_ref, f32[3,8,128]{2,1,0:T(8,128)} %get-tuple-element.14.table_ref, f32[64,128]{1,0:T(8,128)} %get-tuple-element.16.tags_ref, f32[4,8,2048]{2,1,0:T(8,128)} %get-tuple-element.17.rest_0_, f32[4,8,128]{2,1,0:T(8,128)} %get-tuple-element.18.rest_1_, ...), custom_call_target="tpu_custom_call" | custom-call | tf_op jit(solution)/shard_map/pallas_call | solution.py:397
  105.7 3.1 %all-to-all-done.2 = bf16[32,8,512]{2,1,0:T(8,128)(2,1)S(1)} async-done(((bf16[32,8,512]{2,1,0:T(8,128)(2,1)}), bf16[32,8,512]{2,1,0:T(8,128)(2,1)S(1)}, u32[]{:S(2)}, u32[]{:S(2)}) %all-to-all-start.2) | async-done | bytes 262176 | tf_op jit(solution)/shard_map/all_to_all | solution.py:408
  108.8 16.5 %all_to_all.15 = bf16[32,8,768]{2,1,0:T(8,128)(2,1)} all-to-all(bf16[32,8,768]{2,1,0:T(8,128)(2,1)} %bitcast.21), channel_id=1, replica_groups=mesh['pipe'=4,'dp'=8] {'pipe','dp'}, dimensions={0} | all-to-all | bytes 786432 | tf_op jit(solution)/shard_map/all_to_all | solution.py:408
  125.3 2.1 %shard_map.98 = (bf16[32,512]{1,0:T(8,128)(2,1)}, f32[2,256,128]{2,1,0:T(8,128)}, f32[2,256,128]{2,1,0:T(8,128)}) custom-call(s32[4,2]{1,0:T(4,128)} %copy.11.route_ref, bf16[256,768]{1,0:T(8,128)(2,1)} %bitcast.20, bf16[256,512]{1,0:T(8,128)(2,1)} %bitcast.22), custom_call_target="tpu_custom_call" | custom-call | tf_op jit(solution)/shard_map/pallas_call | solution.py:397
  (29 shorter events, 0.2 us)
Async XLA Ops:
  1.6 9.6 %collective-permute-start.15 = (bf16[256,256]{1,0:T(8,128)(2,1)S(1)}, bf16[256,256]{1,0:T(8,128)(2,1)S(1)}, u32[]{:S(2)}, u32[]{:S(2)}) collective-permute-start(bf16[256,256]{1,0:T(8,128)(2,1)S(1)} %pad_maximum_fusion.3), channel_id=1, source_target_pairs={{0,24},{8,16},{16,8},{24,0},{1,25},{9,17},{17,9},{25,1},{2,26},{10... | collective-permute-start | bytes 393224 | tf_op jit(solution)/shard_map/ppermute | solution.py:413
  6.7 17.7 %collective-permute-start.14 = (bf16[256,256]{1,0:T(8,128)(2,1)S(1)}, bf16[256,256]{1,0:T(8,128)(2,1)S(1)}, u32[]{:S(2)}, u32[]{:S(2)}) collective-permute-start(bf16[256,256]{1,0:T(8,128)(2,1)S(1)} %pad_maximum_fusion.3), channel_id=1, source_target_pairs={{0,16},{8,24},{16,0},{24,8},{1,17},{9,25},{17,1},{25,9},{2,18},{10... | collective-permute-start | bytes 393224 | tf_op jit(solution)/shard_map/ppermute | solution.py:413
  6.7 17.7 %collective-permute-start.13 = (bf16[256,256]{1,0:T(8,128)(2,1)S(1)}, bf16[256,256]{1,0:T(8,128)(2,1)S(1)}, u32[]{:S(2)}, u32[]{:S(2)}) collective-permute-start(bf16[256,256]{1,0:T(8,128)(2,1)S(1)} %pad_maximum_fusion.3), channel_id=1, source_target_pairs={{0,8},{8,0},{16,24},{24,16},{1,9},{9,1},{17,25},{25,17},{2,10},{10... | collective-permute-start | bytes 393224 | tf_op jit(solution)/shard_map/ppermute | solution.py:413
  7.4 20.1 %collective-permute-start.5 = (bf16[256,256]{1,0:T(8,128)(2,1)S(1)}, bf16[256,256]{1,0:T(8,128)(2,1)S(1)}, u32[]{:S(2)}, u32[]{:S(2)}) collective-permute-start(bf16[256,256]{1,0:T(8,128)(2,1)S(1)} %pad_maximum_fusion.2), channel_id=1, source_target_pairs={{0,24},{8,16},{16,8},{24,0},{1,25},{9,17},{17,9},{25,1},{2,26},{10... | collective-permute-start | bytes 393224 | tf_op jit(solution)/shard_map/ppermute | solution.py:413
  11.2 17.8 %collective-permute-start.4 = (bf16[256,256]{1,0:T(8,128)(2,1)S(1)}, bf16[256,256]{1,0:T(8,128)(2,1)S(1)}, u32[]{:S(2)}, u32[]{:S(2)}) collective-permute-start(bf16[256,256]{1,0:T(8,128)(2,1)S(1)} %pad_maximum_fusion.2), channel_id=1, source_target_pairs={{0,16},{8,24},{16,0},{24,8},{1,17},{9,25},{17,1},{25,9},{2,18},{10... | collective-permute-start | bytes 393224 | tf_op jit(solution)/shard_map/ppermute | solution.py:413
  11.2 17.8 %collective-permute-start.3 = (bf16[256,256]{1,0:T(8,128)(2,1)S(1)}, bf16[256,256]{1,0:T(8,128)(2,1)S(1)}, u32[]{:S(2)}, u32[]{:S(2)}) collective-permute-start(bf16[256,256]{1,0:T(8,128)(2,1)S(1)} %pad_maximum_fusion.2), channel_id=1, source_target_pairs={{0,8},{8,0},{16,24},{24,16},{1,9},{9,1},{17,25},{25,17},{2,10},{10... | collective-permute-start | bytes 393224 | tf_op jit(solution)/shard_map/ppermute | solution.py:413
  24.4 35.5 %copy-start.1 = (bf16[3,256,256]{2,1,0:T(8,128)(2,1)}, bf16[3,256,256]{2,1,0:T(8,128)(2,1)S(1)}, u32[]{:S(2)}) copy-start(bf16[3,256,256]{2,1,0:T(8,128)(2,1)S(1)} %pad_maximum_fusion.1.rest_6_) | copy-start | bytes 1179652
  24.5 22.2 %collective-permute-start.21 = (bf16[3,256,256]{2,1,0:T(8,128)(2,1)S(1)}, bf16[3,256,256]{2,1,0:T(8,128)(2,1)}, u32[]{:S(2)}, u32[]{:S(2)}) collective-permute-start(bf16[3,256,256]{2,1,0:T(8,128)(2,1)S(1)} %pad_maximum_fusion.1.rest_6_), channel_id=1, source_target_pairs={{0,6},{1,7},{2,4},{3,5},{4,2},{5,3},{6,0},{7,1},{8,14},{9,15},{10,... | collective-permute-start | bytes 1179656 | tf_op jit(solution)/shard_map/ppermute | solution.py:413
  27.0 24.7 %collective-permute-start.19 = (bf16[3,256,256]{2,1,0:T(8,128)(2,1)S(1)}, bf16[3,256,256]{2,1,0:T(8,128)(2,1)}, u32[]{:S(2)}, u32[]{:S(2)}) collective-permute-start(bf16[3,256,256]{2,1,0:T(8,128)(2,1)S(1)} %pad_maximum_fusion.1.rest_6_), channel_id=1, source_target_pairs={{0,4},{1,5},{2,6},{3,7},{4,0},{5,1},{6,2},{7,3},{8,12},{9,13},{10,... | collective-permute-start | bytes 1179656 | tf_op jit(solution)/shard_map/ppermute | solution.py:413
  29.1 3.1 %copy-start.10 = (f32[2,2048]{1,0:T(2,128)S(1)}, f32[2,2048]{1,0:T(2,128)}, u32[]{:S(2)}) copy-start(f32[2,2048]{1,0:T(2,128)} %rest_5_.5) | copy-start | bytes 49156
  29.1 33.2 %copy-start.14 = (s32[4,2]{0,1:T(2,128)S(1)}, s32[4,2]{0,1:T(2,128)}, u32[]{:S(2)}) copy-start(s32[4,2]{0,1:T(2,128)} %param.9) | copy-start | bytes 100
  29.1 48.2 %copy-start = (bf16[3,256,256]{2,1,0:T(8,128)(2,1)}, bf16[3,256,256]{2,1,0:T(8,128)(2,1)S(1)}, u32[]{:S(2)}) copy-start(bf16[3,256,256]{2,1,0:T(8,128)(2,1)S(1)} %pad_maximum_fusion.rest_6_.rest_11_) | copy-start | bytes 1179652
  29.1 22.6 %collective-permute-start.11 = (bf16[3,256,256]{2,1,0:T(8,128)(2,1)S(1)}, bf16[3,256,256]{2,1,0:T(8,128)(2,1)S(1)}, u32[]{:S(2)}, u32[]{:S(2)}) collective-permute-start(bf16[3,256,256]{2,1,0:T(8,128)(2,1)S(1)} %pad_maximum_fusion.rest_6_.rest_11_), channel_id=1, source_target_pairs={{0,6},{1,7},{2,4},{3,5},{4,2},{5,3},{6,0},{7,1},{8,14},{9,15},{10,... | collective-permute-start | bytes 1179656 | tf_op jit(solution)/shard_map/ppermute | solution.py:413
  31.6 28.3 %collective-permute-start.9 = (bf16[3,256,256]{2,1,0:T(8,128)(2,1)S(1)}, bf16[3,256,256]{2,1,0:T(8,128)(2,1)S(1)}, u32[]{:S(2)}, u32[]{:S(2)}) collective-permute-start(bf16[3,256,256]{2,1,0:T(8,128)(2,1)S(1)} %pad_maximum_fusion.rest_6_.rest_11_), channel_id=1, source_target_pairs={{0,4},{1,5},{2,6},{3,7},{4,0},{5,1},{6,2},{7,3},{8,12},{9,13},{10,... | collective-permute-start | bytes 1179656 | tf_op jit(solution)/shard_map/ppermute | solution.py:413
  32.1 5.5 %collective-permute-start.2 = (f32[2,2048]{1,0:T(2,128)S(1)}, f32[2,2048]{1,0:T(2,128)S(1)}, u32[]{:S(2)}, u32[]{:S(2)}) collective-permute-start(f32[2,2048]{1,0:T(2,128)S(1)} %copy-done.10), channel_id=1, source_target_pairs={{0,24},{8,16},{16,8},{24,0},{1,25},{9,17},{17,9},{25,1},{2,26},{10... | collective-permute-start | bytes 49160 | tf_op jit(solution)/shard_map/ppermute | solution.py:413
  37.7 8.9 %copy-start.11 = (f32[2,2048]{1,0:T(2,128)}, f32[2,2048]{1,0:T(2,128)S(1)}, u32[]{:S(2)}) copy-start(f32[2,2048]{1,0:T(2,128)S(1)} %collective-permute-done.2.rest_3_.rest_8_) | copy-start | bytes 49156
  37.7 4.6 %collective-permute-start.1 = (f32[2,2048]{1,0:T(2,128)S(1)}, f32[2,2048]{1,0:T(2,128)S(1)}, u32[]{:S(2)}, u32[]{:S(2)}) collective-permute-start(f32[2,2048]{1,0:T(2,128)S(1)} %copy-done.10), channel_id=1, source_target_pairs={{0,16},{8,24},{16,0},{24,8},{1,17},{9,25},{17,1},{25,9},{2,18},{10... | collective-permute-start | bytes 49160 | tf_op jit(solution)/shard_map/ppermute | solution.py:413
  42.3 4.3 %copy-start.12 = (f32[2,2048]{1,0:T(2,128)}, f32[2,2048]{1,0:T(2,128)S(1)}, u32[]{:S(2)}) copy-start(f32[2,2048]{1,0:T(2,128)S(1)} %collective-permute-done.1.rest_2_.rest_7_) | copy-start | bytes 49156
  42.3 3.7 %collective-permute-start = (f32[2,2048]{1,0:T(2,128)S(1)}, f32[2,2048]{1,0:T(2,128)S(1)}, u32[]{:S(2)}, u32[]{:S(2)}) collective-permute-start(f32[2,2048]{1,0:T(2,128)S(1)} %copy-done.10), channel_id=1, source_target_pairs={{0,8},{8,0},{16,24},{24,16},{1,9},{9,1},{17,25},{25,17},{2,10},{10... | collective-permute-start | bytes 49160 | tf_op jit(solution)/shard_map/ppermute | solution.py:413
  46.1 0.6 copy-start.13
  46.1 13.9 %collective-permute-start.17 = (bf16[3,256,256]{2,1,0:T(8,128)(2,1)S(1)}, bf16[3,256,256]{2,1,0:T(8,128)(2,1)}, u32[]{:S(2)}, u32[]{:S(2)}) collective-permute-start(bf16[3,256,256]{2,1,0:T(8,128)(2,1)S(1)} %pad_maximum_fusion.1.rest_6_), channel_id=1, source_target_pairs={{0,2},{1,3},{2,0},{3,1},{4,6},{5,7},{6,4},{7,5},{8,10},{9,11},{10,... | collective-permute-start | bytes 1179656 | tf_op jit(solution)/shard_map/ppermute | solution.py:413
  46.7 14.6 %collective-permute-start.7 = (bf16[3,256,256]{2,1,0:T(8,128)(2,1)S(1)}, bf16[3,256,256]{2,1,0:T(8,128)(2,1)S(1)}, u32[]{:S(2)}, u32[]{:S(2)}) collective-permute-start(bf16[3,256,256]{2,1,0:T(8,128)(2,1)S(1)} %pad_maximum_fusion.rest_6_.rest_11_), channel_id=1, source_target_pairs={{0,2},{1,3},{2,0},{3,1},{4,6},{5,7},{6,4},{7,5},{8,10},{9,11},{10,... | collective-permute-start | bytes 1179656 | tf_op jit(solution)/shard_map/ppermute | solution.py:413
  51.7 9.6 %collective-permute-start.6 = (bf16[3,256,256]{2,1,0:T(8,128)(2,1)S(1)}, bf16[3,256,256]{2,1,0:T(8,128)(2,1)S(1)}, u32[]{:S(2)}, u32[]{:S(2)}) collective-permute-start(bf16[3,256,256]{2,1,0:T(8,128)(2,1)S(1)} %pad_maximum_fusion.rest_6_.rest_11_), channel_id=1, source_target_pairs={{0,1},{1,0},{2,3},{3,2},{4,5},{5,4},{6,7},{7,6},{8,9},{9,8},{10,11... | collective-permute-start | bytes 1179656 | tf_op jit(solution)/shard_map/ppermute | solution.py:413
  51.7 25.7 %copy-start.2 = (bf16[3,256,256]{2,1,0:T(8,128)(2,1)}, bf16[3,256,256]{2,1,0:T(8,128)(2,1)S(1)}, u32[]{:S(2)}) copy-start(bf16[3,256,256]{2,1,0:T(8,128)(2,1)S(1)} %collective-permute-done.11.rest_12_.rest_17_) | copy-start | bytes 1179652
  51.7 10.1 %collective-permute-start.12 = (bf16[3,256,256]{2,1,0:T(8,128)(2,1)S(1)}, bf16[3,256,256]{2,1,0:T(8,128)(2,1)S(1)}, u32[]{:S(2)}, u32[]{:S(2)}) collective-permute-start(bf16[3,256,256]{2,1,0:T(8,128)(2,1)S(1)} %collective-permute-done.11.rest_12_.rest_17_), channel_id=1, source_target_pairs={{0,1},{1,0},{2,3},{3,2},{4,5},{5,4},{6,7},{7,6},{8,9},{9,8},{10,11... | collective-permute-start | bytes 1179656 | tf_op jit(solution)/shard_map/ppermute | solution.py:413
  59.9 17.4 %copy-start.3 = (bf16[3,256,256]{2,1,0:T(8,128)(2,1)}, bf16[3,256,256]{2,1,0:T(8,128)(2,1)S(1)}, u32[]{:S(2)}) copy-start(bf16[3,256,256]{2,1,0:T(8,128)(2,1)S(1)} %collective-permute-done.9.rest_10_.rest_15_) | copy-start | bytes 1179652
  59.9 1.9 %collective-permute-start.10 = (bf16[3,256,256]{2,1,0:T(8,128)(2,1)S(1)}, bf16[3,256,256]{2,1,0:T(8,128)(2,1)S(1)}, u32[]{:S(2)}, u32[]{:S(2)}) collective-permute-start(bf16[3,256,256]{2,1,0:T(8,128)(2,1)S(1)} %collective-permute-done.9.rest_10_.rest_15_), channel_id=1, source_target_pairs={{0,1},{1,0},{2,3},{3,2},{4,5},{5,4},{6,7},{7,6},{8,9},{9,8},{10,11... | collective-permute-start | bytes 1179656 | tf_op jit(solution)/shard_map/ppermute | solution.py:413
  59.9 25.4 %collective-permute-start.16 = (bf16[3,256,256]{2,1,0:T(8,128)(2,1)S(1)}, bf16[3,256,256]{2,1,0:T(8,128)(2,1)}, u32[]{:S(2)}, u32[]{:S(2)}) collective-permute-start(bf16[3,256,256]{2,1,0:T(8,128)(2,1)S(1)} %pad_maximum_fusion.1.rest_6_), channel_id=1, source_target_pairs={{0,1},{1,0},{2,3},{3,2},{4,5},{5,4},{6,7},{7,6},{8,9},{9,8},{10,11... | collective-permute-start | bytes 1179656 | tf_op jit(solution)/shard_map/ppermute | solution.py:413
  61.2 16.1 %copy-start.4 = (bf16[3,256,256]{2,1,0:T(8,128)(2,1)}, bf16[3,256,256]{2,1,0:T(8,128)(2,1)S(1)}, u32[]{:S(2)}) copy-start(bf16[3,256,256]{2,1,0:T(8,128)(2,1)S(1)} %collective-permute-done.7.rest_8_.rest_13_) | copy-start | bytes 1179652
  61.2 16.1 %collective-permute-start.8 = (bf16[3,256,256]{2,1,0:T(8,128)(2,1)S(1)}, bf16[3,256,256]{2,1,0:T(8,128)(2,1)S(1)}, u32[]{:S(2)}, u32[]{:S(2)}) collective-permute-start(bf16[3,256,256]{2,1,0:T(8,128)(2,1)S(1)} %collective-permute-done.7.rest_8_.rest_13_), channel_id=1, source_target_pairs={{0,1},{1,0},{2,3},{3,2},{4,5},{5,4},{6,7},{7,6},{8,9},{9,8},{10,11... | collective-permute-start | bytes 1179656 | tf_op jit(solution)/shard_map/ppermute | solution.py:413
  61.2 16.1 %copy-start.5 = (bf16[3,256,256]{2,1,0:T(8,128)(2,1)}, bf16[3,256,256]{2,1,0:T(8,128)(2,1)S(1)}, u32[]{:S(2)}) copy-start(bf16[3,256,256]{2,1,0:T(8,128)(2,1)S(1)} %collective-permute-done.6.rest_7_.rest_12_) | copy-start | bytes 1179652
  61.3 24.1 %collective-permute-start.22 = (bf16[3,256,256]{2,1,0:T(8,128)(2,1)}, bf16[3,256,256]{2,1,0:T(8,128)(2,1)}, u32[]{:S(2)}, u32[]{:S(2)}) collective-permute-start(bf16[3,256,256]{2,1,0:T(8,128)(2,1)} %collective-permute-done.21.rest_12_), channel_id=1, source_target_pairs={{0,1},{1,0},{2,3},{3,2},{4,5},{5,4},{6,7},{7,6},{8,9},{9,8},{10,11... | collective-permute-start | bytes 1179656 | tf_op jit(solution)/shard_map/ppermute | solution.py:413
  61.8 15.6 %copy-start.6 = (bf16[3,256,256]{2,1,0:T(8,128)(2,1)}, bf16[3,256,256]{2,1,0:T(8,128)(2,1)S(1)}, u32[]{:S(2)}) copy-start(bf16[3,256,256]{2,1,0:T(8,128)(2,1)S(1)} %collective-permute-done.12.rest_13_.rest_18_) | copy-start | bytes 1179652
  61.8 23.6 %collective-permute-start.20 = (bf16[3,256,256]{2,1,0:T(8,128)(2,1)}, bf16[3,256,256]{2,1,0:T(8,128)(2,1)}, u32[]{:S(2)}, u32[]{:S(2)}) collective-permute-start(bf16[3,256,256]{2,1,0:T(8,128)(2,1)} %collective-permute-done.19.rest_10_), channel_id=1, source_target_pairs={{0,1},{1,0},{2,3},{3,2},{4,5},{5,4},{6,7},{7,6},{8,9},{9,8},{10,11... | collective-permute-start | bytes 1179656 | tf_op jit(solution)/shard_map/ppermute | solution.py:413
  61.8 15.5 %copy-start.7 = (bf16[3,256,256]{2,1,0:T(8,128)(2,1)}, bf16[3,256,256]{2,1,0:T(8,128)(2,1)S(1)}, u32[]{:S(2)}) copy-start(bf16[3,256,256]{2,1,0:T(8,128)(2,1)S(1)} %collective-permute-done.10.rest_11_.rest_16_) | copy-start | bytes 1179652
  61.9 23.5 %collective-permute-start.18 = (bf16[3,256,256]{2,1,0:T(8,128)(2,1)}, bf16[3,256,256]{2,1,0:T(8,128)(2,1)}, u32[]{:S(2)}, u32[]{:S(2)}) collective-permute-start(bf16[3,256,256]{2,1,0:T(8,128)(2,1)} %collective-permute-done.17.rest_8_), channel_id=1, source_target_pairs={{0,1},{1,0},{2,3},{3,2},{4,5},{5,4},{6,7},{7,6},{8,9},{9,8},{10,11... | collective-permute-start | bytes 1179656 | tf_op jit(solution)/shard_map/ppermute | solution.py:413
  64.6 12.7 %all-to-all-start = ((bf16[32,8,384]{2,1,0:T(8,128)(2,1)}), bf16[32,8,384]{2,1,0:T(8,128)(2,1)}, u32[]{:S(2)}, u32[]{:S(2)}) async-start(bf16[32,8,384]{2,1,0:T(8,128)(2,1)} %bitcast.23), calls=%async_computation | async-start | bytes 393216 | tf_op jit(solution)/shard_map/all_to_all | solution.py:408
  77.3 0.8 copy-start.8
  95.5 13.3 %all-to-all-start.2 = ((bf16[32,8,512]{2,1,0:T(8,128)(2,1)}), bf16[32,8,512]{2,1,0:T(8,128)(2,1)S(1)}, u32[]{:S(2)}, u32[]{:S(2)}) async-start(bf16[32,8,512]{2,1,0:T(8,128)(2,1)} %bitcast.24), calls=%async_computation.2 | async-start | bytes 524288 | tf_op jit(solution)/shard_map/all_to_all | solution.py:408
  108.8 16.5 %copy-start.9 = (bf16[32,8,512]{2,1,0:T(8,128)(2,1)}, bf16[32,8,512]{2,1,0:T(8,128)(2,1)S(1)}, u32[]{:S(2)}) copy-start(bf16[32,8,512]{2,1,0:T(8,128)(2,1)S(1)} %all-to-all-done.2) | copy-start | bytes 786436

commit v2 on v1

v2 whole, which is shorter than its diff:
```python
import functools

import jax
import jax.numpy as jnp
from jax import lax
from jax.experimental import pallas as pl
from jax.experimental.pallas import tpu as pltpu
from jax.sharding import PartitionSpec as P

ROPE_BASE = 500000.0
EPSILON = 1e-05
NEGATIVE = -1e30
LANES = 128


def iota(shape, dim):
    return lax.broadcasted_iota(jnp.int32, shape, dim)


def as_float(flags):
    return jnp.where(flags, 1.0, 0.0).astype(jnp.float32)


def contract(left, right, left_dim, right_dim):
    return lax.dot_general(
        left, right, (((left_dim,), (right_dim,)), ((), ())), preferred_element_type=jnp.float32
    )


def pieces_of(column_count):
    return 2 if column_count % (2 * LANES) == 0 else 1


def pack_kernel(lengths_ref, route_ref, hidden_ref, out_ref, *, groups):
    micro_count, doc_count = lengths_ref.shape
    source_rows, column_count = hidden_ref.shape
    row_count = source_rows // micro_count
    half = row_count // 2
    pieces = pieces_of(column_count)
    width = column_count // pieces
    total = out_ref.shape[0]

    shape = (source_rows, LANES)
    batch, offset = iota(shape, 0) // row_count, iota(shape, 0) % row_count
    document = jnp.zeros(shape, jnp.int32)
    opening = jnp.zeros(shape, jnp.int32)
    for micro in range(micro_count):
        end = jnp.int32(0)
        for doc in range(doc_count - 1):
            end = end + lengths_ref[micro, doc]
            passed = (batch == micro) & (offset >= end)
            document = document + jnp.where(passed, 1, 0)
            opening = jnp.where(passed, end, opening)
    lane = iota(shape, 1)
    first = offset < half
    tags = jnp.where(
        lane == 0,
        jnp.where(first, 1, 0),
        jnp.where(
            lane == 1,
            jnp.where(first, 0, 1),
            jnp.where(lane == 2, document, jnp.where(lane == 3, offset - opening, 0)),
        ),
    )
    tags = tags.astype(jnp.float32).astype(jnp.bfloat16)

    shape = (total, source_rows)
    row, source = iota(shape, 0), iota(shape, 1)
    slot = source // half
    target = jnp.full(shape, -1, jnp.int32)
    for micro in range(micro_count):
        for side in range(2):
            target = jnp.where(
                slot == 2 * micro + side, micro * groups + route_ref[micro, side], target
            )
    going = target == row // row_count
    inner, wanted = row % row_count, source % half
    packed = jnp.zeros((total, width), jnp.float32)
    for piece in range(pieces):
        chosen = as_float(going & (inner == piece * half + wanted)).astype(jnp.bfloat16)
        packed += contract(chosen, hidden_ref[:, piece * width : (piece + 1) * width], 1, 0)
    chosen = as_float(going & (inner % half == wanted)).astype(jnp.bfloat16)
    out_ref[:, :width] = packed.astype(jnp.bfloat16)
    out_ref[:, width:] = contract(chosen, tags, 1, 0).astype(jnp.bfloat16)


def choosers(tags, row_count, pieces):
    half = row_count // 2
    shape = (tags.shape[0], row_count)
    inner, wanted = iota(shape, 0) % row_count, iota(shape, 1)
    came = jnp.where(wanted < half, tags[:, 0:1], tags[:, 1:2])
    return [
        jnp.where(inner == piece * half + wanted % half, came, 0.0).astype(jnp.bfloat16)
        for piece in range(pieces)
    ]


def turned(vector, cosine, sine):
    return vector * cosine + pltpu.roll(vector, vector.shape[1] // 2, 1) * sine


def heads_down(rows, head_size):
    count = rows.shape[1] // head_size
    return jnp.concatenate(
        [rows[:, head * head_size : (head + 1) * head_size] for head in range(count)], axis=0
    )


def heads_across(stacked, row_count):
    count = stacked.shape[0] // row_count
    return jnp.concatenate(
        [stacked[head * row_count : (head + 1) * row_count] for head in range(count)], axis=1
    )


def turned_heads(rows, cosine, sine):
    stacked = heads_down(rows, cosine.shape[1])
    repeats = stacked.shape[0] // rows.shape[0]
    return turned(stacked, jnp.tile(cosine, (repeats, 1)), jnp.tile(sine, (repeats, 1)))


def forward_layer(rows, gain_row, weight, cosine, sine, allowed):
    row_count, feature_count = rows.shape
    head_size = cosine.shape[1]
    scale = lax.rsqrt(jnp.sum(rows * rows, axis=1, keepdims=True) / feature_count + EPSILON)
    normed = rows * scale * gain_row
    packed = normed.astype(jnp.bfloat16)
    pair = jnp.dot(packed, weight, preferred_element_type=jnp.float32)
    queries = turned_heads(normed, cosine, sine).astype(jnp.bfloat16)
    keys = turned(pair[:, :head_size], cosine, sine).astype(jnp.bfloat16)
    values = pair[:, head_size:].astype(jnp.bfloat16)
    scores = contract(keys, queries, 1, 1) * head_size ** (-0.5)
    scores = jnp.where(allowed, scores, NEGATIVE)
    raised = jnp.exp(scores - jnp.max(scores, axis=0, keepdims=True))
    weights = raised / jnp.sum(raised, axis=0, keepdims=True)
    mixed = contract(weights.astype(jnp.bfloat16), values, 0, 0)
    kept = (scale, keys, values, weights)
    return rows + heads_across(mixed, row_count), packed, kept


def backward_layer(upstream, rows, gain_row, weight, cosine, sine, kept):
    scale, keys, values, weights = kept
    row_count, feature_count = rows.shape
    head_size = cosine.shape[1]
    queries = turned_heads(rows * scale * gain_row, cosine, sine).astype(jnp.bfloat16)
    stacked = heads_down(upstream, head_size).astype(jnp.bfloat16)
    d_weights = contract(values, stacked, 1, 1).astype(jnp.bfloat16).astype(jnp.float32)
    d_values = contract(weights.astype(jnp.bfloat16), stacked, 1, 0)
    d_scores = weights * (d_weights - jnp.sum(d_weights * weights, axis=0, keepdims=True))
    d_scores = (d_scores * head_size ** (-0.5)).astype(jnp.bfloat16)
    d_keys = contract(d_scores, queries, 1, 0)
    terms = jnp.concatenate([turned(d_keys, cosine, -sine), d_values], axis=1)
    terms = terms.astype(jnp.bfloat16)
    d_queries = contract(d_scores, keys, 0, 0)
    repeats = stacked.shape[0] // row_count
    d_queries = turned(d_queries, jnp.tile(cosine, (repeats, 1)), jnp.tile(-sine, (repeats, 1)))
    d_normed = contract(terms, weight, 1, 1) + heads_across(d_queries, row_count)
    scaled = d_normed * gain_row
    inner = jnp.sum(scaled * rows, axis=1, keepdims=True) / feature_count
    return upstream + scale * scaled - rows * (scale * scale * scale * inner), terms


def state_width(feature_count, head_size):
    return feature_count + 4 * head_size


def save_layer(index, rows, kept, state_ref):
    scale, keys, values, weights = kept
    feature_count, head_size = rows.shape[1], keys.shape[1]
    state_ref[index, :, :feature_count] = rows
    parts = (weights, keys, values, jnp.broadcast_to(scale, keys.shape))
    for place, part in enumerate(parts):
        start = feature_count + place * head_size
        state_ref[index, :, start : start + head_size] = part.astype(jnp.float32)


def load_layer(index, state_ref, feature_count):
    head_size = (state_ref.shape[2] - feature_count) // 4
    parts = []
    for place in range(4):
        start = feature_count + place * head_size
        parts.append(state_ref[index, :, start : start + head_size])
    weights, keys, values, scale = parts
    kept = (scale[:, 0:1], keys.astype(jnp.bfloat16), values.astype(jnp.bfloat16), weights)
    return state_ref[index, :, :feature_count], kept


def repeat_steps(count, step, carry):
    if count <= 8:
        for index in range(count):
            carry = step(index, carry)
        return carry
    return lax.fori_loop(0, count, step, carry)


def forward_steps(rows, own, gain_ref, weight_ref, tables, state_ref, packed_ref):
    cosine, sine, allowed = tables
    groups = packed_ref.shape[1]
    share = weight_ref.shape[1] // groups

    def step(index, rows):
        place = lax.bitwise_xor(own, index)
        gain_row = gain_ref[pl.ds(place, 1), :]
        after, packed, kept = forward_layer(
            rows, gain_row, weight_ref[place], cosine, sine, allowed
        )
        for group in range(groups):
            packed_ref[index, group, :, :share] = packed[:, group * share : (group + 1) * share]
        save_layer(index, rows, kept, state_ref)
        return after

    return repeat_steps(weight_ref.shape[0], step, rows)


def backward_steps(upstream, own, gain_ref, weight_ref, tables, state_ref, terms_ref, start):
    cosine, sine, _ = tables
    count = weight_ref.shape[0]
    width = weight_ref.shape[2]

    def step(back, upstream):
        index = count - 1 - back
        place = lax.bitwise_xor(own, index)
        gain_row = gain_ref[pl.ds(place, 1), :]
        rows, kept = load_layer(index, state_ref, weight_ref.shape[1])
        before, terms = backward_layer(
            upstream, rows, gain_row, weight_ref[place], cosine, sine, kept
        )
        for group in range(terms_ref.shape[1]):
            terms_ref[index, group, :, start : start + width] = terms
        return before

    return repeat_steps(count, step, upstream)


def fill(turn, key_ref, value_ref, shares, weight_ref, sems, start):
    share = shares[0].shape[2]
    sections = shares[0].shape[1] + 1
    head_size = key_ref.shape[2]
    own = lax.axis_index("dp")
    copies = [
        (key_ref.at[turn], weight_ref.at[start, :, :head_size]),
        (value_ref.at[turn], weight_ref.at[start, :, head_size:]),
    ]
    for core, ref in enumerate(shares):
        for chip in range(ref.shape[0]):
            place = lax.bitwise_xor(own, 2 * chip + core) * share
            rows = pl.ds(pl.multiple_of(place, share), share)
            copies.append(
                (ref.at[chip], weight_ref.at[pl.ds(start + 1, sections - 1), rows])
            )
    copies = [
        pltpu.make_async_copy(*pair, sems.at[turn, index]) for index, pair in enumerate(copies)
    ]
    for copy in copies:
        copy.start()
    return copies


def unpack_gains(own_ref, tails_ref, gain_ref):
    sections = tails_ref.shape[0] + 1
    width = tails_ref.shape[2]
    lines = gain_ref.shape[1] // width
    for turn in range(2):
        start = sections * turn
        gain_ref[start : start + 1, :] = own_ref[turn : turn + 1, :]
        for place in range(1, sections):
            tail = tails_ref[place - 1].astype(jnp.float32)
            first = 3 * lines * turn
            terms = [tail[first + lines * term : first + lines * (term + 1)] for term in range(3)]
            total = terms[0] + terms[1] + terms[2]
            for line in range(lines):
                gain_ref[
                    start + place : start + place + 1, line * width : (line + 1) * width
                ] = total[line : line + 1]


def gain_terms(gain, width):
    first = lax.reduce_precision(gain, 8, 7)
    second = lax.reduce_precision(gain - first, 8, 7)
    third = gain - first - second
    terms = jnp.stack([first, second, third], axis=1).astype(jnp.bfloat16)
    return terms.reshape(-1, width)


def first_kernel(
    arrived_ref,
    upstream_ref,
    own_gain_ref,
    tails_ref,
    key_ref,
    value_ref,
    share_ref,
    other_ref,
    state_ref,
    aux_ref,
    gain_ref,
    packed_ref,
    weight_ref,
    sems,
    *,
    sections
):
    copies = fill(0, key_ref, value_ref, (share_ref, other_ref), weight_ref, sems, 0)
    unpack_gains(own_gain_ref, tails_ref, gain_ref)
    state_ref[sections + 1, :, : upstream_ref.shape[1]] = upstream_ref[...]
    row_count, feature_count = upstream_ref.shape
    head_size = weight_ref.shape[2] // 2
    column_count = feature_count // sections
    pieces = pieces_of(column_count)
    width = column_count // pieces
    block = arrived_ref.shape[0] // sections
    tags = arrived_ref[:block, width:].astype(jnp.float32)
    chosen = choosers(tags, row_count, pieces)
    cuts = []
    for section in range(sections):
        part = arrived_ref[section * block : (section + 1) * block, :width]
        cuts += [contract(chooser, part, 0, 0) for chooser in chosen]
    rows = jnp.concatenate(cuts, axis=1)
    own = contract(chosen[0], tags.astype(jnp.bfloat16), 0, 0)
    document, position = own[:, 2:3], own[:, 3:4]
    lane = iota((1, head_size), 1)
    middle = head_size // 2
    exponent = (lane % middle).astype(jnp.float32) * (2.0 / head_size)
    angles = position * jnp.exp(exponent * -jnp.log(jnp.float32(ROPE_BASE)))
    cosine = jnp.cos(angles)
    sine = jnp.where(lane < middle, -jnp.sin(angles), jnp.sin(angles))
    shape = (row_count, row_count * feature_count // head_size)
    pick = as_float(iota(shape, 1) % row_count == iota(shape, 0))
    document_across = jnp.sum(document * pick, axis=0, keepdims=True)
    position_across = jnp.sum(position * pick, axis=0, keepdims=True)
    allowed = (document == document_across) & (position <= position_across)
    for place, table in enumerate((cosine, sine, as_float(allowed))):
        aux_ref[place * row_count : (place + 1) * row_count] = table
    aux_ref[3 * row_count :] = tags
    for copy in copies:
        copy.wait()
    own = lax.axis_index("pipe")
    tables = (cosine, sine, allowed)
    state_ref[sections, :, :feature_count] = forward_steps(
        rows, own, gain_ref, weight_ref, tables, state_ref, packed_ref
    )


def second_kernel(
    first_ref,
    aux_ref,
    gain_ref,
    key_ref,
    value_ref,
    share_ref,
    other_ref,
    late_share_ref,
    late_other_ref,
    out_ref,
    state_ref,
    weight_ref,
    sems,
    *,
    sections
):
    late_copies = fill(
        1, key_ref, value_ref, (late_share_ref, late_other_ref), weight_ref, sems, sections
    )
    copies = fill(0, key_ref, value_ref, (share_ref, other_ref), weight_ref, sems, 0)
    own = lax.axis_index("pipe")
    _, feature_count, term_width = weight_ref.shape
    row_count = first_ref.shape[1]
    groups = out_ref.shape[1]
    share = feature_count // groups
    cosine, sine, allowed = [
        aux_ref[place * row_count : (place + 1) * row_count] for place in range(3)
    ]
    tables = (cosine, sine, allowed > 0.5)
    late_gain = gain_ref.at[pl.ds(sections, sections)]
    late_weight = weight_ref.at[pl.ds(sections, sections)]
    for copy in late_copies:
        copy.wait()
    forward_steps(
        first_ref[sections, :, :feature_count],
        own,
        late_gain,
        late_weight,
        tables,
        state_ref,
        out_ref,
    )
    upstream = backward_steps(
        first_ref[sections + 1, :, :feature_count],
        own,
        late_gain,
        late_weight,
        tables,
        state_ref,
        out_ref,
        share + term_width,
    )
    for copy in copies:
        copy.wait()
    grads = backward_steps(
        upstream,
        own,
        gain_ref.at[pl.ds(0, sections)],
        weight_ref.at[pl.ds(0, sections)],
        tables,
        first_ref,
        out_ref,
        share,
    ).astype(jnp.bfloat16)
    column_count = feature_count // sections
    pieces = pieces_of(column_count)
    width = column_count // pieces
    chosen = choosers(aux_ref[3 * row_count :, :], row_count, pieces)
    for section in range(sections):
        start = section * column_count
        going = contract(chosen[0], grads[:, start : start + width], 1, 0)
        for piece in range(1, pieces):
            left = start + piece * width
            going += contract(chosen[piece], grads[:, left : left + width], 1, 0)
        going = going.astype(jnp.bfloat16)
        for group in range(groups):
            out_ref[section, group, :, share + 2 * term_width :] = going[
                group * row_count : (group + 1) * row_count
            ]


def last_kernel(
    route_ref, first_ref, late_ref, grad_ref, key_ref, value_ref, *, groups
):
    micro_count = route_ref.shape[0]
    source_rows, column_count = grad_ref.shape
    row_count = source_rows // micro_count
    half = row_count // 2
    share, head_size = key_ref.shape[1:]
    term_width = 2 * head_size
    width = late_ref.shape[1] - share - 2 * term_width
    pieces = column_count // width
    for index, packed in enumerate((first_ref[...], late_ref[:, :share])):
        start = share + index * term_width
        total = contract(packed, late_ref[:, start : start + term_width], 0, 0)
        key_ref[index] = total[:, :head_size]
        value_ref[index] = total[:, head_size:]
    shape = (source_rows, late_ref.shape[0])
    row, source = iota(shape, 1), iota(shape, 0)
    slot = source // half
    target = jnp.full(shape, -1, jnp.int32)
    for micro in range(micro_count):
        for side in range(2):
            target = jnp.where(
                slot == 2 * micro + side, micro * groups + route_ref[micro, side], target
            )
    going = target == row // row_count
    inner, wanted = row % row_count, source % half
    for piece in range(pieces):
        chosen = as_float(going & (inner == piece * half + wanted)).astype(jnp.bfloat16)
        grad_ref[:, piece * width : (piece + 1) * width] = contract(
            chosen, late_ref[:, share + 2 * term_width :], 1, 0
        ).astype(jnp.bfloat16)


def call(kernel, outs, operands, scalars=0, whole=0, scratch=(), vmem_bytes=24 << 20, cost=0):
    spaces = [pltpu.SMEM] * scalars + [pltpu.VMEM] * (len(operands) - scalars - whole)
    spaces += [pl.ANY] * whole
    return pl.pallas_call(
        kernel,
        out_shape=outs,
        in_specs=[pl.BlockSpec(memory_space=space) for space in spaces],
        out_specs=[pl.BlockSpec(memory_space=pltpu.VMEM)] * len(outs),
        scratch_shapes=scratch,
        compiler_params=pltpu.CompilerParams(vmem_limit_bytes=vmem_bytes),
        cost_estimate=pl.CostEstimate(flops=0, bytes_accessed=cost, transcendentals=0),
    )(*operands)


def exchange(blocks):
    return lax.all_to_all(blocks, ("pipe", "dp"), split_axis=0, concat_axis=0, tiled=True)


def swapped(value, axis, mask):
    pairs = [(source, source ^ mask) for source in range(lax.axis_size(axis))]
    return lax.ppermute(value, axis, pairs)


def section_pieces(payload):
    return [swapped(payload, "pipe", mask) for mask in range(1, lax.axis_size("pipe"))]


def plane_pieces(column):
    return [swapped(column, "dp", 2 * mask) for mask in range(1, lax.axis_size("dp") // 2)]


def body(hidden, lengths, route, gain, key_weight, value_weight, cotangent):
    groups = lax.axis_size("dp")
    sections = lax.axis_size("pipe")
    group_index = lax.axis_index("dp")
    section_index = lax.axis_index("pipe")
    micro_count = lengths.shape[0]
    assert micro_count == sections
    source_rows, column_count = hidden.shape
    row_count = source_rows // micro_count
    feature_count = gain.shape[1]
    head_size = key_weight.shape[2]
    assert row_count * feature_count == head_size * head_size
    share = feature_count // groups
    width = column_count // pieces_of(column_count)
    devices = sections * groups

    (outgoing,) = call(
        functools.partial(pack_kernel, groups=groups),
        [jax.ShapeDtypeStruct((devices * row_count, width + LANES), jnp.bfloat16)],
        (lengths, route, hidden),
        scalars=2,
    )
    arrived = exchange(outgoing.reshape(devices, row_count, width + LANES)).reshape(
        devices * row_count, width + LANES
    )
    def own_share(turn):
        parts = [
            lax.dynamic_slice(array, (turn, group_index * share, 0), (1, share, head_size))[0]
            for array in (key_weight, value_weight)
        ]
        return jnp.concatenate(parts, axis=1)

    column = jnp.stack(section_pieces(own_share(0)))
    payload = jnp.concatenate([own_share(1), gain_terms(gain, 2 * head_size)], axis=0)
    upstream = lax.dynamic_slice_in_dim(
        cotangent, section_index * row_count, row_count, 0
    ).astype(jnp.float32)
    column, payload, upstream = lax.optimization_barrier((column, payload, upstream))
    plane = jnp.stack([column] + plane_pieces(column))
    came = section_pieces(payload)
    plane, came, arrived = lax.optimization_barrier((plane, came, arrived))
    first_shares = (plane, swapped(plane, "dp", 1))
    column = jnp.stack([piece[:share] for piece in came])
    tails = jnp.stack([piece[share:] for piece in came])
    planes = [column] + plane_pieces(column)

    def layers_call(kernel, turns, outs, operands, shares, scratch, cost):
        places = turns * sections
        return call(
            functools.partial(kernel, sections=sections),
            outs,
            (*operands, key_weight, value_weight, *shares),
            whole=2 + len(shares),
            scratch=[
                *scratch,
                pltpu.VMEM((places, feature_count, 2 * head_size), jnp.bfloat16),
                pltpu.SemaphoreType.DMA((2, groups + 2)),
            ],
            vmem_bytes=(14 << 20) + 5 * places * feature_count * head_size,
            cost=cost,
        )

    def blocks_shape(columns):
        return jax.ShapeDtypeStruct((sections, groups, row_count, columns), jnp.bfloat16)

    def exchanged(blocks):
        columns = blocks.shape[3]
        got = exchange(blocks.reshape(devices, row_count, columns))
        return got.reshape(devices * row_count, columns)

    line = (row_count, state_width(feature_count, head_size))
    state, aux, gains, packed = layers_call(
        first_kernel,
        1,
        [
            jax.ShapeDtypeStruct((sections + 2, *line), jnp.float32),
            jax.ShapeDtypeStruct(((3 + groups) * row_count, head_size), jnp.float32),
            jax.ShapeDtypeStruct((2 * sections, feature_count), jnp.float32),
            blocks_shape(share),
        ],
        (arrived, upstream, gain, tails),
        first_shares,
        (),
        18 << 20,
    )
    state, packed, planes = lax.optimization_barrier((state, packed, planes))
    packed = exchanged(packed)
    plane = jnp.stack(planes)
    second_shares = (plane, swapped(plane, "dp", 1))
    (late,) = layers_call(
        second_kernel,
        2,
        [blocks_shape(share + 4 * head_size + width)],
        (state, aux, gains),
        (*first_shares, *second_shares),
        (pltpu.VMEM((sections, *line), jnp.float32),),
        48 << 20,
    )
    late, packed = lax.optimization_barrier((late, packed))
    late = exchanged(late)
    grad_shape = jax.ShapeDtypeStruct((2, share, head_size), jnp.float32)
    return tuple(
        call(
            functools.partial(last_kernel, groups=groups),
            [jax.ShapeDtypeStruct((source_rows, column_count), jnp.bfloat16)] + [grad_shape] * 2,
            (route, packed, late),
            scalars=1,
        )
    )


def solution(mesh):
    placed = (
        P("dp", "pipe"),
        P("dp", None),
        P("dp", None),
        P("pipe", None),
        P("pipe", None, None),
        P("pipe", None, None),
        P("dp", None),
    )
    return jax.shard_map(
        body,
        mesh=mesh,
        in_specs=placed,
        out_specs=(P("dp", "pipe"), P("pipe", "dp", None), P("pipe", "dp", None)),
        check_vma=False,
    )
```

time: 128 us -> 118 us (0.922)
  local copies, waits for them, and re-layouts: 2.43 us -> 13.5 us
  starting transfers between devices: 35 us -> 25 us
  Pallas kernels: 28.6 us -> 19.8 us
  waiting for transfers between devices: 42.5 us -> 33.7 us
  blocking collectives: 16.5 us -> 20.6 us
  other arithmetic: 1.51 us -> 3.93 us
    ppermute x23 -> x14, starting transfers between devices: 28.4 us -> 17.3 us  [swapped(): return lax.ppermute(value, axis, pairs)]
    all_to_all x2, waiting for transfers between devices: 10.6 us -> 0.01 us  [exchange(): lax.all_to_all(blocks, ('pipe', 'dp'), split_axis=0, concat_axis=0, tiled...]
    pallas_call x5 -> x4, Pallas kernels: 28.6 us -> 19.8 us  [call(): pl.pallas_call(kernel, out_shape=outs, in_specs=[pl.BlockSpec(memory_spac...]
    unnamed x31 -> x27, local copies, waits for them, and re-layouts: 1.47 us -> 7.5 us
    another operation x0 -> x7, local copies, waits for them, and re-layouts: none -> 4.98 us  [the longest x3 2.74 us: body(): column = jnp.stack([piece[:share] for piece in came])]
    all_to_all x1, blocking collectives: 16.5 us -> 20.6 us  [exchange(): lax.all_to_all(blocks, ('pipe', 'dp'), split_axis=0, concat_axis=0, tiled...]
    another operation x2 -> x7, other arithmetic: 0.09 us -> 2.46 us  [the longest x1 1.38 us: body(): plane = jnp.stack(planes)]
    ppermute x23 -> x14, waiting for transfers between devices: 32 us -> 33.6 us  [swapped(): return lax.ppermute(value, axis, pairs)]
  transfers between devices with their start and end apart: 25 -> 16, of which waited for: 10 -> 8; matrix products, arithmetic and copies ran while one was open for 2% -> 6% of each run, Pallas kernels for 13% -> 15%
where the time goes in v2:
time: 118 us; the launch traced here: 117 us
  waiting for transfers between devices  33.7 us (29%)
  starting transfers between devices  25 us (21%)
  blocking collectives  20.6 us (17%)
  Pallas kernels  19.8 us (17%)
  local copies, waits for them, and re-layouts  13.5 us (11%)
  other arithmetic  3.93 us (3%)
    ppermute x14, waiting for transfers between devices, swapped(): return lax.ppermute(value, axis, pairs)  33.6 us
    all_to_all x1, blocking collectives, exchange(): lax.all_to_all(blocks, ('pipe', 'dp'), split_axis=0, concat_axis=0, tiled...  20.6 us
    pallas_call x4, Pallas kernels, call(): pl.pallas_call(kernel, out_shape=outs, in_specs=[pl.BlockSpec(memory_spac...  19.8 us
    ppermute x14, starting transfers between devices, swapped(): return lax.ppermute(value, axis, pairs)  17.3 us
    all_to_all x2, starting transfers between devices, exchange(): lax.all_to_all(blocks, ('pipe', 'dp'), split_axis=0, concat_axis=0, tiled...  7.65 us
    unnamed x27, local copies, waits for them, and re-layouts  7.5 us
    another operation x3, local copies, waits for them, and re-layouts, body(): column = jnp.stack([piece[:share] for piece in came])  2.74 us
  transfers between devices with their start and end apart: 16, of which 8 were waited for; matrix products, arithmetic and copies ran while one was open for 6% of the time, Pallas kernels for 15%

profile of v2, /device:TPU:0, one launch (start us, length us, event | category | flops | bytes accessed | tf_op | source)
XLA Modules:
  0.0 117.2 jit_solution(4444258738496948319)
XLA Ops:
  0.6 0.0 copy-start.12
  0.6 0.0 copy-start.9
  0.7 0.0 copy-start.8
  0.7 1.0 dynamic-slice_bitcast_fusion
  1.7 5.1 %collective-permute-start.2 = (bf16[256,256]{1,0:T(8,128)(2,1)S(1)}, bf16[256,256]{1,0:T(8,128)(2,1)S(1)}, u32[]{:S(2)}, u32[]{:S(2)}) collective-permute-start(bf16[256,256]{1,0:T(8,128)(2,1)S(1)} %pad_maximum_fusion.5), channel_id=1, source_target_pairs={{0,24},{8,16},{16,8},{24,0},{1,25},{9,17},{17,9},{25,1},{2,26},{10... | collective-permute-start | bytes 393224 | tf_op jit(solution)/shard_map/ppermute | solution.py:480
  6.8 0.0 collective-permute-start.1
  6.8 0.6 collective-permute-start
  7.4 0.7 fusion.1
  8.2 0.8 dynamic-slice_convert_fusion.upstream_ref
  9.0 0.7 pad_maximum_fusion.4
  9.7 1.5 %collective-permute-done.2 = bf16[256,256]{1,0:T(8,128)(2,1)S(1)} collective-permute-done((bf16[256,256]{1,0:T(8,128)(2,1)S(1)}, bf16[256,256]{1,0:T(8,128)(2,1)S(1)}, u32[]{:S(2)}, u32[]{:S(2)}) %collective-permute-start.2) | collective-permute-done | bytes 131104 | tf_op jit(solution)/shard_map/ppermute | solution.py:480
  11.2 6.6 %collective-permute-done.1 = bf16[256,256]{1,0:T(8,128)(2,1)S(1)} collective-permute-done((bf16[256,256]{1,0:T(8,128)(2,1)S(1)}, bf16[256,256]{1,0:T(8,128)(2,1)S(1)}, u32[]{:S(2)}, u32[]{:S(2)}) %collective-permute-start.1) | collective-permute-done | bytes 131104 | tf_op jit(solution)/shard_map/ppermute | solution.py:480
  17.8 0.0 collective-permute-done
  17.9 2.5 %collective-permute-start.5 = (bf16[3,256,256]{2,1,0:T(8,128)(2,1)S(1)}, bf16[3,256,256]{2,1,0:T(8,128)(2,1)S(1)}, u32[]{:S(2)}, u32[]{:S(2)}) collective-permute-start(bf16[3,256,256]{2,1,0:T(8,128)(2,1)S(1)} %pad_maximum_fusion.2), channel_id=1, source_target_pairs={{0,6},{1,7},{2,4},{3,5},{4,2},{5,3},{6,0},{7,1},{8,14},{9,15},{10,... | collective-permute-start | bytes 1179656 | tf_op jit(solution)/shard_map/ppermute | solution.py:480
  20.4 0.5 collective-permute-start.4
  20.9 0.5 collective-permute-start.3
  21.5 0.1 copy.15.route_ref
  21.6 0.0 copy-done.8
  21.6 1.5 %shard_map.94 = bf16[256,384]{1,0:T(8,128)(2,1)} custom-call(s32[4,4]{1,0:T(4,128)S(1)} %copy-done.9, s32[4,2]{1,0:T(4,128)S(1)} %copy.15.route_ref, bf16[32,512]{1,0:T(8,128)(2,1)S(1)} %copy-done.8), custom_call_target="tpu_custom_call" | custom-call | tf_op jit(solution)/shard_map/pallas_call | solution.py:463
  23.1 4.7 %all-to-all-start = ((bf16[32,8,384]{2,1,0:T(8,128)(2,1)}), bf16[32,8,384]{2,1,0:T(8,128)(2,1)S(1)}, u32[]{:S(2)}, u32[]{:S(2)}) async-start(bf16[32,8,384]{2,1,0:T(8,128)(2,1)} %bitcast.14), calls=%async_computation | async-start | bytes 393216 | tf_op jit(solution)/shard_map/all_to_all | solution.py:475
  27.8 3.7 %collective-permute-start.8 = (bf16[304,256]{1,0:T(8,128)(2,1)}, bf16[304,256]{1,0:T(8,128)(2,1)S(1)}, u32[]{:S(2)}, u32[]{:S(2)}) collective-permute-start(bf16[304,256]{1,0:T(8,128)(2,1)} %pad_maximum_fusion.4), channel_id=1, source_target_pairs={{0,24},{8,16},{16,8},{24,0},{1,25},{9,17},{17,9},{25,1},{2,26},{10... | collective-permute-start | bytes 466952 | tf_op jit(solution)/shard_map/ppermute | solution.py:480
  31.5 0.0 collective-permute-start.7
  31.5 0.0 collective-permute-done.5
  31.5 0.8 collective-permute-start.6
  32.3 6.9 %collective-permute-done.4 = bf16[3,256,256]{2,1,0:T(8,128)(2,1)S(1)} collective-permute-done((bf16[3,256,256]{2,1,0:T(8,128)(2,1)S(1)}, bf16[3,256,256]{2,1,0:T(8,128)(2,1)S(1)}, u32[]{:S(2)}, u32[]{:S(2)}) %collective-permute-start.4) | collective-permute-done | bytes 393248 | tf_op jit(solution)/shard_map/ppermute | solution.py:480
  39.2 0.1 collective-permute-done.3
  39.3 0.2 pad_maximum_fusion.share_ref
  39.5 0.0 copy-start.7
  39.6 0.0 collective-permute-done.8
  39.6 9.6 %collective-permute-done.7 = bf16[304,256]{1,0:T(8,128)(2,1)S(1)} collective-permute-done((bf16[304,256]{1,0:T(8,128)(2,1)}, bf16[304,256]{1,0:T(8,128)(2,1)S(1)}, u32[]{:S(2)}, u32[]{:S(2)}) %collective-permute-start.7) | collective-permute-done | bytes 155680 | tf_op jit(solution)/shard_map/ppermute | solution.py:480
  49.1 0.7 copy-done.11
  49.8 0.0 collective-permute-done.6
  49.8 0.0 all-to-all-done
  49.8 0.0 collective-permute-start.9
  49.8 0.9 slice_bitcast_fusion.2
  50.7 0.9 slice_bitcast_fusion.1
  51.7 0.9 slice_bitcast_fusion
  52.6 2.5 %collective-permute-start.12 = (bf16[3,256,256]{2,1,0:T(8,128)(2,1)S(1)}, bf16[3,256,256]{2,1,0:T(8,128)(2,1)S(1)}, u32[]{:S(2)}, u32[]{:S(2)}) collective-permute-start(bf16[3,256,256]{2,1,0:T(8,128)(2,1)S(1)} %pad_maximum_fusion.3), channel_id=1, source_target_pairs={{0,6},{1,7},{2,4},{3,5},{4,2},{5,3},{6,0},{7,1},{8,14},{9,15},{10,... | collective-permute-start | bytes 1179656 | tf_op jit(solution)/shard_map/ppermute | solution.py:480
  55.1 0.5 collective-permute-start.11
  55.6 0.6 collective-permute-start.10
  56.2 0.7 slice_bitcast_fusion.5
  56.9 0.7 slice_bitcast_fusion.4
  57.7 0.7 slice_bitcast_fusion.3
  58.4 0.0 collective-permute-done.9.other_ref
  58.4 0.0 copy-start
  58.5 1.2 %copy-done = bf16[2,2048,128]{2,1,0:T(8,128)(2,1)S(1)} copy-done((bf16[2,2048,128]{2,1,0:T(8,128)(2,1)S(1)}, bf16[2,2048,128]{2,1,0:T(8,128)(2,1)}, u32[]{:S(2)}) %copy-start) | copy-done | bytes 1048600
  59.7 1.2 %copy-done.2 = bf16[2,2048,128]{2,1,0:T(8,128)(2,1)S(1)} copy-done((bf16[2,2048,128]{2,1,0:T(8,128)(2,1)S(1)}, bf16[2,2048,128]{2,1,0:T(8,128)(2,1)}, u32[]{:S(2)}) %copy-start.2) | copy-done | bytes 1048600
  60.9 4.6 %shard_map.95 = (f32[6,8,2560]{2,1,0:T(8,128)S(1)}, f32[88,128]{1,0:T(8,128)S(1)}, f32[8,2048]{1,0:T(8,128)S(1)}, bf16[4,8,8,256]{3,2,1,0:T(8,128)(2,1)}) custom-call(bf16[256,384]{1,0:T(8,128)(2,1)S(1)} %bitcast.45, f32[8,2048]{1,0:T(8,128)S(1)} %dynamic-slice_convert_fusion.upstream_ref, f32[2,2048]{1,0:T(2,128)S(1)} %copy-done.7, ...), custom_call_target="tpu_custom_call" | custom-call | bytes 18874368 | tf_op jit(solution)/shard_map/pallas_call | solution.py:463
  65.5 0.0 copy-start.5
  65.5 0.0 collective-permute-done.12
  65.6 8.0 %collective-permute-done.11 = bf16[3,256,256]{2,1,0:T(8,128)(2,1)S(1)} collective-permute-done((bf16[3,256,256]{2,1,0:T(8,128)(2,1)S(1)}, bf16[3,256,256]{2,1,0:T(8,128)(2,1)S(1)}, u32[]{:S(2)}, u32[]{:S(2)}) %collective-permute-start.11) | collective-permute-done | bytes 393248 | tf_op jit(solution)/shard_map/ppermute | solution.py:480
  73.6 0.1 collective-permute-done.10
  73.6 1.4 %pad_maximum_fusion.1.late_share_ref = bf16[4,3,256,256]{3,2,1,0:T(8,128)(2,1)} fusion(bf16[1,3,256,256]{3,2,1,0:T(8,128)(2,1)S(1)} %bitcast.49, bf16[1,3,256,256]{3,2,1,0:T(8,128)(2,1)S(1)} %bitcast.51, bf16[1,3,256,256]{3,2,1,0:T(8,128)(2,1)S(1)} %bitcast.53, bf16[1,3,256,256]{3,2,1,0:T(8,128)(2,1)S(1)} %bitcast.47), kind=kLoop, calls=%fused_computation.1 | loop fusion | flops 2359296 | bytes 3145728 | tf_op jit(solution)/shard_map/stack | solution.py:578
  75.0 0.0 collective-permute-start.13
  75.0 2.9 %all-to-all-start.1 = ((bf16[32,8,256]{2,1,0:T(8,128)(2,1)}), bf16[32,8,256]{2,1,0:T(8,128)(2,1)S(1)}, u32[]{:S(2)}, u32[]{:S(2)}) async-start(bf16[32,8,256]{2,1,0:T(8,128)(2,1)} %bitcast.26), calls=%async_computation.1 | async-start | bytes 262144 | tf_op jit(solution)/shard_map/all_to_all | solution.py:475
  77.9 0.8 collective-permute-done.13.late_other_ref
  78.7 1.2 %copy-done.1 = bf16[2,2048,128]{2,1,0:T(8,128)(2,1)S(1)} copy-done((bf16[2,2048,128]{2,1,0:T(8,128)(2,1)S(1)}, bf16[2,2048,128]{2,1,0:T(8,128)(2,1)}, u32[]{:S(2)}) %copy-start.1) | copy-done | bytes 1048600
  80.0 1.2 %copy-done.3 = bf16[2,2048,128]{2,1,0:T(8,128)(2,1)S(1)} copy-done((bf16[2,2048,128]{2,1,0:T(8,128)(2,1)S(1)}, bf16[2,2048,128]{2,1,0:T(8,128)(2,1)}, u32[]{:S(2)}) %copy-start.3) | copy-done | bytes 1048600
  81.2 1.0 copy-done.6
  82.2 12.0 %shard_map.96 = bf16[4,8,8,1024]{3,2,1,0:T(8,128)(2,1)S(1)} custom-call(f32[6,8,2560]{2,1,0:T(8,128)S(1)} %copy-done.6, f32[88,128]{1,0:T(8,128)S(1)} %get-tuple-element.34.aux_ref, f32[8,2048]{1,0:T(8,128)S(1)} %get-tuple-element.35.gain_ref, bf16[2,2048,128]{2,1,0:T(8,128)(2,1)S(1)} %copy-done.3, bf16[2,2048,128]{2,1,0:T(8,128)(2,1)S(1)} %copy-done.1, ...), custom_call_target="tpu_custom_call" | custom-call | bytes 50331648 | tf_op jit(solution)/shard_map/pallas_call | solution.py:463
  94.2 0.8 copy-done.4
  95.0 0.0 all-to-all-done.1
  95.0 20.6 %all_to_all.15 = bf16[32,8,1024]{2,1,0:T(8,128)(2,1)S(1)} all-to-all(bf16[32,8,1024]{2,1,0:T(8,128)(2,1)} %bitcast.43), channel_id=1, replica_groups=mesh['pipe'=4,'dp'=8] {'pipe','dp'}, dimensions={0} | all-to-all | bytes 1048576 | tf_op jit(solution)/shard_map/all_to_all | solution.py:475
  115.6 1.6 %shard_map.97 = (bf16[32,512]{1,0:T(8,128)(2,1)}, f32[2,256,128]{2,1,0:T(8,128)}, f32[2,256,128]{2,1,0:T(8,128)}) custom-call(s32[4,2]{1,0:T(4,128)S(1)} %copy.15.route_ref, bf16[256,256]{1,0:T(8,128)(2,1)S(1)} %bitcast.46, bf16[256,1024]{1,0:T(8,128)(2,1)S(1)} %bitcast.44), custom_call_target="tpu_custom_call" | custom-call | tf_op jit(solution)/shard_map/pallas_call | solution.py:463
  (19 shorter events, 0.2 us)
Async XLA Ops:
  0.6 20.8 %copy-start.12 = (s32[4,2]{0,1:T(2,128)S(1)}, s32[4,2]{0,1:T(2,128)}, u32[]{:S(2)}) copy-start(s32[4,2]{0,1:T(2,128)} %param.9) | copy-start | bytes 100
  0.6 20.9 %copy-start.9 = (s32[4,4]{1,0:T(4,128)S(1)}, s32[4,4]{1,0:T(4,128)}, u32[]{:S(2)}) copy-start(s32[4,4]{1,0:T(4,128)} %lengths_ref.1) | copy-start | bytes 196
  0.7 20.9 %copy-start.8 = (bf16[32,512]{1,0:T(8,128)(2,1)S(1)}, bf16[32,512]{1,0:T(8,128)(2,1)}, u32[]{:S(2)}) copy-start(bf16[32,512]{1,0:T(8,128)(2,1)} %hidden_ref.1) | copy-start | bytes 98308
  1.7 9.5 %collective-permute-start.2 = (bf16[256,256]{1,0:T(8,128)(2,1)S(1)}, bf16[256,256]{1,0:T(8,128)(2,1)S(1)}, u32[]{:S(2)}, u32[]{:S(2)}) collective-permute-start(bf16[256,256]{1,0:T(8,128)(2,1)S(1)} %pad_maximum_fusion.5), channel_id=1, source_target_pairs={{0,24},{8,16},{16,8},{24,0},{1,25},{9,17},{17,9},{25,1},{2,26},{10... | collective-permute-start | bytes 393224 | tf_op jit(solution)/shard_map/ppermute | solution.py:480
  6.8 11.1 %collective-permute-start.1 = (bf16[256,256]{1,0:T(8,128)(2,1)S(1)}, bf16[256,256]{1,0:T(8,128)(2,1)S(1)}, u32[]{:S(2)}, u32[]{:S(2)}) collective-permute-start(bf16[256,256]{1,0:T(8,128)(2,1)S(1)} %pad_maximum_fusion.5), channel_id=1, source_target_pairs={{0,16},{8,24},{16,0},{24,8},{1,17},{9,25},{17,1},{25,9},{2,18},{10... | collective-permute-start | bytes 393224 | tf_op jit(solution)/shard_map/ppermute | solution.py:480
  6.8 11.1 %collective-permute-start = (bf16[256,256]{1,0:T(8,128)(2,1)S(1)}, bf16[256,256]{1,0:T(8,128)(2,1)S(1)}, u32[]{:S(2)}, u32[]{:S(2)}) collective-permute-start(bf16[256,256]{1,0:T(8,128)(2,1)S(1)} %pad_maximum_fusion.5), channel_id=1, source_target_pairs={{0,8},{8,0},{16,24},{24,16},{1,9},{9,1},{17,25},{25,17},{2,10},{10... | collective-permute-start | bytes 393224 | tf_op jit(solution)/shard_map/ppermute | solution.py:480
  17.9 13.6 %collective-permute-start.5 = (bf16[3,256,256]{2,1,0:T(8,128)(2,1)S(1)}, bf16[3,256,256]{2,1,0:T(8,128)(2,1)S(1)}, u32[]{:S(2)}, u32[]{:S(2)}) collective-permute-start(bf16[3,256,256]{2,1,0:T(8,128)(2,1)S(1)} %pad_maximum_fusion.2), channel_id=1, source_target_pairs={{0,6},{1,7},{2,4},{3,5},{4,2},{5,3},{6,0},{7,1},{8,14},{9,15},{10,... | collective-permute-start | bytes 1179656 | tf_op jit(solution)/shard_map/ppermute | solution.py:480
  20.4 18.8 %collective-permute-start.4 = (bf16[3,256,256]{2,1,0:T(8,128)(2,1)S(1)}, bf16[3,256,256]{2,1,0:T(8,128)(2,1)S(1)}, u32[]{:S(2)}, u32[]{:S(2)}) collective-permute-start(bf16[3,256,256]{2,1,0:T(8,128)(2,1)S(1)} %pad_maximum_fusion.2), channel_id=1, source_target_pairs={{0,4},{1,5},{2,6},{3,7},{4,0},{5,1},{6,2},{7,3},{8,12},{9,13},{10,... | collective-permute-start | bytes 1179656 | tf_op jit(solution)/shard_map/ppermute | solution.py:480
  20.9 18.4 %collective-permute-start.3 = (bf16[3,256,256]{2,1,0:T(8,128)(2,1)S(1)}, bf16[3,256,256]{2,1,0:T(8,128)(2,1)S(1)}, u32[]{:S(2)}, u32[]{:S(2)}) collective-permute-start(bf16[3,256,256]{2,1,0:T(8,128)(2,1)S(1)} %pad_maximum_fusion.2), channel_id=1, source_target_pairs={{0,2},{1,3},{2,0},{3,1},{4,6},{5,7},{6,4},{7,5},{8,10},{9,11},{10,... | collective-permute-start | bytes 1179656 | tf_op jit(solution)/shard_map/ppermute | solution.py:480
  23.1 26.7 %all-to-all-start = ((bf16[32,8,384]{2,1,0:T(8,128)(2,1)}), bf16[32,8,384]{2,1,0:T(8,128)(2,1)S(1)}, u32[]{:S(2)}, u32[]{:S(2)}) async-start(bf16[32,8,384]{2,1,0:T(8,128)(2,1)} %bitcast.14), calls=%async_computation | async-start | bytes 393216 | tf_op jit(solution)/shard_map/all_to_all | solution.py:475
  27.8 11.7 %collective-permute-start.8 = (bf16[304,256]{1,0:T(8,128)(2,1)}, bf16[304,256]{1,0:T(8,128)(2,1)S(1)}, u32[]{:S(2)}, u32[]{:S(2)}) collective-permute-start(bf16[304,256]{1,0:T(8,128)(2,1)} %pad_maximum_fusion.4), channel_id=1, source_target_pairs={{0,24},{8,16},{16,8},{24,0},{1,25},{9,17},{17,9},{25,1},{2,26},{10... | collective-permute-start | bytes 466952 | tf_op jit(solution)/shard_map/ppermute | solution.py:480
  31.5 17.6 %collective-permute-start.7 = (bf16[304,256]{1,0:T(8,128)(2,1)}, bf16[304,256]{1,0:T(8,128)(2,1)S(1)}, u32[]{:S(2)}, u32[]{:S(2)}) collective-permute-start(bf16[304,256]{1,0:T(8,128)(2,1)} %pad_maximum_fusion.4), channel_id=1, source_target_pairs={{0,16},{8,24},{16,0},{24,8},{1,17},{9,25},{17,1},{25,9},{2,18},{10... | collective-permute-start | bytes 466952 | tf_op jit(solution)/shard_map/ppermute | solution.py:480
  31.5 18.3 %collective-permute-start.6 = (bf16[304,256]{1,0:T(8,128)(2,1)}, bf16[304,256]{1,0:T(8,128)(2,1)}, u32[]{:S(2)}, u32[]{:S(2)}) collective-permute-start(bf16[304,256]{1,0:T(8,128)(2,1)} %pad_maximum_fusion.4), channel_id=1, source_target_pairs={{0,8},{8,0},{16,24},{24,16},{1,9},{9,1},{17,25},{25,17},{2,10},{10... | collective-permute-start | bytes 466952 | tf_op jit(solution)/shard_map/ppermute | solution.py:480
  39.5 18.9 %copy-start.7 = (f32[2,2048]{1,0:T(2,128)S(1)}, f32[2,2048]{1,0:T(2,128)}, u32[]{:S(2)}) copy-start(f32[2,2048]{1,0:T(2,128)} %own_gain_ref.1) | copy-start | bytes 49156
  39.6 9.6 %copy-start.10 = (bf16[304,256]{1,0:T(8,128)(2,1)}, bf16[304,256]{1,0:T(8,128)(2,1)S(1)}, u32[]{:S(2)}) copy-start(bf16[304,256]{1,0:T(8,128)(2,1)S(1)} %collective-permute-done.8) | copy-start | bytes 466948
  49.1 0.7 copy-start.11
  49.8 8.6 %collective-permute-start.9 = (bf16[4,3,256,256]{3,2,1,0:T(8,128)(2,1)S(1)}, bf16[4,3,256,256]{3,2,1,0:T(8,128)(2,1)S(1)}, u32[]{:S(2)}, u32[]{:S(2)}) collective-permute-start(bf16[4,3,256,256]{3,2,1,0:T(8,128)(2,1)S(1)} %pad_maximum_fusion.share_ref), channel_id=1, source_target_pairs={{0,1},{1,0},{2,3},{3,2},{4,5},{5,4},{6,7},{7,6},{8,9},{9,8},{10,11... | collective-permute-start | bytes 4718600 | tf_op jit(solution)/shard_map/ppermute | solution.py:480
  52.6 12.9 %collective-permute-start.12 = (bf16[3,256,256]{2,1,0:T(8,128)(2,1)S(1)}, bf16[3,256,256]{2,1,0:T(8,128)(2,1)S(1)}, u32[]{:S(2)}, u32[]{:S(2)}) collective-permute-start(bf16[3,256,256]{2,1,0:T(8,128)(2,1)S(1)} %pad_maximum_fusion.3), channel_id=1, source_target_pairs={{0,6},{1,7},{2,4},{3,5},{4,2},{5,3},{6,0},{7,1},{8,14},{9,15},{10,... | collective-permute-start | bytes 1179656 | tf_op jit(solution)/shard_map/ppermute | solution.py:480
  55.1 18.5 %collective-permute-start.11 = (bf16[3,256,256]{2,1,0:T(8,128)(2,1)S(1)}, bf16[3,256,256]{2,1,0:T(8,128)(2,1)S(1)}, u32[]{:S(2)}, u32[]{:S(2)}) collective-permute-start(bf16[3,256,256]{2,1,0:T(8,128)(2,1)S(1)} %pad_maximum_fusion.3), channel_id=1, source_target_pairs={{0,4},{1,5},{2,6},{3,7},{4,0},{5,1},{6,2},{7,3},{8,12},{9,13},{10,... | collective-permute-start | bytes 1179656 | tf_op jit(solution)/shard_map/ppermute | solution.py:480
  55.6 18.0 %collective-permute-start.10 = (bf16[3,256,256]{2,1,0:T(8,128)(2,1)S(1)}, bf16[3,256,256]{2,1,0:T(8,128)(2,1)S(1)}, u32[]{:S(2)}, u32[]{:S(2)}) collective-permute-start(bf16[3,256,256]{2,1,0:T(8,128)(2,1)S(1)} %pad_maximum_fusion.3), channel_id=1, source_target_pairs={{0,2},{1,3},{2,0},{3,1},{4,6},{5,7},{6,4},{7,5},{8,10},{9,11},{10,... | collective-permute-start | bytes 1179656 | tf_op jit(solution)/shard_map/ppermute | solution.py:480
  58.4 1.2 %copy-start = (bf16[2,2048,128]{2,1,0:T(8,128)(2,1)S(1)}, bf16[2,2048,128]{2,1,0:T(8,128)(2,1)}, u32[]{:S(2)}) copy-start(bf16[2,2048,128]{2,1,0:T(8,128)(2,1)} %value_ref.3) | copy-start | bytes 3145732
  59.7 1.2 %copy-start.2 = (bf16[2,2048,128]{2,1,0:T(8,128)(2,1)S(1)}, bf16[2,2048,128]{2,1,0:T(8,128)(2,1)}, u32[]{:S(2)}) copy-start(bf16[2,2048,128]{2,1,0:T(8,128)(2,1)} %key_ref.3) | copy-start | bytes 3145732
  65.5 9.5 %copy-start.5 = (f32[6,8,2560]{2,1,0:T(8,128)}, f32[6,8,2560]{2,1,0:T(8,128)S(1)}, u32[]{:S(2)}) copy-start(f32[6,8,2560]{2,1,0:T(8,128)S(1)} %get-tuple-element.33.first_ref) | copy-start | bytes 1474564
  75.0 3.8 %collective-permute-start.13 = (bf16[4,3,256,256]{3,2,1,0:T(8,128)(2,1)}, bf16[4,3,256,256]{3,2,1,0:T(8,128)(2,1)}, u32[]{:S(2)}, u32[]{:S(2)}) collective-permute-start(bf16[4,3,256,256]{3,2,1,0:T(8,128)(2,1)} %pad_maximum_fusion.1.late_share_ref), channel_id=1, source_target_pairs={{0,1},{1,0},{2,3},{3,2},{4,5},{5,4},{6,7},{7,6},{8,9},{9,8},{10,11... | collective-permute-start | bytes 4718600 | tf_op jit(solution)/shard_map/ppermute | solution.py:480
  75.0 20.0 %all-to-all-start.1 = ((bf16[32,8,256]{2,1,0:T(8,128)(2,1)}), bf16[32,8,256]{2,1,0:T(8,128)(2,1)S(1)}, u32[]{:S(2)}, u32[]{:S(2)}) async-start(bf16[32,8,256]{2,1,0:T(8,128)(2,1)} %bitcast.26), calls=%async_computation.1 | async-start | bytes 262144 | tf_op jit(solution)/shard_map/all_to_all | solution.py:475
  78.7 1.2 %copy-start.1 = (bf16[2,2048,128]{2,1,0:T(8,128)(2,1)S(1)}, bf16[2,2048,128]{2,1,0:T(8,128)(2,1)}, u32[]{:S(2)}) copy-start(bf16[2,2048,128]{2,1,0:T(8,128)(2,1)} %value_ref.3) | copy-start | bytes 3145732
  80.0 1.2 %copy-start.3 = (bf16[2,2048,128]{2,1,0:T(8,128)(2,1)S(1)}, bf16[2,2048,128]{2,1,0:T(8,128)(2,1)}, u32[]{:S(2)}) copy-start(bf16[2,2048,128]{2,1,0:T(8,128)(2,1)} %key_ref.3) | copy-start | bytes 3145732
  81.2 1.0 copy-start.6
  94.2 0.8 copy-start.4

commit v3 on v2

v3 whole, which is shorter than its diff:
```python
import functools

import jax
import jax.numpy as jnp
from jax import lax
from jax.experimental import pallas as pl
from jax.experimental.pallas import tpu as pltpu
from jax.sharding import PartitionSpec as P

ROPE_BASE = 500000.0
EPSILON = 1e-05
NEGATIVE = -1e30
LANES = 128
GAIN_LINES = 8


def iota(shape, dim):
    return lax.broadcasted_iota(jnp.int32, shape, dim)


def as_float(flags):
    return jnp.where(flags, 1.0, 0.0).astype(jnp.float32)


def contract(left, right, left_dim, right_dim):
    return lax.dot_general(
        left, right, (((left_dim,), (right_dim,)), ((), ())), preferred_element_type=jnp.float32
    )


def pieces_of(column_count):
    return 2 if column_count % (2 * LANES) == 0 else 1


def fold(rows, width):
    row_count, columns = rows.shape
    if columns >= width:
        return jnp.concatenate(
            [rows[:, start : start + width] for start in range(0, columns, width)], axis=0
        )
    lines = row_count * columns // width
    return jnp.concatenate(
        [rows[start : start + lines] for start in range(0, row_count, lines)], axis=1
    )


def unfold(lines, row_count, columns):
    width = lines.shape[1]
    if columns >= width:
        return jnp.concatenate(
            [lines[start : start + row_count] for start in range(0, lines.shape[0], row_count)],
            axis=1,
        )
    return jnp.concatenate(
        [lines[:, start : start + columns] for start in range(0, width, columns)], axis=0
    )


def choosers(source, groups, pieces):
    row_count = source.shape[0]
    half = row_count // 2
    shape = (row_count, groups * row_count)
    row, line = iota(shape, 0), iota(shape, 1)
    back = source.astype(jnp.int32) == line // row_count
    return [
        as_float(back & (line % row_count == piece * half + row % half)).astype(jnp.bfloat16)
        for piece in range(pieces)
    ]


def turned(vector, cosine, sine):
    return vector * cosine + pltpu.roll(vector, vector.shape[1] // 2, 1) * sine


def heads_down(rows, head_size):
    count = rows.shape[1] // head_size
    return jnp.concatenate(
        [rows[:, head * head_size : (head + 1) * head_size] for head in range(count)], axis=0
    )


def heads_across(stacked, row_count):
    count = stacked.shape[0] // row_count
    return jnp.concatenate(
        [stacked[head * row_count : (head + 1) * row_count] for head in range(count)], axis=1
    )


def turned_heads(rows, cosine, sine):
    stacked = heads_down(rows, cosine.shape[1])
    repeats = stacked.shape[0] // rows.shape[0]
    return turned(stacked, jnp.tile(cosine, (repeats, 1)), jnp.tile(sine, (repeats, 1)))


def forward_layer(rows, gain_row, weight, cosine, sine, allowed):
    row_count, feature_count = rows.shape
    head_size = cosine.shape[1]
    scale = lax.rsqrt(jnp.sum(rows * rows, axis=1, keepdims=True) / feature_count + EPSILON)
    normed = rows * scale * gain_row
    packed = normed.astype(jnp.bfloat16)
    share = feature_count // len(weight)
    pair = jnp.zeros((row_count, 2 * head_size), jnp.float32)
    for owner, part in enumerate(weight):
        pair += contract(packed[:, owner * share : (owner + 1) * share], part[...], 1, 0)
    queries = turned_heads(normed, cosine, sine).astype(jnp.bfloat16)
    keys = turned(pair[:, :head_size], cosine, sine).astype(jnp.bfloat16)
    values = pair[:, head_size:].astype(jnp.bfloat16)
    scores = contract(keys, queries, 1, 1) * head_size ** (-0.5)
    scores = jnp.where(allowed, scores, NEGATIVE)
    raised = jnp.exp(scores - jnp.max(scores, axis=0, keepdims=True))
    weights = raised / jnp.sum(raised, axis=0, keepdims=True)
    mixed = contract(weights.astype(jnp.bfloat16), values, 0, 0)
    kept = (scale, keys, values, weights)
    return rows + heads_across(mixed, row_count), packed, kept


def backward_layer(upstream, rows, gain_row, weight, cosine, sine, kept):
    scale, keys, values, weights = kept
    row_count, feature_count = rows.shape
    head_size = cosine.shape[1]
    queries = turned_heads(rows * scale * gain_row, cosine, sine).astype(jnp.bfloat16)
    stacked = heads_down(upstream, head_size).astype(jnp.bfloat16)
    d_weights = contract(values, stacked, 1, 1).astype(jnp.bfloat16).astype(jnp.float32)
    d_values = contract(weights.astype(jnp.bfloat16), stacked, 1, 0)
    d_scores = weights * (d_weights - jnp.sum(d_weights * weights, axis=0, keepdims=True))
    d_scores = (d_scores * head_size ** (-0.5)).astype(jnp.bfloat16)
    d_keys = contract(d_scores, queries, 1, 0)
    terms = jnp.concatenate([turned(d_keys, cosine, -sine), d_values], axis=1)
    terms = terms.astype(jnp.bfloat16)
    d_queries = contract(d_scores, keys, 0, 0)
    repeats = stacked.shape[0] // row_count
    d_queries = turned(d_queries, jnp.tile(cosine, (repeats, 1)), jnp.tile(-sine, (repeats, 1)))
    d_packed = jnp.concatenate([contract(terms, part[...], 1, 1) for part in weight], axis=1)
    d_normed = d_packed + heads_across(d_queries, row_count)
    scaled = d_normed * gain_row
    inner = jnp.sum(scaled * rows, axis=1, keepdims=True) / feature_count
    return upstream + scale * scaled - rows * (scale * scale * scale * inner), terms


def state_width(feature_count, head_size):
    return feature_count + 4 * head_size


def save_layer(index, rows, kept, state_ref):
    scale, keys, values, weights = kept
    feature_count, head_size = rows.shape[1], keys.shape[1]
    state_ref[index, :, :feature_count] = rows
    parts = (weights, keys, values, jnp.broadcast_to(scale, keys.shape))
    for place, part in enumerate(parts):
        start = feature_count + place * head_size
        state_ref[index, :, start : start + head_size] = part.astype(jnp.float32)


def load_layer(index, state_ref, feature_count):
    head_size = (state_ref.shape[2] - feature_count) // 4
    parts = []
    for place in range(4):
        start = feature_count + place * head_size
        parts.append(state_ref[index, :, start : start + head_size])
    weights, keys, values, scale = parts
    kept = (scale[:, 0:1], keys.astype(jnp.bfloat16), values.astype(jnp.bfloat16), weights)
    return state_ref[index, :, :feature_count], kept


def repeat_steps(count, step, carry):
    if count <= 8:
        for index in range(count):
            carry = step(index, carry)
        return carry
    return lax.fori_loop(0, count, step, carry)


def layer_inputs(index, gain_ref, weight_ref, sections):
    place = lax.bitwise_xor(lax.axis_index("pipe"), index)
    share = weight_ref.shape[1] // sections
    rows = pl.ds(pl.multiple_of(place * share, share), share)
    weight = [weight_ref.at[owner, rows] for owner in range(weight_ref.shape[0])]
    return gain_ref[pl.ds(place, 1), :], weight


def forward_steps(rows, gain_ref, weight_ref, tables, state_ref, packed_ref):
    cosine, sine, allowed = tables
    sections, groups = packed_ref.shape[:2]
    share = weight_ref.shape[1] // sections

    def step(index, rows):
        gain_row, weight = layer_inputs(index, gain_ref, weight_ref, sections)
        after, packed, kept = forward_layer(rows, gain_row, weight, cosine, sine, allowed)
        for group in range(groups):
            packed_ref[index, group, :, :share] = packed[:, group * share : (group + 1) * share]
        save_layer(index, rows, kept, state_ref)
        return after

    return repeat_steps(sections, step, rows)


def backward_steps(upstream, gain_ref, weight_ref, tables, state_ref, terms_ref, start):
    cosine, sine, _ = tables
    sections, groups = terms_ref.shape[:2]
    width = weight_ref.shape[2]

    def step(back, upstream):
        index = sections - 1 - back
        gain_row, weight = layer_inputs(index, gain_ref, weight_ref, sections)
        rows, kept = load_layer(index, state_ref, upstream.shape[1])
        before, terms = backward_layer(upstream, rows, gain_row, weight, cosine, sine, kept)
        for group in range(groups):
            terms_ref[index, group, :, start : start + width] = terms
        return before

    return repeat_steps(sections, step, upstream)


def fill(turn, key_ref, value_ref, shares, weight_ref, sems):
    groups, share, head_size = key_ref.shape[1:]
    moved = weight_ref.shape[1] - share
    group = lax.axis_index("dp")
    copies = [
        (key_ref.at[turn], weight_ref.at[:, :share, :head_size]),
        (value_ref.at[turn], weight_ref.at[:, :share, head_size:]),
    ]
    for core, ref in enumerate(shares):
        for chip in range(groups // 2):
            owner = lax.bitwise_xor(group, 2 * chip + core)
            copies.append(
                (ref.at[chip, pl.ds(0, moved)], weight_ref.at[owner, pl.ds(share, moved)])
            )
    copies = [
        pltpu.make_async_copy(*pair, sems.at[turn, index]) for index, pair in enumerate(copies)
    ]
    for copy in copies:
        copy.start()
    return copies


def first_kernel(
    upstream_ref,
    key_ref,
    value_ref,
    share_ref,
    other_ref,
    state_ref,
    packed_ref,
    lines_ref,
    rows_ref,
    gains_ref,
    gain_ref,
    line_sems,
    weight_ref,
    sems,
    *,
    doc_count
):
    sections = packed_ref.shape[0]
    groups, share, head_size = key_ref.shape[1:]
    row_count, feature_count = upstream_ref.shape
    column_count = feature_count // sections
    chips, line_count, width = lines_ref.shape[1:]
    used = share_ref.shape[1] - line_count
    section, group = lax.axis_index("pipe"), lax.axis_index("dp")
    shares = (share_ref, other_ref)
    line_copies = [
        pltpu.make_async_copy(
            ref.at[:, pl.ds(used, line_count)], lines_ref.at[core], line_sems.at[core]
        )
        for core, ref in enumerate(shares)
    ]
    for copy in line_copies:
        copy.start()
    copies = fill(0, key_ref, value_ref, shares, weight_ref, sems)
    state_ref[sections + 1, :, :feature_count] = upstream_ref[...]
    for copy in line_copies:
        copy.wait()

    row = iota((row_count, 1), 0)
    offset = row.astype(jnp.float32)
    document = jnp.zeros((row_count, 1), jnp.float32)
    position = jnp.zeros((row_count, 1), jnp.float32)
    source = jnp.zeros((row_count, 1), jnp.float32)
    parts = [jnp.zeros((row_count, column_count), jnp.float32) for _ in range(sections)]
    folded = row_count * column_count // width
    tail = folded + GAIN_LINES
    for core in range(2):
        for chip in range(chips):
            lines = lines_ref[core, chip].astype(jnp.float32)
            tags = lines[sections * tail :]
            tags = jnp.sum(
                jnp.where(iota(tags.shape, 0) == section, tags, 0.0), axis=0, keepdims=True
            )
            target = jnp.where(
                row < row_count // 2,
                tags[:, doc_count : doc_count + 1],
                tags[:, doc_count + 1 : doc_count + 2],
            )
            came = as_float(target.astype(jnp.int32) == group)
            end = jnp.zeros((1, 1), jnp.float32)
            number = jnp.zeros((row_count, 1), jnp.float32)
            opening = jnp.zeros((row_count, 1), jnp.float32)
            for doc in range(doc_count - 1):
                end = end + tags[:, doc : doc + 1]
                passed = offset >= end
                number = number + as_float(passed)
                opening = jnp.where(passed, end, opening)
            owner = lax.bitwise_xor(group, 2 * chip + core)
            document += came * number
            position += came * (offset - opening)
            source += came * owner.astype(jnp.float32)
            gain_rows = []
            for mask in range(sections):
                piece = lines[mask * tail : mask * tail + folded]
                parts[mask] += came * unfold(piece, row_count, column_count)
                terms = lines[mask * tail + folded : (mask + 1) * tail, :share]
                gain_rows += [
                    terms[3 * turn : 3 * turn + 1]
                    + terms[3 * turn + 1 : 3 * turn + 2]
                    + terms[3 * turn + 2 : 3 * turn + 3]
                    for turn in range(2)
                ]
            gains_ref[owner] = jnp.concatenate(gain_rows[0::2] + gain_rows[1::2], axis=0)
    for owner in range(groups):
        gain_ref[:, owner * share : (owner + 1) * share] = gains_ref[owner]
    for start in range(0, 2 * sections, row_count):
        state_ref[sections + 2 + start // row_count, :, :feature_count] = gain_ref[
            start : start + row_count
        ]
    for mask in range(sections):
        rows_ref[lax.bitwise_xor(section, mask)] = parts[mask]
    rows = jnp.concatenate([rows_ref[index] for index in range(sections)], axis=1)

    lane = iota((1, head_size), 1)
    middle = head_size // 2
    exponent = (lane % middle).astype(jnp.float32) * (2.0 / head_size)
    angles = position * jnp.exp(exponent * -jnp.log(jnp.float32(ROPE_BASE)))
    cosine = jnp.cos(angles)
    sine = jnp.where(lane < middle, -jnp.sin(angles), jnp.sin(angles))
    shape = (row_count, row_count * feature_count // head_size)
    pick = as_float(iota(shape, 1) % row_count == iota(shape, 0))
    document_across = jnp.sum(document * pick, axis=0, keepdims=True)
    position_across = jnp.sum(position * pick, axis=0, keepdims=True)
    allowed = (document == document_across) & (position <= position_across)
    kept = (cosine, sine, as_float(allowed), jnp.broadcast_to(source, cosine.shape))
    for place, table in enumerate(kept):
        start = feature_count + place * head_size
        state_ref[sections, :, start : start + head_size] = table
    tables = (cosine, sine, allowed)
    for copy in copies:
        copy.wait()
    state_ref[sections, :, :feature_count] = forward_steps(
        rows, gain_ref.at[pl.ds(0, sections)], weight_ref, tables, state_ref, packed_ref
    )


def second_kernel(
    first_ref,
    key_ref,
    value_ref,
    share_ref,
    other_ref,
    late_share_ref,
    late_other_ref,
    out_ref,
    state_ref,
    gain_ref,
    late_weight_ref,
    weight_ref,
    sems
):
    sections, groups, row_count, _ = out_ref.shape
    share, head_size = key_ref.shape[2:]
    feature_count, term_width = groups * share, 2 * head_size
    late_shares = (late_share_ref, late_other_ref)
    late_copies = fill(1, key_ref, value_ref, late_shares, late_weight_ref, sems)
    copies = fill(0, key_ref, value_ref, (share_ref, other_ref), weight_ref, sems)
    kept = []
    for place in range(4):
        start = feature_count + place * head_size
        kept.append(first_ref[sections, :, start : start + head_size])
    cosine, sine, allowed, source = kept
    tables = (cosine, sine, allowed > 0.5)
    for start in range(0, 2 * sections, row_count):
        gain_ref[start : start + row_count] = first_ref[
            sections + 2 + start // row_count, :, :feature_count
        ]
    late_gain = gain_ref.at[pl.ds(sections, sections)]
    for copy in late_copies:
        copy.wait()
    forward_steps(
        first_ref[sections, :, :feature_count],
        late_gain,
        late_weight_ref,
        tables,
        state_ref,
        out_ref,
    )
    upstream = backward_steps(
        first_ref[sections + 1, :, :feature_count],
        late_gain,
        late_weight_ref,
        tables,
        state_ref,
        out_ref,
        share + term_width,
    )
    for copy in copies:
        copy.wait()
    grads = backward_steps(
        upstream,
        gain_ref.at[pl.ds(0, sections)],
        weight_ref,
        tables,
        first_ref,
        out_ref,
        share,
    ).astype(jnp.bfloat16)
    column_count = feature_count // sections
    pieces = pieces_of(column_count)
    width = column_count // pieces
    chosen = choosers(source[:, 0:1], groups, pieces)
    for section in range(sections):
        start = section * column_count
        going = contract(chosen[0], grads[:, start : start + width], 0, 0)
        for piece in range(1, pieces):
            left = start + piece * width
            going += contract(chosen[piece], grads[:, left : left + width], 0, 0)
        going = going.astype(jnp.bfloat16)
        for group in range(groups):
            out_ref[section, group, :, share + 2 * term_width :] = going[
                group * row_count : (group + 1) * row_count
            ]


def last_kernel(
    route_ref, first_ref, late_ref, grad_ref, key_ref, value_ref, *, groups
):
    micro_count = route_ref.shape[0]
    source_rows, column_count = grad_ref.shape
    row_count = source_rows // micro_count
    half = row_count // 2
    share, head_size = key_ref.shape[1:]
    term_width = 2 * head_size
    width = late_ref.shape[1] - share - 2 * term_width
    pieces = column_count // width
    for index, packed in enumerate((first_ref[...], late_ref[:, :share])):
        start = share + index * term_width
        total = contract(packed, late_ref[:, start : start + term_width], 0, 0)
        key_ref[index] = total[:, :head_size]
        value_ref[index] = total[:, head_size:]
    shape = (source_rows, late_ref.shape[0])
    row, source = iota(shape, 1), iota(shape, 0)
    slot = source // half
    target = jnp.full(shape, -1, jnp.int32)
    for micro in range(micro_count):
        for side in range(2):
            target = jnp.where(
                slot == 2 * micro + side, micro * groups + route_ref[micro, side], target
            )
    going = target == row // row_count
    inner, wanted = row % row_count, source % half
    for piece in range(pieces):
        chosen = as_float(going & (inner == piece * half + wanted)).astype(jnp.bfloat16)
        grad_ref[:, piece * width : (piece + 1) * width] = contract(
            chosen, late_ref[:, share + 2 * term_width :], 1, 0
        ).astype(jnp.bfloat16)


def call(kernel, outs, operands, scalars=0, whole=0, scratch=(), vmem_bytes=0, cost=0):
    spaces = [pltpu.SMEM] * scalars + [pltpu.VMEM] * (len(operands) - scalars - whole)
    spaces += [pl.ANY] * whole
    return pl.pallas_call(
        kernel,
        out_shape=outs,
        in_specs=[pl.BlockSpec(memory_space=space) for space in spaces],
        out_specs=[pl.BlockSpec(memory_space=pltpu.VMEM)] * len(outs),
        scratch_shapes=scratch,
        compiler_params=pltpu.CompilerParams(vmem_limit_bytes=vmem_bytes),
        cost_estimate=pl.CostEstimate(flops=0, bytes_accessed=cost, transcendentals=0),
    )(*operands)


def exchange(blocks):
    return lax.all_to_all(blocks, ("pipe", "dp"), split_axis=0, concat_axis=0, tiled=True)


def swapped(value, axis, mask):
    pairs = [(source, source ^ mask) for source in range(lax.axis_size(axis))]
    return lax.ppermute(value, axis, pairs)


def relayed(payload, sections):
    pieces = [payload]
    for mask in range(1, sections):
        low = mask & -mask
        pieces.append(swapped(pieces[mask - low], "pipe", low))
    return pieces[1:]


def body(hidden, lengths, route, gain, key_weight, value_weight, cotangent):
    groups = lax.axis_size("dp")
    sections = lax.axis_size("pipe")
    group_index = lax.axis_index("dp")
    section_index = lax.axis_index("pipe")
    micro_count = lengths.shape[0]
    assert micro_count == sections
    source_rows, column_count = hidden.shape
    row_count = source_rows // micro_count
    feature_count = gain.shape[1]
    head_size = key_weight.shape[2]
    assert row_count * feature_count == head_size * head_size
    share = feature_count // groups
    width = column_count // pieces_of(column_count)
    devices = sections * groups

    line_width = 2 * head_size

    def own_share(turn):
        parts = [
            lax.dynamic_slice(array, (turn, group_index * share, 0), (1, share, head_size))[0]
            for array in (key_weight, value_weight)
        ]
        return jnp.concatenate(parts, axis=1)

    def own_rows(mask):
        start = lax.bitwise_xor(section_index, mask) * row_count
        rows = lax.dynamic_slice(hidden, (start, 0), (row_count, column_count))
        return fold(rows, line_width)

    slice_ = lax.dynamic_slice(gain, (0, group_index * share), (2, share))
    high = lax.reduce_precision(slice_, 8, 7)
    middle = lax.reduce_precision(slice_ - high, 8, 7)
    terms = jnp.stack([high, middle, slice_ - high - middle], axis=1).reshape(6, share)
    terms = jnp.pad(
        terms.astype(jnp.bfloat16), ((0, GAIN_LINES - 6), (0, line_width - share))
    )

    first = own_share(0)
    came = [
        swapped(jnp.concatenate([first, own_rows(mask), terms], axis=0), "pipe", mask)
        for mask in range(1, sections)
    ]
    tags = jnp.concatenate([lengths, route], axis=1).astype(jnp.bfloat16)
    tags = jnp.pad(tags, ((0, -micro_count % 16), (0, line_width - tags.shape[1])))
    upstream = lax.dynamic_slice_in_dim(
        cotangent, section_index * row_count, row_count, 0
    ).astype(jnp.float32)
    tags, own_tail, upstream = lax.optimization_barrier(
        (tags, jnp.concatenate([own_rows(0), terms], axis=0), upstream)
    )
    column = jnp.concatenate(
        [piece[:share] for piece in came]
        + [own_tail]
        + [piece[share:] for piece in came]
        + [tags],
        axis=0,
    )
    column, second = lax.optimization_barrier((column, own_share(1)))
    chips = range(1, groups // 2)
    plane = jnp.stack([column] + [swapped(column, "dp", 2 * chip) for chip in chips])
    came = relayed(second, sections)
    plane, came = lax.optimization_barrier((plane, came))
    first_shares = (plane, swapped(plane, "dp", 1))
    column = jnp.concatenate(came, axis=0)
    planes = [column] + [swapped(column, "dp", 2 * chip) for chip in chips]

    key_parts = key_weight.reshape(2, groups, share, head_size)
    value_parts = value_weight.reshape(2, groups, share, head_size)

    def layers_call(kernel, turns, outs, operands, shares, scratch, cost, columns):
        weight = pltpu.VMEM((groups, sections * share, line_width), jnp.bfloat16)
        return call(
            kernel,
            outs,
            (*operands, key_parts, value_parts, *shares),
            whole=2 + len(shares),
            scratch=[
                *scratch,
                *[weight] * turns,
                pltpu.SemaphoreType.DMA((2, groups + 2)),
            ],
            vmem_bytes=(6 << 20)
            + 2 * turns * sections * feature_count * line_width
            + 4 * devices * row_count * columns,
            cost=cost,
        )

    def blocks_shape(columns):
        return jax.ShapeDtypeStruct((sections, groups, row_count, columns), jnp.bfloat16)

    def exchanged(blocks):
        columns = blocks.shape[3]
        got = exchange(blocks.reshape(devices, row_count, columns))
        return got.reshape(devices * row_count, columns)

    line = (row_count, state_width(feature_count, head_size))
    line_count = plane.shape[1] - (sections - 1) * share
    gain_scratch = pltpu.VMEM((2 * sections, feature_count), jnp.float32)
    state, packed = layers_call(
        functools.partial(first_kernel, doc_count=lengths.shape[1]),
        1,
        [
            jax.ShapeDtypeStruct(
                (sections + 2 + 2 * sections // row_count, *line), jnp.float32
            ),
            blocks_shape(share),
        ],
        (upstream,),
        first_shares,
        (
            pltpu.VMEM((2, groups // 2, line_count, line_width), jnp.bfloat16),
            pltpu.VMEM((sections, row_count, column_count), jnp.float32),
            pltpu.VMEM((groups, 2 * sections, share), jnp.float32),
            gain_scratch,
            pltpu.SemaphoreType.DMA((2,)),
        ),
        18 << 20,
        2 * LANES,
    )
    packed = exchanged(packed)
    state, packed, planes = lax.optimization_barrier((state, packed, planes))
    plane = jnp.stack(planes)
    second_shares = (plane, swapped(plane, "dp", 1))
    columns = share + 4 * head_size + width
    (late,) = layers_call(
        second_kernel,
        2,
        [blocks_shape(columns)],
        (state,),
        (*first_shares, *second_shares),
        (pltpu.VMEM((sections, *line), jnp.float32), gain_scratch),
        48 << 20,
        columns,
    )
    late, packed = lax.optimization_barrier((late, packed))
    late = exchanged(late)
    grad_shape = jax.ShapeDtypeStruct((2, share, head_size), jnp.float32)
    return tuple(
        call(
            functools.partial(last_kernel, groups=groups),
            [jax.ShapeDtypeStruct((source_rows, column_count), jnp.bfloat16)] + [grad_shape] * 2,
            (route, packed, late),
            scalars=1,
            vmem_bytes=(4 << 20) + 10000 * devices * row_count,
        )
    )


def solution(mesh):
    placed = (
        P("dp", "pipe"),
        P("dp", None),
        P("dp", None),
        P("pipe", None),
        P("pipe", None, None),
        P("pipe", None, None),
        P("dp", None),
    )
    return jax.shard_map(
        body,
        mesh=mesh,
        in_specs=placed,
        out_specs=(P("dp", "pipe"), P("pipe", "dp", None), P("pipe", "dp", None)),
        check_vma=False,
    )
```

time: 118 us -> 109 us (0.924)
  blocking collectives: 20.6 us -> 0 us
  waiting for transfers between devices: 33.7 us -> 48.5 us
  local copies, waits for them, and re-layouts: 13.5 us -> 5.4 us
  starting transfers between devices: 25 us -> 27.2 us
  Pallas kernels: 19.8 us -> 21.5 us
    all_to_all x1 -> x0, blocking collectives: 20.6 us -> none  [exchange(): lax.all_to_all(blocks, ('pipe', 'dp'), split_axis=0, concat_axis=0, tiled...]
    all_to_all x2, waiting for transfers between devices: 0.01 us -> 17.2 us  [exchange(): lax.all_to_all(blocks, ('pipe', 'dp'), split_axis=0, concat_axis=0, tiled...]
    another operation x7 -> x2, local copies, waits for them, and re-layouts: 4.98 us -> 0.12 us  [the longest x3 2.74 us: body(): column = jnp.stack([piece[:share] for piece in came])]
    unnamed x27 -> x22, local copies, waits for them, and re-layouts: 7.5 us -> 2.81 us
    all_to_all x2, starting transfers between devices: 7.65 us -> 10.7 us  [exchange(): lax.all_to_all(blocks, ('pipe', 'dp'), split_axis=0, concat_axis=0, tiled...]
    ppermute x14, waiting for transfers between devices: 33.6 us -> 31.3 us  [swapped(): return lax.ppermute(value, axis, pairs)]
    pallas_call x4 -> x3, Pallas kernels: 19.8 us -> 21.5 us  [call(): pl.pallas_call(kernel, out_shape=outs, in_specs=[pl.BlockSpec(memory_spac...]
    another operation x6 -> x5, other arithmetic: 1.08 us -> 2.3 us  [the longest x2 0.78 us: gain_terms(): terms = jnp.stack([first, second, third], axis=1).astype(jnp.bfloat16)]
  transfers between devices with their start and end apart: 16 -> 16, of which waited for: 8 -> 10; matrix products, arithmetic and copies ran while one was open for 6% -> 5% of each run, Pallas kernels for 15% -> 5%
where the time goes in v3:
time: 109 us; the launch traced here: 108 us
  waiting for transfers between devices  48.5 us (44%)
  starting transfers between devices  27.2 us (25%)
  Pallas kernels  21.5 us (20%)
  local copies, waits for them, and re-layouts  5.4 us (5%)
  other arithmetic  4.88 us (4%)
    ppermute x14, waiting for transfers between devices, swapped(): return lax.ppermute(value, axis, pairs)  31.3 us
    pallas_call x3, Pallas kernels, call(): pl.pallas_call(kernel, out_shape=outs, in_specs=[pl.BlockSpec(memory_spac...  21.5 us
    all_to_all x2, waiting for transfers between devices, exchange(): lax.all_to_all(blocks, ('pipe', 'dp'), split_axis=0, concat_axis=0, tiled...  17.2 us
    ppermute x14, starting transfers between devices, swapped(): return lax.ppermute(value, axis, pairs)  16.6 us
    all_to_all x2, starting transfers between devices, exchange(): lax.all_to_all(blocks, ('pipe', 'dp'), split_axis=0, concat_axis=0, tiled...  10.7 us
    unnamed x22, local copies, waits for them, and re-layouts  2.81 us
  transfers between devices with their start and end apart: 16, of which 10 were waited for; matrix products, arithmetic and copies ran while one was open for 5% of the time, Pallas kernels for 5%

profile of v3, /device:TPU:0, one launch (start us, length us, event | category | flops | bytes accessed | tf_op | source)
XLA Modules:
  0.0 108.4 jit_solution(10346583312226991610)
XLA Ops:
  0.6 0.7 fusion.8
  1.4 1.0 dynamic-slice_bitcast_fusion
  2.4 0.8 constant_dynamic-slice_fusion.3
  3.2 3.1 %collective-permute-start = (bf16[280,256]{1,0:T(8,128)(2,1)S(1)}, bf16[280,256]{1,0:T(8,128)(2,1)S(1)}, u32[]{:S(2)}, u32[]{:S(2)}) collective-permute-start(bf16[280,256]{1,0:T(8,128)(2,1)S(1)} %get-tuple-element.47), channel_id=1, source_target_pairs={{0,8},{8,0},{16,24},{24,16},{1,9},{9,1},{17,25},{25,17},{2,10},{10... | collective-permute-start | bytes 430088 | tf_op jit(solution)/shard_map/ppermute | solution.py:486
  6.3 2.6 %collective-permute-start.1 = (bf16[280,256]{1,0:T(8,128)(2,1)S(1)}, bf16[280,256]{1,0:T(8,128)(2,1)S(1)}, u32[]{:S(2)}, u32[]{:S(2)}) collective-permute-start(bf16[280,256]{1,0:T(8,128)(2,1)S(1)} %get-tuple-element.46), channel_id=1, source_target_pairs={{0,16},{8,24},{16,0},{24,8},{1,17},{9,25},{17,1},{25,9},{2,18},{10... | collective-permute-start | bytes 430088 | tf_op jit(solution)/shard_map/ppermute | solution.py:486
  8.9 0.0 collective-permute-start.2
  8.9 0.8 dynamic-slice_convert_fusion.upstream_ref
  9.7 0.7 convert.19
  10.4 0.1 copy.16
  10.5 0.7 convert.18
  11.2 0.1 fusion.5
  11.3 0.7 collective-permute-done
  12.0 8.1 %collective-permute-done.1 = bf16[280,256]{1,0:T(8,128)(2,1)S(1)} collective-permute-done((bf16[280,256]{1,0:T(8,128)(2,1)S(1)}, bf16[280,256]{1,0:T(8,128)(2,1)S(1)}, u32[]{:S(2)}, u32[]{:S(2)}) %collective-permute-start.1) | collective-permute-done | bytes 143392 | tf_op jit(solution)/shard_map/ppermute | solution.py:486
  20.1 0.0 collective-permute-done.2
  20.2 1.6 %collective-permute-start.3 = (bf16[880,256]{1,0:T(8,128)(2,1)S(1)}, bf16[880,256]{1,0:T(8,128)(2,1)S(1)}, u32[]{:S(2)}, u32[]{:S(2)}) collective-permute-start(bf16[880,256]{1,0:T(8,128)(2,1)S(1)} %constant_dynamic-update-slice_fusion), channel_id=1, source_target_pairs={{0,2},{1,3},{2,0},{3,1},{4,6},{5,7},{6,4},{7,5},{8,10},{9,11},{10,... | collective-permute-start | bytes 1351688 | tf_op jit(solution)/shard_map/ppermute | solution.py:486
  21.7 1.5 %collective-permute-start.4 = (bf16[880,256]{1,0:T(8,128)(2,1)S(1)}, bf16[880,256]{1,0:T(8,128)(2,1)S(1)}, u32[]{:S(2)}, u32[]{:S(2)}) collective-permute-start(bf16[880,256]{1,0:T(8,128)(2,1)S(1)} %constant_dynamic-update-slice_fusion), channel_id=1, source_target_pairs={{0,4},{1,5},{2,6},{3,7},{4,0},{5,1},{6,2},{7,3},{8,12},{9,13},{10,... | collective-permute-start | bytes 1351688 | tf_op jit(solution)/shard_map/ppermute | solution.py:486
  23.2 0.5 collective-permute-start.5
  23.7 3.2 %collective-permute-start.7 = (bf16[256,256]{1,0:T(8,128)(2,1)S(1)}, bf16[256,256]{1,0:T(8,128)(2,1)S(1)}, u32[]{:S(2)}, u32[]{:S(2)}) collective-permute-start(bf16[256,256]{1,0:T(8,128)(2,1)S(1)} %pad_maximum_fusion.6), channel_id=1, source_target_pairs={{0,16},{8,24},{16,0},{24,8},{1,17},{9,25},{17,1},{25,9},{2,18},{10... | collective-permute-start | bytes 393224 | tf_op jit(solution)/shard_map/ppermute | solution.py:486
  26.9 0.0 collective-permute-start.6
  26.9 4.7 %collective-permute-done.7 = bf16[256,256]{1,0:T(8,128)(2,1)S(1)} collective-permute-done((bf16[256,256]{1,0:T(8,128)(2,1)S(1)}, bf16[256,256]{1,0:T(8,128)(2,1)S(1)}, u32[]{:S(2)}, u32[]{:S(2)}) %collective-permute-start.7) | collective-permute-done | bytes 131104 | tf_op jit(solution)/shard_map/ppermute | solution.py:486
  31.6 0.3 collective-permute-start.8
  31.9 1.6 %collective-permute-done.3 = bf16[880,256]{1,0:T(8,128)(2,1)S(1)} collective-permute-done((bf16[880,256]{1,0:T(8,128)(2,1)S(1)}, bf16[880,256]{1,0:T(8,128)(2,1)S(1)}, u32[]{:S(2)}, u32[]{:S(2)}) %collective-permute-start.3) | collective-permute-done | bytes 450592 | tf_op jit(solution)/shard_map/ppermute | solution.py:486
  33.5 7.2 %collective-permute-done.4 = bf16[880,256]{1,0:T(8,128)(2,1)S(1)} collective-permute-done((bf16[880,256]{1,0:T(8,128)(2,1)S(1)}, bf16[880,256]{1,0:T(8,128)(2,1)S(1)}, u32[]{:S(2)}, u32[]{:S(2)}) %collective-permute-start.4) | collective-permute-done | bytes 450592 | tf_op jit(solution)/shard_map/ppermute | solution.py:486
  40.7 0.0 collective-permute-done.5
  40.7 0.0 copy-start.2
  40.7 0.0 copy-start.3
  40.7 0.2 pad_maximum_fusion.share_ref
  40.9 0.0 collective-permute-done.6
  40.9 0.0 collective-permute-done.8
  40.9 0.1 collective-permute-start.9
  41.0 0.7 constant_dynamic-update-slice_fusion.7
  41.7 0.7 constant_dynamic-update-slice_fusion.6
  42.3 0.7 constant_dynamic-update-slice_fusion.5
  43.0 1.2 %collective-permute-start.10 = (bf16[768,256]{1,0:T(8,128)(2,1)}, bf16[768,256]{1,0:T(8,128)(2,1)}, u32[]{:S(2)}, u32[]{:S(2)}) collective-permute-start(bf16[768,256]{1,0:T(8,128)(2,1)} %constant_dynamic-update-slice_fusion.5), channel_id=1, source_target_pairs={{0,2},{1,3},{2,0},{3,1},{4,6},{5,7},{6,4},{7,5},{8,10},{9,11},{10,... | collective-permute-start | bytes 1179656 | tf_op jit(solution)/shard_map/ppermute | solution.py:486
  44.2 0.8 collective-permute-start.11
  45.1 1.4 %collective-permute-start.12 = (bf16[768,256]{1,0:T(8,128)(2,1)}, bf16[768,256]{1,0:T(8,128)(2,1)}, u32[]{:S(2)}, u32[]{:S(2)}) collective-permute-start(bf16[768,256]{1,0:T(8,128)(2,1)} %constant_dynamic-update-slice_fusion.5), channel_id=1, source_target_pairs={{0,6},{1,7},{2,4},{3,5},{4,2},{5,3},{6,0},{7,1},{8,14},{9,15},{10,... | collective-permute-start | bytes 1179656 | tf_op jit(solution)/shard_map/ppermute | solution.py:486
  46.5 0.0 collective-permute-done.9.other_ref
  46.5 0.0 copy-start
  46.5 0.0 copy-done.2
  46.5 0.0 copy-done.3
  46.5 5.8 %shard_map.94 = (f32[7,8,2560]{2,1,0:T(8,128)S(1)}, bf16[4,8,8,256]{3,2,1,0:T(8,128)(2,1)S(1)}) custom-call(f32[8,2048]{1,0:T(8,128)S(1)} %dynamic-slice_convert_fusion.upstream_ref, bf16[2,8,256,128]{3,2,1,0:T(8,128)(2,1)S(1)} %bitcast.28, bf16[2,8,256,128]{3,2,1,0:T(8,128)(2,1)S(1)} %bitcast.30, bf16[4,880,256]{2,1,0:T(8,128)(2,1)S(1)} %pad_maximum_fusion.share_ref, ...), custom_call_target="tpu_custom_call" | custom-call | bytes 18874368 | tf_op jit(solution)/shard_map/pallas_call | solution.py:469
  52.3 0.0 copy-done
  52.3 0.0 copy-start.5
  52.3 0.6 copy-done.5
  53.0 6.1 %all-to-all-start = ((bf16[32,8,256]{2,1,0:T(8,128)(2,1)}), bf16[32,8,256]{2,1,0:T(8,128)(2,1)S(1)}, u32[]{:S(2)}, u32[]{:S(2)}) async-start(bf16[32,8,256]{2,1,0:T(8,128)(2,1)} %bitcast.34), calls=%async_computation | async-start | bytes 262144 | tf_op jit(solution)/shard_map/all_to_all | solution.py:481
  59.0 0.0 collective-permute-done.10
  59.0 4.2 %collective-permute-done.11 = bf16[768,256]{1,0:T(8,128)(2,1)} collective-permute-done((bf16[768,256]{1,0:T(8,128)(2,1)}, bf16[768,256]{1,0:T(8,128)(2,1)}, u32[]{:S(2)}, u32[]{:S(2)}) %collective-permute-start.11) | collective-permute-done | bytes 393248 | tf_op jit(solution)/shard_map/ppermute | solution.py:486
  63.2 1.6 %collective-permute-done.12 = bf16[768,256]{1,0:T(8,128)(2,1)} collective-permute-done((bf16[768,256]{1,0:T(8,128)(2,1)}, bf16[768,256]{1,0:T(8,128)(2,1)}, u32[]{:S(2)}, u32[]{:S(2)}) %collective-permute-start.12) | collective-permute-done | bytes 393248 | tf_op jit(solution)/shard_map/ppermute | solution.py:486
  64.9 2.4 %all-to-all-done = bf16[32,8,256]{2,1,0:T(8,128)(2,1)S(1)} async-done(((bf16[32,8,256]{2,1,0:T(8,128)(2,1)}), bf16[32,8,256]{2,1,0:T(8,128)(2,1)S(1)}, u32[]{:S(2)}, u32[]{:S(2)}) %all-to-all-start) | async-done | bytes 131104 | tf_op jit(solution)/shard_map/all_to_all | solution.py:481
  67.2 0.0 copy-start.1
  67.2 0.0 copy-start.4
  67.3 1.7 %pad_maximum_fusion.1.late_share_ref = bf16[4,768,256]{2,1,0:T(8,128)(2,1)S(1)} fusion(bf16[1,768,256]{2,1,0:T(8,128)(2,1)} %bitcast.18, bf16[1,768,256]{2,1,0:T(8,128)(2,1)} %bitcast.17, bf16[1,768,256]{2,1,0:T(8,128)(2,1)} %bitcast.16, bf16[1,768,256]{2,1,0:T(8,128)(2,1)} %bitcast.15), kind=kLoop, calls=%fused_computation.1 | loop fusion | flops 2359296 | bytes 3145728 | tf_op jit(solution)/shard_map/stack | solution.py:619
  69.0 0.3 collective-permute-start.13
  69.2 3.2 %collective-permute-done.13.late_other_ref = bf16[4,768,256]{2,1,0:T(8,128)(2,1)S(1)} collective-permute-done((bf16[4,768,256]{2,1,0:T(8,128)(2,1)S(1)}, bf16[4,768,256]{2,1,0:T(8,128)(2,1)S(1)}, u32[]{:S(2)}, u32[]{:S(2)}) %collective-permute-start.13) | collective-permute-done | bytes 1572896 | tf_op jit(solution)/shard_map/ppermute | solution.py:486
  72.4 0.0 copy-done.1
  72.4 0.0 copy-done.4
  72.4 14.2 %shard_map.95 = bf16[4,8,8,1024]{3,2,1,0:T(8,128)(2,1)} custom-call(f32[7,8,2560]{2,1,0:T(8,128)S(1)} %get-tuple-element.33.first_ref, bf16[2,8,256,128]{3,2,1,0:T(8,128)(2,1)S(1)} %bitcast.29, bf16[2,8,256,128]{3,2,1,0:T(8,128)(2,1)S(1)} %bitcast.31, bf16[4,880,256]{2,1,0:T(8,128)(2,1)S(1)} %pad_maximum_fusion.share_ref, ...), custom_call_target="tpu_custom_call" | custom-call | bytes 50331648 | tf_op jit(solution)/shard_map/pallas_call | solution.py:469
  86.6 4.6 %all-to-all-start.1 = ((bf16[32,8,1024]{2,1,0:T(8,128)(2,1)}), bf16[32,8,1024]{2,1,0:T(8,128)(2,1)S(1)}, u32[]{:S(2)}, u32[]{:S(2)}) async-start(bf16[32,8,1024]{2,1,0:T(8,128)(2,1)} %bitcast.19), calls=%async_computation.1 | async-start | bytes 1048576 | tf_op jit(solution)/shard_map/all_to_all | solution.py:481
  91.2 0.8 copy.18.route_ref
  92.0 14.8 %all-to-all-done.1 = bf16[32,8,1024]{2,1,0:T(8,128)(2,1)S(1)} async-done(((bf16[32,8,1024]{2,1,0:T(8,128)(2,1)}), bf16[32,8,1024]{2,1,0:T(8,128)(2,1)S(1)}, u32[]{:S(2)}, u32[]{:S(2)}) %all-to-all-start.1) | async-done | bytes 524320 | tf_op jit(solution)/shard_map/all_to_all | solution.py:481
  106.7 1.6 %shard_map.96 = (bf16[32,512]{1,0:T(8,128)(2,1)}, f32[2,256,128]{2,1,0:T(8,128)}, f32[2,256,128]{2,1,0:T(8,128)}) custom-call(s32[4,2]{1,0:T(4,128)S(1)} %copy.18.route_ref, bf16[256,256]{1,0:T(8,128)(2,1)S(1)} %bitcast.33, bf16[256,1024]{1,0:T(8,128)(2,1)S(1)} %bitcast.32), custom_call_target="tpu_custom_call" | custom-call | tf_op jit(solution)/shard_map/pallas_call | solution.py:469
  (15 shorter events, 0.1 us)
Async XLA Ops:
  3.2 8.7 %collective-permute-start = (bf16[280,256]{1,0:T(8,128)(2,1)S(1)}, bf16[280,256]{1,0:T(8,128)(2,1)S(1)}, u32[]{:S(2)}, u32[]{:S(2)}) collective-permute-start(bf16[280,256]{1,0:T(8,128)(2,1)S(1)} %get-tuple-element.47), channel_id=1, source_target_pairs={{0,8},{8,0},{16,24},{24,16},{1,9},{9,1},{17,25},{25,17},{2,10},{10... | collective-permute-start | bytes 430088 | tf_op jit(solution)/shard_map/ppermute | solution.py:486
  6.3 13.7 %collective-permute-start.1 = (bf16[280,256]{1,0:T(8,128)(2,1)S(1)}, bf16[280,256]{1,0:T(8,128)(2,1)S(1)}, u32[]{:S(2)}, u32[]{:S(2)}) collective-permute-start(bf16[280,256]{1,0:T(8,128)(2,1)S(1)} %get-tuple-element.46), channel_id=1, source_target_pairs={{0,16},{8,24},{16,0},{24,8},{1,17},{9,25},{17,1},{25,9},{2,18},{10... | collective-permute-start | bytes 430088 | tf_op jit(solution)/shard_map/ppermute | solution.py:486
  8.9 11.2 %collective-permute-start.2 = (bf16[280,256]{1,0:T(8,128)(2,1)S(1)}, bf16[280,256]{1,0:T(8,128)(2,1)S(1)}, u32[]{:S(2)}, u32[]{:S(2)}) collective-permute-start(bf16[280,256]{1,0:T(8,128)(2,1)S(1)} %get-tuple-element.45), channel_id=1, source_target_pairs={{0,24},{8,16},{16,8},{24,0},{1,25},{9,17},{17,9},{25,1},{2,26},{10... | collective-permute-start | bytes 430088 | tf_op jit(solution)/shard_map/ppermute | solution.py:486
  20.2 13.3 %collective-permute-start.3 = (bf16[880,256]{1,0:T(8,128)(2,1)S(1)}, bf16[880,256]{1,0:T(8,128)(2,1)S(1)}, u32[]{:S(2)}, u32[]{:S(2)}) collective-permute-start(bf16[880,256]{1,0:T(8,128)(2,1)S(1)} %constant_dynamic-update-slice_fusion), channel_id=1, source_target_pairs={{0,2},{1,3},{2,0},{3,1},{4,6},{5,7},{6,4},{7,5},{8,10},{9,11},{10,... | collective-permute-start | bytes 1351688 | tf_op jit(solution)/shard_map/ppermute | solution.py:486
  21.7 19.0 %collective-permute-start.4 = (bf16[880,256]{1,0:T(8,128)(2,1)S(1)}, bf16[880,256]{1,0:T(8,128)(2,1)S(1)}, u32[]{:S(2)}, u32[]{:S(2)}) collective-permute-start(bf16[880,256]{1,0:T(8,128)(2,1)S(1)} %constant_dynamic-update-slice_fusion), channel_id=1, source_target_pairs={{0,4},{1,5},{2,6},{3,7},{4,0},{5,1},{6,2},{7,3},{8,12},{9,13},{10,... | collective-permute-start | bytes 1351688 | tf_op jit(solution)/shard_map/ppermute | solution.py:486
  23.2 17.4 %collective-permute-start.5 = (bf16[880,256]{1,0:T(8,128)(2,1)S(1)}, bf16[880,256]{1,0:T(8,128)(2,1)S(1)}, u32[]{:S(2)}, u32[]{:S(2)}) collective-permute-start(bf16[880,256]{1,0:T(8,128)(2,1)S(1)} %constant_dynamic-update-slice_fusion), channel_id=1, source_target_pairs={{0,6},{1,7},{2,4},{3,5},{4,2},{5,3},{6,0},{7,1},{8,14},{9,15},{10,... | collective-permute-start | bytes 1351688 | tf_op jit(solution)/shard_map/ppermute | solution.py:486
  23.7 7.9 %collective-permute-start.7 = (bf16[256,256]{1,0:T(8,128)(2,1)S(1)}, bf16[256,256]{1,0:T(8,128)(2,1)S(1)}, u32[]{:S(2)}, u32[]{:S(2)}) collective-permute-start(bf16[256,256]{1,0:T(8,128)(2,1)S(1)} %pad_maximum_fusion.6), channel_id=1, source_target_pairs={{0,16},{8,24},{16,0},{24,8},{1,17},{9,25},{17,1},{25,9},{2,18},{10... | collective-permute-start | bytes 393224 | tf_op jit(solution)/shard_map/ppermute | solution.py:486
  26.9 14.0 %collective-permute-start.6 = (bf16[256,256]{1,0:T(8,128)(2,1)S(1)}, bf16[256,256]{1,0:T(8,128)(2,1)S(1)}, u32[]{:S(2)}, u32[]{:S(2)}) collective-permute-start(bf16[256,256]{1,0:T(8,128)(2,1)S(1)} %pad_maximum_fusion.6), channel_id=1, source_target_pairs={{0,8},{8,0},{16,24},{24,16},{1,9},{9,1},{17,25},{25,17},{2,10},{10... | collective-permute-start | bytes 393224 | tf_op jit(solution)/shard_map/ppermute | solution.py:486
  31.6 9.4 %collective-permute-start.8 = (bf16[256,256]{1,0:T(8,128)(2,1)S(1)}, bf16[256,256]{1,0:T(8,128)(2,1)S(1)}, u32[]{:S(2)}, u32[]{:S(2)}) collective-permute-start(bf16[256,256]{1,0:T(8,128)(2,1)S(1)} %collective-permute-done.7), channel_id=1, source_target_pairs={{0,8},{8,0},{16,24},{24,16},{1,9},{9,1},{17,25},{25,17},{2,10},{10... | collective-permute-start | bytes 393224 | tf_op jit(solution)/shard_map/ppermute | solution.py:486
  40.7 5.8 %copy-start.2 = (bf16[2,2048,128]{2,1,0:T(8,128)(2,1)S(1)}, bf16[2,2048,128]{2,1,0:T(8,128)(2,1)}, u32[]{:S(2)}) copy-start(bf16[2,2048,128]{2,1,0:T(8,128)(2,1)} %param.11) | copy-start | bytes 3145732
  40.7 5.8 %copy-start.3 = (bf16[2,2048,128]{2,1,0:T(8,128)(2,1)S(1)}, bf16[2,2048,128]{2,1,0:T(8,128)(2,1)}, u32[]{:S(2)}) copy-start(bf16[2,2048,128]{2,1,0:T(8,128)(2,1)} %param.12) | copy-start | bytes 3145732
  40.9 5.6 %collective-permute-start.9 = (bf16[4,880,256]{2,1,0:T(8,128)(2,1)S(1)}, bf16[4,880,256]{2,1,0:T(8,128)(2,1)S(1)}, u32[]{:S(2)}, u32[]{:S(2)}) collective-permute-start(bf16[4,880,256]{2,1,0:T(8,128)(2,1)S(1)} %pad_maximum_fusion.share_ref), channel_id=1, source_target_pairs={{0,1},{1,0},{2,3},{3,2},{4,5},{5,4},{6,7},{7,6},{8,9},{9,8},{10,11... | collective-permute-start | bytes 5406728 | tf_op jit(solution)/shard_map/ppermute | solution.py:486
  43.0 16.0 %collective-permute-start.10 = (bf16[768,256]{1,0:T(8,128)(2,1)}, bf16[768,256]{1,0:T(8,128)(2,1)}, u32[]{:S(2)}, u32[]{:S(2)}) collective-permute-start(bf16[768,256]{1,0:T(8,128)(2,1)} %constant_dynamic-update-slice_fusion.5), channel_id=1, source_target_pairs={{0,2},{1,3},{2,0},{3,1},{4,6},{5,7},{6,4},{7,5},{8,10},{9,11},{10,... | collective-permute-start | bytes 1179656 | tf_op jit(solution)/shard_map/ppermute | solution.py:486
  44.2 19.0 %collective-permute-start.11 = (bf16[768,256]{1,0:T(8,128)(2,1)}, bf16[768,256]{1,0:T(8,128)(2,1)}, u32[]{:S(2)}, u32[]{:S(2)}) collective-permute-start(bf16[768,256]{1,0:T(8,128)(2,1)} %constant_dynamic-update-slice_fusion.5), channel_id=1, source_target_pairs={{0,4},{1,5},{2,6},{3,7},{4,0},{5,1},{6,2},{7,3},{8,12},{9,13},{10,... | collective-permute-start | bytes 1179656 | tf_op jit(solution)/shard_map/ppermute | solution.py:486
  45.1 19.8 %collective-permute-start.12 = (bf16[768,256]{1,0:T(8,128)(2,1)}, bf16[768,256]{1,0:T(8,128)(2,1)}, u32[]{:S(2)}, u32[]{:S(2)}) collective-permute-start(bf16[768,256]{1,0:T(8,128)(2,1)} %constant_dynamic-update-slice_fusion.5), channel_id=1, source_target_pairs={{0,6},{1,7},{2,4},{3,5},{4,2},{5,3},{6,0},{7,1},{8,14},{9,15},{10,... | collective-permute-start | bytes 1179656 | tf_op jit(solution)/shard_map/ppermute | solution.py:486
  46.5 5.8 %copy-start = (bf16[4,880,256]{2,1,0:T(8,128)(2,1)}, bf16[4,880,256]{2,1,0:T(8,128)(2,1)S(1)}, u32[]{:S(2)}) copy-start(bf16[4,880,256]{2,1,0:T(8,128)(2,1)S(1)} %collective-permute-done.9.other_ref) | copy-start | bytes 5406724
  52.3 0.7 copy-start.5
  53.0 14.3 %all-to-all-start = ((bf16[32,8,256]{2,1,0:T(8,128)(2,1)}), bf16[32,8,256]{2,1,0:T(8,128)(2,1)S(1)}, u32[]{:S(2)}, u32[]{:S(2)}) async-start(bf16[32,8,256]{2,1,0:T(8,128)(2,1)} %bitcast.34), calls=%async_computation | async-start | bytes 262144 | tf_op jit(solution)/shard_map/all_to_all | solution.py:481
  67.2 5.2 %copy-start.1 = (bf16[4,880,256]{2,1,0:T(8,128)(2,1)S(1)}, bf16[4,880,256]{2,1,0:T(8,128)(2,1)}, u32[]{:S(2)}) copy-start(bf16[4,880,256]{2,1,0:T(8,128)(2,1)} %copy-done) | copy-start | bytes 5406724
  67.2 5.2 %copy-start.4 = (bf16[2,2048,128]{2,1,0:T(8,128)(2,1)S(1)}, bf16[2,2048,128]{2,1,0:T(8,128)(2,1)}, u32[]{:S(2)}) copy-start(bf16[2,2048,128]{2,1,0:T(8,128)(2,1)} %param.12) | copy-start | bytes 3145732
  69.0 3.5 %collective-permute-start.13 = (bf16[4,768,256]{2,1,0:T(8,128)(2,1)S(1)}, bf16[4,768,256]{2,1,0:T(8,128)(2,1)S(1)}, u32[]{:S(2)}, u32[]{:S(2)}) collective-permute-start(bf16[4,768,256]{2,1,0:T(8,128)(2,1)S(1)} %pad_maximum_fusion.1.late_share_ref), channel_id=1, source_target_pairs={{0,1},{1,0},{2,3},{3,2},{4,5},{5,4},{6,7},{7,6},{8,9},{9,8},{10,11... | collective-permute-start | bytes 4718600 | tf_op jit(solution)/shard_map/ppermute | solution.py:486
  86.6 20.2 %all-to-all-start.1 = ((bf16[32,8,1024]{2,1,0:T(8,128)(2,1)}), bf16[32,8,1024]{2,1,0:T(8,128)(2,1)S(1)}, u32[]{:S(2)}, u32[]{:S(2)}) async-start(bf16[32,8,1024]{2,1,0:T(8,128)(2,1)} %bitcast.19), calls=%async_computation.1 | async-start | bytes 1048576 | tf_op jit(solution)/shard_map/all_to_all | solution.py:481

commit v4 on v3

--- a/solution.py
+++ b/solution.py
@@ -98,10 +98,7 @@
     scale = lax.rsqrt(jnp.sum(rows * rows, axis=1, keepdims=True) / feature_count + EPSILON)
     normed = rows * scale * gain_row
     packed = normed.astype(jnp.bfloat16)
-    share = feature_count // len(weight)
-    pair = jnp.zeros((row_count, 2 * head_size), jnp.float32)
-    for owner, part in enumerate(weight):
-        pair += contract(packed[:, owner * share : (owner + 1) * share], part[...], 1, 0)
+    pair = contract(packed, weight, 1, 0)
     queries = turned_heads(normed, cosine, sine).astype(jnp.bfloat16)
     keys = turned(pair[:, :head_size], cosine, sine).astype(jnp.bfloat16)
     values = pair[:, head_size:].astype(jnp.bfloat16)
@@ -130,8 +127,7 @@
     d_queries = contract(d_scores, keys, 0, 0)
     repeats = stacked.shape[0] // row_count
     d_queries = turned(d_queries, jnp.tile(cosine, (repeats, 1)), jnp.tile(-sine, (repeats, 1)))
-    d_packed = jnp.concatenate([contract(terms, part[...], 1, 1) for part in weight], axis=1)
-    d_normed = d_packed + heads_across(d_queries, row_count)
+    d_normed = contract(terms, weight, 1, 1) + heads_across(d_queries, row_count)
     scaled = d_normed * gain_row
     inner = jnp.sum(scaled * rows, axis=1, keepdims=True) / feature_count
     return upstream + scale * scaled - rows * (scale * scale * scale * inner), terms
@@ -172,10 +168,15 @@
 
 def layer_inputs(index, gain_ref, weight_ref, sections):
     place = lax.bitwise_xor(lax.axis_index("pipe"), index)
+    groups = weight_ref.shape[0]
     share = weight_ref.shape[1] // sections
     rows = pl.ds(pl.multiple_of(place * share, share), share)
-    weight = [weight_ref.at[owner, rows] for owner in range(weight_ref.shape[0])]
-    return gain_ref[pl.ds(place, 1), :], weight
+    weight = []
+    for owner in range(groups):
+        mask = lax.bitwise_xor(lax.axis_index("dp"), owner)
+        line = lax.rem(mask, 2) * (groups // 2) + lax.div(mask, 2)
+        weight.append(weight_ref[jnp.where(place == 0, owner, line), rows, :])
+    return gain_ref[pl.ds(place, 1), :], jnp.concatenate(weight, axis=0)
 
 
 def forward_steps(rows, gain_ref, weight_ref, tables, state_ref, packed_ref):
@@ -214,17 +215,13 @@
 def fill(turn, key_ref, value_ref, shares, weight_ref, sems):
     groups, share, head_size = key_ref.shape[1:]
     moved = weight_ref.shape[1] - share
-    group = lax.axis_index("dp")
     copies = [
         (key_ref.at[turn], weight_ref.at[:, :share, :head_size]),
         (value_ref.at[turn], weight_ref.at[:, :share, head_size:]),
     ]
     for core, ref in enumerate(shares):
-        for chip in range(groups // 2):
-            owner = lax.bitwise_xor(group, 2 * chip + core)
-            copies.append(
-                (ref.at[chip, pl.ds(0, moved)], weight_ref.at[owner, pl.ds(share, moved)])
-            )
+        lines = pl.ds(core * (groups // 2), groups // 2)
+        copies.append((ref.at[:, pl.ds(0, moved)], weight_ref.at[lines, pl.ds(share, moved)]))
     copies = [
         pltpu.make_async_copy(*pair, sems.at[turn, index]) for index, pair in enumerate(copies)
     ]
@@ -239,8 +236,9 @@
     value_ref,
     share_ref,
     other_ref,
+    state_out,
+    packed_ref,
     state_ref,
-    packed_ref,
     lines_ref,
     rows_ref,
     gains_ref,
@@ -348,10 +346,13 @@
     state_ref[sections, :, :feature_count] = forward_steps(
         rows, gain_ref.at[pl.ds(0, sections)], weight_ref, tables, state_ref, packed_ref
     )
+    state_copy = pltpu.make_async_copy(state_ref, state_out, line_sems.at[2])
+    state_copy.start()
+    state_copy.wait()
 
 
 def second_kernel(
-    first_ref,
+    state_in,
     key_ref,
     value_ref,
     share_ref,
@@ -359,18 +360,22 @@
     late_share_ref,
     late_other_ref,
     out_ref,
+    first_ref,
     state_ref,
     gain_ref,
+    state_sem,
     late_weight_ref,
     weight_ref,
     sems
 ):
+    state_copy = pltpu.make_async_copy(state_in, first_ref, state_sem.at[0])
+    state_copy.start()
     sections, groups, row_count, _ = out_ref.shape
     share, head_size = key_ref.shape[2:]
     feature_count, term_width = groups * share, 2 * head_size
     late_shares = (late_share_ref, late_other_ref)
     late_copies = fill(1, key_ref, value_ref, late_shares, late_weight_ref, sems)
-    copies = fill(0, key_ref, value_ref, (share_ref, other_ref), weight_ref, sems)
+    state_copy.wait()
     kept = []
     for place in range(4):
         start = feature_count + place * head_size
@@ -384,6 +389,7 @@
     late_gain = gain_ref.at[pl.ds(sections, sections)]
     for copy in late_copies:
         copy.wait()
+    copies = fill(0, key_ref, value_ref, (share_ref, other_ref), weight_ref, sems)
     forward_steps(
         first_ref[sections, :, :feature_count],
         late_gain,
@@ -463,14 +469,17 @@
         ).astype(jnp.bfloat16)
 
 
-def call(kernel, outs, operands, scalars=0, whole=0, scratch=(), vmem_bytes=0, cost=0):
+def call(kernel, outs, operands, scalars=0, whole=0, any_outs=0, scratch=(), vmem_bytes=0, cost=0):
     spaces = [pltpu.SMEM] * scalars + [pltpu.VMEM] * (len(operands) - scalars - whole)
     spaces += [pl.ANY] * whole
     return pl.pallas_call(
         kernel,
         out_shape=outs,
         in_specs=[pl.BlockSpec(memory_space=space) for space in spaces],
-        out_specs=[pl.BlockSpec(memory_space=pltpu.VMEM)] * len(outs),
+        out_specs=[
+            pl.BlockSpec(memory_space=pl.ANY if place < any_outs else pltpu.VMEM)
+            for place in range(len(outs))
+        ],
         scratch_shapes=scratch,
         compiler_params=pltpu.CompilerParams(vmem_limit_bytes=vmem_bytes),
         cost_estimate=pl.CostEstimate(flops=0, bytes_accessed=cost, transcendentals=0),
@@ -486,12 +495,18 @@
     return lax.ppermute(value, axis, pairs)
 
 
-def relayed(payload, sections):
-    pieces = [payload]
+def direct_pieces(payload, sections):
+    masks = [mask for mask in range(1, sections) if mask & (mask - 1) == 0]
+    return {mask: swapped(payload, "pipe", mask) for mask in masks}
+
+
+def relayed_pieces(pieces, sections):
+    pieces = dict(pieces)
     for mask in range(1, sections):
         low = mask & -mask
-        pieces.append(swapped(pieces[mask - low], "pipe", low))
-    return pieces[1:]
+        if mask != low:
+            pieces[mask] = swapped(pieces[mask - low], "pipe", low)
+    return [pieces[mask] for mask in range(1, sections)]
 
 
 def body(hidden, lengths, route, gain, key_weight, value_weight, cotangent):
@@ -512,9 +527,9 @@
 
     line_width = 2 * head_size
 
-    def own_share(turn):
+    def share_of(turn, owner):
         parts = [
-            lax.dynamic_slice(array, (turn, group_index * share, 0), (1, share, head_size))[0]
+            lax.dynamic_slice(array, (turn, owner * share, 0), (1, share, head_size))[0]
             for array in (key_weight, value_weight)
         ]
         return jnp.concatenate(parts, axis=1)
@@ -532,7 +547,7 @@
         terms.astype(jnp.bfloat16), ((0, GAIN_LINES - 6), (0, line_width - share))
     )
 
-    first = own_share(0)
+    first = share_of(0, group_index)
     came = [
         swapped(jnp.concatenate([first, own_rows(mask), terms], axis=0), "pipe", mask)
         for mask in range(1, sections)
@@ -552,33 +567,39 @@
         + [tags],
         axis=0,
     )
-    column, second = lax.optimization_barrier((column, own_share(1)))
+    distant = share_of(1, lax.bitwise_xor(group_index, groups - 2))
+    column, second, distant = lax.optimization_barrier(
+        (column, share_of(1, group_index), distant)
+    )
     chips = range(1, groups // 2)
     plane = jnp.stack([column] + [swapped(column, "dp", 2 * chip) for chip in chips])
-    came = relayed(second, sections)
-    plane, came = lax.optimization_barrier((plane, came))
+    came = direct_pieces(second, sections)
+    came[sections // 2], distant = lax.optimization_barrier((came[sections // 2], distant))
+    came = relayed_pieces(came, sections)
+    far = swapped(distant, "pipe", sections // 2)
+    plane, came, far, distant = lax.optimization_barrier((plane, came, far, distant))
     first_shares = (plane, swapped(plane, "dp", 1))
     column = jnp.concatenate(came, axis=0)
-    planes = [column] + [swapped(column, "dp", 2 * chip) for chip in chips]
+    planes = [column] + [swapped(column, "dp", 2 * chip) for chip in chips[:-1]]
+    far = relayed_pieces({**direct_pieces(distant, sections // 2), sections // 2: far}, sections)
 
     key_parts = key_weight.reshape(2, groups, share, head_size)
     value_parts = value_weight.reshape(2, groups, share, head_size)
 
-    def layers_call(kernel, turns, outs, operands, shares, scratch, cost, columns):
+    def layers_call(kernel, turns, outs, operands, shares, scratch, cost, vmem_bytes, whole, any_outs):
         weight = pltpu.VMEM((groups, sections * share, line_width), jnp.bfloat16)
         return call(
             kernel,
             outs,
             (*operands, key_parts, value_parts, *shares),
-            whole=2 + len(shares),
+            whole=2 + len(shares) + whole,
+            any_outs=any_outs,
             scratch=[
                 *scratch,
                 *[weight] * turns,
-                pltpu.SemaphoreType.DMA((2, groups + 2)),
+                pltpu.SemaphoreType.DMA((2, 4)),
             ],
-            vmem_bytes=(6 << 20)
-            + 2 * turns * sections * feature_count * line_width
-            + 4 * devices * row_count * columns,
+            vmem_bytes=vmem_bytes,
             cost=cost,
         )
 
@@ -593,30 +614,30 @@
     line = (row_count, state_width(feature_count, head_size))
     line_count = plane.shape[1] - (sections - 1) * share
     gain_scratch = pltpu.VMEM((2 * sections, feature_count), jnp.float32)
+    state_shape = (sections + 2 + 2 * sections // row_count, *line)
     state, packed = layers_call(
         functools.partial(first_kernel, doc_count=lengths.shape[1]),
         1,
-        [
-            jax.ShapeDtypeStruct(
-                (sections + 2 + 2 * sections // row_count, *line), jnp.float32
-            ),
-            blocks_shape(share),
-        ],
+        [jax.ShapeDtypeStruct(state_shape, jnp.float32), blocks_shape(share)],
         (upstream,),
         first_shares,
         (
+            pltpu.VMEM(state_shape, jnp.float32),
             pltpu.VMEM((2, groups // 2, line_count, line_width), jnp.bfloat16),
             pltpu.VMEM((sections, row_count, column_count), jnp.float32),
             pltpu.VMEM((groups, 2 * sections, share), jnp.float32),
             gain_scratch,
-            pltpu.SemaphoreType.DMA((2,)),
+            pltpu.SemaphoreType.DMA((3,)),
         ),
         18 << 20,
-        2 * LANES,
-    )
+        (8 << 20) + sections * feature_count * 2 * line_width + 1024 * devices * row_count,
+        0,
+        1,
+    )
+    state, planes, far = lax.optimization_barrier((state, planes, far))
+    plane = jnp.stack(planes + [jnp.concatenate(far, axis=0)])
+    plane, packed = lax.optimization_barrier((plane, packed))
     packed = exchanged(packed)
-    state, packed, planes = lax.optimization_barrier((state, packed, planes))
-    plane = jnp.stack(planes)
     second_shares = (plane, swapped(plane, "dp", 1))
     columns = share + 4 * head_size + width
     (late,) = layers_call(
@@ -625,9 +646,16 @@
         [blocks_shape(columns)],
         (state,),
         (*first_shares, *second_shares),
-        (pltpu.VMEM((sections, *line), jnp.float32), gain_scratch),
+        (
+            pltpu.VMEM(state_shape, jnp.float32),
+            pltpu.VMEM((sections, *line), jnp.float32),
+            gain_scratch,
+            pltpu.SemaphoreType.DMA((1,)),
+        ),
         48 << 20,
-        columns,
+        60 << 20,
+        1,
+        0,
     )
     late, packed = lax.optimization_barrier((late, packed))
     late = exchanged(late)

time: 109 us -> 99.6 us (0.914)
  waiting for transfers between devices: 48.5 us -> 36.2 us
  starting transfers between devices: 27.2 us -> 34 us
  local copies, waits for them, and re-layouts: 5.4 us -> 3.38 us
  other arithmetic: 4.88 us -> 3.43 us
    ppermute x14 -> x16, waiting for transfers between devices: 31.3 us -> 20.8 us  [swapped(): return lax.ppermute(value, axis, pairs)]
    ppermute x14 -> x16, starting transfers between devices: 16.6 us -> 21.7 us  [swapped(): return lax.ppermute(value, axis, pairs)]
    all_to_all x2, waiting for transfers between devices: 17.2 us -> 15.4 us  [exchange(): lax.all_to_all(blocks, ('pipe', 'dp'), split_axis=0, concat_axis=0, tiled...]
    all_to_all x2, starting transfers between devices: 10.7 us -> 12.2 us  [exchange(): lax.all_to_all(blocks, ('pipe', 'dp'), split_axis=0, concat_axis=0, tiled...]
    another operation x3 -> x4, other arithmetic: 3.06 us -> 1.59 us  [the longest x1 1.7 us: body(): plane = jnp.stack(planes)]
    unnamed x22 -> x26, local copies, waits for them, and re-layouts: 2.81 us -> 1.37 us
  transfers between devices with their start and end apart: 16 -> 18, of which waited for: 10 -> 8; matrix products, arithmetic and copies ran while one was open for 5% -> 3% of each run, Pallas kernels for 5% -> 20%
where the time goes in v4:
time: 99.6 us; the launch traced here: 99.1 us
  waiting for transfers between devices  36.2 us (36%)
  starting transfers between devices  34 us (34%)
  Pallas kernels  21.1 us (21%)
  other arithmetic  3.43 us (3%)
  local copies, waits for them, and re-layouts  3.38 us (3%)
  between operations  1 us (1%)
    ppermute x16, starting transfers between devices, swapped(): return lax.ppermute(value, axis, pairs)  21.7 us
    pallas_call x3, Pallas kernels, call(): pl.pallas_call(kernel, out_shape=outs, in_specs=[pl.BlockSpec(memory_spac...  21.1 us
    ppermute x16, waiting for transfers between devices, swapped(): return lax.ppermute(value, axis, pairs)  20.8 us
    all_to_all x2, waiting for transfers between devices, exchange(): lax.all_to_all(blocks, ('pipe', 'dp'), split_axis=0, concat_axis=0, tiled...  15.4 us
    all_to_all x2, starting transfers between devices, exchange(): lax.all_to_all(blocks, ('pipe', 'dp'), split_axis=0, concat_axis=0, tiled...  12.2 us
  transfers between devices with their start and end apart: 18, of which 8 were waited for; matrix products, arithmetic and copies ran while one was open for 3% of the time, Pallas kernels for 20%

profile of v4, /device:TPU:0, one launch (start us, length us, event | category | flops | bytes accessed | tf_op | source)
XLA Modules:
  0.0 99.1 jit_solution(12339408753230720151)
XLA Ops:
  0.7 0.7 fusion.8
  1.4 1.0 %dynamic-slice_bitcast_fusion = (bf16[256,128]{1,0:T(8,128)(2,1)S(1)}, bf16[256,128]{1,0:T(8,128)(2,1)S(1)}, bf16[256,128]{1,0:T(8,128)(2,1)S(1)}, bf16[256,128]...) fusion(bf16[2,2048,128]{2,1,0:T(8,128)(2,1)} %param.12, s32[]{:T(128)S(6)} %select_n.29, ...), kind=kLoop, calls=%fused_computation.12 | loop fusion | bytes 786440 | tf_op jit(solution)/shard_map/squeeze | solution.py:532
  2.5 0.8 constant_dynamic-slice_fusion.3
  3.3 3.1 %collective-permute-start = (bf16[280,256]{1,0:T(8,128)(2,1)S(1)}, bf16[280,256]{1,0:T(8,128)(2,1)S(1)}, u32[]{:S(2)}, u32[]{:S(2)}) collective-permute-start(bf16[280,256]{1,0:T(8,128)(2,1)S(1)} %get-tuple-element.65), channel_id=1, source_target_pairs={{0,8},{8,0},{16,24},{24,16},{1,9},{9,1},{17,25},{25,17},{2,10},{10... | collective-permute-start | bytes 430088 | tf_op jit(solution)/shard_map/ppermute | solution.py:495
  6.4 2.6 %collective-permute-start.1 = (bf16[280,256]{1,0:T(8,128)(2,1)S(1)}, bf16[280,256]{1,0:T(8,128)(2,1)S(1)}, u32[]{:S(2)}, u32[]{:S(2)}) collective-permute-start(bf16[280,256]{1,0:T(8,128)(2,1)S(1)} %get-tuple-element.64), channel_id=1, source_target_pairs={{0,16},{8,24},{16,0},{24,8},{1,17},{9,25},{17,1},{25,9},{2,18},{10... | collective-permute-start | bytes 430088 | tf_op jit(solution)/shard_map/ppermute | solution.py:495
  9.0 0.0 collective-permute-start.2
  9.0 0.8 dynamic-slice_convert_fusion.upstream_ref
  9.8 0.7 convert.19
  10.4 0.1 copy.16
  10.6 0.7 convert.18
  11.3 0.1 fusion.5
  11.4 0.7 collective-permute-done
  12.1 8.1 %collective-permute-done.1 = bf16[280,256]{1,0:T(8,128)(2,1)S(1)} collective-permute-done((bf16[280,256]{1,0:T(8,128)(2,1)S(1)}, bf16[280,256]{1,0:T(8,128)(2,1)S(1)}, u32[]{:S(2)}, u32[]{:S(2)}) %collective-permute-start.1) | collective-permute-done | bytes 143392 | tf_op jit(solution)/shard_map/ppermute | solution.py:495
  20.1 0.0 collective-permute-done.2
  20.2 1.6 %collective-permute-start.3 = (bf16[880,256]{1,0:T(8,128)(2,1)S(1)}, bf16[880,256]{1,0:T(8,128)(2,1)S(1)}, u32[]{:S(2)}, u32[]{:S(2)}) collective-permute-start(bf16[880,256]{1,0:T(8,128)(2,1)S(1)} %constant_dynamic-update-slice_fusion), channel_id=1, source_target_pairs={{0,2},{1,3},{2,0},{3,1},{4,6},{5,7},{6,4},{7,5},{8,10},{9,11},{10,... | collective-permute-start | bytes 1351688 | tf_op jit(solution)/shard_map/ppermute | solution.py:495
  21.8 1.5 %collective-permute-start.4 = (bf16[880,256]{1,0:T(8,128)(2,1)S(1)}, bf16[880,256]{1,0:T(8,128)(2,1)S(1)}, u32[]{:S(2)}, u32[]{:S(2)}) collective-permute-start(bf16[880,256]{1,0:T(8,128)(2,1)S(1)} %constant_dynamic-update-slice_fusion), channel_id=1, source_target_pairs={{0,4},{1,5},{2,6},{3,7},{4,0},{5,1},{6,2},{7,3},{8,12},{9,13},{10,... | collective-permute-start | bytes 1351688 | tf_op jit(solution)/shard_map/ppermute | solution.py:495
  23.3 0.5 collective-permute-start.5
  23.8 3.2 %collective-permute-start.7 = (bf16[256,256]{1,0:T(8,128)(2,1)S(1)}, bf16[256,256]{1,0:T(8,128)(2,1)S(1)}, u32[]{:S(2)}, u32[]{:S(2)}) collective-permute-start(bf16[256,256]{1,0:T(8,128)(2,1)S(1)} %pad_maximum_fusion.6), channel_id=1, source_target_pairs={{0,16},{8,24},{16,0},{24,8},{1,17},{9,25},{17,1},{25,9},{2,18},{10... | collective-permute-start | bytes 393224 | tf_op jit(solution)/shard_map/ppermute | solution.py:495
  27.0 0.0 collective-permute-start.6
  27.0 4.7 %collective-permute-done.7 = bf16[256,256]{1,0:T(8,128)(2,1)S(1)} collective-permute-done((bf16[256,256]{1,0:T(8,128)(2,1)S(1)}, bf16[256,256]{1,0:T(8,128)(2,1)S(1)}, u32[]{:S(2)}, u32[]{:S(2)}) %collective-permute-start.7) | collective-permute-done | bytes 131104 | tf_op jit(solution)/shard_map/ppermute | solution.py:495
  31.6 0.3 collective-permute-start.8
  31.9 1.6 %collective-permute-done.3 = bf16[880,256]{1,0:T(8,128)(2,1)S(1)} collective-permute-done((bf16[880,256]{1,0:T(8,128)(2,1)S(1)}, bf16[880,256]{1,0:T(8,128)(2,1)S(1)}, u32[]{:S(2)}, u32[]{:S(2)}) %collective-permute-start.3) | collective-permute-done | bytes 450592 | tf_op jit(solution)/shard_map/ppermute | solution.py:495
  33.6 3.2 %collective-permute-start.9 = (bf16[256,256]{1,0:T(8,128)(2,1)S(1)}, bf16[256,256]{1,0:T(8,128)(2,1)S(1)}, u32[]{:S(2)}, u32[]{:S(2)}) collective-permute-start(bf16[256,256]{1,0:T(8,128)(2,1)S(1)} %pad_maximum_fusion.7), channel_id=1, source_target_pairs={{0,16},{8,24},{16,0},{24,8},{1,17},{9,25},{17,1},{25,9},{2,18},{10... | collective-permute-start | bytes 393224 | tf_op jit(solution)/shard_map/ppermute | solution.py:495
  36.8 4.0 %collective-permute-done.4 = bf16[880,256]{1,0:T(8,128)(2,1)S(1)} collective-permute-done((bf16[880,256]{1,0:T(8,128)(2,1)S(1)}, bf16[880,256]{1,0:T(8,128)(2,1)S(1)}, u32[]{:S(2)}, u32[]{:S(2)}) %collective-permute-start.4) | collective-permute-done | bytes 450592 | tf_op jit(solution)/shard_map/ppermute | solution.py:495
  40.8 0.0 collective-permute-done.5
  40.8 0.0 copy-start.2
  40.8 0.2 pad_maximum_fusion.share_ref
  41.0 0.0 copy-start
  41.0 0.0 collective-permute-done.6
  41.0 0.0 collective-permute-done.8
  41.0 0.0 collective-permute-done.9
  41.0 0.1 collective-permute-start.10
  41.2 1.3 %collective-permute-start.11 = (bf16[768,256]{1,0:T(8,128)(2,1)S(1)}, bf16[768,256]{1,0:T(8,128)(2,1)S(1)}, u32[]{:S(2)}, u32[]{:S(2)}) collective-permute-start(bf16[768,256]{1,0:T(8,128)(2,1)S(1)} %constant_dynamic-update-slice_fusion.5), channel_id=1, source_target_pairs={{0,2},{1,3},{2,0},{3,1},{4,6},{5,7},{6,4},{7,5},{8,10},{9,11},{10,... | collective-permute-start | bytes 1179656 | tf_op jit(solution)/shard_map/ppermute | solution.py:495
  42.5 0.8 collective-permute-start.12
  43.3 3.5 %collective-permute-start.13 = (bf16[256,256]{1,0:T(8,128)(2,1)S(1)}, bf16[256,256]{1,0:T(8,128)(2,1)S(1)}, u32[]{:S(2)}, u32[]{:S(2)}) collective-permute-start(bf16[256,256]{1,0:T(8,128)(2,1)S(1)} %pad_maximum_fusion.7), channel_id=1, source_target_pairs={{0,8},{8,0},{16,24},{24,16},{1,9},{9,1},{17,25},{25,17},{2,10},{10... | collective-permute-start | bytes 393224 | tf_op jit(solution)/shard_map/ppermute | solution.py:495
  46.8 0.0 collective-permute-start.14
  46.9 0.0 collective-permute-done.10.other_ref
  46.9 0.0 copy-done.2
  46.9 0.0 copy-done.3
  46.9 5.1 %shard_map.94 = (f32[7,8,2560]{2,1,0:T(8,128)S(1)}, bf16[4,8,8,256]{3,2,1,0:T(8,128)(2,1)}) custom-call(f32[8,2048]{1,0:T(8,128)S(1)} %dynamic-slice_convert_fusion.upstream_ref, bf16[2,8,256,128]{3,2,1,0:T(8,128)(2,1)S(1)} %bitcast.34, bf16[2,8,256,128]{3,2,1,0:T(8,128)(2,1)S(1)} %bitcast.36, bf16[4,880,256]{2,1,0:T(8,128)(2,1)S(1)} %pad_maximum_fusion.share_ref, ...), custom_call_target="tpu_custom_call" | custom-call | bytes 18874368 | tf_op jit(solution)/shard_map/pallas_call | solution.py:475
  51.9 0.0 copy-done
  52.0 0.0 copy-done.1
  52.0 0.0 copy-start.4
  52.0 0.0 collective-permute-done.13
  52.0 1.2 %collective-permute-done.14 = bf16[256,256]{1,0:T(8,128)(2,1)S(1)} collective-permute-done((bf16[256,256]{1,0:T(8,128)(2,1)S(1)}, bf16[256,256]{1,0:T(8,128)(2,1)S(1)}, u32[]{:S(2)}, u32[]{:S(2)}) %collective-permute-start.14) | collective-permute-done | bytes 131104 | tf_op jit(solution)/shard_map/ppermute | solution.py:495
  53.2 0.0 collective-permute-done.11
  53.2 0.5 collective-permute-done.12
  53.7 0.2 pad_maximum_fusion.1.late_share_ref
  53.9 0.0 copy-done.4
  53.9 0.0 copy-start.5
  54.0 0.1 collective-permute-start.15
  54.0 6.4 %all-to-all-start = ((bf16[32,8,256]{2,1,0:T(8,128)(2,1)}), bf16[32,8,256]{2,1,0:T(8,128)(2,1)S(1)}, u32[]{:S(2)}, u32[]{:S(2)}) async-start(bf16[32,8,256]{2,1,0:T(8,128)(2,1)} %bitcast.19), calls=%async_computation | async-start | bytes 262144 | tf_op jit(solution)/shard_map/all_to_all | solution.py:490
  60.4 0.0 copy-start.7
  60.4 0.0 collective-permute-done.15.late_other_ref
  60.5 0.0 copy-done.5
  60.5 0.0 copy-start.6
  60.5 1.2 %copy-done.6 = bf16[4,768,256]{2,1,0:T(8,128)(2,1)} copy-done((bf16[4,768,256]{2,1,0:T(8,128)(2,1)}, bf16[4,768,256]{2,1,0:T(8,128)(2,1)S(1)}, u32[]{:S(2)}) %copy-start.6) | copy-done | bytes 1572888
  61.7 14.4 %shard_map.95 = bf16[4,8,8,1024]{3,2,1,0:T(8,128)(2,1)} custom-call(f32[7,8,2560]{2,1,0:T(8,128)} %copy-done.4, bf16[2,8,256,128]{3,2,1,0:T(8,128)(2,1)} %bitcast.33, bf16[2,8,256,128]{3,2,1,0:T(8,128)(2,1)} %bitcast.35, bf16[4,880,256]{2,1,0:T(8,128)(2,1)} %copy-done, bf16[4,880,256]{2,1,0:T(8,128)(2,1)} %copy-done.1, bf16[4,768,256]{2,1,0:T(8,128)(2,1)} %copy-done.5, ...), custom_call_target="tpu_custom_call" | custom-call | bytes 50331648 | tf_op jit(solution)/shard_map/pallas_call | solution.py:475
  76.1 0.0 all-to-all-done
  76.1 5.8 %all-to-all-start.1 = ((bf16[32,8,1024]{2,1,0:T(8,128)(2,1)}), bf16[32,8,1024]{2,1,0:T(8,128)(2,1)S(1)}, u32[]{:S(2)}, u32[]{:S(2)}) async-start(bf16[32,8,1024]{2,1,0:T(8,128)(2,1)} %bitcast.39), calls=%async_computation.1 | async-start | bytes 1048576 | tf_op jit(solution)/shard_map/all_to_all | solution.py:490
  81.9 0.0 copy-done.7
  81.9 0.1 copy.18.route_ref
  82.0 15.4 %all-to-all-done.1 = bf16[32,8,1024]{2,1,0:T(8,128)(2,1)S(1)} async-done(((bf16[32,8,1024]{2,1,0:T(8,128)(2,1)}), bf16[32,8,1024]{2,1,0:T(8,128)(2,1)S(1)}, u32[]{:S(2)}, u32[]{:S(2)}) %all-to-all-start.1) | async-done | bytes 524320 | tf_op jit(solution)/shard_map/all_to_all | solution.py:490
  97.5 1.6 %shard_map.96 = (bf16[32,512]{1,0:T(8,128)(2,1)}, f32[2,256,128]{2,1,0:T(8,128)}, f32[2,256,128]{2,1,0:T(8,128)}) custom-call(s32[4,2]{1,0:T(4,128)S(1)} %copy.18.route_ref, bf16[256,256]{1,0:T(8,128)(2,1)S(1)} %bitcast.38, bf16[256,1024]{1,0:T(8,128)(2,1)S(1)} %bitcast.37), custom_call_target="tpu_custom_call" | custom-call | tf_op jit(solution)/shard_map/pallas_call | solution.py:475
  (22 shorter events, 0.2 us)
Async XLA Ops:
  3.3 8.7 %collective-permute-start = (bf16[280,256]{1,0:T(8,128)(2,1)S(1)}, bf16[280,256]{1,0:T(8,128)(2,1)S(1)}, u32[]{:S(2)}, u32[]{:S(2)}) collective-permute-start(bf16[280,256]{1,0:T(8,128)(2,1)S(1)} %get-tuple-element.65), channel_id=1, source_target_pairs={{0,8},{8,0},{16,24},{24,16},{1,9},{9,1},{17,25},{25,17},{2,10},{10... | collective-permute-start | bytes 430088 | tf_op jit(solution)/shard_map/ppermute | solution.py:495
  6.4 13.7 %collective-permute-start.1 = (bf16[280,256]{1,0:T(8,128)(2,1)S(1)}, bf16[280,256]{1,0:T(8,128)(2,1)S(1)}, u32[]{:S(2)}, u32[]{:S(2)}) collective-permute-start(bf16[280,256]{1,0:T(8,128)(2,1)S(1)} %get-tuple-element.64), channel_id=1, source_target_pairs={{0,16},{8,24},{16,0},{24,8},{1,17},{9,25},{17,1},{25,9},{2,18},{10... | collective-permute-start | bytes 430088 | tf_op jit(solution)/shard_map/ppermute | solution.py:495
  9.0 11.2 %collective-permute-start.2 = (bf16[280,256]{1,0:T(8,128)(2,1)S(1)}, bf16[280,256]{1,0:T(8,128)(2,1)S(1)}, u32[]{:S(2)}, u32[]{:S(2)}) collective-permute-start(bf16[280,256]{1,0:T(8,128)(2,1)S(1)} %get-tuple-element.63), channel_id=1, source_target_pairs={{0,24},{8,16},{16,8},{24,0},{1,25},{9,17},{17,9},{25,1},{2,26},{10... | collective-permute-start | bytes 430088 | tf_op jit(solution)/shard_map/ppermute | solution.py:495
  20.2 13.3 %collective-permute-start.3 = (bf16[880,256]{1,0:T(8,128)(2,1)S(1)}, bf16[880,256]{1,0:T(8,128)(2,1)S(1)}, u32[]{:S(2)}, u32[]{:S(2)}) collective-permute-start(bf16[880,256]{1,0:T(8,128)(2,1)S(1)} %constant_dynamic-update-slice_fusion), channel_id=1, source_target_pairs={{0,2},{1,3},{2,0},{3,1},{4,6},{5,7},{6,4},{7,5},{8,10},{9,11},{10,... | collective-permute-start | bytes 1351688 | tf_op jit(solution)/shard_map/ppermute | solution.py:495
  21.8 19.0 %collective-permute-start.4 = (bf16[880,256]{1,0:T(8,128)(2,1)S(1)}, bf16[880,256]{1,0:T(8,128)(2,1)S(1)}, u32[]{:S(2)}, u32[]{:S(2)}) collective-permute-start(bf16[880,256]{1,0:T(8,128)(2,1)S(1)} %constant_dynamic-update-slice_fusion), channel_id=1, source_target_pairs={{0,4},{1,5},{2,6},{3,7},{4,0},{5,1},{6,2},{7,3},{8,12},{9,13},{10,... | collective-permute-start | bytes 1351688 | tf_op jit(solution)/shard_map/ppermute | solution.py:495
  23.3 17.4 %collective-permute-start.5 = (bf16[880,256]{1,0:T(8,128)(2,1)S(1)}, bf16[880,256]{1,0:T(8,128)(2,1)S(1)}, u32[]{:S(2)}, u32[]{:S(2)}) collective-permute-start(bf16[880,256]{1,0:T(8,128)(2,1)S(1)} %constant_dynamic-update-slice_fusion), channel_id=1, source_target_pairs={{0,6},{1,7},{2,4},{3,5},{4,2},{5,3},{6,0},{7,1},{8,14},{9,15},{10,... | collective-permute-start | bytes 1351688 | tf_op jit(solution)/shard_map/ppermute | solution.py:495
  23.8 7.9 %collective-permute-start.7 = (bf16[256,256]{1,0:T(8,128)(2,1)S(1)}, bf16[256,256]{1,0:T(8,128)(2,1)S(1)}, u32[]{:S(2)}, u32[]{:S(2)}) collective-permute-start(bf16[256,256]{1,0:T(8,128)(2,1)S(1)} %pad_maximum_fusion.6), channel_id=1, source_target_pairs={{0,16},{8,24},{16,0},{24,8},{1,17},{9,25},{17,1},{25,9},{2,18},{10... | collective-permute-start | bytes 393224 | tf_op jit(solution)/shard_map/ppermute | solution.py:495
  27.0 14.0 %collective-permute-start.6 = (bf16[256,256]{1,0:T(8,128)(2,1)S(1)}, bf16[256,256]{1,0:T(8,128)(2,1)S(1)}, u32[]{:S(2)}, u32[]{:S(2)}) collective-permute-start(bf16[256,256]{1,0:T(8,128)(2,1)S(1)} %pad_maximum_fusion.6), channel_id=1, source_target_pairs={{0,8},{8,0},{16,24},{24,16},{1,9},{9,1},{17,25},{25,17},{2,10},{10... | collective-permute-start | bytes 393224 | tf_op jit(solution)/shard_map/ppermute | solution.py:495
  31.6 9.4 %collective-permute-start.8 = (bf16[256,256]{1,0:T(8,128)(2,1)S(1)}, bf16[256,256]{1,0:T(8,128)(2,1)S(1)}, u32[]{:S(2)}, u32[]{:S(2)}) collective-permute-start(bf16[256,256]{1,0:T(8,128)(2,1)S(1)} %collective-permute-done.7), channel_id=1, source_target_pairs={{0,8},{8,0},{16,24},{24,16},{1,9},{9,1},{17,25},{25,17},{2,10},{10... | collective-permute-start | bytes 393224 | tf_op jit(solution)/shard_map/ppermute | solution.py:495
  33.6 7.4 %collective-permute-start.9 = (bf16[256,256]{1,0:T(8,128)(2,1)S(1)}, bf16[256,256]{1,0:T(8,128)(2,1)S(1)}, u32[]{:S(2)}, u32[]{:S(2)}) collective-permute-start(bf16[256,256]{1,0:T(8,128)(2,1)S(1)} %pad_maximum_fusion.7), channel_id=1, source_target_pairs={{0,16},{8,24},{16,0},{24,8},{1,17},{9,25},{17,1},{25,9},{2,18},{10... | collective-permute-start | bytes 393224 | tf_op jit(solution)/shard_map/ppermute | solution.py:495
  40.8 6.1 %copy-start.2 = (bf16[2,2048,128]{2,1,0:T(8,128)(2,1)S(1)}, bf16[2,2048,128]{2,1,0:T(8,128)(2,1)}, u32[]{:S(2)}) copy-start(bf16[2,2048,128]{2,1,0:T(8,128)(2,1)} %param.11) | copy-start | bytes 3145732
  40.8 6.1 %copy-start.3 = (bf16[2,2048,128]{2,1,0:T(8,128)(2,1)S(1)}, bf16[2,2048,128]{2,1,0:T(8,128)(2,1)}, u32[]{:S(2)}) copy-start(bf16[2,2048,128]{2,1,0:T(8,128)(2,1)} %param.12) | copy-start | bytes 3145732
  41.0 10.9 %copy-start = (bf16[4,880,256]{2,1,0:T(8,128)(2,1)}, bf16[4,880,256]{2,1,0:T(8,128)(2,1)S(1)}, u32[]{:S(2)}) copy-start(bf16[4,880,256]{2,1,0:T(8,128)(2,1)S(1)} %pad_maximum_fusion.share_ref) | copy-start | bytes 5406724
  41.0 5.8 %collective-permute-start.10 = (bf16[4,880,256]{2,1,0:T(8,128)(2,1)S(1)}, bf16[4,880,256]{2,1,0:T(8,128)(2,1)S(1)}, u32[]{:S(2)}, u32[]{:S(2)}) collective-permute-start(bf16[4,880,256]{2,1,0:T(8,128)(2,1)S(1)} %pad_maximum_fusion.share_ref), channel_id=1, source_target_pairs={{0,1},{1,0},{2,3},{3,2},{4,5},{5,4},{6,7},{7,6},{8,9},{9,8},{10,11... | collective-permute-start | bytes 5406728 | tf_op jit(solution)/shard_map/ppermute | solution.py:495
  41.2 12.1 %collective-permute-start.11 = (bf16[768,256]{1,0:T(8,128)(2,1)S(1)}, bf16[768,256]{1,0:T(8,128)(2,1)S(1)}, u32[]{:S(2)}, u32[]{:S(2)}) collective-permute-start(bf16[768,256]{1,0:T(8,128)(2,1)S(1)} %constant_dynamic-update-slice_fusion.5), channel_id=1, source_target_pairs={{0,2},{1,3},{2,0},{3,1},{4,6},{5,7},{6,4},{7,5},{8,10},{9,11},{10,... | collective-permute-start | bytes 1179656 | tf_op jit(solution)/shard_map/ppermute | solution.py:495
  42.5 11.2 %collective-permute-start.12 = (bf16[768,256]{1,0:T(8,128)(2,1)S(1)}, bf16[768,256]{1,0:T(8,128)(2,1)S(1)}, u32[]{:S(2)}, u32[]{:S(2)}) collective-permute-start(bf16[768,256]{1,0:T(8,128)(2,1)S(1)} %constant_dynamic-update-slice_fusion.5), channel_id=1, source_target_pairs={{0,4},{1,5},{2,6},{3,7},{4,0},{5,1},{6,2},{7,3},{8,12},{9,13},{10,... | collective-permute-start | bytes 1179656 | tf_op jit(solution)/shard_map/ppermute | solution.py:495
  43.3 8.7 %collective-permute-start.13 = (bf16[256,256]{1,0:T(8,128)(2,1)S(1)}, bf16[256,256]{1,0:T(8,128)(2,1)S(1)}, u32[]{:S(2)}, u32[]{:S(2)}) collective-permute-start(bf16[256,256]{1,0:T(8,128)(2,1)S(1)} %pad_maximum_fusion.7), channel_id=1, source_target_pairs={{0,8},{8,0},{16,24},{24,16},{1,9},{9,1},{17,25},{25,17},{2,10},{10... | collective-permute-start | bytes 393224 | tf_op jit(solution)/shard_map/ppermute | solution.py:495
  46.8 6.4 %collective-permute-start.14 = (bf16[256,256]{1,0:T(8,128)(2,1)S(1)}, bf16[256,256]{1,0:T(8,128)(2,1)S(1)}, u32[]{:S(2)}, u32[]{:S(2)}) collective-permute-start(bf16[256,256]{1,0:T(8,128)(2,1)S(1)} %collective-permute-done.9), channel_id=1, source_target_pairs={{0,8},{8,0},{16,24},{24,16},{1,9},{9,1},{17,25},{25,17},{2,10},{10... | collective-permute-start | bytes 393224 | tf_op jit(solution)/shard_map/ppermute | solution.py:495
  46.9 5.1 %copy-start.1 = (bf16[4,880,256]{2,1,0:T(8,128)(2,1)}, bf16[4,880,256]{2,1,0:T(8,128)(2,1)S(1)}, u32[]{:S(2)}) copy-start(bf16[4,880,256]{2,1,0:T(8,128)(2,1)S(1)} %collective-permute-done.10.other_ref) | copy-start | bytes 5406724
  52.0 2.0 %copy-start.4 = (f32[7,8,2560]{2,1,0:T(8,128)}, f32[7,8,2560]{2,1,0:T(8,128)S(1)}, u32[]{:S(2)}) copy-start(f32[7,8,2560]{2,1,0:T(8,128)S(1)} %get-tuple-element.45.state_in) | copy-start | bytes 1720324
  53.9 6.5 %copy-start.5 = (bf16[4,768,256]{2,1,0:T(8,128)(2,1)}, bf16[4,768,256]{2,1,0:T(8,128)(2,1)S(1)}, u32[]{:S(2)}) copy-start(bf16[4,768,256]{2,1,0:T(8,128)(2,1)S(1)} %pad_maximum_fusion.1.late_share_ref) | copy-start | bytes 4718596
  54.0 6.5 %collective-permute-start.15 = (bf16[4,768,256]{2,1,0:T(8,128)(2,1)S(1)}, bf16[4,768,256]{2,1,0:T(8,128)(2,1)S(1)}, u32[]{:S(2)}, u32[]{:S(2)}) collective-permute-start(bf16[4,768,256]{2,1,0:T(8,128)(2,1)S(1)} %pad_maximum_fusion.1.late_share_ref), channel_id=1, source_target_pairs={{0,1},{1,0},{2,3},{3,2},{4,5},{5,4},{6,7},{7,6},{8,9},{9,8},{10,11... | collective-permute-start | bytes 4718600 | tf_op jit(solution)/shard_map/ppermute | solution.py:495
  54.0 22.0 %all-to-all-start = ((bf16[32,8,256]{2,1,0:T(8,128)(2,1)}), bf16[32,8,256]{2,1,0:T(8,128)(2,1)S(1)}, u32[]{:S(2)}, u32[]{:S(2)}) async-start(bf16[32,8,256]{2,1,0:T(8,128)(2,1)} %bitcast.19), calls=%async_computation | async-start | bytes 262144 | tf_op jit(solution)/shard_map/all_to_all | solution.py:490
  60.4 21.5 %copy-start.7 = (s32[4,2]{0,1:T(2,128)S(1)}, s32[4,2]{0,1:T(2,128)}, u32[]{:S(2)}) copy-start(s32[4,2]{0,1:T(2,128)} %param.9) | copy-start | bytes 100
  60.5 1.2 %copy-start.6 = (bf16[4,768,256]{2,1,0:T(8,128)(2,1)}, bf16[4,768,256]{2,1,0:T(8,128)(2,1)S(1)}, u32[]{:S(2)}) copy-start(bf16[4,768,256]{2,1,0:T(8,128)(2,1)S(1)} %collective-permute-done.15.late_other_ref) | copy-start | bytes 4718596
  76.1 21.4 %all-to-all-start.1 = ((bf16[32,8,1024]{2,1,0:T(8,128)(2,1)}), bf16[32,8,1024]{2,1,0:T(8,128)(2,1)S(1)}, u32[]{:S(2)}, u32[]{:S(2)}) async-start(bf16[32,8,1024]{2,1,0:T(8,128)(2,1)} %bitcast.39), calls=%async_computation.1 | async-start | bytes 1048576 | tf_op jit(solution)/shard_map/all_to_all | solution.py:490

commit v5 on v4

--- a/solution.py
+++ b/solution.py
@@ -375,6 +375,7 @@
     feature_count, term_width = groups * share, 2 * head_size
     late_shares = (late_share_ref, late_other_ref)
     late_copies = fill(1, key_ref, value_ref, late_shares, late_weight_ref, sems)
+    copies = fill(0, key_ref, value_ref, (share_ref, other_ref), weight_ref, sems)
     state_copy.wait()
     kept = []
     for place in range(4):
@@ -389,7 +390,6 @@
     late_gain = gain_ref.at[pl.ds(sections, sections)]
     for copy in late_copies:
         copy.wait()
-    copies = fill(0, key_ref, value_ref, (share_ref, other_ref), weight_ref, sems)
     forward_steps(
         first_ref[sections, :, :feature_count],
         late_gain,
@@ -653,7 +653,7 @@
             pltpu.SemaphoreType.DMA((1,)),
         ),
         48 << 20,
-        60 << 20,
+        58 << 20,
         1,
         0,
     )

time: 99.6 us -> 98.2 us (0.986)
  Pallas kernels: 21.1 us -> 19.7 us
    pallas_call x3, Pallas kernels: 21.1 us -> 19.7 us  [call(): pl.pallas_call(kernel, out_shape=outs, in_specs=[pl.BlockSpec(memory_spac...]
  transfers between devices with their start and end apart: 18 -> 18, of which waited for: 8 -> 8; matrix products, arithmetic and copies ran while one was open for 3% -> 3% of each run, Pallas kernels for 20% -> 19%
where the time goes in v5:
time: 98.2 us; the launch traced here: 97.7 us
  waiting for transfers between devices  36.2 us (37%)
  starting transfers between devices  34 us (35%)
  Pallas kernels  19.7 us (20%)
  other arithmetic  3.43 us (3%)
  local copies, waits for them, and re-layouts  3.38 us (3%)
  between operations  1 us (1%)
    ppermute x16, starting transfers between devices, swapped(): return lax.ppermute(value, axis, pairs)  21.7 us
    ppermute x16, waiting for transfers between devices, swapped(): return lax.ppermute(value, axis, pairs)  20.8 us
    pallas_call x3, Pallas kernels, call(): pl.pallas_call(kernel, out_shape=outs, in_specs=[pl.BlockSpec(memory_spac...  19.7 us
    all_to_all x2, waiting for transfers between devices, exchange(): lax.all_to_all(blocks, ('pipe', 'dp'), split_axis=0, concat_axis=0, tiled...  15.4 us
    all_to_all x2, starting transfers between devices, exchange(): lax.all_to_all(blocks, ('pipe', 'dp'), split_axis=0, concat_axis=0, tiled...  12.2 us
  transfers between devices with their start and end apart: 18, of which 8 were waited for; matrix products, arithmetic and copies ran while one was open for 3% of the time, Pallas kernels for 19%

profile of v5, /device:TPU:0, one launch (start us, length us, event | category | flops | bytes accessed | tf_op | source)
XLA Modules:
  0.0 97.7 jit_solution(2717460036929440169)
XLA Ops:
  0.7 0.7 fusion.8
  1.4 1.0 %dynamic-slice_bitcast_fusion = (bf16[256,128]{1,0:T(8,128)(2,1)S(1)}, bf16[256,128]{1,0:T(8,128)(2,1)S(1)}, bf16[256,128]{1,0:T(8,128)(2,1)S(1)}, bf16[256,128]...) fusion(bf16[2,2048,128]{2,1,0:T(8,128)(2,1)} %param.12, s32[]{:T(128)S(6)} %select_n.29, ...), kind=kLoop, calls=%fused_computation.12 | loop fusion | bytes 786440 | tf_op jit(solution)/shard_map/squeeze | solution.py:532
  2.5 0.8 constant_dynamic-slice_fusion.3
  3.3 3.1 %collective-permute-start = (bf16[280,256]{1,0:T(8,128)(2,1)S(1)}, bf16[280,256]{1,0:T(8,128)(2,1)S(1)}, u32[]{:S(2)}, u32[]{:S(2)}) collective-permute-start(bf16[280,256]{1,0:T(8,128)(2,1)S(1)} %get-tuple-element.65), channel_id=1, source_target_pairs={{0,8},{8,0},{16,24},{24,16},{1,9},{9,1},{17,25},{25,17},{2,10},{10... | collective-permute-start | bytes 430088 | tf_op jit(solution)/shard_map/ppermute | solution.py:495
  6.4 2.6 %collective-permute-start.1 = (bf16[280,256]{1,0:T(8,128)(2,1)S(1)}, bf16[280,256]{1,0:T(8,128)(2,1)S(1)}, u32[]{:S(2)}, u32[]{:S(2)}) collective-permute-start(bf16[280,256]{1,0:T(8,128)(2,1)S(1)} %get-tuple-element.64), channel_id=1, source_target_pairs={{0,16},{8,24},{16,0},{24,8},{1,17},{9,25},{17,1},{25,9},{2,18},{10... | collective-permute-start | bytes 430088 | tf_op jit(solution)/shard_map/ppermute | solution.py:495
  9.0 0.0 collective-permute-start.2
  9.0 0.8 dynamic-slice_convert_fusion.upstream_ref
  9.8 0.7 convert.19
  10.4 0.1 copy.16
  10.6 0.7 convert.18
  11.3 0.1 fusion.5
  11.4 0.7 collective-permute-done
  12.1 8.1 %collective-permute-done.1 = bf16[280,256]{1,0:T(8,128)(2,1)S(1)} collective-permute-done((bf16[280,256]{1,0:T(8,128)(2,1)S(1)}, bf16[280,256]{1,0:T(8,128)(2,1)S(1)}, u32[]{:S(2)}, u32[]{:S(2)}) %collective-permute-start.1) | collective-permute-done | bytes 143392 | tf_op jit(solution)/shard_map/ppermute | solution.py:495
  20.1 0.0 collective-permute-done.2
  20.2 1.6 %collective-permute-start.3 = (bf16[880,256]{1,0:T(8,128)(2,1)S(1)}, bf16[880,256]{1,0:T(8,128)(2,1)S(1)}, u32[]{:S(2)}, u32[]{:S(2)}) collective-permute-start(bf16[880,256]{1,0:T(8,128)(2,1)S(1)} %constant_dynamic-update-slice_fusion), channel_id=1, source_target_pairs={{0,2},{1,3},{2,0},{3,1},{4,6},{5,7},{6,4},{7,5},{8,10},{9,11},{10,... | collective-permute-start | bytes 1351688 | tf_op jit(solution)/shard_map/ppermute | solution.py:495
  21.8 1.5 %collective-permute-start.4 = (bf16[880,256]{1,0:T(8,128)(2,1)S(1)}, bf16[880,256]{1,0:T(8,128)(2,1)S(1)}, u32[]{:S(2)}, u32[]{:S(2)}) collective-permute-start(bf16[880,256]{1,0:T(8,128)(2,1)S(1)} %constant_dynamic-update-slice_fusion), channel_id=1, source_target_pairs={{0,4},{1,5},{2,6},{3,7},{4,0},{5,1},{6,2},{7,3},{8,12},{9,13},{10,... | collective-permute-start | bytes 1351688 | tf_op jit(solution)/shard_map/ppermute | solution.py:495
  23.3 0.5 collective-permute-start.5
  23.8 3.2 %collective-permute-start.7 = (bf16[256,256]{1,0:T(8,128)(2,1)S(1)}, bf16[256,256]{1,0:T(8,128)(2,1)S(1)}, u32[]{:S(2)}, u32[]{:S(2)}) collective-permute-start(bf16[256,256]{1,0:T(8,128)(2,1)S(1)} %pad_maximum_fusion.6), channel_id=1, source_target_pairs={{0,16},{8,24},{16,0},{24,8},{1,17},{9,25},{17,1},{25,9},{2,18},{10... | collective-permute-start | bytes 393224 | tf_op jit(solution)/shard_map/ppermute | solution.py:495
  27.0 0.0 collective-permute-start.6
  27.0 4.7 %collective-permute-done.7 = bf16[256,256]{1,0:T(8,128)(2,1)S(1)} collective-permute-done((bf16[256,256]{1,0:T(8,128)(2,1)S(1)}, bf16[256,256]{1,0:T(8,128)(2,1)S(1)}, u32[]{:S(2)}, u32[]{:S(2)}) %collective-permute-start.7) | collective-permute-done | bytes 131104 | tf_op jit(solution)/shard_map/ppermute | solution.py:495
  31.6 0.3 collective-permute-start.8
  31.9 1.6 %collective-permute-done.3 = bf16[880,256]{1,0:T(8,128)(2,1)S(1)} collective-permute-done((bf16[880,256]{1,0:T(8,128)(2,1)S(1)}, bf16[880,256]{1,0:T(8,128)(2,1)S(1)}, u32[]{:S(2)}, u32[]{:S(2)}) %collective-permute-start.3) | collective-permute-done | bytes 450592 | tf_op jit(solution)/shard_map/ppermute | solution.py:495
  33.6 3.2 %collective-permute-start.9 = (bf16[256,256]{1,0:T(8,128)(2,1)S(1)}, bf16[256,256]{1,0:T(8,128)(2,1)S(1)}, u32[]{:S(2)}, u32[]{:S(2)}) collective-permute-start(bf16[256,256]{1,0:T(8,128)(2,1)S(1)} %pad_maximum_fusion.7), channel_id=1, source_target_pairs={{0,16},{8,24},{16,0},{24,8},{1,17},{9,25},{17,1},{25,9},{2,18},{10... | collective-permute-start | bytes 393224 | tf_op jit(solution)/shard_map/ppermute | solution.py:495
  36.8 4.0 %collective-permute-done.4 = bf16[880,256]{1,0:T(8,128)(2,1)S(1)} collective-permute-done((bf16[880,256]{1,0:T(8,128)(2,1)S(1)}, bf16[880,256]{1,0:T(8,128)(2,1)S(1)}, u32[]{:S(2)}, u32[]{:S(2)}) %collective-permute-start.4) | collective-permute-done | bytes 450592 | tf_op jit(solution)/shard_map/ppermute | solution.py:495
  40.8 0.0 collective-permute-done.5
  40.8 0.0 copy-start.2
  40.8 0.2 pad_maximum_fusion.share_ref
  41.0 0.0 copy-start
  41.0 0.0 collective-permute-done.6
  41.0 0.0 collective-permute-done.8
  41.0 0.0 collective-permute-done.9
  41.0 0.1 collective-permute-start.10
  41.2 1.3 %collective-permute-start.11 = (bf16[768,256]{1,0:T(8,128)(2,1)S(1)}, bf16[768,256]{1,0:T(8,128)(2,1)S(1)}, u32[]{:S(2)}, u32[]{:S(2)}) collective-permute-start(bf16[768,256]{1,0:T(8,128)(2,1)S(1)} %constant_dynamic-update-slice_fusion.5), channel_id=1, source_target_pairs={{0,2},{1,3},{2,0},{3,1},{4,6},{5,7},{6,4},{7,5},{8,10},{9,11},{10,... | collective-permute-start | bytes 1179656 | tf_op jit(solution)/shard_map/ppermute | solution.py:495
  42.5 0.8 collective-permute-start.12
  43.3 3.5 %collective-permute-start.13 = (bf16[256,256]{1,0:T(8,128)(2,1)S(1)}, bf16[256,256]{1,0:T(8,128)(2,1)S(1)}, u32[]{:S(2)}, u32[]{:S(2)}) collective-permute-start(bf16[256,256]{1,0:T(8,128)(2,1)S(1)} %pad_maximum_fusion.7), channel_id=1, source_target_pairs={{0,8},{8,0},{16,24},{24,16},{1,9},{9,1},{17,25},{25,17},{2,10},{10... | collective-permute-start | bytes 393224 | tf_op jit(solution)/shard_map/ppermute | solution.py:495
  46.8 0.0 collective-permute-start.14
  46.9 0.0 collective-permute-done.10.other_ref
  46.9 0.0 copy-done.2
  46.9 0.0 copy-done.3
  46.9 5.1 %shard_map.94 = (f32[7,8,2560]{2,1,0:T(8,128)S(1)}, bf16[4,8,8,256]{3,2,1,0:T(8,128)(2,1)}) custom-call(f32[8,2048]{1,0:T(8,128)S(1)} %dynamic-slice_convert_fusion.upstream_ref, bf16[2,8,256,128]{3,2,1,0:T(8,128)(2,1)S(1)} %bitcast.34, bf16[2,8,256,128]{3,2,1,0:T(8,128)(2,1)S(1)} %bitcast.36, bf16[4,880,256]{2,1,0:T(8,128)(2,1)S(1)} %pad_maximum_fusion.share_ref, ...), custom_call_target="tpu_custom_call" | custom-call | bytes 18874368 | tf_op jit(solution)/shard_map/pallas_call | solution.py:475
  51.9 0.0 copy-done
  52.0 0.0 copy-done.1
  52.0 0.0 copy-start.4
  52.0 0.0 collective-permute-done.13
  52.0 1.2 %collective-permute-done.14 = bf16[256,256]{1,0:T(8,128)(2,1)S(1)} collective-permute-done((bf16[256,256]{1,0:T(8,128)(2,1)S(1)}, bf16[256,256]{1,0:T(8,128)(2,1)S(1)}, u32[]{:S(2)}, u32[]{:S(2)}) %collective-permute-start.14) | collective-permute-done | bytes 131104 | tf_op jit(solution)/shard_map/ppermute | solution.py:495
  53.2 0.0 collective-permute-done.11
  53.2 0.5 collective-permute-done.12
  53.7 0.2 pad_maximum_fusion.1.late_share_ref
  53.9 0.0 copy-done.4
  53.9 0.0 copy-start.5
  54.0 0.1 collective-permute-start.15
  54.0 6.4 %all-to-all-start = ((bf16[32,8,256]{2,1,0:T(8,128)(2,1)}), bf16[32,8,256]{2,1,0:T(8,128)(2,1)S(1)}, u32[]{:S(2)}, u32[]{:S(2)}) async-start(bf16[32,8,256]{2,1,0:T(8,128)(2,1)} %bitcast.19), calls=%async_computation | async-start | bytes 262144 | tf_op jit(solution)/shard_map/all_to_all | solution.py:490
  60.4 0.0 copy-start.7
  60.4 0.0 collective-permute-done.15.late_other_ref
  60.5 0.0 copy-done.5
  60.5 0.0 copy-start.6
  60.5 1.2 %copy-done.6 = bf16[4,768,256]{2,1,0:T(8,128)(2,1)} copy-done((bf16[4,768,256]{2,1,0:T(8,128)(2,1)}, bf16[4,768,256]{2,1,0:T(8,128)(2,1)S(1)}, u32[]{:S(2)}) %copy-start.6) | copy-done | bytes 1572888
  61.7 13.0 %shard_map.95 = bf16[4,8,8,1024]{3,2,1,0:T(8,128)(2,1)} custom-call(f32[7,8,2560]{2,1,0:T(8,128)} %copy-done.4, bf16[2,8,256,128]{3,2,1,0:T(8,128)(2,1)} %bitcast.33, bf16[2,8,256,128]{3,2,1,0:T(8,128)(2,1)} %bitcast.35, bf16[4,880,256]{2,1,0:T(8,128)(2,1)} %copy-done, bf16[4,880,256]{2,1,0:T(8,128)(2,1)} %copy-done.1, bf16[4,768,256]{2,1,0:T(8,128)(2,1)} %copy-done.5, ...), custom_call_target="tpu_custom_call" | custom-call | bytes 50331648 | tf_op jit(solution)/shard_map/pallas_call | solution.py:475
  74.7 0.0 all-to-all-done
  74.7 5.8 %all-to-all-start.1 = ((bf16[32,8,1024]{2,1,0:T(8,128)(2,1)}), bf16[32,8,1024]{2,1,0:T(8,128)(2,1)S(1)}, u32[]{:S(2)}, u32[]{:S(2)}) async-start(bf16[32,8,1024]{2,1,0:T(8,128)(2,1)} %bitcast.39), calls=%async_computation.1 | async-start | bytes 1048576 | tf_op jit(solution)/shard_map/all_to_all | solution.py:490
  80.6 0.0 copy-done.7
  80.6 0.1 copy.18.route_ref
  80.7 15.4 %all-to-all-done.1 = bf16[32,8,1024]{2,1,0:T(8,128)(2,1)S(1)} async-done(((bf16[32,8,1024]{2,1,0:T(8,128)(2,1)}), bf16[32,8,1024]{2,1,0:T(8,128)(2,1)S(1)}, u32[]{:S(2)}, u32[]{:S(2)}) %all-to-all-start.1) | async-done | bytes 524320 | tf_op jit(solution)/shard_map/all_to_all | solution.py:490
  96.1 1.6 %shard_map.96 = (bf16[32,512]{1,0:T(8,128)(2,1)}, f32[2,256,128]{2,1,0:T(8,128)}, f32[2,256,128]{2,1,0:T(8,128)}) custom-call(s32[4,2]{1,0:T(4,128)S(1)} %copy.18.route_ref, bf16[256,256]{1,0:T(8,128)(2,1)S(1)} %bitcast.38, bf16[256,1024]{1,0:T(8,128)(2,1)S(1)} %bitcast.37), custom_call_target="tpu_custom_call" | custom-call | tf_op jit(solution)/shard_map/pallas_call | solution.py:475
  (22 shorter events, 0.2 us)
Async XLA Ops:
  3.3 8.7 %collective-permute-start = (bf16[280,256]{1,0:T(8,128)(2,1)S(1)}, bf16[280,256]{1,0:T(8,128)(2,1)S(1)}, u32[]{:S(2)}, u32[]{:S(2)}) collective-permute-start(bf16[280,256]{1,0:T(8,128)(2,1)S(1)} %get-tuple-element.65), channel_id=1, source_target_pairs={{0,8},{8,0},{16,24},{24,16},{1,9},{9,1},{17,25},{25,17},{2,10},{10... | collective-permute-start | bytes 430088 | tf_op jit(solution)/shard_map/ppermute | solution.py:495
  6.4 13.7 %collective-permute-start.1 = (bf16[280,256]{1,0:T(8,128)(2,1)S(1)}, bf16[280,256]{1,0:T(8,128)(2,1)S(1)}, u32[]{:S(2)}, u32[]{:S(2)}) collective-permute-start(bf16[280,256]{1,0:T(8,128)(2,1)S(1)} %get-tuple-element.64), channel_id=1, source_target_pairs={{0,16},{8,24},{16,0},{24,8},{1,17},{9,25},{17,1},{25,9},{2,18},{10... | collective-permute-start | bytes 430088 | tf_op jit(solution)/shard_map/ppermute | solution.py:495
  9.0 11.2 %collective-permute-start.2 = (bf16[280,256]{1,0:T(8,128)(2,1)S(1)}, bf16[280,256]{1,0:T(8,128)(2,1)S(1)}, u32[]{:S(2)}, u32[]{:S(2)}) collective-permute-start(bf16[280,256]{1,0:T(8,128)(2,1)S(1)} %get-tuple-element.63), channel_id=1, source_target_pairs={{0,24},{8,16},{16,8},{24,0},{1,25},{9,17},{17,9},{25,1},{2,26},{10... | collective-permute-start | bytes 430088 | tf_op jit(solution)/shard_map/ppermute | solution.py:495
  20.2 13.3 %collective-permute-start.3 = (bf16[880,256]{1,0:T(8,128)(2,1)S(1)}, bf16[880,256]{1,0:T(8,128)(2,1)S(1)}, u32[]{:S(2)}, u32[]{:S(2)}) collective-permute-start(bf16[880,256]{1,0:T(8,128)(2,1)S(1)} %constant_dynamic-update-slice_fusion), channel_id=1, source_target_pairs={{0,2},{1,3},{2,0},{3,1},{4,6},{5,7},{6,4},{7,5},{8,10},{9,11},{10,... | collective-permute-start | bytes 1351688 | tf_op jit(solution)/shard_map/ppermute | solution.py:495
  21.8 19.0 %collective-permute-start.4 = (bf16[880,256]{1,0:T(8,128)(2,1)S(1)}, bf16[880,256]{1,0:T(8,128)(2,1)S(1)}, u32[]{:S(2)}, u32[]{:S(2)}) collective-permute-start(bf16[880,256]{1,0:T(8,128)(2,1)S(1)} %constant_dynamic-update-slice_fusion), channel_id=1, source_target_pairs={{0,4},{1,5},{2,6},{3,7},{4,0},{5,1},{6,2},{7,3},{8,12},{9,13},{10,... | collective-permute-start | bytes 1351688 | tf_op jit(solution)/shard_map/ppermute | solution.py:495
  23.3 17.4 %collective-permute-start.5 = (bf16[880,256]{1,0:T(8,128)(2,1)S(1)}, bf16[880,256]{1,0:T(8,128)(2,1)S(1)}, u32[]{:S(2)}, u32[]{:S(2)}) collective-permute-start(bf16[880,256]{1,0:T(8,128)(2,1)S(1)} %constant_dynamic-update-slice_fusion), channel_id=1, source_target_pairs={{0,6},{1,7},{2,4},{3,5},{4,2},{5,3},{6,0},{7,1},{8,14},{9,15},{10,... | collective-permute-start | bytes 1351688 | tf_op jit(solution)/shard_map/ppermute | solution.py:495
  23.8 7.9 %collective-permute-start.7 = (bf16[256,256]{1,0:T(8,128)(2,1)S(1)}, bf16[256,256]{1,0:T(8,128)(2,1)S(1)}, u32[]{:S(2)}, u32[]{:S(2)}) collective-permute-start(bf16[256,256]{1,0:T(8,128)(2,1)S(1)} %pad_maximum_fusion.6), channel_id=1, source_target_pairs={{0,16},{8,24},{16,0},{24,8},{1,17},{9,25},{17,1},{25,9},{2,18},{10... | collective-permute-start | bytes 393224 | tf_op jit(solution)/shard_map/ppermute | solution.py:495
  27.0 14.0 %collective-permute-start.6 = (bf16[256,256]{1,0:T(8,128)(2,1)S(1)}, bf16[256,256]{1,0:T(8,128)(2,1)S(1)}, u32[]{:S(2)}, u32[]{:S(2)}) collective-permute-start(bf16[256,256]{1,0:T(8,128)(2,1)S(1)} %pad_maximum_fusion.6), channel_id=1, source_target_pairs={{0,8},{8,0},{16,24},{24,16},{1,9},{9,1},{17,25},{25,17},{2,10},{10... | collective-permute-start | bytes 393224 | tf_op jit(solution)/shard_map/ppermute | solution.py:495
  31.6 9.4 %collective-permute-start.8 = (bf16[256,256]{1,0:T(8,128)(2,1)S(1)}, bf16[256,256]{1,0:T(8,128)(2,1)S(1)}, u32[]{:S(2)}, u32[]{:S(2)}) collective-permute-start(bf16[256,256]{1,0:T(8,128)(2,1)S(1)} %collective-permute-done.7), channel_id=1, source_target_pairs={{0,8},{8,0},{16,24},{24,16},{1,9},{9,1},{17,25},{25,17},{2,10},{10... | collective-permute-start | bytes 393224 | tf_op jit(solution)/shard_map/ppermute | solution.py:495
  33.6 7.4 %collective-permute-start.9 = (bf16[256,256]{1,0:T(8,128)(2,1)S(1)}, bf16[256,256]{1,0:T(8,128)(2,1)S(1)}, u32[]{:S(2)}, u32[]{:S(2)}) collective-permute-start(bf16[256,256]{1,0:T(8,128)(2,1)S(1)} %pad_maximum_fusion.7), channel_id=1, source_target_pairs={{0,16},{8,24},{16,0},{24,8},{1,17},{9,25},{17,1},{25,9},{2,18},{10... | collective-permute-start | bytes 393224 | tf_op jit(solution)/shard_map/ppermute | solution.py:495
  40.8 6.1 %copy-start.2 = (bf16[2,2048,128]{2,1,0:T(8,128)(2,1)S(1)}, bf16[2,2048,128]{2,1,0:T(8,128)(2,1)}, u32[]{:S(2)}) copy-start(bf16[2,2048,128]{2,1,0:T(8,128)(2,1)} %param.11) | copy-start | bytes 3145732
  40.8 6.1 %copy-start.3 = (bf16[2,2048,128]{2,1,0:T(8,128)(2,1)S(1)}, bf16[2,2048,128]{2,1,0:T(8,128)(2,1)}, u32[]{:S(2)}) copy-start(bf16[2,2048,128]{2,1,0:T(8,128)(2,1)} %param.12) | copy-start | bytes 3145732
  41.0 10.9 %copy-start = (bf16[4,880,256]{2,1,0:T(8,128)(2,1)}, bf16[4,880,256]{2,1,0:T(8,128)(2,1)S(1)}, u32[]{:S(2)}) copy-start(bf16[4,880,256]{2,1,0:T(8,128)(2,1)S(1)} %pad_maximum_fusion.share_ref) | copy-start | bytes 5406724
  41.0 5.8 %collective-permute-start.10 = (bf16[4,880,256]{2,1,0:T(8,128)(2,1)S(1)}, bf16[4,880,256]{2,1,0:T(8,128)(2,1)S(1)}, u32[]{:S(2)}, u32[]{:S(2)}) collective-permute-start(bf16[4,880,256]{2,1,0:T(8,128)(2,1)S(1)} %pad_maximum_fusion.share_ref), channel_id=1, source_target_pairs={{0,1},{1,0},{2,3},{3,2},{4,5},{5,4},{6,7},{7,6},{8,9},{9,8},{10,11... | collective-permute-start | bytes 5406728 | tf_op jit(solution)/shard_map/ppermute | solution.py:495
  41.2 12.1 %collective-permute-start.11 = (bf16[768,256]{1,0:T(8,128)(2,1)S(1)}, bf16[768,256]{1,0:T(8,128)(2,1)S(1)}, u32[]{:S(2)}, u32[]{:S(2)}) collective-permute-start(bf16[768,256]{1,0:T(8,128)(2,1)S(1)} %constant_dynamic-update-slice_fusion.5), channel_id=1, source_target_pairs={{0,2},{1,3},{2,0},{3,1},{4,6},{5,7},{6,4},{7,5},{8,10},{9,11},{10,... | collective-permute-start | bytes 1179656 | tf_op jit(solution)/shard_map/ppermute | solution.py:495
  42.5 11.2 %collective-permute-start.12 = (bf16[768,256]{1,0:T(8,128)(2,1)S(1)}, bf16[768,256]{1,0:T(8,128)(2,1)S(1)}, u32[]{:S(2)}, u32[]{:S(2)}) collective-permute-start(bf16[768,256]{1,0:T(8,128)(2,1)S(1)} %constant_dynamic-update-slice_fusion.5), channel_id=1, source_target_pairs={{0,4},{1,5},{2,6},{3,7},{4,0},{5,1},{6,2},{7,3},{8,12},{9,13},{10,... | collective-permute-start | bytes 1179656 | tf_op jit(solution)/shard_map/ppermute | solution.py:495
  43.3 8.7 %collective-permute-start.13 = (bf16[256,256]{1,0:T(8,128)(2,1)S(1)}, bf16[256,256]{1,0:T(8,128)(2,1)S(1)}, u32[]{:S(2)}, u32[]{:S(2)}) collective-permute-start(bf16[256,256]{1,0:T(8,128)(2,1)S(1)} %pad_maximum_fusion.7), channel_id=1, source_target_pairs={{0,8},{8,0},{16,24},{24,16},{1,9},{9,1},{17,25},{25,17},{2,10},{10... | collective-permute-start | bytes 393224 | tf_op jit(solution)/shard_map/ppermute | solution.py:495
  46.8 6.4 %collective-permute-start.14 = (bf16[256,256]{1,0:T(8,128)(2,1)S(1)}, bf16[256,256]{1,0:T(8,128)(2,1)S(1)}, u32[]{:S(2)}, u32[]{:S(2)}) collective-permute-start(bf16[256,256]{1,0:T(8,128)(2,1)S(1)} %collective-permute-done.9), channel_id=1, source_target_pairs={{0,8},{8,0},{16,24},{24,16},{1,9},{9,1},{17,25},{25,17},{2,10},{10... | collective-permute-start | bytes 393224 | tf_op jit(solution)/shard_map/ppermute | solution.py:495
  46.9 5.1 %copy-start.1 = (bf16[4,880,256]{2,1,0:T(8,128)(2,1)}, bf16[4,880,256]{2,1,0:T(8,128)(2,1)S(1)}, u32[]{:S(2)}) copy-start(bf16[4,880,256]{2,1,0:T(8,128)(2,1)S(1)} %collective-permute-done.10.other_ref) | copy-start | bytes 5406724
  52.0 2.0 %copy-start.4 = (f32[7,8,2560]{2,1,0:T(8,128)}, f32[7,8,2560]{2,1,0:T(8,128)S(1)}, u32[]{:S(2)}) copy-start(f32[7,8,2560]{2,1,0:T(8,128)S(1)} %get-tuple-element.45.state_in) | copy-start | bytes 1720324
  53.9 6.5 %copy-start.5 = (bf16[4,768,256]{2,1,0:T(8,128)(2,1)}, bf16[4,768,256]{2,1,0:T(8,128)(2,1)S(1)}, u32[]{:S(2)}) copy-start(bf16[4,768,256]{2,1,0:T(8,128)(2,1)S(1)} %pad_maximum_fusion.1.late_share_ref) | copy-start | bytes 4718596
  54.0 6.5 %collective-permute-start.15 = (bf16[4,768,256]{2,1,0:T(8,128)(2,1)S(1)}, bf16[4,768,256]{2,1,0:T(8,128)(2,1)S(1)}, u32[]{:S(2)}, u32[]{:S(2)}) collective-permute-start(bf16[4,768,256]{2,1,0:T(8,128)(2,1)S(1)} %pad_maximum_fusion.1.late_share_ref), channel_id=1, source_target_pairs={{0,1},{1,0},{2,3},{3,2},{4,5},{5,4},{6,7},{7,6},{8,9},{9,8},{10,11... | collective-permute-start | bytes 4718600 | tf_op jit(solution)/shard_map/ppermute | solution.py:495
  54.0 20.7 %all-to-all-start = ((bf16[32,8,256]{2,1,0:T(8,128)(2,1)}), bf16[32,8,256]{2,1,0:T(8,128)(2,1)S(1)}, u32[]{:S(2)}, u32[]{:S(2)}) async-start(bf16[32,8,256]{2,1,0:T(8,128)(2,1)} %bitcast.19), calls=%async_computation | async-start | bytes 262144 | tf_op jit(solution)/shard_map/all_to_all | solution.py:490
  60.4 20.1 %copy-start.7 = (s32[4,2]{0,1:T(2,128)S(1)}, s32[4,2]{0,1:T(2,128)}, u32[]{:S(2)}) copy-start(s32[4,2]{0,1:T(2,128)} %param.9) | copy-start | bytes 100
  60.5 1.2 %copy-start.6 = (bf16[4,768,256]{2,1,0:T(8,128)(2,1)}, bf16[4,768,256]{2,1,0:T(8,128)(2,1)S(1)}, u32[]{:S(2)}) copy-start(bf16[4,768,256]{2,1,0:T(8,128)(2,1)S(1)} %collective-permute-done.15.late_other_ref) | copy-start | bytes 4718596
  74.7 21.4 %all-to-all-start.1 = ((bf16[32,8,1024]{2,1,0:T(8,128)(2,1)}), bf16[32,8,1024]{2,1,0:T(8,128)(2,1)S(1)}, u32[]{:S(2)}, u32[]{:S(2)}) async-start(bf16[32,8,1024]{2,1,0:T(8,128)(2,1)} %bitcast.39), calls=%async_computation.1 | async-start | bytes 1048576 | tf_op jit(solution)/shard_map/all_to_all | solution.py:490

commit v6 on v5

--- a/solution.py
+++ b/solution.py
@@ -653,7 +653,7 @@
             pltpu.SemaphoreType.DMA((1,)),
         ),
         48 << 20,
-        58 << 20,
+        44 << 20,
         1,
         0,
     )

time: 98.2 us -> 102 us (1.039)
  local copies, waits for them, and re-layouts: 3.38 us -> 7.96 us
  Pallas kernels: 19.7 us -> 17.7 us
    unnamed x26 -> x32, local copies, waits for them, and re-layouts: 1.37 us -> 5.95 us
    pallas_call x3, Pallas kernels: 19.7 us -> 17.7 us  [call(): pl.pallas_call(kernel, out_shape=outs, in_specs=[pl.BlockSpec(memory_spac...]
  transfers between devices with their start and end apart: 18 -> 18, of which waited for: 8 -> 8; matrix products, arithmetic and copies ran while one was open for 3% -> 3% of each run, Pallas kernels for 19% -> 16%
where the time goes in v6:
time: 102 us; the launch traced here: 101 us
  waiting for transfers between devices  36.9 us (36%)
  starting transfers between devices  34 us (33%)
  Pallas kernels  17.7 us (17%)
  local copies, waits for them, and re-layouts  7.96 us (8%)
  other arithmetic  3.43 us (3%)
    ppermute x16, starting transfers between devices, swapped(): return lax.ppermute(value, axis, pairs)  21.7 us
    ppermute x16, waiting for transfers between devices, swapped(): return lax.ppermute(value, axis, pairs)  21.4 us
    pallas_call x3, Pallas kernels, call(): pl.pallas_call(kernel, out_shape=outs, in_specs=[pl.BlockSpec(memory_spac...  17.7 us
    all_to_all x2, waiting for transfers between devices, exchange(): lax.all_to_all(blocks, ('pipe', 'dp'), split_axis=0, concat_axis=0, tiled...  15.4 us
    all_to_all x2, starting transfers between devices, exchange(): lax.all_to_all(blocks, ('pipe', 'dp'), split_axis=0, concat_axis=0, tiled...  12.2 us
    unnamed x32, local copies, waits for them, and re-layouts  5.95 us
  transfers between devices with their start and end apart: 18, of which 8 were waited for; matrix products, arithmetic and copies ran while one was open for 3% of the time, Pallas kernels for 16%

profile of v6, /device:TPU:0, one launch (start us, length us, event | category | flops | bytes accessed | tf_op | source)
XLA Modules:
  0.0 100.9 jit_solution(354074053837839491)
XLA Ops:
  0.7 0.7 fusion.8
  1.4 1.0 %dynamic-slice_bitcast_fusion = (bf16[256,128]{1,0:T(8,128)(2,1)S(1)}, bf16[256,128]{1,0:T(8,128)(2,1)S(1)}, bf16[256,128]{1,0:T(8,128)(2,1)S(1)}, bf16[256,128]...) fusion(bf16[2,2048,128]{2,1,0:T(8,128)(2,1)} %param.12, s32[]{:T(128)S(6)} %select_n.29, ...), kind=kLoop, calls=%fused_computation.12 | loop fusion | bytes 786440 | tf_op jit(solution)/shard_map/squeeze | solution.py:532
  2.5 0.8 constant_dynamic-slice_fusion.3
  3.3 3.1 %collective-permute-start = (bf16[280,256]{1,0:T(8,128)(2,1)S(1)}, bf16[280,256]{1,0:T(8,128)(2,1)S(1)}, u32[]{:S(2)}, u32[]{:S(2)}) collective-permute-start(bf16[280,256]{1,0:T(8,128)(2,1)S(1)} %get-tuple-element.65), channel_id=1, source_target_pairs={{0,8},{8,0},{16,24},{24,16},{1,9},{9,1},{17,25},{25,17},{2,10},{10... | collective-permute-start | bytes 430088 | tf_op jit(solution)/shard_map/ppermute | solution.py:495
  6.4 2.6 %collective-permute-start.1 = (bf16[280,256]{1,0:T(8,128)(2,1)S(1)}, bf16[280,256]{1,0:T(8,128)(2,1)S(1)}, u32[]{:S(2)}, u32[]{:S(2)}) collective-permute-start(bf16[280,256]{1,0:T(8,128)(2,1)S(1)} %get-tuple-element.64), channel_id=1, source_target_pairs={{0,16},{8,24},{16,0},{24,8},{1,17},{9,25},{17,1},{25,9},{2,18},{10... | collective-permute-start | bytes 430088 | tf_op jit(solution)/shard_map/ppermute | solution.py:495
  9.0 0.0 collective-permute-start.2
  9.0 0.8 dynamic-slice_convert_fusion.upstream_ref
  9.8 0.7 convert.19
  10.4 0.1 copy.16
  10.6 0.7 convert.18
  11.3 0.1 fusion.5
  11.4 0.7 collective-permute-done
  12.1 8.1 %collective-permute-done.1 = bf16[280,256]{1,0:T(8,128)(2,1)S(1)} collective-permute-done((bf16[280,256]{1,0:T(8,128)(2,1)S(1)}, bf16[280,256]{1,0:T(8,128)(2,1)S(1)}, u32[]{:S(2)}, u32[]{:S(2)}) %collective-permute-start.1) | collective-permute-done | bytes 143392 | tf_op jit(solution)/shard_map/ppermute | solution.py:495
  20.1 0.0 collective-permute-done.2
  20.2 1.6 %collective-permute-start.3 = (bf16[880,256]{1,0:T(8,128)(2,1)S(1)}, bf16[880,256]{1,0:T(8,128)(2,1)S(1)}, u32[]{:S(2)}, u32[]{:S(2)}) collective-permute-start(bf16[880,256]{1,0:T(8,128)(2,1)S(1)} %constant_dynamic-update-slice_fusion), channel_id=1, source_target_pairs={{0,2},{1,3},{2,0},{3,1},{4,6},{5,7},{6,4},{7,5},{8,10},{9,11},{10,... | collective-permute-start | bytes 1351688 | tf_op jit(solution)/shard_map/ppermute | solution.py:495
  21.8 1.5 %collective-permute-start.4 = (bf16[880,256]{1,0:T(8,128)(2,1)S(1)}, bf16[880,256]{1,0:T(8,128)(2,1)S(1)}, u32[]{:S(2)}, u32[]{:S(2)}) collective-permute-start(bf16[880,256]{1,0:T(8,128)(2,1)S(1)} %constant_dynamic-update-slice_fusion), channel_id=1, source_target_pairs={{0,4},{1,5},{2,6},{3,7},{4,0},{5,1},{6,2},{7,3},{8,12},{9,13},{10,... | collective-permute-start | bytes 1351688 | tf_op jit(solution)/shard_map/ppermute | solution.py:495
  23.3 0.5 collective-permute-start.5
  23.8 3.2 %collective-permute-start.7 = (bf16[256,256]{1,0:T(8,128)(2,1)S(1)}, bf16[256,256]{1,0:T(8,128)(2,1)S(1)}, u32[]{:S(2)}, u32[]{:S(2)}) collective-permute-start(bf16[256,256]{1,0:T(8,128)(2,1)S(1)} %pad_maximum_fusion.6), channel_id=1, source_target_pairs={{0,16},{8,24},{16,0},{24,8},{1,17},{9,25},{17,1},{25,9},{2,18},{10... | collective-permute-start | bytes 393224 | tf_op jit(solution)/shard_map/ppermute | solution.py:495
  27.0 0.0 collective-permute-start.6
  27.0 4.7 %collective-permute-done.7 = bf16[256,256]{1,0:T(8,128)(2,1)S(1)} collective-permute-done((bf16[256,256]{1,0:T(8,128)(2,1)S(1)}, bf16[256,256]{1,0:T(8,128)(2,1)S(1)}, u32[]{:S(2)}, u32[]{:S(2)}) %collective-permute-start.7) | collective-permute-done | bytes 131104 | tf_op jit(solution)/shard_map/ppermute | solution.py:495
  31.6 0.3 collective-permute-start.8
  31.9 1.6 %collective-permute-done.3 = bf16[880,256]{1,0:T(8,128)(2,1)S(1)} collective-permute-done((bf16[880,256]{1,0:T(8,128)(2,1)S(1)}, bf16[880,256]{1,0:T(8,128)(2,1)S(1)}, u32[]{:S(2)}, u32[]{:S(2)}) %collective-permute-start.3) | collective-permute-done | bytes 450592 | tf_op jit(solution)/shard_map/ppermute | solution.py:495
  33.6 3.2 %collective-permute-start.9 = (bf16[256,256]{1,0:T(8,128)(2,1)S(1)}, bf16[256,256]{1,0:T(8,128)(2,1)S(1)}, u32[]{:S(2)}, u32[]{:S(2)}) collective-permute-start(bf16[256,256]{1,0:T(8,128)(2,1)S(1)} %pad_maximum_fusion.7), channel_id=1, source_target_pairs={{0,16},{8,24},{16,0},{24,8},{1,17},{9,25},{17,1},{25,9},{2,18},{10... | collective-permute-start | bytes 393224 | tf_op jit(solution)/shard_map/ppermute | solution.py:495
  36.8 4.0 %collective-permute-done.4 = bf16[880,256]{1,0:T(8,128)(2,1)S(1)} collective-permute-done((bf16[880,256]{1,0:T(8,128)(2,1)S(1)}, bf16[880,256]{1,0:T(8,128)(2,1)S(1)}, u32[]{:S(2)}, u32[]{:S(2)}) %collective-permute-start.4) | collective-permute-done | bytes 450592 | tf_op jit(solution)/shard_map/ppermute | solution.py:495
  40.8 0.0 collective-permute-done.5
  40.8 0.2 pad_maximum_fusion.share_ref
  41.0 0.0 collective-permute-done.6
  41.0 0.0 collective-permute-done.8
  41.0 0.0 collective-permute-done.9
  41.0 0.1 collective-permute-start.10
  41.2 1.3 %collective-permute-start.11 = (bf16[768,256]{1,0:T(8,128)(2,1)S(1)}, bf16[768,256]{1,0:T(8,128)(2,1)S(1)}, u32[]{:S(2)}, u32[]{:S(2)}) collective-permute-start(bf16[768,256]{1,0:T(8,128)(2,1)S(1)} %constant_dynamic-update-slice_fusion.5), channel_id=1, source_target_pairs={{0,2},{1,3},{2,0},{3,1},{4,6},{5,7},{6,4},{7,5},{8,10},{9,11},{10,... | collective-permute-start | bytes 1179656 | tf_op jit(solution)/shard_map/ppermute | solution.py:495
  42.5 0.8 collective-permute-start.12
  43.3 3.5 %collective-permute-start.13 = (bf16[256,256]{1,0:T(8,128)(2,1)S(1)}, bf16[256,256]{1,0:T(8,128)(2,1)S(1)}, u32[]{:S(2)}, u32[]{:S(2)}) collective-permute-start(bf16[256,256]{1,0:T(8,128)(2,1)S(1)} %pad_maximum_fusion.7), channel_id=1, source_target_pairs={{0,8},{8,0},{16,24},{24,16},{1,9},{9,1},{17,25},{25,17},{2,10},{10... | collective-permute-start | bytes 393224 | tf_op jit(solution)/shard_map/ppermute | solution.py:495
  46.8 0.0 collective-permute-start.14
  46.9 0.0 collective-permute-done.10.other_ref
  46.9 0.0 copy-done.2
  46.9 0.0 copy-done.4
  46.9 4.4 %shard_map.94 = (f32[7,8,2560]{2,1,0:T(8,128)S(1)}, bf16[4,8,8,256]{3,2,1,0:T(8,128)(2,1)S(1)}) custom-call(f32[8,2048]{1,0:T(8,128)S(1)} %dynamic-slice_convert_fusion.upstream_ref, bf16[2,8,256,128]{3,2,1,0:T(8,128)(2,1)S(1)} %bitcast.33, bf16[2,8,256,128]{3,2,1,0:T(8,128)(2,1)S(1)} %bitcast.35, bf16[4,880,256]{2,1,0:T(8,128)(2,1)S(1)} %pad_maximum_fusion.share_ref, ...), custom_call_target="tpu_custom_call" | custom-call | bytes 18874368 | tf_op jit(solution)/shard_map/pallas_call | solution.py:475
  51.3 0.0 copy-done
  51.3 0.0 copy-start.7
  51.3 0.0 copy-start.9
  51.3 0.0 collective-permute-done.13
  51.3 1.9 %collective-permute-done.14 = bf16[256,256]{1,0:T(8,128)(2,1)S(1)} collective-permute-done((bf16[256,256]{1,0:T(8,128)(2,1)S(1)}, bf16[256,256]{1,0:T(8,128)(2,1)S(1)}, u32[]{:S(2)}, u32[]{:S(2)}) %collective-permute-start.14) | collective-permute-done | bytes 131104 | tf_op jit(solution)/shard_map/ppermute | solution.py:495
  53.2 0.0 collective-permute-done.11
  53.2 0.5 collective-permute-done.12
  53.7 0.0 copy-done.7
  53.7 0.0 copy-done.9
  53.7 0.2 pad_maximum_fusion.1.late_share_ref
  53.9 0.1 collective-permute-start.15
  54.0 6.4 %all-to-all-start = ((bf16[32,8,256]{2,1,0:T(8,128)(2,1)}), bf16[32,8,256]{2,1,0:T(8,128)(2,1)S(1)}, u32[]{:S(2)}, u32[]{:S(2)}) async-start(bf16[32,8,256]{2,1,0:T(8,128)(2,1)} %bitcast.40), calls=%async_computation | async-start | bytes 262144 | tf_op jit(solution)/shard_map/all_to_all | solution.py:490
  60.4 0.0 collective-permute-done.15.late_other_ref
  60.4 0.0 copy-start.1
  60.4 1.5 %copy-done.1 = bf16[4,880,256]{2,1,0:T(8,128)(2,1)S(1)} copy-done((bf16[4,880,256]{2,1,0:T(8,128)(2,1)S(1)}, bf16[4,880,256]{2,1,0:T(8,128)(2,1)}, u32[]{:S(2)}) %copy-start.1) | copy-done | bytes 1802264
  61.9 1.2 %copy-done.3 = bf16[2,2048,128]{2,1,0:T(8,128)(2,1)S(1)} copy-done((bf16[2,2048,128]{2,1,0:T(8,128)(2,1)S(1)}, bf16[2,2048,128]{2,1,0:T(8,128)(2,1)}, u32[]{:S(2)}) %copy-start.3) | copy-done | bytes 1048600
  63.2 1.2 %copy-done.5 = bf16[2,2048,128]{2,1,0:T(8,128)(2,1)S(1)} copy-done((bf16[2,2048,128]{2,1,0:T(8,128)(2,1)S(1)}, bf16[2,2048,128]{2,1,0:T(8,128)(2,1)}, u32[]{:S(2)}) %copy-start.5) | copy-done | bytes 1048600
  64.4 1.1 %copy-done.8 = f32[7,8,2560]{2,1,0:T(8,128)S(1)} copy-done((f32[7,8,2560]{2,1,0:T(8,128)S(1)}, f32[7,8,2560]{2,1,0:T(8,128)}, u32[]{:S(2)}) %copy-start.8) | copy-done | bytes 573464
  65.4 11.6 %shard_map.95 = bf16[4,8,8,1024]{3,2,1,0:T(8,128)(2,1)S(1)} custom-call(f32[7,8,2560]{2,1,0:T(8,128)S(1)} %copy-done.8, bf16[2,8,256,128]{3,2,1,0:T(8,128)(2,1)S(1)} %bitcast.34, bf16[2,8,256,128]{3,2,1,0:T(8,128)(2,1)S(1)} %bitcast.36, bf16[4,880,256]{2,1,0:T(8,128)(2,1)S(1)} %pad_maximum_fusion.share_ref, bf16[4,880,256]{2,1,0:T(8,128)(2,1)S(1)} %copy-done.1, ...), custom_call_target="tpu_custom_call" | custom-call | bytes 50331648 | tf_op jit(solution)/shard_map/pallas_call | solution.py:475
  77.1 0.0 copy-start.6
  77.1 0.8 copy-done.6
  77.9 0.0 all-to-all-done
  77.9 5.8 %all-to-all-start.1 = ((bf16[32,8,1024]{2,1,0:T(8,128)(2,1)}), bf16[32,8,1024]{2,1,0:T(8,128)(2,1)S(1)}, u32[]{:S(2)}, u32[]{:S(2)}) async-start(bf16[32,8,1024]{2,1,0:T(8,128)(2,1)} %bitcast.37), calls=%async_computation.1 | async-start | bytes 1048576 | tf_op jit(solution)/shard_map/all_to_all | solution.py:490
  83.7 0.1 copy.18.route_ref
  83.8 15.4 %all-to-all-done.1 = bf16[32,8,1024]{2,1,0:T(8,128)(2,1)S(1)} async-done(((bf16[32,8,1024]{2,1,0:T(8,128)(2,1)}), bf16[32,8,1024]{2,1,0:T(8,128)(2,1)S(1)}, u32[]{:S(2)}, u32[]{:S(2)}) %all-to-all-start.1) | async-done | bytes 524320 | tf_op jit(solution)/shard_map/all_to_all | solution.py:490
  99.3 1.6 %shard_map.96 = (bf16[32,512]{1,0:T(8,128)(2,1)}, f32[2,256,128]{2,1,0:T(8,128)}, f32[2,256,128]{2,1,0:T(8,128)}) custom-call(s32[4,2]{1,0:T(4,128)S(1)} %copy.18.route_ref, bf16[256,256]{1,0:T(8,128)(2,1)S(1)} %bitcast.39, bf16[256,1024]{1,0:T(8,128)(2,1)S(1)} %bitcast.38), custom_call_target="tpu_custom_call" | custom-call | tf_op jit(solution)/shard_map/pallas_call | solution.py:475
  (28 shorter events, 0.2 us)
Async XLA Ops:
  3.3 8.7 %collective-permute-start = (bf16[280,256]{1,0:T(8,128)(2,1)S(1)}, bf16[280,256]{1,0:T(8,128)(2,1)S(1)}, u32[]{:S(2)}, u32[]{:S(2)}) collective-permute-start(bf16[280,256]{1,0:T(8,128)(2,1)S(1)} %get-tuple-element.65), channel_id=1, source_target_pairs={{0,8},{8,0},{16,24},{24,16},{1,9},{9,1},{17,25},{25,17},{2,10},{10... | collective-permute-start | bytes 430088 | tf_op jit(solution)/shard_map/ppermute | solution.py:495
  6.4 13.7 %collective-permute-start.1 = (bf16[280,256]{1,0:T(8,128)(2,1)S(1)}, bf16[280,256]{1,0:T(8,128)(2,1)S(1)}, u32[]{:S(2)}, u32[]{:S(2)}) collective-permute-start(bf16[280,256]{1,0:T(8,128)(2,1)S(1)} %get-tuple-element.64), channel_id=1, source_target_pairs={{0,16},{8,24},{16,0},{24,8},{1,17},{9,25},{17,1},{25,9},{2,18},{10... | collective-permute-start | bytes 430088 | tf_op jit(solution)/shard_map/ppermute | solution.py:495
  9.0 11.2 %collective-permute-start.2 = (bf16[280,256]{1,0:T(8,128)(2,1)S(1)}, bf16[280,256]{1,0:T(8,128)(2,1)S(1)}, u32[]{:S(2)}, u32[]{:S(2)}) collective-permute-start(bf16[280,256]{1,0:T(8,128)(2,1)S(1)} %get-tuple-element.63), channel_id=1, source_target_pairs={{0,24},{8,16},{16,8},{24,0},{1,25},{9,17},{17,9},{25,1},{2,26},{10... | collective-permute-start | bytes 430088 | tf_op jit(solution)/shard_map/ppermute | solution.py:495
  20.2 13.3 %collective-permute-start.3 = (bf16[880,256]{1,0:T(8,128)(2,1)S(1)}, bf16[880,256]{1,0:T(8,128)(2,1)S(1)}, u32[]{:S(2)}, u32[]{:S(2)}) collective-permute-start(bf16[880,256]{1,0:T(8,128)(2,1)S(1)} %constant_dynamic-update-slice_fusion), channel_id=1, source_target_pairs={{0,2},{1,3},{2,0},{3,1},{4,6},{5,7},{6,4},{7,5},{8,10},{9,11},{10,... | collective-permute-start | bytes 1351688 | tf_op jit(solution)/shard_map/ppermute | solution.py:495
  21.8 19.0 %collective-permute-start.4 = (bf16[880,256]{1,0:T(8,128)(2,1)S(1)}, bf16[880,256]{1,0:T(8,128)(2,1)S(1)}, u32[]{:S(2)}, u32[]{:S(2)}) collective-permute-start(bf16[880,256]{1,0:T(8,128)(2,1)S(1)} %constant_dynamic-update-slice_fusion), channel_id=1, source_target_pairs={{0,4},{1,5},{2,6},{3,7},{4,0},{5,1},{6,2},{7,3},{8,12},{9,13},{10,... | collective-permute-start | bytes 1351688 | tf_op jit(solution)/shard_map/ppermute | solution.py:495
  23.3 17.4 %collective-permute-start.5 = (bf16[880,256]{1,0:T(8,128)(2,1)S(1)}, bf16[880,256]{1,0:T(8,128)(2,1)S(1)}, u32[]{:S(2)}, u32[]{:S(2)}) collective-permute-start(bf16[880,256]{1,0:T(8,128)(2,1)S(1)} %constant_dynamic-update-slice_fusion), channel_id=1, source_target_pairs={{0,6},{1,7},{2,4},{3,5},{4,2},{5,3},{6,0},{7,1},{8,14},{9,15},{10,... | collective-permute-start | bytes 1351688 | tf_op jit(solution)/shard_map/ppermute | solution.py:495
  23.8 7.9 %collective-permute-start.7 = (bf16[256,256]{1,0:T(8,128)(2,1)S(1)}, bf16[256,256]{1,0:T(8,128)(2,1)S(1)}, u32[]{:S(2)}, u32[]{:S(2)}) collective-permute-start(bf16[256,256]{1,0:T(8,128)(2,1)S(1)} %pad_maximum_fusion.6), channel_id=1, source_target_pairs={{0,16},{8,24},{16,0},{24,8},{1,17},{9,25},{17,1},{25,9},{2,18},{10... | collective-permute-start | bytes 393224 | tf_op jit(solution)/shard_map/ppermute | solution.py:495
  27.0 14.0 %collective-permute-start.6 = (bf16[256,256]{1,0:T(8,128)(2,1)S(1)}, bf16[256,256]{1,0:T(8,128)(2,1)S(1)}, u32[]{:S(2)}, u32[]{:S(2)}) collective-permute-start(bf16[256,256]{1,0:T(8,128)(2,1)S(1)} %pad_maximum_fusion.6), channel_id=1, source_target_pairs={{0,8},{8,0},{16,24},{24,16},{1,9},{9,1},{17,25},{25,17},{2,10},{10... | collective-permute-start | bytes 393224 | tf_op jit(solution)/shard_map/ppermute | solution.py:495
  31.6 9.4 %collective-permute-start.8 = (bf16[256,256]{1,0:T(8,128)(2,1)S(1)}, bf16[256,256]{1,0:T(8,128)(2,1)S(1)}, u32[]{:S(2)}, u32[]{:S(2)}) collective-permute-start(bf16[256,256]{1,0:T(8,128)(2,1)S(1)} %collective-permute-done.7), channel_id=1, source_target_pairs={{0,8},{8,0},{16,24},{24,16},{1,9},{9,1},{17,25},{25,17},{2,10},{10... | collective-permute-start | bytes 393224 | tf_op jit(solution)/shard_map/ppermute | solution.py:495
  33.6 7.4 %collective-permute-start.9 = (bf16[256,256]{1,0:T(8,128)(2,1)S(1)}, bf16[256,256]{1,0:T(8,128)(2,1)S(1)}, u32[]{:S(2)}, u32[]{:S(2)}) collective-permute-start(bf16[256,256]{1,0:T(8,128)(2,1)S(1)} %pad_maximum_fusion.7), channel_id=1, source_target_pairs={{0,16},{8,24},{16,0},{24,8},{1,17},{9,25},{17,1},{25,9},{2,18},{10... | collective-permute-start | bytes 393224 | tf_op jit(solution)/shard_map/ppermute | solution.py:495
  40.8 6.1 %copy-start.2 = (bf16[2,2048,128]{2,1,0:T(8,128)(2,1)S(1)}, bf16[2,2048,128]{2,1,0:T(8,128)(2,1)}, u32[]{:S(2)}) copy-start(bf16[2,2048,128]{2,1,0:T(8,128)(2,1)} %param.11) | copy-start | bytes 3145732
  40.8 6.1 %copy-start.4 = (bf16[2,2048,128]{2,1,0:T(8,128)(2,1)S(1)}, bf16[2,2048,128]{2,1,0:T(8,128)(2,1)}, u32[]{:S(2)}) copy-start(bf16[2,2048,128]{2,1,0:T(8,128)(2,1)} %param.12) | copy-start | bytes 3145732
  41.0 5.8 %collective-permute-start.10 = (bf16[4,880,256]{2,1,0:T(8,128)(2,1)S(1)}, bf16[4,880,256]{2,1,0:T(8,128)(2,1)S(1)}, u32[]{:S(2)}, u32[]{:S(2)}) collective-permute-start(bf16[4,880,256]{2,1,0:T(8,128)(2,1)S(1)} %pad_maximum_fusion.share_ref), channel_id=1, source_target_pairs={{0,1},{1,0},{2,3},{3,2},{4,5},{5,4},{6,7},{7,6},{8,9},{9,8},{10,11... | collective-permute-start | bytes 5406728 | tf_op jit(solution)/shard_map/ppermute | solution.py:495
  41.2 12.1 %collective-permute-start.11 = (bf16[768,256]{1,0:T(8,128)(2,1)S(1)}, bf16[768,256]{1,0:T(8,128)(2,1)S(1)}, u32[]{:S(2)}, u32[]{:S(2)}) collective-permute-start(bf16[768,256]{1,0:T(8,128)(2,1)S(1)} %constant_dynamic-update-slice_fusion.5), channel_id=1, source_target_pairs={{0,2},{1,3},{2,0},{3,1},{4,6},{5,7},{6,4},{7,5},{8,10},{9,11},{10,... | collective-permute-start | bytes 1179656 | tf_op jit(solution)/shard_map/ppermute | solution.py:495
  42.5 11.2 %collective-permute-start.12 = (bf16[768,256]{1,0:T(8,128)(2,1)S(1)}, bf16[768,256]{1,0:T(8,128)(2,1)S(1)}, u32[]{:S(2)}, u32[]{:S(2)}) collective-permute-start(bf16[768,256]{1,0:T(8,128)(2,1)S(1)} %constant_dynamic-update-slice_fusion.5), channel_id=1, source_target_pairs={{0,4},{1,5},{2,6},{3,7},{4,0},{5,1},{6,2},{7,3},{8,12},{9,13},{10,... | collective-permute-start | bytes 1179656 | tf_op jit(solution)/shard_map/ppermute | solution.py:495
  43.3 8.0 %collective-permute-start.13 = (bf16[256,256]{1,0:T(8,128)(2,1)S(1)}, bf16[256,256]{1,0:T(8,128)(2,1)S(1)}, u32[]{:S(2)}, u32[]{:S(2)}) collective-permute-start(bf16[256,256]{1,0:T(8,128)(2,1)S(1)} %pad_maximum_fusion.7), channel_id=1, source_target_pairs={{0,8},{8,0},{16,24},{24,16},{1,9},{9,1},{17,25},{25,17},{2,10},{10... | collective-permute-start | bytes 393224 | tf_op jit(solution)/shard_map/ppermute | solution.py:495
  46.8 6.4 %collective-permute-start.14 = (bf16[256,256]{1,0:T(8,128)(2,1)S(1)}, bf16[256,256]{1,0:T(8,128)(2,1)S(1)}, u32[]{:S(2)}, u32[]{:S(2)}) collective-permute-start(bf16[256,256]{1,0:T(8,128)(2,1)S(1)} %collective-permute-done.9), channel_id=1, source_target_pairs={{0,8},{8,0},{16,24},{24,16},{1,9},{9,1},{17,25},{25,17},{2,10},{10... | collective-permute-start | bytes 393224 | tf_op jit(solution)/shard_map/ppermute | solution.py:495
  46.9 4.4 %copy-start = (bf16[4,880,256]{2,1,0:T(8,128)(2,1)}, bf16[4,880,256]{2,1,0:T(8,128)(2,1)S(1)}, u32[]{:S(2)}) copy-start(bf16[4,880,256]{2,1,0:T(8,128)(2,1)S(1)} %collective-permute-done.10.other_ref) | copy-start | bytes 5406724
  51.3 2.4 %copy-start.7 = (f32[7,8,2560]{2,1,0:T(8,128)}, f32[7,8,2560]{2,1,0:T(8,128)S(1)}, u32[]{:S(2)}) copy-start(f32[7,8,2560]{2,1,0:T(8,128)S(1)} %get-tuple-element.45.state_in) | copy-start | bytes 1720324
  51.3 2.4 %copy-start.9 = (bf16[4,8,8,256]{3,2,1,0:T(8,128)(2,1)}, bf16[4,8,8,256]{3,2,1,0:T(8,128)(2,1)S(1)}, u32[]{:S(2)}) copy-start(bf16[4,8,8,256]{3,2,1,0:T(8,128)(2,1)S(1)} %get-tuple-element.54) | copy-start | bytes 393220
  53.9 6.5 %collective-permute-start.15 = (bf16[4,768,256]{2,1,0:T(8,128)(2,1)S(1)}, bf16[4,768,256]{2,1,0:T(8,128)(2,1)}, u32[]{:S(2)}, u32[]{:S(2)}) collective-permute-start(bf16[4,768,256]{2,1,0:T(8,128)(2,1)S(1)} %pad_maximum_fusion.1.late_share_ref), channel_id=1, source_target_pairs={{0,1},{1,0},{2,3},{3,2},{4,5},{5,4},{6,7},{7,6},{8,9},{9,8},{10,11... | collective-permute-start | bytes 4718600 | tf_op jit(solution)/shard_map/ppermute | solution.py:495
  54.0 23.8 %all-to-all-start = ((bf16[32,8,256]{2,1,0:T(8,128)(2,1)}), bf16[32,8,256]{2,1,0:T(8,128)(2,1)S(1)}, u32[]{:S(2)}, u32[]{:S(2)}) async-start(bf16[32,8,256]{2,1,0:T(8,128)(2,1)} %bitcast.40), calls=%async_computation | async-start | bytes 262144 | tf_op jit(solution)/shard_map/all_to_all | solution.py:490
  60.4 1.5 %copy-start.1 = (bf16[4,880,256]{2,1,0:T(8,128)(2,1)S(1)}, bf16[4,880,256]{2,1,0:T(8,128)(2,1)}, u32[]{:S(2)}) copy-start(bf16[4,880,256]{2,1,0:T(8,128)(2,1)} %copy-done) | copy-start | bytes 5406724
  61.9 1.2 %copy-start.3 = (bf16[2,2048,128]{2,1,0:T(8,128)(2,1)S(1)}, bf16[2,2048,128]{2,1,0:T(8,128)(2,1)}, u32[]{:S(2)}) copy-start(bf16[2,2048,128]{2,1,0:T(8,128)(2,1)} %param.11) | copy-start | bytes 3145732
  63.1 1.2 %copy-start.5 = (bf16[2,2048,128]{2,1,0:T(8,128)(2,1)S(1)}, bf16[2,2048,128]{2,1,0:T(8,128)(2,1)}, u32[]{:S(2)}) copy-start(bf16[2,2048,128]{2,1,0:T(8,128)(2,1)} %param.12) | copy-start | bytes 3145732
  64.4 1.1 %copy-start.8 = (f32[7,8,2560]{2,1,0:T(8,128)S(1)}, f32[7,8,2560]{2,1,0:T(8,128)}, u32[]{:S(2)}) copy-start(f32[7,8,2560]{2,1,0:T(8,128)} %copy-done.7) | copy-start | bytes 1720324
  65.4 18.3 %copy-start.10 = (s32[4,2]{0,1:T(2,128)S(1)}, s32[4,2]{0,1:T(2,128)}, u32[]{:S(2)}) copy-start(s32[4,2]{0,1:T(2,128)} %param.9) | copy-start | bytes 100
  77.1 0.8 copy-start.6
  77.9 21.4 %all-to-all-start.1 = ((bf16[32,8,1024]{2,1,0:T(8,128)(2,1)}), bf16[32,8,1024]{2,1,0:T(8,128)(2,1)S(1)}, u32[]{:S(2)}, u32[]{:S(2)}) async-start(bf16[32,8,1024]{2,1,0:T(8,128)(2,1)} %bitcast.37), calls=%async_computation.1 | async-start | bytes 1048576 | tf_op jit(solution)/shard_map/all_to_all | solution.py:490

commit v7 on v6

--- a/solution.py
+++ b/solution.py
@@ -527,10 +527,10 @@
 
     line_width = 2 * head_size
 
-    def share_of(turn, owner):
+    def share_of(turn, owner, arrays):
         parts = [
             lax.dynamic_slice(array, (turn, owner * share, 0), (1, share, head_size))[0]
-            for array in (key_weight, value_weight)
+            for array in arrays
         ]
         return jnp.concatenate(parts, axis=1)
 
@@ -547,7 +547,7 @@
         terms.astype(jnp.bfloat16), ((0, GAIN_LINES - 6), (0, line_width - share))
     )
 
-    first = share_of(0, group_index)
+    first = share_of(0, group_index, (key_weight, value_weight))
     came = [
         swapped(jnp.concatenate([first, own_rows(mask), terms], axis=0), "pipe", mask)
         for mask in range(1, sections)
@@ -560,6 +560,7 @@
     tags, own_tail, upstream = lax.optimization_barrier(
         (tags, jnp.concatenate([own_rows(0), terms], axis=0), upstream)
     )
+    _, *arrays = lax.optimization_barrier((tags, key_weight, value_weight))
     column = jnp.concatenate(
         [piece[:share] for piece in came]
         + [own_tail]
@@ -567,9 +568,9 @@
         + [tags],
         axis=0,
     )
-    distant = share_of(1, lax.bitwise_xor(group_index, groups - 2))
+    distant = share_of(1, lax.bitwise_xor(group_index, groups - 2), arrays)
     column, second, distant = lax.optimization_barrier(
-        (column, share_of(1, group_index), distant)
+        (column, share_of(1, group_index, arrays), distant)
     )
     chips = range(1, groups // 2)
     plane = jnp.stack([column] + [swapped(column, "dp", 2 * chip) for chip in chips])
@@ -653,7 +654,7 @@
             pltpu.SemaphoreType.DMA((1,)),
         ),
         48 << 20,
-        44 << 20,
+        50 << 20,
         1,
         0,
     )

time: 102 us -> 97.8 us (0.959)
  local copies, waits for them, and re-layouts: 7.96 us -> 3 us
  Pallas kernels: 17.7 us -> 19.5 us
  waiting for transfers between devices: 36.9 us -> 35.3 us
  other arithmetic: 3.43 us -> 4.59 us
    unnamed x32 -> x22, local copies, waits for them, and re-layouts: 5.95 us -> 0.19 us
    pallas_call x3, Pallas kernels: 17.7 us -> 19.5 us  [call(): pl.pallas_call(kernel, out_shape=outs, in_specs=[pl.BlockSpec(memory_spac...]
    ppermute x16, waiting for transfers between devices: 21.4 us -> 19.8 us  [swapped(): return lax.ppermute(value, axis, pairs)]
    another operation x2, other arithmetic: 0.23 us -> 1.39 us  [body(): plane = jnp.stack(planes + [jnp.concatenate(far, axis=0)])]
  transfers between devices with their start and end apart: 18 -> 18, of which waited for: 8 -> 7; matrix products, arithmetic and copies ran while one was open for 3% -> 4% of each run, Pallas kernels for 16% -> 18%
where the time goes in v7:
time: 97.8 us; the launch traced here: 97.2 us
  waiting for transfers between devices  35.3 us (36%)
  starting transfers between devices  33.9 us (35%)
  Pallas kernels  19.5 us (20%)
  other arithmetic  4.59 us (5%)
  local copies, waits for them, and re-layouts  3 us (3%)
  between operations  0.98 us (1%)
    ppermute x16, starting transfers between devices, swapped(): return lax.ppermute(value, axis, pairs)  21.7 us
    ppermute x16, waiting for transfers between devices, swapped(): return lax.ppermute(value, axis, pairs)  19.8 us
    pallas_call x3, Pallas kernels, call(): pl.pallas_call(kernel, out_shape=outs, in_specs=[pl.BlockSpec(memory_spac...  19.5 us
    all_to_all x2, waiting for transfers between devices, exchange(): lax.all_to_all(blocks, ('pipe', 'dp'), split_axis=0, concat_axis=0, tiled...  15.4 us
    all_to_all x2, starting transfers between devices, exchange(): lax.all_to_all(blocks, ('pipe', 'dp'), split_axis=0, concat_axis=0, tiled...  12.2 us
  transfers between devices with their start and end apart: 18, of which 7 were waited for; matrix products, arithmetic and copies ran while one was open for 4% of the time, Pallas kernels for 18%

profile of v7, /device:TPU:0, one launch (start us, length us, event | category | flops | bytes accessed | tf_op | source)
XLA Modules:
  0.0 97.2 jit_solution(10637321030795224338)
XLA Ops:
  0.6 0.7 fusion.8
  1.4 0.9 dynamic-slice_bitcast_fusion.4
  2.3 0.8 constant_dynamic-slice_fusion.3
  3.2 3.1 %collective-permute-start = (bf16[280,256]{1,0:T(8,128)(2,1)S(1)}, bf16[280,256]{1,0:T(8,128)(2,1)S(1)}, u32[]{:S(2)}, u32[]{:S(2)}) collective-permute-start(bf16[280,256]{1,0:T(8,128)(2,1)S(1)} %get-tuple-element.67), channel_id=1, source_target_pairs={{0,8},{8,0},{16,24},{24,16},{1,9},{9,1},{17,25},{25,17},{2,10},{10... | collective-permute-start | bytes 430088 | tf_op jit(solution)/shard_map/ppermute | solution.py:495
  6.2 2.6 %collective-permute-start.1 = (bf16[280,256]{1,0:T(8,128)(2,1)S(1)}, bf16[280,256]{1,0:T(8,128)(2,1)S(1)}, u32[]{:S(2)}, u32[]{:S(2)}) collective-permute-start(bf16[280,256]{1,0:T(8,128)(2,1)S(1)} %get-tuple-element.66), channel_id=1, source_target_pairs={{0,16},{8,24},{16,0},{24,8},{1,17},{9,25},{17,1},{25,9},{2,18},{10... | collective-permute-start | bytes 430088 | tf_op jit(solution)/shard_map/ppermute | solution.py:495
  8.8 0.0 collective-permute-start.2
  8.8 0.8 dynamic-slice_convert_fusion.upstream_ref
  9.6 0.7 convert.19
  10.3 0.1 copy.16
  10.4 0.7 convert.18
  11.1 0.1 fusion.5
  11.2 1.0 dynamic-slice_bitcast_fusion
  12.2 0.0 collective-permute-done
  12.2 7.8 %collective-permute-done.1 = bf16[280,256]{1,0:T(8,128)(2,1)S(1)} collective-permute-done((bf16[280,256]{1,0:T(8,128)(2,1)S(1)}, bf16[280,256]{1,0:T(8,128)(2,1)S(1)}, u32[]{:S(2)}, u32[]{:S(2)}) %collective-permute-start.1) | collective-permute-done | bytes 143392 | tf_op jit(solution)/shard_map/ppermute | solution.py:495
  20.0 0.0 collective-permute-done.2
  20.1 1.6 %collective-permute-start.3 = (bf16[880,256]{1,0:T(8,128)(2,1)S(1)}, bf16[880,256]{1,0:T(8,128)(2,1)S(1)}, u32[]{:S(2)}, u32[]{:S(2)}) collective-permute-start(bf16[880,256]{1,0:T(8,128)(2,1)S(1)} %constant_dynamic-update-slice_fusion), channel_id=1, source_target_pairs={{0,2},{1,3},{2,0},{3,1},{4,6},{5,7},{6,4},{7,5},{8,10},{9,11},{10,... | collective-permute-start | bytes 1351688 | tf_op jit(solution)/shard_map/ppermute | solution.py:495
  21.6 1.5 %collective-permute-start.4 = (bf16[880,256]{1,0:T(8,128)(2,1)S(1)}, bf16[880,256]{1,0:T(8,128)(2,1)S(1)}, u32[]{:S(2)}, u32[]{:S(2)}) collective-permute-start(bf16[880,256]{1,0:T(8,128)(2,1)S(1)} %constant_dynamic-update-slice_fusion), channel_id=1, source_target_pairs={{0,4},{1,5},{2,6},{3,7},{4,0},{5,1},{6,2},{7,3},{8,12},{9,13},{10,... | collective-permute-start | bytes 1351688 | tf_op jit(solution)/shard_map/ppermute | solution.py:495
  23.2 0.5 collective-permute-start.5
  23.6 3.2 %collective-permute-start.7 = (bf16[256,256]{1,0:T(8,128)(2,1)S(1)}, bf16[256,256]{1,0:T(8,128)(2,1)S(1)}, u32[]{:S(2)}, u32[]{:S(2)}) collective-permute-start(bf16[256,256]{1,0:T(8,128)(2,1)S(1)} %pad_maximum_fusion.6), channel_id=1, source_target_pairs={{0,16},{8,24},{16,0},{24,8},{1,17},{9,25},{17,1},{25,9},{2,18},{10... | collective-permute-start | bytes 393224 | tf_op jit(solution)/shard_map/ppermute | solution.py:495
  26.8 0.0 collective-permute-start.6
  26.8 4.7 %collective-permute-done.7 = bf16[256,256]{1,0:T(8,128)(2,1)S(1)} collective-permute-done((bf16[256,256]{1,0:T(8,128)(2,1)S(1)}, bf16[256,256]{1,0:T(8,128)(2,1)S(1)}, u32[]{:S(2)}, u32[]{:S(2)}) %collective-permute-start.7) | collective-permute-done | bytes 131104 | tf_op jit(solution)/shard_map/ppermute | solution.py:495
  31.5 0.3 collective-permute-start.8
  31.8 1.6 %collective-permute-done.3 = bf16[880,256]{1,0:T(8,128)(2,1)S(1)} collective-permute-done((bf16[880,256]{1,0:T(8,128)(2,1)S(1)}, bf16[880,256]{1,0:T(8,128)(2,1)S(1)}, u32[]{:S(2)}, u32[]{:S(2)}) %collective-permute-start.3) | collective-permute-done | bytes 450592 | tf_op jit(solution)/shard_map/ppermute | solution.py:495
  33.4 3.2 %collective-permute-start.9 = (bf16[256,256]{1,0:T(8,128)(2,1)S(1)}, bf16[256,256]{1,0:T(8,128)(2,1)S(1)}, u32[]{:S(2)}, u32[]{:S(2)}) collective-permute-start(bf16[256,256]{1,0:T(8,128)(2,1)S(1)} %pad_maximum_fusion.7), channel_id=1, source_target_pairs={{0,16},{8,24},{16,0},{24,8},{1,17},{9,25},{17,1},{25,9},{2,18},{10... | collective-permute-start | bytes 393224 | tf_op jit(solution)/shard_map/ppermute | solution.py:495
  36.6 4.0 %collective-permute-done.4 = bf16[880,256]{1,0:T(8,128)(2,1)S(1)} collective-permute-done((bf16[880,256]{1,0:T(8,128)(2,1)S(1)}, bf16[880,256]{1,0:T(8,128)(2,1)S(1)}, u32[]{:S(2)}, u32[]{:S(2)}) %collective-permute-start.4) | collective-permute-done | bytes 450592 | tf_op jit(solution)/shard_map/ppermute | solution.py:495
  40.6 0.0 collective-permute-done.5
  40.6 0.0 copy-start.2
  40.6 0.0 copy-start.3
  40.6 0.2 pad_maximum_fusion.share_ref
  40.8 0.0 copy-start
  40.9 0.0 collective-permute-done.6
  40.9 0.0 collective-permute-done.8
  40.9 0.0 collective-permute-done.9
  40.9 0.1 collective-permute-start.10
  41.0 1.3 %collective-permute-start.11 = (bf16[768,256]{1,0:T(8,128)(2,1)S(1)}, bf16[768,256]{1,0:T(8,128)(2,1)S(1)}, u32[]{:S(2)}, u32[]{:S(2)}) collective-permute-start(bf16[768,256]{1,0:T(8,128)(2,1)S(1)} %constant_dynamic-update-slice_fusion.5), channel_id=1, source_target_pairs={{0,2},{1,3},{2,0},{3,1},{4,6},{5,7},{6,4},{7,5},{8,10},{9,11},{10,... | collective-permute-start | bytes 1179656 | tf_op jit(solution)/shard_map/ppermute | solution.py:495
  42.3 0.8 collective-permute-start.12
  43.1 3.5 %collective-permute-start.13 = (bf16[256,256]{1,0:T(8,128)(2,1)S(1)}, bf16[256,256]{1,0:T(8,128)(2,1)S(1)}, u32[]{:S(2)}, u32[]{:S(2)}) collective-permute-start(bf16[256,256]{1,0:T(8,128)(2,1)S(1)} %pad_maximum_fusion.7), channel_id=1, source_target_pairs={{0,8},{8,0},{16,24},{24,16},{1,9},{9,1},{17,25},{25,17},{2,10},{10... | collective-permute-start | bytes 393224 | tf_op jit(solution)/shard_map/ppermute | solution.py:495
  46.7 0.0 collective-permute-start.14
  46.7 0.0 collective-permute-done.10.other_ref
  46.7 0.0 copy-start.1
  46.7 0.0 copy-done.2
  46.7 0.0 copy-done.3
  46.7 5.1 %shard_map.94 = (f32[7,8,2560]{2,1,0:T(8,128)S(1)}, bf16[4,8,8,256]{3,2,1,0:T(8,128)(2,1)}) custom-call(f32[8,2048]{1,0:T(8,128)S(1)} %dynamic-slice_convert_fusion.upstream_ref, bf16[2,8,256,128]{3,2,1,0:T(8,128)(2,1)S(1)} %bitcast.33, bf16[2,8,256,128]{3,2,1,0:T(8,128)(2,1)S(1)} %bitcast.35, bf16[4,880,256]{2,1,0:T(8,128)(2,1)S(1)} %pad_maximum_fusion.share_ref, ...), custom_call_target="tpu_custom_call" | custom-call | bytes 18874368 | tf_op jit(solution)/shard_map/pallas_call | solution.py:475
  51.8 0.0 copy-done
  51.8 0.0 copy-done.1
  51.8 0.0 collective-permute-done.13
  51.8 1.3 %collective-permute-done.14 = bf16[256,256]{1,0:T(8,128)(2,1)S(1)} collective-permute-done((bf16[256,256]{1,0:T(8,128)(2,1)S(1)}, bf16[256,256]{1,0:T(8,128)(2,1)S(1)}, u32[]{:S(2)}, u32[]{:S(2)}) %collective-permute-start.14) | collective-permute-done | bytes 131104 | tf_op jit(solution)/shard_map/ppermute | solution.py:495
  53.1 0.0 collective-permute-done.11
  53.1 0.5 collective-permute-done.12
  53.6 0.0 copy-start.4
  53.6 1.4 %pad_maximum_fusion.1.late_share_ref = bf16[4,768,256]{2,1,0:T(8,128)(2,1)} fusion(bf16[1,768,256]{2,1,0:T(8,128)(2,1)S(1)} %maximum_bitcast_fusion, bf16[1,768,256]{2,1,0:T(8,128)(2,1)S(1)} %bitcast.45, bf16[1,768,256]{2,1,0:T(8,128)(2,1)S(1)} %bitcast.44, bf16[1,768,256]{2,1,0:T(8,128)(2,1)S(1)} %bitcast.40), kind=kLoop, calls=%fused_computation.1 | loop fusion | flops 2359296 | bytes 3145728 | tf_op jit(solution)/shard_map/stack | solution.py:639
  54.9 0.0 collective-permute-start.15
  55.0 6.4 %all-to-all-start = ((bf16[32,8,256]{2,1,0:T(8,128)(2,1)}), bf16[32,8,256]{2,1,0:T(8,128)(2,1)S(1)}, u32[]{:S(2)}, u32[]{:S(2)}) async-start(bf16[32,8,256]{2,1,0:T(8,128)(2,1)} %bitcast.19), calls=%async_computation | async-start | bytes 262144 | tf_op jit(solution)/shard_map/all_to_all | solution.py:490
  61.4 0.0 copy-start.5
  61.4 0.0 collective-permute-done.15.late_other_ref
  61.4 0.0 copy-done.4
  61.4 12.8 %shard_map.95 = bf16[4,8,8,1024]{3,2,1,0:T(8,128)(2,1)} custom-call(f32[7,8,2560]{2,1,0:T(8,128)S(1)} %get-tuple-element.49.state_in, bf16[2,8,256,128]{3,2,1,0:T(8,128)(2,1)S(1)} %bitcast.34, bf16[2,8,256,128]{3,2,1,0:T(8,128)(2,1)S(1)} %bitcast.36, bf16[4,880,256]{2,1,0:T(8,128)(2,1)} %copy-done, bf16[4,880,256]{2,1,0:T(8,128)(2,1)} %copy-done.1, ...), custom_call_target="tpu_custom_call" | custom-call | bytes 50331648 | tf_op jit(solution)/shard_map/pallas_call | solution.py:475
  74.2 0.0 all-to-all-done
  74.2 5.8 %all-to-all-start.1 = ((bf16[32,8,1024]{2,1,0:T(8,128)(2,1)}), bf16[32,8,1024]{2,1,0:T(8,128)(2,1)S(1)}, u32[]{:S(2)}, u32[]{:S(2)}) async-start(bf16[32,8,1024]{2,1,0:T(8,128)(2,1)} %bitcast.21), calls=%async_computation.1 | async-start | bytes 1048576 | tf_op jit(solution)/shard_map/all_to_all | solution.py:490
  80.1 0.0 copy-done.5
  80.1 0.1 copy.18.route_ref
  80.2 15.4 %all-to-all-done.1 = bf16[32,8,1024]{2,1,0:T(8,128)(2,1)S(1)} async-done(((bf16[32,8,1024]{2,1,0:T(8,128)(2,1)}), bf16[32,8,1024]{2,1,0:T(8,128)(2,1)S(1)}, u32[]{:S(2)}, u32[]{:S(2)}) %all-to-all-start.1) | async-done | bytes 524320 | tf_op jit(solution)/shard_map/all_to_all | solution.py:490
  95.6 1.6 %shard_map.96 = (bf16[32,512]{1,0:T(8,128)(2,1)}, f32[2,256,128]{2,1,0:T(8,128)}, f32[2,256,128]{2,1,0:T(8,128)}) custom-call(s32[4,2]{1,0:T(4,128)S(1)} %copy.18.route_ref, bf16[256,256]{1,0:T(8,128)(2,1)S(1)} %bitcast.38, bf16[256,1024]{1,0:T(8,128)(2,1)S(1)} %bitcast.37), custom_call_target="tpu_custom_call" | custom-call | tf_op jit(solution)/shard_map/pallas_call | solution.py:475
  (20 shorter events, 0.2 us)
Async XLA Ops:
  3.2 9.0 %collective-permute-start = (bf16[280,256]{1,0:T(8,128)(2,1)S(1)}, bf16[280,256]{1,0:T(8,128)(2,1)S(1)}, u32[]{:S(2)}, u32[]{:S(2)}) collective-permute-start(bf16[280,256]{1,0:T(8,128)(2,1)S(1)} %get-tuple-element.67), channel_id=1, source_target_pairs={{0,8},{8,0},{16,24},{24,16},{1,9},{9,1},{17,25},{25,17},{2,10},{10... | collective-permute-start | bytes 430088 | tf_op jit(solution)/shard_map/ppermute | solution.py:495
  6.2 13.7 %collective-permute-start.1 = (bf16[280,256]{1,0:T(8,128)(2,1)S(1)}, bf16[280,256]{1,0:T(8,128)(2,1)S(1)}, u32[]{:S(2)}, u32[]{:S(2)}) collective-permute-start(bf16[280,256]{1,0:T(8,128)(2,1)S(1)} %get-tuple-element.66), channel_id=1, source_target_pairs={{0,16},{8,24},{16,0},{24,8},{1,17},{9,25},{17,1},{25,9},{2,18},{10... | collective-permute-start | bytes 430088 | tf_op jit(solution)/shard_map/ppermute | solution.py:495
  8.8 11.2 %collective-permute-start.2 = (bf16[280,256]{1,0:T(8,128)(2,1)S(1)}, bf16[280,256]{1,0:T(8,128)(2,1)S(1)}, u32[]{:S(2)}, u32[]{:S(2)}) collective-permute-start(bf16[280,256]{1,0:T(8,128)(2,1)S(1)} %get-tuple-element.65), channel_id=1, source_target_pairs={{0,24},{8,16},{16,8},{24,0},{1,25},{9,17},{17,9},{25,1},{2,26},{10... | collective-permute-start | bytes 430088 | tf_op jit(solution)/shard_map/ppermute | solution.py:495
  20.1 13.3 %collective-permute-start.3 = (bf16[880,256]{1,0:T(8,128)(2,1)S(1)}, bf16[880,256]{1,0:T(8,128)(2,1)S(1)}, u32[]{:S(2)}, u32[]{:S(2)}) collective-permute-start(bf16[880,256]{1,0:T(8,128)(2,1)S(1)} %constant_dynamic-update-slice_fusion), channel_id=1, source_target_pairs={{0,2},{1,3},{2,0},{3,1},{4,6},{5,7},{6,4},{7,5},{8,10},{9,11},{10,... | collective-permute-start | bytes 1351688 | tf_op jit(solution)/shard_map/ppermute | solution.py:495
  21.6 19.0 %collective-permute-start.4 = (bf16[880,256]{1,0:T(8,128)(2,1)S(1)}, bf16[880,256]{1,0:T(8,128)(2,1)S(1)}, u32[]{:S(2)}, u32[]{:S(2)}) collective-permute-start(bf16[880,256]{1,0:T(8,128)(2,1)S(1)} %constant_dynamic-update-slice_fusion), channel_id=1, source_target_pairs={{0,4},{1,5},{2,6},{3,7},{4,0},{5,1},{6,2},{7,3},{8,12},{9,13},{10,... | collective-permute-start | bytes 1351688 | tf_op jit(solution)/shard_map/ppermute | solution.py:495
  23.2 17.4 %collective-permute-start.5 = (bf16[880,256]{1,0:T(8,128)(2,1)S(1)}, bf16[880,256]{1,0:T(8,128)(2,1)S(1)}, u32[]{:S(2)}, u32[]{:S(2)}) collective-permute-start(bf16[880,256]{1,0:T(8,128)(2,1)S(1)} %constant_dynamic-update-slice_fusion), channel_id=1, source_target_pairs={{0,6},{1,7},{2,4},{3,5},{4,2},{5,3},{6,0},{7,1},{8,14},{9,15},{10,... | collective-permute-start | bytes 1351688 | tf_op jit(solution)/shard_map/ppermute | solution.py:495
  23.6 7.9 %collective-permute-start.7 = (bf16[256,256]{1,0:T(8,128)(2,1)S(1)}, bf16[256,256]{1,0:T(8,128)(2,1)S(1)}, u32[]{:S(2)}, u32[]{:S(2)}) collective-permute-start(bf16[256,256]{1,0:T(8,128)(2,1)S(1)} %pad_maximum_fusion.6), channel_id=1, source_target_pairs={{0,16},{8,24},{16,0},{24,8},{1,17},{9,25},{17,1},{25,9},{2,18},{10... | collective-permute-start | bytes 393224 | tf_op jit(solution)/shard_map/ppermute | solution.py:495
  26.8 14.0 %collective-permute-start.6 = (bf16[256,256]{1,0:T(8,128)(2,1)S(1)}, bf16[256,256]{1,0:T(8,128)(2,1)S(1)}, u32[]{:S(2)}, u32[]{:S(2)}) collective-permute-start(bf16[256,256]{1,0:T(8,128)(2,1)S(1)} %pad_maximum_fusion.6), channel_id=1, source_target_pairs={{0,8},{8,0},{16,24},{24,16},{1,9},{9,1},{17,25},{25,17},{2,10},{10... | collective-permute-start | bytes 393224 | tf_op jit(solution)/shard_map/ppermute | solution.py:495
  31.5 9.4 %collective-permute-start.8 = (bf16[256,256]{1,0:T(8,128)(2,1)S(1)}, bf16[256,256]{1,0:T(8,128)(2,1)S(1)}, u32[]{:S(2)}, u32[]{:S(2)}) collective-permute-start(bf16[256,256]{1,0:T(8,128)(2,1)S(1)} %collective-permute-done.7), channel_id=1, source_target_pairs={{0,8},{8,0},{16,24},{24,16},{1,9},{9,1},{17,25},{25,17},{2,10},{10... | collective-permute-start | bytes 393224 | tf_op jit(solution)/shard_map/ppermute | solution.py:495
  33.4 7.4 %collective-permute-start.9 = (bf16[256,256]{1,0:T(8,128)(2,1)S(1)}, bf16[256,256]{1,0:T(8,128)(2,1)S(1)}, u32[]{:S(2)}, u32[]{:S(2)}) collective-permute-start(bf16[256,256]{1,0:T(8,128)(2,1)S(1)} %pad_maximum_fusion.7), channel_id=1, source_target_pairs={{0,16},{8,24},{16,0},{24,8},{1,17},{9,25},{17,1},{25,9},{2,18},{10... | collective-permute-start | bytes 393224 | tf_op jit(solution)/shard_map/ppermute | solution.py:495
  40.6 6.1 %copy-start.2 = (bf16[2,2048,128]{2,1,0:T(8,128)(2,1)S(1)}, bf16[2,2048,128]{2,1,0:T(8,128)(2,1)}, u32[]{:S(2)}) copy-start(bf16[2,2048,128]{2,1,0:T(8,128)(2,1)} %param.11) | copy-start | bytes 3145732
  40.6 6.1 %copy-start.3 = (bf16[2,2048,128]{2,1,0:T(8,128)(2,1)S(1)}, bf16[2,2048,128]{2,1,0:T(8,128)(2,1)}, u32[]{:S(2)}) copy-start(bf16[2,2048,128]{2,1,0:T(8,128)(2,1)} %param.12) | copy-start | bytes 3145732
  40.8 10.9 %copy-start = (bf16[4,880,256]{2,1,0:T(8,128)(2,1)}, bf16[4,880,256]{2,1,0:T(8,128)(2,1)S(1)}, u32[]{:S(2)}) copy-start(bf16[4,880,256]{2,1,0:T(8,128)(2,1)S(1)} %pad_maximum_fusion.share_ref) | copy-start | bytes 5406724
  40.9 5.8 %collective-permute-start.10 = (bf16[4,880,256]{2,1,0:T(8,128)(2,1)S(1)}, bf16[4,880,256]{2,1,0:T(8,128)(2,1)S(1)}, u32[]{:S(2)}, u32[]{:S(2)}) collective-permute-start(bf16[4,880,256]{2,1,0:T(8,128)(2,1)S(1)} %pad_maximum_fusion.share_ref), channel_id=1, source_target_pairs={{0,1},{1,0},{2,3},{3,2},{4,5},{5,4},{6,7},{7,6},{8,9},{9,8},{10,11... | collective-permute-start | bytes 5406728 | tf_op jit(solution)/shard_map/ppermute | solution.py:495
  41.0 12.1 %collective-permute-start.11 = (bf16[768,256]{1,0:T(8,128)(2,1)S(1)}, bf16[768,256]{1,0:T(8,128)(2,1)S(1)}, u32[]{:S(2)}, u32[]{:S(2)}) collective-permute-start(bf16[768,256]{1,0:T(8,128)(2,1)S(1)} %constant_dynamic-update-slice_fusion.5), channel_id=1, source_target_pairs={{0,2},{1,3},{2,0},{3,1},{4,6},{5,7},{6,4},{7,5},{8,10},{9,11},{10,... | collective-permute-start | bytes 1179656 | tf_op jit(solution)/shard_map/ppermute | solution.py:495
  42.3 11.2 %collective-permute-start.12 = (bf16[768,256]{1,0:T(8,128)(2,1)S(1)}, bf16[768,256]{1,0:T(8,128)(2,1)S(1)}, u32[]{:S(2)}, u32[]{:S(2)}) collective-permute-start(bf16[768,256]{1,0:T(8,128)(2,1)S(1)} %constant_dynamic-update-slice_fusion.5), channel_id=1, source_target_pairs={{0,4},{1,5},{2,6},{3,7},{4,0},{5,1},{6,2},{7,3},{8,12},{9,13},{10,... | collective-permute-start | bytes 1179656 | tf_op jit(solution)/shard_map/ppermute | solution.py:495
  43.1 8.7 %collective-permute-start.13 = (bf16[256,256]{1,0:T(8,128)(2,1)S(1)}, bf16[256,256]{1,0:T(8,128)(2,1)S(1)}, u32[]{:S(2)}, u32[]{:S(2)}) collective-permute-start(bf16[256,256]{1,0:T(8,128)(2,1)S(1)} %pad_maximum_fusion.7), channel_id=1, source_target_pairs={{0,8},{8,0},{16,24},{24,16},{1,9},{9,1},{17,25},{25,17},{2,10},{10... | collective-permute-start | bytes 393224 | tf_op jit(solution)/shard_map/ppermute | solution.py:495
  46.7 6.4 %collective-permute-start.14 = (bf16[256,256]{1,0:T(8,128)(2,1)S(1)}, bf16[256,256]{1,0:T(8,128)(2,1)S(1)}, u32[]{:S(2)}, u32[]{:S(2)}) collective-permute-start(bf16[256,256]{1,0:T(8,128)(2,1)S(1)} %collective-permute-done.9), channel_id=1, source_target_pairs={{0,8},{8,0},{16,24},{24,16},{1,9},{9,1},{17,25},{25,17},{2,10},{10... | collective-permute-start | bytes 393224 | tf_op jit(solution)/shard_map/ppermute | solution.py:495
  46.7 5.1 %copy-start.1 = (bf16[4,880,256]{2,1,0:T(8,128)(2,1)}, bf16[4,880,256]{2,1,0:T(8,128)(2,1)S(1)}, u32[]{:S(2)}) copy-start(bf16[4,880,256]{2,1,0:T(8,128)(2,1)S(1)} %collective-permute-done.10.other_ref) | copy-start | bytes 5406724
  53.6 7.8 %copy-start.4 = (bf16[2,2048,128]{2,1,0:T(8,128)(2,1)S(1)}, bf16[2,2048,128]{2,1,0:T(8,128)(2,1)}, u32[]{:S(2)}) copy-start(bf16[2,2048,128]{2,1,0:T(8,128)(2,1)} %param.12) | copy-start | bytes 3145732
  54.9 6.4 %collective-permute-start.15 = (bf16[4,768,256]{2,1,0:T(8,128)(2,1)}, bf16[4,768,256]{2,1,0:T(8,128)(2,1)}, u32[]{:S(2)}, u32[]{:S(2)}) collective-permute-start(bf16[4,768,256]{2,1,0:T(8,128)(2,1)} %pad_maximum_fusion.1.late_share_ref), channel_id=1, source_target_pairs={{0,1},{1,0},{2,3},{3,2},{4,5},{5,4},{6,7},{7,6},{8,9},{9,8},{10,11... | collective-permute-start | bytes 4718600 | tf_op jit(solution)/shard_map/ppermute | solution.py:495
  55.0 19.3 %all-to-all-start = ((bf16[32,8,256]{2,1,0:T(8,128)(2,1)}), bf16[32,8,256]{2,1,0:T(8,128)(2,1)S(1)}, u32[]{:S(2)}, u32[]{:S(2)}) async-start(bf16[32,8,256]{2,1,0:T(8,128)(2,1)} %bitcast.19), calls=%async_computation | async-start | bytes 262144 | tf_op jit(solution)/shard_map/all_to_all | solution.py:490
  61.4 18.7 %copy-start.5 = (s32[4,2]{0,1:T(2,128)S(1)}, s32[4,2]{0,1:T(2,128)}, u32[]{:S(2)}) copy-start(s32[4,2]{0,1:T(2,128)} %param.9) | copy-start | bytes 100
  74.2 21.4 %all-to-all-start.1 = ((bf16[32,8,1024]{2,1,0:T(8,128)(2,1)}), bf16[32,8,1024]{2,1,0:T(8,128)(2,1)S(1)}, u32[]{:S(2)}, u32[]{:S(2)}) async-start(bf16[32,8,1024]{2,1,0:T(8,128)(2,1)} %bitcast.21), calls=%async_computation.1 | async-start | bytes 1048576 | tf_op jit(solution)/shard_map/all_to_all | solution.py:490

commit v8 on v7

--- a/solution.py
+++ b/solution.py
@@ -654,7 +654,7 @@
             pltpu.SemaphoreType.DMA((1,)),
         ),
         48 << 20,
-        50 << 20,
+        47 << 20,
         1,
         0,
     )

time: 97.8 us -> 97.5 us (level)
  local copies, waits for them, and re-layouts: 3 us -> 4.21 us
  other arithmetic: 4.59 us -> 3.43 us
    unnamed x22, local copies, waits for them, and re-layouts: 0.19 us -> 1.4 us
    another operation x2, other arithmetic: 1.39 us -> 0.23 us  [body(): plane = jnp.stack(planes + [jnp.concatenate(far, axis=0)])]
where the time goes in v8:
time: 97.5 us; the launch traced here: 97 us
  waiting for transfers between devices  35.3 us (36%)
  starting transfers between devices  34 us (35%)
  Pallas kernels  19.1 us (20%)
  local copies, waits for them, and re-layouts  4.21 us (4%)
  other arithmetic  3.43 us (4%)
  between operations  0.98 us (1%)
    ppermute x16, starting transfers between devices, swapped(): return lax.ppermute(value, axis, pairs)  21.7 us
    ppermute x16, waiting for transfers between devices, swapped(): return lax.ppermute(value, axis, pairs)  19.8 us
    pallas_call x3, Pallas kernels, call(): pl.pallas_call(kernel, out_shape=outs, in_specs=[pl.BlockSpec(memory_spac...  19.1 us
    all_to_all x2, waiting for transfers between devices, exchange(): lax.all_to_all(blocks, ('pipe', 'dp'), split_axis=0, concat_axis=0, tiled...  15.4 us
    all_to_all x2, starting transfers between devices, exchange(): lax.all_to_all(blocks, ('pipe', 'dp'), split_axis=0, concat_axis=0, tiled...  12.2 us
  transfers between devices with their start and end apart: 18, of which 7 were waited for; matrix products, arithmetic and copies ran while one was open for 4% of the time, Pallas kernels for 18%

profile of v8, /device:TPU:0, one launch (start us, length us, event | category | flops | bytes accessed | tf_op | source)
XLA Modules:
  0.0 97.0 jit_solution(5796967158260105002)
XLA Ops:
  0.6 0.7 fusion.8
  1.4 0.9 dynamic-slice_bitcast_fusion.4
  2.3 0.8 constant_dynamic-slice_fusion.3
  3.2 3.1 %collective-permute-start = (bf16[280,256]{1,0:T(8,128)(2,1)S(1)}, bf16[280,256]{1,0:T(8,128)(2,1)S(1)}, u32[]{:S(2)}, u32[]{:S(2)}) collective-permute-start(bf16[280,256]{1,0:T(8,128)(2,1)S(1)} %get-tuple-element.67), channel_id=1, source_target_pairs={{0,8},{8,0},{16,24},{24,16},{1,9},{9,1},{17,25},{25,17},{2,10},{10... | collective-permute-start | bytes 430088 | tf_op jit(solution)/shard_map/ppermute | solution.py:495
  6.2 2.6 %collective-permute-start.1 = (bf16[280,256]{1,0:T(8,128)(2,1)S(1)}, bf16[280,256]{1,0:T(8,128)(2,1)S(1)}, u32[]{:S(2)}, u32[]{:S(2)}) collective-permute-start(bf16[280,256]{1,0:T(8,128)(2,1)S(1)} %get-tuple-element.66), channel_id=1, source_target_pairs={{0,16},{8,24},{16,0},{24,8},{1,17},{9,25},{17,1},{25,9},{2,18},{10... | collective-permute-start | bytes 430088 | tf_op jit(solution)/shard_map/ppermute | solution.py:495
  8.8 0.0 collective-permute-start.2
  8.8 0.8 dynamic-slice_convert_fusion.upstream_ref
  9.6 0.7 convert.19
  10.3 0.1 copy.16
  10.4 0.7 convert.18
  11.1 0.1 fusion.5
  11.2 1.0 dynamic-slice_bitcast_fusion
  12.2 0.0 collective-permute-done
  12.2 7.8 %collective-permute-done.1 = bf16[280,256]{1,0:T(8,128)(2,1)S(1)} collective-permute-done((bf16[280,256]{1,0:T(8,128)(2,1)S(1)}, bf16[280,256]{1,0:T(8,128)(2,1)S(1)}, u32[]{:S(2)}, u32[]{:S(2)}) %collective-permute-start.1) | collective-permute-done | bytes 143392 | tf_op jit(solution)/shard_map/ppermute | solution.py:495
  20.0 0.0 collective-permute-done.2
  20.1 1.6 %collective-permute-start.3 = (bf16[880,256]{1,0:T(8,128)(2,1)S(1)}, bf16[880,256]{1,0:T(8,128)(2,1)S(1)}, u32[]{:S(2)}, u32[]{:S(2)}) collective-permute-start(bf16[880,256]{1,0:T(8,128)(2,1)S(1)} %constant_dynamic-update-slice_fusion), channel_id=1, source_target_pairs={{0,2},{1,3},{2,0},{3,1},{4,6},{5,7},{6,4},{7,5},{8,10},{9,11},{10,... | collective-permute-start | bytes 1351688 | tf_op jit(solution)/shard_map/ppermute | solution.py:495
  21.6 1.5 %collective-permute-start.4 = (bf16[880,256]{1,0:T(8,128)(2,1)S(1)}, bf16[880,256]{1,0:T(8,128)(2,1)S(1)}, u32[]{:S(2)}, u32[]{:S(2)}) collective-permute-start(bf16[880,256]{1,0:T(8,128)(2,1)S(1)} %constant_dynamic-update-slice_fusion), channel_id=1, source_target_pairs={{0,4},{1,5},{2,6},{3,7},{4,0},{5,1},{6,2},{7,3},{8,12},{9,13},{10,... | collective-permute-start | bytes 1351688 | tf_op jit(solution)/shard_map/ppermute | solution.py:495
  23.2 0.5 collective-permute-start.5
  23.6 3.2 %collective-permute-start.7 = (bf16[256,256]{1,0:T(8,128)(2,1)S(1)}, bf16[256,256]{1,0:T(8,128)(2,1)S(1)}, u32[]{:S(2)}, u32[]{:S(2)}) collective-permute-start(bf16[256,256]{1,0:T(8,128)(2,1)S(1)} %pad_maximum_fusion.6), channel_id=1, source_target_pairs={{0,16},{8,24},{16,0},{24,8},{1,17},{9,25},{17,1},{25,9},{2,18},{10... | collective-permute-start | bytes 393224 | tf_op jit(solution)/shard_map/ppermute | solution.py:495
  26.8 0.0 collective-permute-start.6
  26.8 4.7 %collective-permute-done.7 = bf16[256,256]{1,0:T(8,128)(2,1)S(1)} collective-permute-done((bf16[256,256]{1,0:T(8,128)(2,1)S(1)}, bf16[256,256]{1,0:T(8,128)(2,1)S(1)}, u32[]{:S(2)}, u32[]{:S(2)}) %collective-permute-start.7) | collective-permute-done | bytes 131104 | tf_op jit(solution)/shard_map/ppermute | solution.py:495
  31.5 0.3 collective-permute-start.8
  31.8 1.6 %collective-permute-done.3 = bf16[880,256]{1,0:T(8,128)(2,1)S(1)} collective-permute-done((bf16[880,256]{1,0:T(8,128)(2,1)S(1)}, bf16[880,256]{1,0:T(8,128)(2,1)S(1)}, u32[]{:S(2)}, u32[]{:S(2)}) %collective-permute-start.3) | collective-permute-done | bytes 450592 | tf_op jit(solution)/shard_map/ppermute | solution.py:495
  33.4 3.2 %collective-permute-start.9 = (bf16[256,256]{1,0:T(8,128)(2,1)S(1)}, bf16[256,256]{1,0:T(8,128)(2,1)S(1)}, u32[]{:S(2)}, u32[]{:S(2)}) collective-permute-start(bf16[256,256]{1,0:T(8,128)(2,1)S(1)} %pad_maximum_fusion.7), channel_id=1, source_target_pairs={{0,16},{8,24},{16,0},{24,8},{1,17},{9,25},{17,1},{25,9},{2,18},{10... | collective-permute-start | bytes 393224 | tf_op jit(solution)/shard_map/ppermute | solution.py:495
  36.6 4.0 %collective-permute-done.4 = bf16[880,256]{1,0:T(8,128)(2,1)S(1)} collective-permute-done((bf16[880,256]{1,0:T(8,128)(2,1)S(1)}, bf16[880,256]{1,0:T(8,128)(2,1)S(1)}, u32[]{:S(2)}, u32[]{:S(2)}) %collective-permute-start.4) | collective-permute-done | bytes 450592 | tf_op jit(solution)/shard_map/ppermute | solution.py:495
  40.6 0.0 collective-permute-done.5
  40.6 0.0 copy-start.2
  40.6 0.0 copy-start.3
  40.6 0.2 pad_maximum_fusion.share_ref
  40.8 0.0 copy-start
  40.9 0.0 collective-permute-done.6
  40.9 0.0 collective-permute-done.8
  40.9 0.0 collective-permute-done.9
  40.9 0.1 collective-permute-start.10
  41.0 1.3 %collective-permute-start.11 = (bf16[768,256]{1,0:T(8,128)(2,1)S(1)}, bf16[768,256]{1,0:T(8,128)(2,1)S(1)}, u32[]{:S(2)}, u32[]{:S(2)}) collective-permute-start(bf16[768,256]{1,0:T(8,128)(2,1)S(1)} %constant_dynamic-update-slice_fusion.5), channel_id=1, source_target_pairs={{0,2},{1,3},{2,0},{3,1},{4,6},{5,7},{6,4},{7,5},{8,10},{9,11},{10,... | collective-permute-start | bytes 1179656 | tf_op jit(solution)/shard_map/ppermute | solution.py:495
  42.3 0.8 collective-permute-start.12
  43.1 3.5 %collective-permute-start.13 = (bf16[256,256]{1,0:T(8,128)(2,1)S(1)}, bf16[256,256]{1,0:T(8,128)(2,1)S(1)}, u32[]{:S(2)}, u32[]{:S(2)}) collective-permute-start(bf16[256,256]{1,0:T(8,128)(2,1)S(1)} %pad_maximum_fusion.7), channel_id=1, source_target_pairs={{0,8},{8,0},{16,24},{24,16},{1,9},{9,1},{17,25},{25,17},{2,10},{10... | collective-permute-start | bytes 393224 | tf_op jit(solution)/shard_map/ppermute | solution.py:495
  46.7 0.0 collective-permute-start.14
  46.7 0.0 collective-permute-done.10.other_ref
  46.7 0.0 copy-start.1
  46.7 0.0 copy-done.2
  46.7 0.0 copy-done.3
  46.7 5.1 %shard_map.94 = (f32[7,8,2560]{2,1,0:T(8,128)S(1)}, bf16[4,8,8,256]{3,2,1,0:T(8,128)(2,1)}) custom-call(f32[8,2048]{1,0:T(8,128)S(1)} %dynamic-slice_convert_fusion.upstream_ref, bf16[2,8,256,128]{3,2,1,0:T(8,128)(2,1)S(1)} %bitcast.33, bf16[2,8,256,128]{3,2,1,0:T(8,128)(2,1)S(1)} %bitcast.35, bf16[4,880,256]{2,1,0:T(8,128)(2,1)S(1)} %pad_maximum_fusion.share_ref, ...), custom_call_target="tpu_custom_call" | custom-call | bytes 18874368 | tf_op jit(solution)/shard_map/pallas_call | solution.py:475
  51.8 0.0 copy-done
  51.8 0.0 copy-done.1
  51.8 0.0 collective-permute-done.13
  51.8 1.3 %collective-permute-done.14 = bf16[256,256]{1,0:T(8,128)(2,1)S(1)} collective-permute-done((bf16[256,256]{1,0:T(8,128)(2,1)S(1)}, bf16[256,256]{1,0:T(8,128)(2,1)S(1)}, u32[]{:S(2)}, u32[]{:S(2)}) %collective-permute-start.14) | collective-permute-done | bytes 131104 | tf_op jit(solution)/shard_map/ppermute | solution.py:495
  53.1 0.0 collective-permute-done.11
  53.1 0.5 collective-permute-done.12
  53.6 0.2 pad_maximum_fusion.1.late_share_ref
  53.8 0.1 collective-permute-start.15
  53.9 6.4 %all-to-all-start = ((bf16[32,8,256]{2,1,0:T(8,128)(2,1)}), bf16[32,8,256]{2,1,0:T(8,128)(2,1)S(1)}, u32[]{:S(2)}, u32[]{:S(2)}) async-start(bf16[32,8,256]{2,1,0:T(8,128)(2,1)} %bitcast.19), calls=%async_computation | async-start | bytes 262144 | tf_op jit(solution)/shard_map/all_to_all | solution.py:490
  60.3 0.0 collective-permute-done.15.late_other_ref
  60.3 0.0 copy-start.4
  60.3 1.2 %copy-done.4 = bf16[2,2048,128]{2,1,0:T(8,128)(2,1)S(1)} copy-done((bf16[2,2048,128]{2,1,0:T(8,128)(2,1)S(1)}, bf16[2,2048,128]{2,1,0:T(8,128)(2,1)}, u32[]{:S(2)}) %copy-start.4) | copy-done | bytes 1048600
  61.5 0.0 copy-start.5
  61.5 12.5 %shard_map.95 = bf16[4,8,8,1024]{3,2,1,0:T(8,128)(2,1)} custom-call(f32[7,8,2560]{2,1,0:T(8,128)S(1)} %get-tuple-element.49.state_in, bf16[2,8,256,128]{3,2,1,0:T(8,128)(2,1)S(1)} %bitcast.34, bf16[2,8,256,128]{3,2,1,0:T(8,128)(2,1)S(1)} %bitcast.36, bf16[4,880,256]{2,1,0:T(8,128)(2,1)} %copy-done, bf16[4,880,256]{2,1,0:T(8,128)(2,1)} %copy-done.1, ...), custom_call_target="tpu_custom_call" | custom-call | bytes 50331648 | tf_op jit(solution)/shard_map/pallas_call | solution.py:475
  74.0 0.0 all-to-all-done
  74.0 5.8 %all-to-all-start.1 = ((bf16[32,8,1024]{2,1,0:T(8,128)(2,1)}), bf16[32,8,1024]{2,1,0:T(8,128)(2,1)S(1)}, u32[]{:S(2)}, u32[]{:S(2)}) async-start(bf16[32,8,1024]{2,1,0:T(8,128)(2,1)} %bitcast.21), calls=%async_computation.1 | async-start | bytes 1048576 | tf_op jit(solution)/shard_map/all_to_all | solution.py:490
  79.8 0.0 copy-done.5
  79.8 0.1 copy.18.route_ref
  79.9 15.4 %all-to-all-done.1 = bf16[32,8,1024]{2,1,0:T(8,128)(2,1)S(1)} async-done(((bf16[32,8,1024]{2,1,0:T(8,128)(2,1)}), bf16[32,8,1024]{2,1,0:T(8,128)(2,1)S(1)}, u32[]{:S(2)}, u32[]{:S(2)}) %all-to-all-start.1) | async-done | bytes 524320 | tf_op jit(solution)/shard_map/all_to_all | solution.py:490
  95.4 1.6 %shard_map.96 = (bf16[32,512]{1,0:T(8,128)(2,1)}, f32[2,256,128]{2,1,0:T(8,128)}, f32[2,256,128]{2,1,0:T(8,128)}) custom-call(s32[4,2]{1,0:T(4,128)S(1)} %copy.18.route_ref, bf16[256,256]{1,0:T(8,128)(2,1)S(1)} %bitcast.38, bf16[256,1024]{1,0:T(8,128)(2,1)S(1)} %bitcast.37), custom_call_target="tpu_custom_call" | custom-call | tf_op jit(solution)/shard_map/pallas_call | solution.py:475
  (20 shorter events, 0.2 us)
Async XLA Ops:
  3.2 9.0 %collective-permute-start = (bf16[280,256]{1,0:T(8,128)(2,1)S(1)}, bf16[280,256]{1,0:T(8,128)(2,1)S(1)}, u32[]{:S(2)}, u32[]{:S(2)}) collective-permute-start(bf16[280,256]{1,0:T(8,128)(2,1)S(1)} %get-tuple-element.67), channel_id=1, source_target_pairs={{0,8},{8,0},{16,24},{24,16},{1,9},{9,1},{17,25},{25,17},{2,10},{10... | collective-permute-start | bytes 430088 | tf_op jit(solution)/shard_map/ppermute | solution.py:495
  6.2 13.7 %collective-permute-start.1 = (bf16[280,256]{1,0:T(8,128)(2,1)S(1)}, bf16[280,256]{1,0:T(8,128)(2,1)S(1)}, u32[]{:S(2)}, u32[]{:S(2)}) collective-permute-start(bf16[280,256]{1,0:T(8,128)(2,1)S(1)} %get-tuple-element.66), channel_id=1, source_target_pairs={{0,16},{8,24},{16,0},{24,8},{1,17},{9,25},{17,1},{25,9},{2,18},{10... | collective-permute-start | bytes 430088 | tf_op jit(solution)/shard_map/ppermute | solution.py:495
  8.8 11.2 %collective-permute-start.2 = (bf16[280,256]{1,0:T(8,128)(2,1)S(1)}, bf16[280,256]{1,0:T(8,128)(2,1)S(1)}, u32[]{:S(2)}, u32[]{:S(2)}) collective-permute-start(bf16[280,256]{1,0:T(8,128)(2,1)S(1)} %get-tuple-element.65), channel_id=1, source_target_pairs={{0,24},{8,16},{16,8},{24,0},{1,25},{9,17},{17,9},{25,1},{2,26},{10... | collective-permute-start | bytes 430088 | tf_op jit(solution)/shard_map/ppermute | solution.py:495
  20.1 13.3 %collective-permute-start.3 = (bf16[880,256]{1,0:T(8,128)(2,1)S(1)}, bf16[880,256]{1,0:T(8,128)(2,1)S(1)}, u32[]{:S(2)}, u32[]{:S(2)}) collective-permute-start(bf16[880,256]{1,0:T(8,128)(2,1)S(1)} %constant_dynamic-update-slice_fusion), channel_id=1, source_target_pairs={{0,2},{1,3},{2,0},{3,1},{4,6},{5,7},{6,4},{7,5},{8,10},{9,11},{10,... | collective-permute-start | bytes 1351688 | tf_op jit(solution)/shard_map/ppermute | solution.py:495
  21.6 19.0 %collective-permute-start.4 = (bf16[880,256]{1,0:T(8,128)(2,1)S(1)}, bf16[880,256]{1,0:T(8,128)(2,1)S(1)}, u32[]{:S(2)}, u32[]{:S(2)}) collective-permute-start(bf16[880,256]{1,0:T(8,128)(2,1)S(1)} %constant_dynamic-update-slice_fusion), channel_id=1, source_target_pairs={{0,4},{1,5},{2,6},{3,7},{4,0},{5,1},{6,2},{7,3},{8,12},{9,13},{10,... | collective-permute-start | bytes 1351688 | tf_op jit(solution)/shard_map/ppermute | solution.py:495
  23.2 17.4 %collective-permute-start.5 = (bf16[880,256]{1,0:T(8,128)(2,1)S(1)}, bf16[880,256]{1,0:T(8,128)(2,1)S(1)}, u32[]{:S(2)}, u32[]{:S(2)}) collective-permute-start(bf16[880,256]{1,0:T(8,128)(2,1)S(1)} %constant_dynamic-update-slice_fusion), channel_id=1, source_target_pairs={{0,6},{1,7},{2,4},{3,5},{4,2},{5,3},{6,0},{7,1},{8,14},{9,15},{10,... | collective-permute-start | bytes 1351688 | tf_op jit(solution)/shard_map/ppermute | solution.py:495
  23.6 7.9 %collective-permute-start.7 = (bf16[256,256]{1,0:T(8,128)(2,1)S(1)}, bf16[256,256]{1,0:T(8,128)(2,1)S(1)}, u32[]{:S(2)}, u32[]{:S(2)}) collective-permute-start(bf16[256,256]{1,0:T(8,128)(2,1)S(1)} %pad_maximum_fusion.6), channel_id=1, source_target_pairs={{0,16},{8,24},{16,0},{24,8},{1,17},{9,25},{17,1},{25,9},{2,18},{10... | collective-permute-start | bytes 393224 | tf_op jit(solution)/shard_map/ppermute | solution.py:495
  26.8 14.0 %collective-permute-start.6 = (bf16[256,256]{1,0:T(8,128)(2,1)S(1)}, bf16[256,256]{1,0:T(8,128)(2,1)S(1)}, u32[]{:S(2)}, u32[]{:S(2)}) collective-permute-start(bf16[256,256]{1,0:T(8,128)(2,1)S(1)} %pad_maximum_fusion.6), channel_id=1, source_target_pairs={{0,8},{8,0},{16,24},{24,16},{1,9},{9,1},{17,25},{25,17},{2,10},{10... | collective-permute-start | bytes 393224 | tf_op jit(solution)/shard_map/ppermute | solution.py:495
  31.5 9.4 %collective-permute-start.8 = (bf16[256,256]{1,0:T(8,128)(2,1)S(1)}, bf16[256,256]{1,0:T(8,128)(2,1)S(1)}, u32[]{:S(2)}, u32[]{:S(2)}) collective-permute-start(bf16[256,256]{1,0:T(8,128)(2,1)S(1)} %collective-permute-done.7), channel_id=1, source_target_pairs={{0,8},{8,0},{16,24},{24,16},{1,9},{9,1},{17,25},{25,17},{2,10},{10... | collective-permute-start | bytes 393224 | tf_op jit(solution)/shard_map/ppermute | solution.py:495
  33.4 7.4 %collective-permute-start.9 = (bf16[256,256]{1,0:T(8,128)(2,1)S(1)}, bf16[256,256]{1,0:T(8,128)(2,1)S(1)}, u32[]{:S(2)}, u32[]{:S(2)}) collective-permute-start(bf16[256,256]{1,0:T(8,128)(2,1)S(1)} %pad_maximum_fusion.7), channel_id=1, source_target_pairs={{0,16},{8,24},{16,0},{24,8},{1,17},{9,25},{17,1},{25,9},{2,18},{10... | collective-permute-start | bytes 393224 | tf_op jit(solution)/shard_map/ppermute | solution.py:495
  40.6 6.1 %copy-start.2 = (bf16[2,2048,128]{2,1,0:T(8,128)(2,1)S(1)}, bf16[2,2048,128]{2,1,0:T(8,128)(2,1)}, u32[]{:S(2)}) copy-start(bf16[2,2048,128]{2,1,0:T(8,128)(2,1)} %param.11) | copy-start | bytes 3145732
  40.6 6.1 %copy-start.3 = (bf16[2,2048,128]{2,1,0:T(8,128)(2,1)S(1)}, bf16[2,2048,128]{2,1,0:T(8,128)(2,1)}, u32[]{:S(2)}) copy-start(bf16[2,2048,128]{2,1,0:T(8,128)(2,1)} %param.12) | copy-start | bytes 3145732
  40.8 10.9 %copy-start = (bf16[4,880,256]{2,1,0:T(8,128)(2,1)}, bf16[4,880,256]{2,1,0:T(8,128)(2,1)S(1)}, u32[]{:S(2)}) copy-start(bf16[4,880,256]{2,1,0:T(8,128)(2,1)S(1)} %pad_maximum_fusion.share_ref) | copy-start | bytes 5406724
  40.9 5.8 %collective-permute-start.10 = (bf16[4,880,256]{2,1,0:T(8,128)(2,1)S(1)}, bf16[4,880,256]{2,1,0:T(8,128)(2,1)S(1)}, u32[]{:S(2)}, u32[]{:S(2)}) collective-permute-start(bf16[4,880,256]{2,1,0:T(8,128)(2,1)S(1)} %pad_maximum_fusion.share_ref), channel_id=1, source_target_pairs={{0,1},{1,0},{2,3},{3,2},{4,5},{5,4},{6,7},{7,6},{8,9},{9,8},{10,11... | collective-permute-start | bytes 5406728 | tf_op jit(solution)/shard_map/ppermute | solution.py:495
  41.0 12.1 %collective-permute-start.11 = (bf16[768,256]{1,0:T(8,128)(2,1)S(1)}, bf16[768,256]{1,0:T(8,128)(2,1)S(1)}, u32[]{:S(2)}, u32[]{:S(2)}) collective-permute-start(bf16[768,256]{1,0:T(8,128)(2,1)S(1)} %constant_dynamic-update-slice_fusion.5), channel_id=1, source_target_pairs={{0,2},{1,3},{2,0},{3,1},{4,6},{5,7},{6,4},{7,5},{8,10},{9,11},{10,... | collective-permute-start | bytes 1179656 | tf_op jit(solution)/shard_map/ppermute | solution.py:495
  42.3 11.2 %collective-permute-start.12 = (bf16[768,256]{1,0:T(8,128)(2,1)S(1)}, bf16[768,256]{1,0:T(8,128)(2,1)S(1)}, u32[]{:S(2)}, u32[]{:S(2)}) collective-permute-start(bf16[768,256]{1,0:T(8,128)(2,1)S(1)} %constant_dynamic-update-slice_fusion.5), channel_id=1, source_target_pairs={{0,4},{1,5},{2,6},{3,7},{4,0},{5,1},{6,2},{7,3},{8,12},{9,13},{10,... | collective-permute-start | bytes 1179656 | tf_op jit(solution)/shard_map/ppermute | solution.py:495
  43.1 8.7 %collective-permute-start.13 = (bf16[256,256]{1,0:T(8,128)(2,1)S(1)}, bf16[256,256]{1,0:T(8,128)(2,1)S(1)}, u32[]{:S(2)}, u32[]{:S(2)}) collective-permute-start(bf16[256,256]{1,0:T(8,128)(2,1)S(1)} %pad_maximum_fusion.7), channel_id=1, source_target_pairs={{0,8},{8,0},{16,24},{24,16},{1,9},{9,1},{17,25},{25,17},{2,10},{10... | collective-permute-start | bytes 393224 | tf_op jit(solution)/shard_map/ppermute | solution.py:495
  46.7 6.4 %collective-permute-start.14 = (bf16[256,256]{1,0:T(8,128)(2,1)S(1)}, bf16[256,256]{1,0:T(8,128)(2,1)S(1)}, u32[]{:S(2)}, u32[]{:S(2)}) collective-permute-start(bf16[256,256]{1,0:T(8,128)(2,1)S(1)} %collective-permute-done.9), channel_id=1, source_target_pairs={{0,8},{8,0},{16,24},{24,16},{1,9},{9,1},{17,25},{25,17},{2,10},{10... | collective-permute-start | bytes 393224 | tf_op jit(solution)/shard_map/ppermute | solution.py:495
  46.7 5.1 %copy-start.1 = (bf16[4,880,256]{2,1,0:T(8,128)(2,1)}, bf16[4,880,256]{2,1,0:T(8,128)(2,1)S(1)}, u32[]{:S(2)}) copy-start(bf16[4,880,256]{2,1,0:T(8,128)(2,1)S(1)} %collective-permute-done.10.other_ref) | copy-start | bytes 5406724
  53.8 6.5 %collective-permute-start.15 = (bf16[4,768,256]{2,1,0:T(8,128)(2,1)S(1)}, bf16[4,768,256]{2,1,0:T(8,128)(2,1)}, u32[]{:S(2)}, u32[]{:S(2)}) collective-permute-start(bf16[4,768,256]{2,1,0:T(8,128)(2,1)S(1)} %pad_maximum_fusion.1.late_share_ref), channel_id=1, source_target_pairs={{0,1},{1,0},{2,3},{3,2},{4,5},{5,4},{6,7},{7,6},{8,9},{9,8},{10,11... | collective-permute-start | bytes 4718600 | tf_op jit(solution)/shard_map/ppermute | solution.py:495
  53.9 20.1 %all-to-all-start = ((bf16[32,8,256]{2,1,0:T(8,128)(2,1)}), bf16[32,8,256]{2,1,0:T(8,128)(2,1)S(1)}, u32[]{:S(2)}, u32[]{:S(2)}) async-start(bf16[32,8,256]{2,1,0:T(8,128)(2,1)} %bitcast.19), calls=%async_computation | async-start | bytes 262144 | tf_op jit(solution)/shard_map/all_to_all | solution.py:490
  60.3 1.2 %copy-start.4 = (bf16[2,2048,128]{2,1,0:T(8,128)(2,1)S(1)}, bf16[2,2048,128]{2,1,0:T(8,128)(2,1)}, u32[]{:S(2)}) copy-start(bf16[2,2048,128]{2,1,0:T(8,128)(2,1)} %param.12) | copy-start | bytes 3145732
  61.5 18.3 %copy-start.5 = (s32[4,2]{0,1:T(2,128)S(1)}, s32[4,2]{0,1:T(2,128)}, u32[]{:S(2)}) copy-start(s32[4,2]{0,1:T(2,128)} %param.9) | copy-start | bytes 100
  74.0 21.4 %all-to-all-start.1 = ((bf16[32,8,1024]{2,1,0:T(8,128)(2,1)}), bf16[32,8,1024]{2,1,0:T(8,128)(2,1)S(1)}, u32[]{:S(2)}, u32[]{:S(2)}) async-start(bf16[32,8,1024]{2,1,0:T(8,128)(2,1)} %bitcast.21), calls=%async_computation.1 | async-start | bytes 1048576 | tf_op jit(solution)/shard_map/all_to_all | solution.py:490

commit v9 on v8

--- a/solution.py
+++ b/solution.py
@@ -654,7 +654,7 @@
             pltpu.SemaphoreType.DMA((1,)),
         ),
         48 << 20,
-        47 << 20,
+        48 << 20,
         1,
         0,
     )

time: 97.5 us -> 97.5 us (level)
  no operation moved by 1% of the time
where the time goes in v9:
time: 97.5 us; the launch traced here: 97 us
  waiting for transfers between devices  35.3 us (36%)
  starting transfers between devices  34 us (35%)
  Pallas kernels  19.1 us (20%)
  local copies, waits for them, and re-layouts  4.21 us (4%)
  other arithmetic  3.43 us (4%)
  between operations  0.98 us (1%)
    ppermute x16, starting transfers between devices, swapped(): return lax.ppermute(value, axis, pairs)  21.7 us
    ppermute x16, waiting for transfers between devices, swapped(): return lax.ppermute(value, axis, pairs)  19.8 us
    pallas_call x3, Pallas kernels, call(): pl.pallas_call(kernel, out_shape=outs, in_specs=[pl.BlockSpec(memory_spac...  19.1 us
    all_to_all x2, waiting for transfers between devices, exchange(): lax.all_to_all(blocks, ('pipe', 'dp'), split_axis=0, concat_axis=0, tiled...  15.4 us
    all_to_all x2, starting transfers between devices, exchange(): lax.all_to_all(blocks, ('pipe', 'dp'), split_axis=0, concat_axis=0, tiled...  12.2 us
  transfers between devices with their start and end apart: 18, of which 7 were waited for; matrix products, arithmetic and copies ran while one was open for 4% of the time, Pallas kernels for 18%

profile of v9, /device:TPU:0, one launch (start us, length us, event | category | flops | bytes accessed | tf_op | source)
XLA Modules:
  0.0 97.0 jit_solution(12428916064829896928)
XLA Ops:
  0.6 0.7 fusion.8
  1.4 0.9 dynamic-slice_bitcast_fusion.4
  2.3 0.8 constant_dynamic-slice_fusion.3
  3.2 3.1 %collective-permute-start = (bf16[280,256]{1,0:T(8,128)(2,1)S(1)}, bf16[280,256]{1,0:T(8,128)(2,1)S(1)}, u32[]{:S(2)}, u32[]{:S(2)}) collective-permute-start(bf16[280,256]{1,0:T(8,128)(2,1)S(1)} %get-tuple-element.67), channel_id=1, source_target_pairs={{0,8},{8,0},{16,24},{24,16},{1,9},{9,1},{17,25},{25,17},{2,10},{10... | collective-permute-start | bytes 430088 | tf_op jit(solution)/shard_map/ppermute | solution.py:495
  6.2 2.6 %collective-permute-start.1 = (bf16[280,256]{1,0:T(8,128)(2,1)S(1)}, bf16[280,256]{1,0:T(8,128)(2,1)S(1)}, u32[]{:S(2)}, u32[]{:S(2)}) collective-permute-start(bf16[280,256]{1,0:T(8,128)(2,1)S(1)} %get-tuple-element.66), channel_id=1, source_target_pairs={{0,16},{8,24},{16,0},{24,8},{1,17},{9,25},{17,1},{25,9},{2,18},{10... | collective-permute-start | bytes 430088 | tf_op jit(solution)/shard_map/ppermute | solution.py:495
  8.8 0.0 collective-permute-start.2
  8.8 0.8 dynamic-slice_convert_fusion.upstream_ref
  9.6 0.7 convert.19
  10.3 0.1 copy.16
  10.4 0.7 convert.18
  11.1 0.1 fusion.5
  11.2 1.0 dynamic-slice_bitcast_fusion
  12.2 0.0 collective-permute-done
  12.2 7.8 %collective-permute-done.1 = bf16[280,256]{1,0:T(8,128)(2,1)S(1)} collective-permute-done((bf16[280,256]{1,0:T(8,128)(2,1)S(1)}, bf16[280,256]{1,0:T(8,128)(2,1)S(1)}, u32[]{:S(2)}, u32[]{:S(2)}) %collective-permute-start.1) | collective-permute-done | bytes 143392 | tf_op jit(solution)/shard_map/ppermute | solution.py:495
  20.0 0.0 collective-permute-done.2
  20.1 1.6 %collective-permute-start.3 = (bf16[880,256]{1,0:T(8,128)(2,1)S(1)}, bf16[880,256]{1,0:T(8,128)(2,1)S(1)}, u32[]{:S(2)}, u32[]{:S(2)}) collective-permute-start(bf16[880,256]{1,0:T(8,128)(2,1)S(1)} %constant_dynamic-update-slice_fusion), channel_id=1, source_target_pairs={{0,2},{1,3},{2,0},{3,1},{4,6},{5,7},{6,4},{7,5},{8,10},{9,11},{10,... | collective-permute-start | bytes 1351688 | tf_op jit(solution)/shard_map/ppermute | solution.py:495
  21.6 1.5 %collective-permute-start.4 = (bf16[880,256]{1,0:T(8,128)(2,1)S(1)}, bf16[880,256]{1,0:T(8,128)(2,1)S(1)}, u32[]{:S(2)}, u32[]{:S(2)}) collective-permute-start(bf16[880,256]{1,0:T(8,128)(2,1)S(1)} %constant_dynamic-update-slice_fusion), channel_id=1, source_target_pairs={{0,4},{1,5},{2,6},{3,7},{4,0},{5,1},{6,2},{7,3},{8,12},{9,13},{10,... | collective-permute-start | bytes 1351688 | tf_op jit(solution)/shard_map/ppermute | solution.py:495
  23.2 0.5 collective-permute-start.5
  23.6 3.2 %collective-permute-start.7 = (bf16[256,256]{1,0:T(8,128)(2,1)S(1)}, bf16[256,256]{1,0:T(8,128)(2,1)S(1)}, u32[]{:S(2)}, u32[]{:S(2)}) collective-permute-start(bf16[256,256]{1,0:T(8,128)(2,1)S(1)} %pad_maximum_fusion.6), channel_id=1, source_target_pairs={{0,16},{8,24},{16,0},{24,8},{1,17},{9,25},{17,1},{25,9},{2,18},{10... | collective-permute-start | bytes 393224 | tf_op jit(solution)/shard_map/ppermute | solution.py:495
  26.8 0.0 collective-permute-start.6
  26.8 4.7 %collective-permute-done.7 = bf16[256,256]{1,0:T(8,128)(2,1)S(1)} collective-permute-done((bf16[256,256]{1,0:T(8,128)(2,1)S(1)}, bf16[256,256]{1,0:T(8,128)(2,1)S(1)}, u32[]{:S(2)}, u32[]{:S(2)}) %collective-permute-start.7) | collective-permute-done | bytes 131104 | tf_op jit(solution)/shard_map/ppermute | solution.py:495
  31.5 0.3 collective-permute-start.8
  31.8 1.6 %collective-permute-done.3 = bf16[880,256]{1,0:T(8,128)(2,1)S(1)} collective-permute-done((bf16[880,256]{1,0:T(8,128)(2,1)S(1)}, bf16[880,256]{1,0:T(8,128)(2,1)S(1)}, u32[]{:S(2)}, u32[]{:S(2)}) %collective-permute-start.3) | collective-permute-done | bytes 450592 | tf_op jit(solution)/shard_map/ppermute | solution.py:495
  33.4 3.2 %collective-permute-start.9 = (bf16[256,256]{1,0:T(8,128)(2,1)S(1)}, bf16[256,256]{1,0:T(8,128)(2,1)S(1)}, u32[]{:S(2)}, u32[]{:S(2)}) collective-permute-start(bf16[256,256]{1,0:T(8,128)(2,1)S(1)} %pad_maximum_fusion.7), channel_id=1, source_target_pairs={{0,16},{8,24},{16,0},{24,8},{1,17},{9,25},{17,1},{25,9},{2,18},{10... | collective-permute-start | bytes 393224 | tf_op jit(solution)/shard_map/ppermute | solution.py:495
  36.6 4.0 %collective-permute-done.4 = bf16[880,256]{1,0:T(8,128)(2,1)S(1)} collective-permute-done((bf16[880,256]{1,0:T(8,128)(2,1)S(1)}, bf16[880,256]{1,0:T(8,128)(2,1)S(1)}, u32[]{:S(2)}, u32[]{:S(2)}) %collective-permute-start.4) | collective-permute-done | bytes 450592 | tf_op jit(solution)/shard_map/ppermute | solution.py:495
  40.6 0.0 collective-permute-done.5
  40.6 0.0 copy-start.2
  40.6 0.0 copy-start.3
  40.6 0.2 pad_maximum_fusion.share_ref
  40.8 0.0 copy-start
  40.9 0.0 collective-permute-done.6
  40.9 0.0 collective-permute-done.8
  40.9 0.0 collective-permute-done.9
  40.9 0.1 collective-permute-start.10
  41.0 1.3 %collective-permute-start.11 = (bf16[768,256]{1,0:T(8,128)(2,1)S(1)}, bf16[768,256]{1,0:T(8,128)(2,1)S(1)}, u32[]{:S(2)}, u32[]{:S(2)}) collective-permute-start(bf16[768,256]{1,0:T(8,128)(2,1)S(1)} %constant_dynamic-update-slice_fusion.5), channel_id=1, source_target_pairs={{0,2},{1,3},{2,0},{3,1},{4,6},{5,7},{6,4},{7,5},{8,10},{9,11},{10,... | collective-permute-start | bytes 1179656 | tf_op jit(solution)/shard_map/ppermute | solution.py:495
  42.3 0.8 collective-permute-start.12
  43.1 3.5 %collective-permute-start.13 = (bf16[256,256]{1,0:T(8,128)(2,1)S(1)}, bf16[256,256]{1,0:T(8,128)(2,1)S(1)}, u32[]{:S(2)}, u32[]{:S(2)}) collective-permute-start(bf16[256,256]{1,0:T(8,128)(2,1)S(1)} %pad_maximum_fusion.7), channel_id=1, source_target_pairs={{0,8},{8,0},{16,24},{24,16},{1,9},{9,1},{17,25},{25,17},{2,10},{10... | collective-permute-start | bytes 393224 | tf_op jit(solution)/shard_map/ppermute | solution.py:495
  46.7 0.0 collective-permute-start.14
  46.7 0.0 collective-permute-done.10.other_ref
  46.7 0.0 copy-start.1
  46.7 0.0 copy-done.2
  46.7 0.0 copy-done.3
  46.7 5.1 %shard_map.94 = (f32[7,8,2560]{2,1,0:T(8,128)S(1)}, bf16[4,8,8,256]{3,2,1,0:T(8,128)(2,1)}) custom-call(f32[8,2048]{1,0:T(8,128)S(1)} %dynamic-slice_convert_fusion.upstream_ref, bf16[2,8,256,128]{3,2,1,0:T(8,128)(2,1)S(1)} %bitcast.33, bf16[2,8,256,128]{3,2,1,0:T(8,128)(2,1)S(1)} %bitcast.35, bf16[4,880,256]{2,1,0:T(8,128)(2,1)S(1)} %pad_maximum_fusion.share_ref, ...), custom_call_target="tpu_custom_call" | custom-call | bytes 18874368 | tf_op jit(solution)/shard_map/pallas_call | solution.py:475
  51.8 0.0 copy-done
  51.8 0.0 copy-done.1
  51.8 0.0 collective-permute-done.13
  51.8 1.3 %collective-permute-done.14 = bf16[256,256]{1,0:T(8,128)(2,1)S(1)} collective-permute-done((bf16[256,256]{1,0:T(8,128)(2,1)S(1)}, bf16[256,256]{1,0:T(8,128)(2,1)S(1)}, u32[]{:S(2)}, u32[]{:S(2)}) %collective-permute-start.14) | collective-permute-done | bytes 131104 | tf_op jit(solution)/shard_map/ppermute | solution.py:495
  53.1 0.0 collective-permute-done.11
  53.1 0.5 collective-permute-done.12
  53.6 0.2 pad_maximum_fusion.1.late_share_ref
  53.8 0.1 collective-permute-start.15
  53.9 6.4 %all-to-all-start = ((bf16[32,8,256]{2,1,0:T(8,128)(2,1)}), bf16[32,8,256]{2,1,0:T(8,128)(2,1)S(1)}, u32[]{:S(2)}, u32[]{:S(2)}) async-start(bf16[32,8,256]{2,1,0:T(8,128)(2,1)} %bitcast.19), calls=%async_computation | async-start | bytes 262144 | tf_op jit(solution)/shard_map/all_to_all | solution.py:490
  60.3 0.0 collective-permute-done.15.late_other_ref
  60.3 0.0 copy-start.4
  60.3 1.2 %copy-done.4 = bf16[2,2048,128]{2,1,0:T(8,128)(2,1)S(1)} copy-done((bf16[2,2048,128]{2,1,0:T(8,128)(2,1)S(1)}, bf16[2,2048,128]{2,1,0:T(8,128)(2,1)}, u32[]{:S(2)}) %copy-start.4) | copy-done | bytes 1048600
  61.5 0.0 copy-start.5
  61.5 12.5 %shard_map.95 = bf16[4,8,8,1024]{3,2,1,0:T(8,128)(2,1)} custom-call(f32[7,8,2560]{2,1,0:T(8,128)S(1)} %get-tuple-element.49.state_in, bf16[2,8,256,128]{3,2,1,0:T(8,128)(2,1)S(1)} %bitcast.34, bf16[2,8,256,128]{3,2,1,0:T(8,128)(2,1)S(1)} %bitcast.36, bf16[4,880,256]{2,1,0:T(8,128)(2,1)} %copy-done, bf16[4,880,256]{2,1,0:T(8,128)(2,1)} %copy-done.1, ...), custom_call_target="tpu_custom_call" | custom-call | bytes 50331648 | tf_op jit(solution)/shard_map/pallas_call | solution.py:475
  74.0 0.0 all-to-all-done
  74.0 5.8 %all-to-all-start.1 = ((bf16[32,8,1024]{2,1,0:T(8,128)(2,1)}), bf16[32,8,1024]{2,1,0:T(8,128)(2,1)S(1)}, u32[]{:S(2)}, u32[]{:S(2)}) async-start(bf16[32,8,1024]{2,1,0:T(8,128)(2,1)} %bitcast.21), calls=%async_computation.1 | async-start | bytes 1048576 | tf_op jit(solution)/shard_map/all_to_all | solution.py:490
  79.8 0.0 copy-done.5
  79.8 0.1 copy.18.route_ref
  79.9 15.4 %all-to-all-done.1 = bf16[32,8,1024]{2,1,0:T(8,128)(2,1)S(1)} async-done(((bf16[32,8,1024]{2,1,0:T(8,128)(2,1)}), bf16[32,8,1024]{2,1,0:T(8,128)(2,1)S(1)}, u32[]{:S(2)}, u32[]{:S(2)}) %all-to-all-start.1) | async-done | bytes 524320 | tf_op jit(solution)/shard_map/all_to_all | solution.py:490
  95.4 1.6 %shard_map.96 = (bf16[32,512]{1,0:T(8,128)(2,1)}, f32[2,256,128]{2,1,0:T(8,128)}, f32[2,256,128]{2,1,0:T(8,128)}) custom-call(s32[4,2]{1,0:T(4,128)S(1)} %copy.18.route_ref, bf16[256,256]{1,0:T(8,128)(2,1)S(1)} %bitcast.38, bf16[256,1024]{1,0:T(8,128)(2,1)S(1)} %bitcast.37), custom_call_target="tpu_custom_call" | custom-call | tf_op jit(solution)/shard_map/pallas_call | solution.py:475
  (20 shorter events, 0.2 us)
Async XLA Ops:
  3.2 9.0 %collective-permute-start = (bf16[280,256]{1,0:T(8,128)(2,1)S(1)}, bf16[280,256]{1,0:T(8,128)(2,1)S(1)}, u32[]{:S(2)}, u32[]{:S(2)}) collective-permute-start(bf16[280,256]{1,0:T(8,128)(2,1)S(1)} %get-tuple-element.67), channel_id=1, source_target_pairs={{0,8},{8,0},{16,24},{24,16},{1,9},{9,1},{17,25},{25,17},{2,10},{10... | collective-permute-start | bytes 430088 | tf_op jit(solution)/shard_map/ppermute | solution.py:495
  6.2 13.7 %collective-permute-start.1 = (bf16[280,256]{1,0:T(8,128)(2,1)S(1)}, bf16[280,256]{1,0:T(8,128)(2,1)S(1)}, u32[]{:S(2)}, u32[]{:S(2)}) collective-permute-start(bf16[280,256]{1,0:T(8,128)(2,1)S(1)} %get-tuple-element.66), channel_id=1, source_target_pairs={{0,16},{8,24},{16,0},{24,8},{1,17},{9,25},{17,1},{25,9},{2,18},{10... | collective-permute-start | bytes 430088 | tf_op jit(solution)/shard_map/ppermute | solution.py:495
  8.8 11.2 %collective-permute-start.2 = (bf16[280,256]{1,0:T(8,128)(2,1)S(1)}, bf16[280,256]{1,0:T(8,128)(2,1)S(1)}, u32[]{:S(2)}, u32[]{:S(2)}) collective-permute-start(bf16[280,256]{1,0:T(8,128)(2,1)S(1)} %get-tuple-element.65), channel_id=1, source_target_pairs={{0,24},{8,16},{16,8},{24,0},{1,25},{9,17},{17,9},{25,1},{2,26},{10... | collective-permute-start | bytes 430088 | tf_op jit(solution)/shard_map/ppermute | solution.py:495
  20.1 13.3 %collective-permute-start.3 = (bf16[880,256]{1,0:T(8,128)(2,1)S(1)}, bf16[880,256]{1,0:T(8,128)(2,1)S(1)}, u32[]{:S(2)}, u32[]{:S(2)}) collective-permute-start(bf16[880,256]{1,0:T(8,128)(2,1)S(1)} %constant_dynamic-update-slice_fusion), channel_id=1, source_target_pairs={{0,2},{1,3},{2,0},{3,1},{4,6},{5,7},{6,4},{7,5},{8,10},{9,11},{10,... | collective-permute-start | bytes 1351688 | tf_op jit(solution)/shard_map/ppermute | solution.py:495
  21.6 19.0 %collective-permute-start.4 = (bf16[880,256]{1,0:T(8,128)(2,1)S(1)}, bf16[880,256]{1,0:T(8,128)(2,1)S(1)}, u32[]{:S(2)}, u32[]{:S(2)}) collective-permute-start(bf16[880,256]{1,0:T(8,128)(2,1)S(1)} %constant_dynamic-update-slice_fusion), channel_id=1, source_target_pairs={{0,4},{1,5},{2,6},{3,7},{4,0},{5,1},{6,2},{7,3},{8,12},{9,13},{10,... | collective-permute-start | bytes 1351688 | tf_op jit(solution)/shard_map/ppermute | solution.py:495
  23.2 17.4 %collective-permute-start.5 = (bf16[880,256]{1,0:T(8,128)(2,1)S(1)}, bf16[880,256]{1,0:T(8,128)(2,1)S(1)}, u32[]{:S(2)}, u32[]{:S(2)}) collective-permute-start(bf16[880,256]{1,0:T(8,128)(2,1)S(1)} %constant_dynamic-update-slice_fusion), channel_id=1, source_target_pairs={{0,6},{1,7},{2,4},{3,5},{4,2},{5,3},{6,0},{7,1},{8,14},{9,15},{10,... | collective-permute-start | bytes 1351688 | tf_op jit(solution)/shard_map/ppermute | solution.py:495
  23.6 7.9 %collective-permute-start.7 = (bf16[256,256]{1,0:T(8,128)(2,1)S(1)}, bf16[256,256]{1,0:T(8,128)(2,1)S(1)}, u32[]{:S(2)}, u32[]{:S(2)}) collective-permute-start(bf16[256,256]{1,0:T(8,128)(2,1)S(1)} %pad_maximum_fusion.6), channel_id=1, source_target_pairs={{0,16},{8,24},{16,0},{24,8},{1,17},{9,25},{17,1},{25,9},{2,18},{10... | collective-permute-start | bytes 393224 | tf_op jit(solution)/shard_map/ppermute | solution.py:495
  26.8 14.0 %collective-permute-start.6 = (bf16[256,256]{1,0:T(8,128)(2,1)S(1)}, bf16[256,256]{1,0:T(8,128)(2,1)S(1)}, u32[]{:S(2)}, u32[]{:S(2)}) collective-permute-start(bf16[256,256]{1,0:T(8,128)(2,1)S(1)} %pad_maximum_fusion.6), channel_id=1, source_target_pairs={{0,8},{8,0},{16,24},{24,16},{1,9},{9,1},{17,25},{25,17},{2,10},{10... | collective-permute-start | bytes 393224 | tf_op jit(solution)/shard_map/ppermute | solution.py:495
  31.5 9.4 %collective-permute-start.8 = (bf16[256,256]{1,0:T(8,128)(2,1)S(1)}, bf16[256,256]{1,0:T(8,128)(2,1)S(1)}, u32[]{:S(2)}, u32[]{:S(2)}) collective-permute-start(bf16[256,256]{1,0:T(8,128)(2,1)S(1)} %collective-permute-done.7), channel_id=1, source_target_pairs={{0,8},{8,0},{16,24},{24,16},{1,9},{9,1},{17,25},{25,17},{2,10},{10... | collective-permute-start | bytes 393224 | tf_op jit(solution)/shard_map/ppermute | solution.py:495
  33.4 7.4 %collective-permute-start.9 = (bf16[256,256]{1,0:T(8,128)(2,1)S(1)}, bf16[256,256]{1,0:T(8,128)(2,1)S(1)}, u32[]{:S(2)}, u32[]{:S(2)}) collective-permute-start(bf16[256,256]{1,0:T(8,128)(2,1)S(1)} %pad_maximum_fusion.7), channel_id=1, source_target_pairs={{0,16},{8,24},{16,0},{24,8},{1,17},{9,25},{17,1},{25,9},{2,18},{10... | collective-permute-start | bytes 393224 | tf_op jit(solution)/shard_map/ppermute | solution.py:495
  40.6 6.1 %copy-start.2 = (bf16[2,2048,128]{2,1,0:T(8,128)(2,1)S(1)}, bf16[2,2048,128]{2,1,0:T(8,128)(2,1)}, u32[]{:S(2)}) copy-start(bf16[2,2048,128]{2,1,0:T(8,128)(2,1)} %param.11) | copy-start | bytes 3145732
  40.6 6.1 %copy-start.3 = (bf16[2,2048,128]{2,1,0:T(8,128)(2,1)S(1)}, bf16[2,2048,128]{2,1,0:T(8,128)(2,1)}, u32[]{:S(2)}) copy-start(bf16[2,2048,128]{2,1,0:T(8,128)(2,1)} %param.12) | copy-start | bytes 3145732
  40.8 10.9 %copy-start = (bf16[4,880,256]{2,1,0:T(8,128)(2,1)}, bf16[4,880,256]{2,1,0:T(8,128)(2,1)S(1)}, u32[]{:S(2)}) copy-start(bf16[4,880,256]{2,1,0:T(8,128)(2,1)S(1)} %pad_maximum_fusion.share_ref) | copy-start | bytes 5406724
  40.9 5.8 %collective-permute-start.10 = (bf16[4,880,256]{2,1,0:T(8,128)(2,1)S(1)}, bf16[4,880,256]{2,1,0:T(8,128)(2,1)S(1)}, u32[]{:S(2)}, u32[]{:S(2)}) collective-permute-start(bf16[4,880,256]{2,1,0:T(8,128)(2,1)S(1)} %pad_maximum_fusion.share_ref), channel_id=1, source_target_pairs={{0,1},{1,0},{2,3},{3,2},{4,5},{5,4},{6,7},{7,6},{8,9},{9,8},{10,11... | collective-permute-start | bytes 5406728 | tf_op jit(solution)/shard_map/ppermute | solution.py:495
  41.0 12.1 %collective-permute-start.11 = (bf16[768,256]{1,0:T(8,128)(2,1)S(1)}, bf16[768,256]{1,0:T(8,128)(2,1)S(1)}, u32[]{:S(2)}, u32[]{:S(2)}) collective-permute-start(bf16[768,256]{1,0:T(8,128)(2,1)S(1)} %constant_dynamic-update-slice_fusion.5), channel_id=1, source_target_pairs={{0,2},{1,3},{2,0},{3,1},{4,6},{5,7},{6,4},{7,5},{8,10},{9,11},{10,... | collective-permute-start | bytes 1179656 | tf_op jit(solution)/shard_map/ppermute | solution.py:495
  42.3 11.2 %collective-permute-start.12 = (bf16[768,256]{1,0:T(8,128)(2,1)S(1)}, bf16[768,256]{1,0:T(8,128)(2,1)S(1)}, u32[]{:S(2)}, u32[]{:S(2)}) collective-permute-start(bf16[768,256]{1,0:T(8,128)(2,1)S(1)} %constant_dynamic-update-slice_fusion.5), channel_id=1, source_target_pairs={{0,4},{1,5},{2,6},{3,7},{4,0},{5,1},{6,2},{7,3},{8,12},{9,13},{10,... | collective-permute-start | bytes 1179656 | tf_op jit(solution)/shard_map/ppermute | solution.py:495
  43.1 8.7 %collective-permute-start.13 = (bf16[256,256]{1,0:T(8,128)(2,1)S(1)}, bf16[256,256]{1,0:T(8,128)(2,1)S(1)}, u32[]{:S(2)}, u32[]{:S(2)}) collective-permute-start(bf16[256,256]{1,0:T(8,128)(2,1)S(1)} %pad_maximum_fusion.7), channel_id=1, source_target_pairs={{0,8},{8,0},{16,24},{24,16},{1,9},{9,1},{17,25},{25,17},{2,10},{10... | collective-permute-start | bytes 393224 | tf_op jit(solution)/shard_map/ppermute | solution.py:495
  46.7 6.4 %collective-permute-start.14 = (bf16[256,256]{1,0:T(8,128)(2,1)S(1)}, bf16[256,256]{1,0:T(8,128)(2,1)S(1)}, u32[]{:S(2)}, u32[]{:S(2)}) collective-permute-start(bf16[256,256]{1,0:T(8,128)(2,1)S(1)} %collective-permute-done.9), channel_id=1, source_target_pairs={{0,8},{8,0},{16,24},{24,16},{1,9},{9,1},{17,25},{25,17},{2,10},{10... | collective-permute-start | bytes 393224 | tf_op jit(solution)/shard_map/ppermute | solution.py:495
  46.7 5.1 %copy-start.1 = (bf16[4,880,256]{2,1,0:T(8,128)(2,1)}, bf16[4,880,256]{2,1,0:T(8,128)(2,1)S(1)}, u32[]{:S(2)}) copy-start(bf16[4,880,256]{2,1,0:T(8,128)(2,1)S(1)} %collective-permute-done.10.other_ref) | copy-start | bytes 5406724
  53.8 6.5 %collective-permute-start.15 = (bf16[4,768,256]{2,1,0:T(8,128)(2,1)S(1)}, bf16[4,768,256]{2,1,0:T(8,128)(2,1)}, u32[]{:S(2)}, u32[]{:S(2)}) collective-permute-start(bf16[4,768,256]{2,1,0:T(8,128)(2,1)S(1)} %pad_maximum_fusion.1.late_share_ref), channel_id=1, source_target_pairs={{0,1},{1,0},{2,3},{3,2},{4,5},{5,4},{6,7},{7,6},{8,9},{9,8},{10,11... | collective-permute-start | bytes 4718600 | tf_op jit(solution)/shard_map/ppermute | solution.py:495
  53.9 20.1 %all-to-all-start = ((bf16[32,8,256]{2,1,0:T(8,128)(2,1)}), bf16[32,8,256]{2,1,0:T(8,128)(2,1)S(1)}, u32[]{:S(2)}, u32[]{:S(2)}) async-start(bf16[32,8,256]{2,1,0:T(8,128)(2,1)} %bitcast.19), calls=%async_computation | async-start | bytes 262144 | tf_op jit(solution)/shard_map/all_to_all | solution.py:490
  60.3 1.2 %copy-start.4 = (bf16[2,2048,128]{2,1,0:T(8,128)(2,1)S(1)}, bf16[2,2048,128]{2,1,0:T(8,128)(2,1)}, u32[]{:S(2)}) copy-start(bf16[2,2048,128]{2,1,0:T(8,128)(2,1)} %param.12) | copy-start | bytes 3145732
  61.5 18.3 %copy-start.5 = (s32[4,2]{0,1:T(2,128)S(1)}, s32[4,2]{0,1:T(2,128)}, u32[]{:S(2)}) copy-start(s32[4,2]{0,1:T(2,128)} %param.9) | copy-start | bytes 100
  74.0 21.4 %all-to-all-start.1 = ((bf16[32,8,1024]{2,1,0:T(8,128)(2,1)}), bf16[32,8,1024]{2,1,0:T(8,128)(2,1)S(1)}, u32[]{:S(2)}, u32[]{:S(2)}) async-start(bf16[32,8,1024]{2,1,0:T(8,128)(2,1)} %bitcast.21), calls=%async_computation.1 | async-start | bytes 1048576 | tf_op jit(solution)/shard_map/all_to_all | solution.py:490
